TPU v7x, 32 devices: a whole 2x2x4 slice. The times are simulated.
32 devices in a mesh: gx: 4 (over y, core), gy: 8 (over z, x).
Axes of the slice: x: 2, y: 2, z: 4, core: 2. Of those that a mesh axis runs over, the one named last changes fastest.
Arguments:
- hidden_in: bfloat16 [16384, 768], P(('gx', 'gy')), may hold values from -6 to 6
- route: int32 [16384, 1], P(('gx', 'gy')), may hold values from 0 to 7; in each aligned block of 512 rows (0 to 511, 512 to 1023, ...) at most 128 rows name the same one
- piece_ids: int32 [16384], P(('gx', 'gy')), may hold values from 0 to 1, as said below
- buckets: int32 [1023], replicated, may hold values from 0 to 31
- rel_table: bfloat16 [32, 12], replicated, may hold values from -4 to 4
- gain_attn: bfloat16 [2, 768], replicated, may hold values from 0.25 to 1.75
- gain_ffn: bfloat16 [2, 768], replicated, may hold values from 0.25 to 1.75
- w_query: bfloat16 [2, 768, 768], P(None, 'gx', 'gy'), may hold values from -0.21875 to 0.21875
- w_key: bfloat16 [2, 768, 768], P(None, 'gx', 'gy'), may hold values from -0.21875 to 0.21875
- w_value: bfloat16 [2, 768, 768], P(None, 'gx', 'gy'), may hold values from -0.21875 to 0.21875
- w_output: bfloat16 [2, 768, 768], P(None, 'gx', 'gy'), may hold values from -0.875 to 0.875
- w_router: bfloat16 [2, 768, 8], P(None, 'gx', 'gy'), may hold values from -0.15625 to 0.15625
- w_in: bfloat16 [2, 8, 768, 3072], P(None, 'gy', None, 'gx'), may hold values from -0.21875 to 0.21875
- w_out: bfloat16 [2, 8, 768, 3072], P(None, 'gy', None, 'gx'), may hold values from -1.5 to 1.5
- cotangent: bfloat16 [16384, 768], P(('gx', 'gy')), may hold values from -6 to 6
Outputs:
- hidden_out: float32 [16384, 768], P(('gx', 'gy'))
- grad_input: float32 [16384, 768], P(('gx', 'gy'))
- grad_rel_table: float32 [32, 12], replicated
- grad_gain_attn: float32 [2, 768], replicated
- grad_gain_ffn: float32 [2, 768], replicated
- grad_w_query: float32 [2, 768, 768], P(None, 'gx', 'gy')
- grad_w_key: float32 [2, 768, 768], P(None, 'gx', 'gy')
- grad_w_value: float32 [2, 768, 768], P(None, 'gx', 'gy')
- grad_w_output: float32 [2, 768, 768], P(None, 'gx', 'gy')
- grad_w_router: float32 [2, 768, 8], P(None, 'gx', 'gy')
- grad_w_in: float32 [2, 8, 768, 3072], P(None, 'gy', None, 'gx')
- grad_w_out: float32 [2, 8, 768, 3072], P(None, 'gy', None, 'gx')
Inputs may be any that keep to these rules, and one draw needn't show every extreme that they name: `route`: within the rows of one device (aligned blocks of 512 tokens, one sequence), no expert is named by more than 128 tokens. `piece_ids`: each sequence is cut into windows of 512 tokens; window w of a sequence holds one picture piece of exactly 256 consecutive tokens with id w + 1, at an offset of 0 to 256 within it; all other tokens have id 0.
All inputs are finite; a program needn't handle non-finite values.
Results may differ from a plain program's by a relative error of at most 0.025.
Values may be sent and summed in bfloat16 or wider, within the bound.
A program may use at most 320 MiB of HBM per device.

v0:
```python
from functools import partial

import jax
import jax.numpy as jnp
from jax import lax
from jax.sharding import PartitionSpec as P

eps_norm = 1e-06
block_limit = 512
highest = lax.Precision.HIGHEST


def rms_scale(hidden, gain_vec):
    return (
        hidden * lax.rsqrt(jnp.mean(hidden * hidden, axis=-1, keepdims=True) + eps_norm) * gain_vec
    )


def gelu_tanh(pre_vals):
    return jax.nn.gelu(pre_vals, approximate=True)


def gate_of(chosen_f, logits):
    return jnp.sum(jax.nn.softmax(logits, axis=-1) * chosen_f, axis=1)


def unblock(stacked, grid_count_first, grid_count_second):
    height = stacked.shape[1]
    breadth = stacked.shape[2]
    parted = stacked.reshape(grid_count_first, grid_count_second, height, breadth)
    return parted.transpose(0, 2, 1, 3).reshape(
        grid_count_first * height, grid_count_second * breadth
    )


def regroup_blocks(weight_matrix, grid_count_first, grid_count_second):
    height = weight_matrix.shape[0] // grid_count_first
    breadth = weight_matrix.shape[1] // grid_count_second
    parted = weight_matrix.reshape(grid_count_first, height, grid_count_second, breadth)
    return parted.transpose(0, 2, 1, 3).reshape(
        grid_count_first * grid_count_second, height, breadth
    )


def offset_table(bucket_row, bias_table):
    return jnp.take(bias_table.astype(jnp.float32), bucket_row, axis=0).T


def block_terms(piece_row, row_start, row_count, offset_bias):
    seq_len = piece_row.shape[0]
    row_pos = row_start + jnp.arange(row_count, dtype=jnp.int32)
    col_pos = jnp.arange(seq_len, dtype=jnp.int32)
    allowed = (col_pos[None, :] <= row_pos[:, None]) | (
        piece_row[:, None] == piece_row[None, :]
    ) & (piece_row[:, None] > 0)
    rel_bias = jnp.take(offset_bias, row_pos[:, None] - col_pos[None, :] + (seq_len - 1), axis=1)
    return (allowed, rel_bias)


def diagonal_sums(values):
    num_heads, row_count, seq_len = values.shape
    width_new = seq_len + row_count - 1
    flipped = values[:, :, ::-1]
    padded = jnp.pad(flipped, ((0, 0), (0, 0), (0, row_count)))
    flat = padded.reshape(num_heads, row_count * (seq_len + row_count))[:, : row_count * width_new]
    return jnp.sum(flat.reshape(num_heads, row_count, width_new), axis=1)


def attend_forward(q_low, k_low, v_low, piece_row, bucket_row, bias_table, attn_scale):
    seq_len, num_heads, head_dim = q_low.shape
    rows_blk = min(block_limit, seq_len)
    offset_bias = offset_table(bucket_row, bias_table)

    def one_block(row_start):
        allowed, rel_bias = block_terms(piece_row, row_start, rows_blk, offset_bias)
        scores = (
            jnp.einsum("qhd,khd->hqk", q_low, k_low, preferred_element_type=jnp.float32)
            * attn_scale
            + rel_bias
        )
        scores = jnp.where(allowed[None], scores, -jnp.inf)
        row_max = jnp.max(scores, axis=-1, keepdims=True)
        raised = jnp.exp(scores - row_max)
        row_sum = jnp.sum(raised, axis=-1, keepdims=True)
        probs_low = (raised / row_sum).astype(jnp.bfloat16)
        attended = jnp.einsum("hqk,khd->qhd", probs_low, v_low, preferred_element_type=jnp.float32)
        return (attended, (row_max + jnp.log(row_sum))[:, :, 0])

    starts = jnp.arange(seq_len // rows_blk, dtype=jnp.int32) * rows_blk
    attended, log_sums = lax.map(one_block, starts)
    return (attended.reshape(seq_len, num_heads * head_dim), log_sums)


def attend_backward(
    q_low, k_low, v_low, d_out, log_sums, piece_row, bucket_row, bias_table, attn_scale
):
    seq_len, num_heads, head_dim = q_low.shape
    rows_blk = min(block_limit, seq_len)
    offset_bias = offset_table(bucket_row, bias_table)

    def one_block(carried, inputs):
        d_keys, d_values, d_offsets = carried
        row_start, lse_blk = inputs
        allowed, rel_bias = block_terms(piece_row, row_start, rows_blk, offset_bias)
        scores = (
            jnp.einsum("qhd,khd->hqk", q_low, k_low, preferred_element_type=jnp.float32)
            * attn_scale
            + rel_bias
        )
        scores = jnp.where(allowed[None], scores, -jnp.inf)
        probs_now = jnp.exp(scores - lse_blk[:, :, None])
        d_values = d_values + jnp.einsum(
            "hqk,qhd->khd",
            probs_now.astype(jnp.bfloat16),
            d_out,
            preferred_element_type=jnp.float32,
        )
        d_probs = jnp.einsum("qhd,khd->hqk", d_out, v_low, preferred_element_type=jnp.float32)
        inner_sum = jnp.sum(probs_now * d_probs, axis=-1, keepdims=True)
        d_scores = (probs_now * (d_probs - inner_sum)).astype(jnp.bfloat16)
        d_query = (
            jnp.einsum("hqk,khd->qhd", d_scores, k_low, preferred_element_type=jnp.float32)
            * attn_scale
        )
        d_keys = (
            d_keys
            + jnp.einsum("hqk,qhd->khd", d_scores, q_low, preferred_element_type=jnp.float32)
            * attn_scale
        )
        sums_here = diagonal_sums(d_scores.astype(jnp.float32))
        present = d_offsets
        d_offsets = present + sums_here
        return ((d_keys, d_values, d_offsets), d_query)

    starts = jnp.arange(seq_len // rows_blk, dtype=jnp.int32) * rows_blk
    zeros_kv = jnp.zeros((seq_len, num_heads, head_dim), jnp.float32)
    zeros_offsets = jnp.zeros((num_heads, 2 * seq_len - 1), jnp.float32)
    carried, d_query = lax.scan(one_block, (zeros_kv, zeros_kv, zeros_offsets), (starts, log_sums))
    bucket_onehot = (
        bucket_row[:, None] == jnp.arange(bias_table.shape[0], dtype=jnp.int32)[None, :]
    ).astype(jnp.float32)
    d_table = jnp.dot(carried[2], bucket_onehot, precision=highest).T
    return (d_query.reshape(seq_len, num_heads, head_dim), carried[0], carried[1], d_table)


def body(
    hidden_in,
    route,
    piece_ids,
    buckets,
    rel_table,
    gain_attn,
    gain_ffn,
    w_query,
    w_key,
    w_value,
    w_output,
    w_router,
    w_in,
    w_out,
    cotangent,
):
    grid_count_first = lax.axis_size("gx")
    grid_count_second = lax.axis_size("gy")
    seq_len, feat_width = hidden_in.shape
    num_layers = w_query.shape[0]
    num_heads = rel_table.shape[1]
    head_dim = feat_width // num_heads
    attn_scale = head_dim ** (-0.5)
    num_experts = w_router.shape[2] * grid_count_second
    capacity = 2 * seq_len // num_experts
    expert_of = route[:, 0]
    chosen = (expert_of[:, None] == jnp.arange(num_experts, dtype=jnp.int32)[None, :]).astype(
        jnp.int32
    )
    ranked = jnp.sum((jnp.cumsum(chosen, axis=0) - 1) * chosen, axis=1)
    slot_of = ranked * num_experts + expert_of
    placing = (
        slot_of[:, None] == jnp.arange(capacity * num_experts, dtype=jnp.int32)[None, :]
    ).astype(jnp.bfloat16)
    chosen_f = chosen.astype(jnp.float32)
    hidden = hidden_in.astype(jnp.float32)
    kept_state = []
    for layer_idx in range(num_layers):
        fetched = (
            lax.all_gather(w_query[layer_idx][None], ("gx", "gy"), axis=0, tiled=True),
            lax.all_gather(w_key[layer_idx][None], ("gx", "gy"), axis=0, tiled=True),
            lax.all_gather(w_value[layer_idx][None], ("gx", "gy"), axis=0, tiled=True),
            lax.all_gather(w_output[layer_idx][None], ("gx", "gy"), axis=0, tiled=True),
            lax.all_gather(w_router[layer_idx][None], ("gx", "gy"), axis=0, tiled=True),
        )
        full_mats = [
            unblock(group_member, grid_count_first, grid_count_second) for group_member in fetched
        ]
        normed_low = rms_scale(hidden, gain_attn[layer_idx].astype(jnp.float32)).astype(
            jnp.bfloat16
        )
        q_low = (
            jnp.dot(normed_low, full_mats[0], preferred_element_type=jnp.float32)
            .astype(jnp.bfloat16)
            .reshape(seq_len, num_heads, head_dim)
        )
        k_low = (
            jnp.dot(normed_low, full_mats[1], preferred_element_type=jnp.float32)
            .astype(jnp.bfloat16)
            .reshape(seq_len, num_heads, head_dim)
        )
        v_low = (
            jnp.dot(normed_low, full_mats[2], preferred_element_type=jnp.float32)
            .astype(jnp.bfloat16)
            .reshape(seq_len, num_heads, head_dim)
        )
        attended, log_sums = attend_forward(
            q_low, k_low, v_low, piece_ids, buckets, rel_table, attn_scale
        )
        attended_low = attended.astype(jnp.bfloat16)
        middle = hidden + jnp.dot(attended_low, full_mats[3], preferred_element_type=jnp.float32)
        ffn_low = rms_scale(middle, gain_ffn[layer_idx].astype(jnp.float32)).astype(jnp.bfloat16)
        logits = jnp.dot(ffn_low, full_mats[4], preferred_element_type=jnp.float32)
        gate_value = gate_of(chosen_f, logits)
        sent_rows = (
            jnp.einsum("ts,td->sd", placing, ffn_low, preferred_element_type=jnp.float32)
            .astype(jnp.bfloat16)
            .reshape(capacity, num_experts, feat_width)
        )
        arrived = lax.all_to_all(sent_rows, "gy", split_axis=1, concat_axis=0, tiled=True)
        full_in, full_out = (
            lax.all_gather(w_in[layer_idx], "gx", axis=2, tiled=True),
            lax.all_gather(w_out[layer_idx], "gx", axis=2, tiled=True),
        )
        pre_act = jnp.einsum("red,edf->ref", arrived, full_in, preferred_element_type=jnp.float32)
        activated = gelu_tanh(pre_act).astype(jnp.bfloat16)
        made_rows = jnp.einsum(
            "ref,edf->red", activated, full_out, preferred_element_type=jnp.float32
        )
        expert_state = (full_in, full_out, pre_act, activated)
        returned = lax.all_to_all(
            made_rows.astype(jnp.bfloat16), "gy", split_axis=0, concat_axis=1, tiled=True
        )
        combined = jnp.dot(
            placing,
            returned.reshape(capacity * num_experts, feat_width),
            preferred_element_type=jnp.float32,
        )
        kept_state.append(
            (
                hidden,
                full_mats,
                normed_low,
                q_low,
                k_low,
                v_low,
                log_sums,
                attended_low,
                middle,
                ffn_low,
                logits,
                gate_value,
                combined,
                arrived,
                expert_state,
            )
        )
        hidden = middle + gate_value[:, None] * combined
    grad_now = cotangent.astype(jnp.float32)
    table_grad = jnp.zeros(rel_table.shape, jnp.float32)
    attn_parts = []
    gain_attn_parts = []
    gain_ffn_parts = []
    in_parts = []
    out_parts = []
    for layer_idx in reversed(range(num_layers)):
        (
            prior_hidden_state,
            mats_now,
            normed_low,
            q_low,
            k_low,
            v_low,
            log_sums,
            attended_low,
            middle,
            ffn_low,
            logits,
            gate_value,
            combined,
            arrived,
            expert_state,
        ) = kept_state[layer_idx]
        d_gate = jnp.sum(grad_now * combined, axis=1)
        d_comb = (gate_value[:, None] * grad_now).astype(jnp.bfloat16)
        d_sent = (
            jnp.einsum("ts,td->sd", placing, d_comb, preferred_element_type=jnp.float32)
            .astype(jnp.bfloat16)
            .reshape(capacity, num_experts, feat_width)
        )
        d_arrived = lax.all_to_all(d_sent, "gy", split_axis=1, concat_axis=0, tiled=True)
        full_in, full_out, pre_act, activated = expert_state
        d_activated = jnp.einsum(
            "red,edf->ref", d_arrived, full_out, preferred_element_type=jnp.float32
        )
        d_pre = jax.vjp(gelu_tanh, pre_act)[1](d_activated)[0].astype(jnp.bfloat16)
        out_full = jnp.einsum(
            "red,ref->edf", d_arrived, activated, preferred_element_type=jnp.float32
        )
        in_full = jnp.einsum("red,ref->edf", arrived, d_pre, preferred_element_type=jnp.float32)
        d_rows = jnp.einsum("ref,edf->red", d_pre, full_in, preferred_element_type=jnp.float32)
        grad_in_part, grad_out_part = (
            lax.psum_scatter(
                in_full.astype(jnp.bfloat16), "gx", scatter_dimension=2, tiled=True
            ).astype(jnp.float32),
            lax.psum_scatter(
                out_full.astype(jnp.bfloat16), "gx", scatter_dimension=2, tiled=True
            ).astype(jnp.float32),
        )
        d_back = lax.all_to_all(
            d_rows.astype(jnp.bfloat16), "gy", split_axis=0, concat_axis=1, tiled=True
        )
        d_ffn = jnp.dot(
            placing,
            d_back.reshape(capacity * num_experts, feat_width),
            preferred_element_type=jnp.float32,
        )
        d_logits = jax.vjp(partial(gate_of, chosen_f), logits)[1](d_gate)[0].astype(jnp.bfloat16)
        grad_router = jnp.einsum("td,te->de", ffn_low, d_logits, preferred_element_type=jnp.float32)
        d_ffn = d_ffn + jnp.einsum(
            "te,de->td", d_logits, mats_now[4], preferred_element_type=jnp.float32
        )
        norm_pull = jax.vjp(rms_scale, middle, gain_ffn[layer_idx].astype(jnp.float32))[1]
        d_middle, grad_gain_two = norm_pull(d_ffn)
        d_middle = d_middle + grad_now
        d_att = d_middle.astype(jnp.bfloat16)
        grad_output = jnp.einsum(
            "td,te->de", attended_low, d_att, preferred_element_type=jnp.float32
        )
        d_attended = (
            jnp.einsum("te,de->td", d_att, mats_now[3], preferred_element_type=jnp.float32)
            .astype(jnp.bfloat16)
            .reshape(seq_len, num_heads, head_dim)
        )
        d_query, d_key, d_value, d_tab = attend_backward(
            q_low, k_low, v_low, d_attended, log_sums, piece_ids, buckets, rel_table, attn_scale
        )
        table_grad = table_grad + d_tab
        dq_low = d_query.reshape(seq_len, feat_width).astype(jnp.bfloat16)
        dk_low = d_key.reshape(seq_len, feat_width).astype(jnp.bfloat16)
        dv_low = d_value.reshape(seq_len, feat_width).astype(jnp.bfloat16)
        grad_query = jnp.einsum("td,te->de", normed_low, dq_low, preferred_element_type=jnp.float32)
        grad_key = jnp.einsum("td,te->de", normed_low, dk_low, preferred_element_type=jnp.float32)
        grad_value = jnp.einsum("td,te->de", normed_low, dv_low, preferred_element_type=jnp.float32)
        d_normed = jnp.einsum("te,de->td", dq_low, mats_now[0], preferred_element_type=jnp.float32)
        d_normed = d_normed + jnp.einsum(
            "te,de->td", dk_low, mats_now[1], preferred_element_type=jnp.float32
        )
        d_normed = d_normed + jnp.einsum(
            "te,de->td", dv_low, mats_now[2], preferred_element_type=jnp.float32
        )
        norm_pull = jax.vjp(
            rms_scale, prior_hidden_state, gain_attn[layer_idx].astype(jnp.float32)
        )[1]
        d_hidden, grad_gain_one = norm_pull(d_normed)
        grad_now = d_hidden + d_middle
        blocked = [
            regroup_blocks(group_member, grid_count_first, grid_count_second)
            for group_member in (grad_query, grad_key, grad_value, grad_output, grad_router)
        ]
        reduced = (
            lax.psum_scatter(blocked[0], ("gx", "gy"), scatter_dimension=0, tiled=True),
            lax.psum_scatter(blocked[1], ("gx", "gy"), scatter_dimension=0, tiled=True),
            lax.psum_scatter(blocked[2], ("gx", "gy"), scatter_dimension=0, tiled=True),
            lax.psum_scatter(blocked[3], ("gx", "gy"), scatter_dimension=0, tiled=True),
            lax.psum_scatter(blocked[4], ("gx", "gy"), scatter_dimension=0, tiled=True),
        )
        attn_parts.append([group_member[0] for group_member in reduced])
        gain_attn_parts.append(grad_gain_one)
        gain_ffn_parts.append(grad_gain_two)
        in_parts.append(grad_in_part)
        out_parts.append(grad_out_part)
    attn_parts = attn_parts[::-1]
    grad_w_in_all = jnp.stack(in_parts[::-1])
    grad_w_out_all = jnp.stack(out_parts[::-1])
    attn_final = [jnp.stack([parts_one[index] for parts_one in attn_parts]) for index in range(5)]
    small_sums = lax.psum(
        (table_grad, jnp.stack(gain_attn_parts[::-1]), jnp.stack(gain_ffn_parts[::-1])),
        ("gx", "gy"),
    )
    return (
        hidden,
        grad_now,
        small_sums[0],
        small_sums[1],
        small_sums[2],
        attn_final[0],
        attn_final[1],
        attn_final[2],
        attn_final[3],
        attn_final[4],
        grad_w_in_all,
        grad_w_out_all,
    )


def solution(mesh):
    placed = (
        P(("gx", "gy"), None),
        P(("gx", "gy"), None),
        P(("gx", "gy")),
        P(),
        P(),
        P(),
        P(),
        P(None, "gx", "gy"),
        P(None, "gx", "gy"),
        P(None, "gx", "gy"),
        P(None, "gx", "gy"),
        P(None, "gx", "gy"),
        P(None, "gy", None, "gx"),
        P(None, "gy", None, "gx"),
        P(("gx", "gy"), None),
    )
    return jax.shard_map(
        body,
        mesh=mesh,
        in_specs=placed,
        out_specs=(
            P(("gx", "gy"), None),
            P(("gx", "gy"), None),
            P(),
            P(),
            P(),
            P(None, "gx", "gy"),
            P(None, "gx", "gy"),
            P(None, "gx", "gy"),
            P(None, "gx", "gy"),
            P(None, "gx", "gy"),
            P(None, "gy", None, "gx"),
            P(None, "gy", None, "gx"),
        ),
        check_vma=False,
    )
```

profile of v0, /device:TPU:0, one launch (start us, length us, event | category | flops | bytes accessed | tf_op | source)
XLA Modules:
  0.0 2737.1 jit_solution(6618684861392216867)
XLA Ops:
  26.1 860.0 %gather_fusion.1 = f32[262144,12]{1,0:T(8,128)} fusion(f32[12,1023]{0,1:T(8,128)S(1)} %select_bitcast_fusion, s32[262144]{0:T(1024)S(1)} %broadcast_clamp_fusion), kind=kCustom, calls=%fused_computation.1.clone | custom fusion | bytes 26214400 | tf_op jit(solution)/shard_map/while/body/eval_jaxpr/jit(_take)/gather | solution.py:56
  886.1 73.5 %copy.217 = f32[512,512,12]{0,1,2:T(8,128)} copy(f32[512,512,12]{2,1,0:T(8,128)} %bitcast.10) | data formatting | bytes 25165824 | tf_op jit(solution)/shard_map/while/body/eval_jaxpr/jit(_take)/gather | solution.py:56
  1013.7 7.3 all-to-all-start
  1021.6 36.4 %all-to-all-done = bf16[128,8,768]{2,0,1:T(8,128)(2,1)} async-done(((bf16[128,8,768]{2,0,1:T(8,128)(2,1)}), bf16[128,8,768]{2,0,1:T(8,128)(2,1)}, u32[]{:S(2)}, u32[]{:S(2)}) %all-to-all-start) | async-done | bytes 1572896 | tf_op jit(solution)/shard_map/all_to_all | solution.py:226
  1058.0 10.2 fusion.74
  1068.2 12.6 fusion.162
  1094.1 91.1 %all_gather.46 = bf16[32,192,1]{1,2,0:T(2,128)(2,1)S(1)} all-gather(bf16[1,192,1]{1,2,0:T(2,128)(2,1)S(1)} %get-tuple-element.177), channel_id=1, replica_groups=mesh['gx'=4,'gy'=8] {'gx','gy'}, dimensions={0}, use_global_device_ids=true | all-gather | bytes 12672 | tf_op jit(solution)/shard_map/all_gather | solution.py:190
  1263.7 34.4 %all-to-all-done.2 = bf16[128,8,768]{2,0,1:T(8,128)(2,1)} async-done(((bf16[128,8,768]{2,0,1:T(8,128)(2,1)}), bf16[128,8,768]{2,0,1:T(8,128)(2,1)}, u32[]{:S(2)}, u32[]{:S(2)}) %all-to-all-start.2) | async-done | bytes 1572896 | tf_op jit(solution)/shard_map/all_to_all | solution.py:226
  1298.1 10.1 fusion.68
  1308.2 12.6 fusion.157
  1332.7 91.5 %all_gather.53 = bf16[32,192,1]{1,2,0:T(2,128)(2,1)S(1)} all-gather(bf16[1,192,1]{1,2,0:T(2,128)(2,1)S(1)} %get-tuple-element.176), channel_id=1, replica_groups=mesh['gx'=4,'gy'=8] {'gx','gy'}, dimensions={0}, use_global_device_ids=true | all-gather | bytes 12672 | tf_op jit(solution)/shard_map/all_gather | solution.py:190
  1438.6 36.8 %all_to_all.120 = bf16[128,8,768]{2,0,1:T(8,128)(2,1)S(1)} all-to-all(bf16[128,8,768]{2,0,1:T(8,128)(2,1)S(1)} %copy.238), channel_id=1, replica_groups=mesh['gx'=4,'gy'=8] {'gy'}, dimensions={1} | all-to-all | bytes 3145728 | tf_op jit(solution)/shard_map/all_to_all | solution.py:297
  1475.4 14.5 fusion.13
  1512.8 33.8 %all-to-all-done.5 = bf16[8,2,49152]{2,1,0:T(2,128)(2,1)} async-done(((bf16[8,2,49152]{2,1,0:T(2,128)(2,1)}), bf16[8,2,49152]{2,1,0:T(2,128)(2,1)}, u32[]{:S(2)}, u32[]{:S(2)}) %all-to-all-start.5) | async-done | bytes 1572896 | tf_op jit(solution)/shard_map/all_to_all | solution.py:316
  1568.8 8.9 multiply_reduce_fusion.1
  1577.7 7.1 multiply_convert_fusion.1
  1596.3 40.8 %all_to_all.121 = bf16[128,8,768]{2,0,1:T(8,128)(2,1)S(1)} all-to-all(bf16[128,8,768]{2,0,1:T(8,128)(2,1)S(1)} %copy.245), channel_id=1, replica_groups=mesh['gx'=4,'gy'=8] {'gy'}, dimensions={1} | all-to-all | bytes 3145728 | tf_op jit(solution)/shard_map/all_to_all | solution.py:297
  1637.1 14.5 fusion.6
  1680.4 28.5 %all-to-all-done.7 = bf16[8,2,49152]{2,1,0:T(2,128)(2,1)} async-done(((bf16[8,2,49152]{2,1,0:T(2,128)(2,1)}), bf16[8,2,49152]{2,1,0:T(2,128)(2,1)}, u32[]{:S(2)}, u32[]{:S(2)}) %all-to-all-start.7) | async-done | bytes 1572896 | tf_op jit(solution)/shard_map/all_to_all | solution.py:316
  1726.5 10.5 multiply_reduce_fusion
  1739.6 7.5 multiply_convert_fusion
  1786.5 9.1 fusion.79
  1795.7 9.2 fusion.76
  1806.3 10.1 fusion.82
  1817.9 10.1 fusion.85
  1830.1 91.0 %rev.8 = f32[12,512,512]{1,2,0:T(8,128)} reverse(bf16[12,512,512]{1,2,0:T(8,128)(2,1)} %copy-done.2), dimensions={2} | reverse | bytes 18874368 | tf_op jit(solution)/shard_map/while/body/eval_jaxpr/rev | solution.py:63
  1921.1 12.7 copy.282
  1933.8 14.5 pad.9.clone
  1948.4 11.0 pad.31
  1959.4 39.7 %copy.285 = f32[2,8,512,1024]{3,1,2,0:T(8,128)} copy(f32[2,8,512,1024]{3,2,1,0:T(8,128)S(1)} %bitcast.598) | data formatting | bytes 67108864
  1999.1 23.1 slice.99
  2022.2 42.3 %reshape.602 = f32[12,512,1023]{2,1,0:T(8,128)} reshape(f32[12,523776]{1,0:T(8,128)} %slice.99) | data formatting | bytes 50282496 | tf_op jit(solution)/shard_map/while/body/eval_jaxpr/reshape | solution.py:66
  2064.6 9.3 reduce_sum.288
  2074.8 91.0 %rev.9 = f32[12,512,512]{1,2,0:T(8,128)} reverse(bf16[12,512,512]{1,2,0:T(8,128)(2,1)} %copy-done.3), dimensions={2} | reverse | bytes 18874368 | tf_op jit(solution)/shard_map/while/body/eval_jaxpr/rev | solution.py:63
  2165.9 12.6 copy.283
  2178.5 14.6 pad.10.clone
  2193.0 10.9 pad.32
  2204.0 39.7 %copy.286 = f32[2,8,512,1024]{3,1,2,0:T(8,128)} copy(f32[2,8,512,1024]{3,2,1,0:T(8,128)S(1)} %bitcast.599) | data formatting | bytes 67108864
  2243.7 23.0 slice.100
  2266.7 41.9 %reshape.604 = f32[12,512,1023]{2,1,0:T(8,128)} reshape(f32[12,523776]{1,0:T(8,128)} %slice.100) | data formatting | bytes 50282496 | tf_op jit(solution)/shard_map/while/body/eval_jaxpr/reshape | solution.py:66
  2308.6 9.0 reduce_sum.292
  2318.1 40.9 %all-reduce.4 = (f32[32,12]{0,1:T(8,128)}, f32[2,768]{1,0:T(2,128)}, f32[2,768]{1,0:T(2,128)}, f32[32,192,1]{1,2,0:T(1,128)S(1)}, f32[32,192,1]{1,2,0:T(1,128)S(1)}) all-reduce(f32[32,12]{0,1:T(8,128)S(1)} %convolution_add_fusion.1, f32[2,768]{1,0:T(2,128)S(1)} %pad_maximum_fusion.4, ...), channel_id=1, replica_groups=mesh['gx'=4,'gy'=8] {'gx','gy'}, use_global_device_ids=true, to_apply=%region_29.32 | all-reduce | flops 15744 | bytes 125952 | tf_op jit(solution)/shard_map/psum | solution.py:383
  2364.6 53.7 %reduce-scatter.27.cloned.1.call-done = f32[1,192,96]{2,1,0:T(8,128)} async-done(((f32[32,192,96]{2,1,0:T(8,128)}), f32[1,192,96]{2,1,0:T(8,128)}) %reduce-scatter.27.cloned.1.call-update) | async-done | bytes 73744 | tf_op jit(solution)/shard_map/reduce_scatter | solution.py:371
  2418.3 105.8 %reduce-scatter.25.cloned.1.call-done = f32[1,192,96]{2,1,0:T(8,128)} async-done(((f32[32,192,96]{2,1,0:T(8,128)}), f32[1,192,96]{2,1,0:T(8,128)}) %reduce-scatter.25.cloned.1.call-update) | async-done | bytes 73744 | tf_op jit(solution)/shard_map/reduce_scatter | solution.py:371
  2525.7 48.3 %reduce-scatter.31.cloned.1.call-done = bf16[1,768,768]{2,1,0:T(8,128)(2,1)} async-done(((bf16[1,768,3072]{2,1,0:T(8,128)(2,1)}), bf16[1,768,768]{2,1,0:T(8,128)(2,1)}) %reduce-scatter.31.cloned.1.call-update) | async-done | bytes 1179664 | tf_op jit(solution)/shard_map/reduce_scatter | solution.py:309
  2574.0 51.1 %reduce-scatter.29.cloned.1.call-done = bf16[1,768,768]{2,1,0:T(8,128)(2,1)} async-done(((bf16[1,768,3072]{2,1,0:T(8,128)(2,1)}), bf16[1,768,768]{2,1,0:T(8,128)(2,1)}) %reduce-scatter.29.cloned.1.call-update) | async-done | bytes 1179664 | tf_op jit(solution)/shard_map/reduce_scatter | solution.py:309
  2629.2 46.3 %reduce-scatter.35.cloned.1.call-done = bf16[1,768,768]{2,1,0:T(8,128)(2,1)} async-done(((bf16[1,768,3072]{2,1,0:T(8,128)(2,1)}), bf16[1,768,768]{2,1,0:T(8,128)(2,1)}) %reduce-scatter.35.cloned.1.call-update) | async-done | bytes 1179664 | tf_op jit(solution)/shard_map/reduce_scatter | solution.py:312
  2675.5 50.4 %reduce-scatter.33.cloned.1.call-done = bf16[1,768,768]{2,1,0:T(8,128)(2,1)} async-done(((bf16[1,768,3072]{2,1,0:T(8,128)(2,1)}), bf16[1,768,768]{2,1,0:T(8,128)(2,1)}) %reduce-scatter.33.cloned.1.call-update) | async-done | bytes 1179664 | tf_op jit(solution)/shard_map/reduce_scatter | solution.py:312
  (536 shorter events, 356.6 us)
Async XLA Ops:
  7.2 955.4 %all-gather.17.cloned.1.call-start = ((), (), s32[]{:S(2)}) async-start(), calls=%async_computation.20 | async-start | bytes 1622016 | tf_op jit(solution)/shard_map/all_gather | solution.py:188
  8.7 961.8 %all-gather.19.cloned.1.call-start = ((), (), s32[]{:S(2)}) async-start(), calls=%async_computation.21 | async-start | bytes 1622016 | tf_op jit(solution)/shard_map/all_gather | solution.py:186
  10.3 967.2 %all-gather.21.cloned.1.call-start = ((), (), s32[]{:S(2)}) async-start(), calls=%async_computation.22 | async-start | bytes 1622016 | tf_op jit(solution)/shard_map/all_gather | solution.py:187
  11.8 992.0 %all-gather.23.cloned.1.call-start = ((), (), s32[]{:S(2)}) async-start(), calls=%async_computation.23 | async-start | bytes 1622016 | tf_op jit(solution)/shard_map/all_gather | solution.py:189
  13.3 1044.7 %all-gather.33.cloned.1.call-start = ((), (), s32[]{:S(2)}) async-start(), calls=%async_computation.40 | async-start | bytes 5898240 | tf_op jit(solution)/shard_map/all_gather | solution.py:228
  16.8 1051.4 %all-gather.35.cloned.1.call-start = ((), (), s32[]{:S(2)}) async-start(), calls=%async_computation.41 | async-start | bytes 5898240 | tf_op jit(solution)/shard_map/all_gather | solution.py:229
  18.4 1166.9 %all-gather.25.cloned.1.call-start = ((), (), s32[]{:S(2)}) async-start(), calls=%async_computation.24 | async-start | bytes 1622016 | tf_op jit(solution)/shard_map/all_gather | solution.py:188
  19.2 1173.9 %all-gather.27.cloned.1.call-start = ((), (), s32[]{:S(2)}) async-start(), calls=%async_computation.25 | async-start | bytes 1622016 | tf_op jit(solution)/shard_map/all_gather | solution.py:186
  19.9 1180.5 %all-gather.29.cloned.1.call-start = ((), (), s32[]{:S(2)}) async-start(), calls=%async_computation.26 | async-start | bytes 1622016 | tf_op jit(solution)/shard_map/all_gather | solution.py:187
  20.7 1187.1 %all-gather.31.cloned.1.call-start = ((), (), s32[]{:S(2)}) async-start(), calls=%async_computation.27 | async-start | bytes 1622016 | tf_op jit(solution)/shard_map/all_gather | solution.py:189
  22.1 963.0 %copy-start.89 = (f32[768]{0:T(1024)}, f32[768]{0:T(1024)S(1)}, u32[]{:S(2)}) copy-start(f32[768]{0:T(1024)S(1)} %get-tuple-element.123) | copy-start | bytes 9220
  22.4 962.7 %copy-start.104 = (f32[512]{0:T(512)}, f32[512]{0:T(512)S(1)}, u32[]{:S(2)}) copy-start(f32[512]{0:T(512)S(1)} %fusion.210) | copy-start | bytes 6148
  886.1 73.9 %copy-start.95 = (s32[512]{0:T(512)S(1)}, s32[512]{0:T(512)}, u32[]{:S(2)}) copy-start(s32[512]{0:T(512)} %param.21) | copy-start | bytes 6148
  886.1 74.9 %copy-start.113 = (bf16[2,768]{1,0:T(2,128)(2,1)S(1)}, bf16[2,768]{1,0:T(2,128)(2,1)}, u32[]{:S(2)}) copy-start(bf16[2,768]{1,0:T(2,128)(2,1)} %param.25) | copy-start | bytes 9220
  886.1 74.9 %copy-start.72 = (s32[512,1]{0,1:T(1,128)S(1)}, s32[512,1]{0,1:T(1,128)}, u32[]{:S(2)}) copy-start(s32[512,1]{0,1:T(1,128)} %param.20) | copy-start | bytes 6148
  961.0 49.8 %copy-start.91 = (f32[768]{0:T(1024)}, f32[768]{0:T(1024)S(1)}, u32[]{:S(2)}) copy-start(f32[768]{0:T(1024)S(1)} %get-tuple-element.121) | copy-start | bytes 9220
  1010.8 213.2 %copy-start.4 = (f32[512,768]{1,0:T(8,128)}, f32[512,768]{1,0:T(8,128)S(1)}, u32[]{:S(2)}) copy-start(f32[512,768]{1,0:T(8,128)S(1)} %get-tuple-element.181) | copy-start | bytes 4718596
  1011.1 204.1 %copy-start.10 = (bf16[512,768]{1,0:T(8,128)(2,1)}, bf16[512,768]{1,0:T(8,128)(2,1)S(1)}, u32[]{:S(2)}) copy-start(bf16[512,768]{1,0:T(8,128)(2,1)S(1)} %multiply_convert_fusion.9) | copy-start | bytes 2359300
  1013.7 44.4 %all-to-all-start = ((bf16[128,8,768]{2,0,1:T(8,128)(2,1)}), bf16[128,8,768]{2,0,1:T(8,128)(2,1)}, u32[]{:S(2)}, u32[]{:S(2)}) async-start(bf16[128,8,768]{2,0,1:T(8,128)(2,1)} %copy.222), calls=%async_computation | async-start | bytes 3145728 | tf_op jit(solution)/shard_map/all_to_all | solution.py:226
  1020.9 242.8 %all-gather.37.cloned.1.call-start = ((), (), s32[]{:S(2)}) async-start(), calls=%async_computation.42 | async-start | bytes 5898240 | tf_op jit(solution)/shard_map/all_gather | solution.py:228
  1089.0 126.5 %all-to-all-start.1 = ((bf16[8,2,49152]{2,1,0:T(2,128)(2,1)}), bf16[8,2,49152]{2,1,0:T(2,128)(2,1)}, u32[]{:S(2)}, u32[]{:S(2)}) async-start(bf16[8,2,49152]{2,1,0:T(2,128)(2,1)} %reshape.675), calls=%async_computation.1 | async-start | bytes 3145728 | tf_op jit(solution)/shard_map/all_to_all | solution.py:237
  1093.5 214.7 %all-gather.39.cloned.1.call-start = ((), (), s32[]{:S(2)}) async-start(), calls=%async_computation.43 | async-start | bytes 5898240 | tf_op jit(solution)/shard_map/all_gather | solution.py:229
  1259.1 39.0 %all-to-all-start.2 = ((bf16[128,8,768]{2,0,1:T(8,128)(2,1)}), bf16[128,8,768]{2,0,1:T(8,128)(2,1)}, u32[]{:S(2)}, u32[]{:S(2)}) async-start(bf16[128,8,768]{2,0,1:T(8,128)(2,1)} %copy.235), calls=%async_computation.2 | async-start | bytes 3145728 | tf_op jit(solution)/shard_map/all_to_all | solution.py:226
  1328.4 97.4 %all-to-all-start.3 = ((bf16[8,2,49152]{2,1,0:T(2,128)(2,1)}), bf16[8,2,49152]{2,1,0:T(2,128)(2,1)}, u32[]{:S(2)}, u32[]{:S(2)}) async-start(bf16[8,2,49152]{2,1,0:T(2,128)(2,1)} %reshape.677), calls=%async_computation.3 | async-start | bytes 3145728 | tf_op jit(solution)/shard_map/all_to_all | solution.py:237
  1425.8 85.4 %copy-start.68 = (f32[512,8]{0,1:T(8,128)}, f32[512,8]{0,1:T(8,128)S(1)}, u32[]{:S(2)}) copy-start(f32[512,8]{0,1:T(8,128)S(1)} %get-tuple-element.190) | copy-start | bytes 49156
  1425.8 85.4 %copy-start.82 = (f32[512]{0:T(512)}, f32[512]{0:T(512)S(1)}, u32[]{:S(2)}) copy-start(f32[512]{0:T(512)S(1)} %get-tuple-element.189) | copy-start | bytes 6148
  1425.8 85.4 %copy-start.87 = (f32[512]{0:T(512)}, f32[512]{0:T(512)S(1)}, u32[]{:S(2)}) copy-start(f32[512]{0:T(512)S(1)} %fusion.209) | copy-start | bytes 6148
  1437.0 74.1 %copy-start.100 = (f32[512]{0:T(512)}, f32[512]{0:T(512)S(1)}, u32[]{:S(2)}) copy-start(f32[512]{0:T(512)S(1)} %get-tuple-element.191) | copy-start | bytes 6148
  1438.6 54.0 %slice-start.10 = ((s8[4718592]{0:T(1024)(128)(4,1)}), s8[4194304]{0:T(1024)(128)(4,1)S(1)}, s32[]{:S(2)}) async-start(s8[4718592]{0:T(1024)(128)(4,1)} %bitcast.707), calls=%async_computation.54 | async-start | bytes 8388608
  1506.4 40.2 %all-to-all-start.5 = ((bf16[8,2,49152]{2,1,0:T(2,128)(2,1)}), bf16[8,2,49152]{2,1,0:T(2,128)(2,1)}, u32[]{:S(2)}, u32[]{:S(2)}) async-start(bf16[8,2,49152]{2,1,0:T(2,128)(2,1)} %reshape.679), calls=%async_computation.5 | async-start | bytes 3145728 | tf_op jit(solution)/shard_map/all_to_all | solution.py:316
  1511.2 41.7 %copy-start.96 = (f32[512]{0:T(512)}, f32[512]{0:T(512)S(1)}, u32[]{:S(2)}) copy-start(f32[512]{0:T(512)S(1)} %neg.12) | copy-start | bytes 6148
  1594.1 43.0 %slice-start.8 = ((s8[4718592]{0:T(1024)(128)(4,1)}), s8[4194304]{0:T(1024)(128)(4,1)S(1)}, s32[]{:S(2)}) async-start(s8[4718592]{0:T(1024)(128)(4,1)} %bitcast.705), calls=%async_computation.52 | async-start | bytes 8388608
  1594.7 83.4 %copy-start.93 = (f32[512]{0:T(512)}, f32[512]{0:T(512)S(1)}, u32[]{:S(2)}) copy-start(f32[512]{0:T(512)S(1)} %get-tuple-element.145) | copy-start | bytes 6148
  1594.7 42.4 %slice-start.9 = ((s8[4718592]{0:T(1024)(128)(4,1)}), s8[524288]{0:T(1024)(128)(4,1)S(1)}, s32[]{:S(2)}) async-start(s8[4718592]{0:T(1024)(128)(4,1)} %bitcast.705), calls=%async_computation.53 | async-start | bytes 1048576
  1596.0 58.4 %slice-start.6 = ((s8[4718592]{0:T(1024)(128)(4,1)}), s8[4194304]{0:T(1024)(128)(4,1)S(1)}, s32[]{:S(2)}) async-start(s8[4718592]{0:T(1024)(128)(4,1)} %bitcast.703), calls=%async_computation.50 | async-start | bytes 8388608
  1668.2 40.6 %all-to-all-start.7 = ((bf16[8,2,49152]{2,1,0:T(2,128)(2,1)}), bf16[8,2,49152]{2,1,0:T(2,128)(2,1)}, u32[]{:S(2)}, u32[]{:S(2)}) async-start(bf16[8,2,49152]{2,1,0:T(2,128)(2,1)} %reshape.681), calls=%async_computation.7 | async-start | bytes 3145728 | tf_op jit(solution)/shard_map/all_to_all | solution.py:316
  1672.6 687.0 %reduce-scatter.15.cloned.1.call-start = ((), (), s32[]{:S(2)}) async-start(), calls=%async_computation.29 | async-start | bytes 3244032 | tf_op jit(solution)/shard_map/reduce_scatter | solution.py:368
  1678.1 681.5 %reduce-scatter.13.cloned.1.call-start = ((), (), s32[]{:S(2)}) async-start(), calls=%async_computation.28 | async-start | bytes 3244032 | tf_op jit(solution)/shard_map/reduce_scatter | solution.py:368
  1765.1 596.2 %reduce-scatter.19.cloned.1.call-start = ((), (), s32[]{:S(2)}) async-start(), calls=%async_computation.31 | async-start | bytes 3244032 | tf_op jit(solution)/shard_map/reduce_scatter | solution.py:369
  1768.9 592.4 %reduce-scatter.17.cloned.1.call-start = ((), (), s32[]{:S(2)}) async-start(), calls=%async_computation.30 | async-start | bytes 3244032 | tf_op jit(solution)/shard_map/reduce_scatter | solution.py:369
  1772.9 590.0 %reduce-scatter.23.cloned.1.call-start = ((), (), s32[]{:S(2)}) async-start(), calls=%async_computation.33 | async-start | bytes 3244032 | tf_op jit(solution)/shard_map/reduce_scatter | solution.py:370
  1775.6 587.3 %reduce-scatter.21.cloned.1.call-start = ((), (), s32[]{:S(2)}) async-start(), calls=%async_computation.32 | async-start | bytes 3244032 | tf_op jit(solution)/shard_map/reduce_scatter | solution.py:370
  1778.3 640.0 %reduce-scatter.27.cloned.1.call-start = ((), (), s32[]{:S(2)}) async-start(), calls=%async_computation.35 | async-start | bytes 3244032 | tf_op jit(solution)/shard_map/reduce_scatter | solution.py:371
  1782.4 741.7 %reduce-scatter.25.cloned.1.call-start = ((), (), s32[]{:S(2)}) async-start(), calls=%async_computation.34 | async-start | bytes 3244032 | tf_op jit(solution)/shard_map/reduce_scatter | solution.py:371
  1786.5 787.5 %reduce-scatter.31.cloned.1.call-start = ((), (), s32[]{:S(2)}) async-start(), calls=%async_computation.37 | async-start | bytes 5898240 | tf_op jit(solution)/shard_map/reduce_scatter | solution.py:309
  1795.6 829.5 %reduce-scatter.29.cloned.1.call-start = ((), (), s32[]{:S(2)}) async-start(), calls=%async_computation.36 | async-start | bytes 5898240 | tf_op jit(solution)/shard_map/reduce_scatter | solution.py:309
  1804.9 870.6 %reduce-scatter.35.cloned.1.call-start = ((), (), s32[]{:S(2)}) async-start(), calls=%async_computation.39 | async-start | bytes 5898240 | tf_op jit(solution)/shard_map/reduce_scatter | solution.py:312
  1816.5 909.5 %reduce-scatter.33.cloned.1.call-start = ((), (), s32[]{:S(2)}) async-start(), calls=%async_computation.38 | async-start | bytes 5898240 | tf_op jit(solution)/shard_map/reduce_scatter | solution.py:312
  (118 other events, 630.2 us)
Sparse Core Ops, SparseCore 0:
  11.6 57.7 all-gather.16
  72.9 53.9 all-gather.18
  130.5 53.9 all-gather.20
  187.3 53.9 all-gather.22
  243.3 36.3 all-gather.32
  281.6 37.4 all-gather.34
  322.7 55.0 all-gather.24
  381.3 53.9 all-gather.26
  438.3 53.9 all-gather.28
  495.1 53.9 all-gather.30
  1023.3 38.8 all-gather.36
  1096.1 38.8 all-gather.38
  1678.9 104.4 reduce-scatter.14
  1788.7 100.4 reduce-scatter.12
  1894.4 100.4 reduce-scatter.18
  2000.2 100.4 reduce-scatter.16
  2106.0 100.4 reduce-scatter.22
  2211.9 100.4 reduce-scatter.20
  2317.8 100.4 reduce-scatter.26
  2423.6 100.4 reduce-scatter.24
  2527.2 46.7 reduce-scatter.30
  2577.2 47.8 reduce-scatter.28
  2627.7 47.8 reduce-scatter.34
  2678.1 47.8 reduce-scatter.32
where the time goes:
time: 2770 us; the launch traced here: 2740 us
  local copies, waits for them, and re-layouts  1560 us (56%)
  waiting for transfers between devices  493 us (18%)
  blocking collectives  301 us (11%)
  matrix products  252 us (9%)
  other arithmetic  79.2 us (3%)
  starting transfers between devices  31.3 us (1%)
    gather x2, local copies, waits for them, and re-layouts, block_terms(): jnp.take(offset_bias, row_pos[:, None] - col_pos[None, :] + (seq_len - 1)...  933 us
    unnamed x295, local copies, waits for them, and re-layouts  205 us
    all_gather x2, blocking collectives, body(): lax.all_gather(w_router[layer_idx][None], ('gx', 'gy'), axis=0, tiled=True)  183 us
    rev x2, local copies, waits for them, and re-layouts, diagonal_sums(): flipped = values[:, :, ::-1]  182 us
    reduce_scatter x2, waiting for transfers between devices, body(): lax.psum_scatter(blocked[3], ('gx', 'gy'), scatter_dimension=0, tiled=True)  160 us
    reduce_scatter x2, waiting for transfers between devices, body(): lax.psum_scatter(in_full.astype(jnp.bfloat16), 'gx', scatter_dimension=2,...  99.4 us
    reduce_scatter x2, waiting for transfers between devices, body(): lax.psum_scatter(out_full.astype(jnp.bfloat16), 'gx', scatter_dimension=2...  96.7 us
    reshape x2, local copies, waits for them, and re-layouts, diagonal_sums(): return jnp.sum(flat.reshape(num_heads, row_count, width_new), axis=1)  84.2 us
  transfers between devices with their start and end apart: 30, of which 10 were waited for; matrix products, arithmetic and copies ran while one was open for 63% of the time, Pallas kernels for 0%

commit v1 on v0

v1 whole, which is shorter than its diff:
```python
from functools import partial

import jax
import jax.numpy as jnp
from jax import lax
from jax.experimental import pallas as pl
from jax.experimental.pallas import tpu as pltpu
from jax.sharding import PartitionSpec as P

eps_norm = 1e-06
highest = lax.Precision.HIGHEST
f32 = jnp.float32
bf16 = jnp.bfloat16
masked_out = -1e30
vmem_bytes = 56 * 1024 * 1024


def whole(shape):
    zeros = (0,) * len(shape)
    return pl.BlockSpec(shape, lambda *_: zeros, pipeline_mode=pl.Buffered(1))


def whole_of(arrays):
    return [whole(array.shape) for array in arrays]


def params():
    return pltpu.CompilerParams(vmem_limit_bytes=vmem_bytes)


def dot(lhs, rhs, lhs_dim=1, rhs_dim=0):
    return lax.dot_general(
        lhs, rhs, (((lhs_dim,), (rhs_dim,)), ((), ())), preferred_element_type=f32
    )


def rms_factor(hidden):
    return lax.rsqrt(jnp.mean(hidden * hidden, axis=-1, keepdims=True) + eps_norm)


def rms_pull(hidden, gain_row, d_normed):
    factor = rms_factor(hidden)
    scaled = gain_row * d_normed
    inner = jnp.mean(hidden * scaled, axis=-1, keepdims=True)
    d_hidden = factor * scaled - hidden * (factor * factor * factor * inner)
    d_gain = jnp.sum(d_normed * hidden * factor, axis=0, keepdims=True)
    return d_hidden, d_gain


def placing_rows(slot_row, slots):
    places = lax.broadcasted_iota(jnp.int32, (slots, slot_row.shape[1]), 0)
    return (places == slot_row).astype(f32).astype(bf16)


def placing_cols(slot_col, slots):
    places = lax.broadcasted_iota(jnp.int32, (slot_col.shape[0], slots), 1)
    return (places == slot_col).astype(f32).astype(bf16)


def bias_kernel(offsets_ref, piece_col_ref, piece_row_ref, bias_ref):
    seq_len = piece_col_ref.shape[0]
    row = jnp.broadcast_to(offsets_ref[0], (seq_len, 2 * seq_len))
    shifted = pltpu.roll(row, seq_len + 1, 1, stride=1, stride_axis=0)[:, :seq_len]
    key_pos = lax.broadcasted_iota(jnp.int32, (seq_len, seq_len), 0)
    query_pos = lax.broadcasted_iota(jnp.int32, (seq_len, seq_len), 1)
    piece_col = piece_col_ref[...]
    same = (piece_col == piece_row_ref[...]) & (piece_col > 0)
    allowed = (key_pos <= query_pos) | same
    bias_ref[0] = jnp.where(allowed, shifted, masked_out).astype(bf16)


def bias_of(offsets, piece_ids):
    heads, seq_len = offsets.shape[0], piece_ids.shape[0]
    return pl.pallas_call(
        bias_kernel,
        grid=(heads,),
        in_specs=[
            pl.BlockSpec((1, 1, 2 * seq_len), lambda h: (h, 0, 0)),
            whole((seq_len, 1)),
            whole((1, seq_len)),
        ],
        out_specs=pl.BlockSpec((1, seq_len, seq_len), lambda h: (h, 0, 0)),
        out_shape=jax.ShapeDtypeStruct((heads, seq_len, seq_len), bf16),
        compiler_params=params(),
        name="bias_table",
    )(offsets[:, None, :], piece_ids[:, None], piece_ids[None, :])


def half_masks(rows, width):
    lane = lax.broadcasted_iota(jnp.int32, (rows, width), 1)
    return lane < (width // 2)


def forward_kernel(
    head_dim,
    hidden_ref,
    gain_attn_ref,
    gain_ffn_ref,
    wq_ref,
    wk_ref,
    wv_ref,
    wo_ref,
    wr_ref,
    slot_row_ref,
    bias_ref,
    q_ref,
    k_ref,
    v_ref,
    att_ref,
    lse_ref,
    middle_ref,
    logits_ref,
    sent_ref,
):
    pair, pairs = pl.program_id(0), pl.num_programs(0)
    seq_len = hidden_ref.shape[0]
    width = 2 * head_dim
    step = min(256, seq_len)

    @pl.when(pair == 0)
    def _():
        hidden = hidden_ref[...].astype(f32)
        normed = (hidden * rms_factor(hidden) * gain_attn_ref[...]).astype(bf16)
        q_ref[...] = dot(normed, wq_ref[...]).astype(bf16)
        k_ref[...] = dot(normed, wk_ref[...]).astype(bf16)
        v_ref[...] = dot(normed, wv_ref[...]).astype(bf16)

    lanes = pl.ds(pl.multiple_of(pair * width, width), width)
    q2 = q_ref[:, lanes] * jnp.asarray(head_dim**-0.5, bf16)
    k2 = k_ref[:, lanes]
    v2t = v_ref[:, lanes].T
    first = half_masks(seq_len, width)
    for half in range(2):
        q_one = jnp.where(first if half == 0 else ~first, q2, jnp.zeros_like(q2))
        v_one = v2t[half * head_dim : (half + 1) * head_dim]
        for start in range(0, seq_len, step):
            cols = slice(start, start + step)
            scores = dot(k2, q_one[cols], 1, 1) + bias_ref[half, :, cols].astype(f32)
            top = jnp.max(scores, axis=0, keepdims=True)
            raised = jnp.exp(scores - top)
            total = jnp.sum(raised, axis=0, keepdims=True)
            probs = (raised * (1.0 / total)).astype(bf16)
            rows = pl.ds(pl.multiple_of(pair * width + half * head_dim, head_dim), head_dim)
            att_ref[rows, cols] = dot(v_one, probs).astype(bf16)
            lse_ref[0, half : half + 1, cols] = top + jnp.log(total)

    @pl.when(pair == pairs - 1)
    def _():
        middle = hidden_ref[...].astype(f32) + dot(att_ref[...].T, wo_ref[...])
        middle_ref[...] = middle
        ffn_in = (middle * rms_factor(middle) * gain_ffn_ref[...]).astype(bf16)
        logits_ref[...] = dot(ffn_in, wr_ref[...])
        placing = placing_rows(slot_row_ref[...], sent_ref.shape[0])
        sent_ref[...] = dot(placing, ffn_in).astype(bf16)


def attention_forward(hidden, gain_attn, gain_ffn, mats, slot_row, bias):
    seq_len, width = hidden.shape
    heads = bias.shape[0]
    head_dim = width // heads
    experts = mats[4].shape[1]
    slots = 2 * seq_len
    ins = (hidden, gain_attn, gain_ffn, *mats, slot_row)
    tall = jax.ShapeDtypeStruct((seq_len, width), bf16)
    outs = (
        tall,
        tall,
        tall,
        jax.ShapeDtypeStruct((width, seq_len), bf16),
        jax.ShapeDtypeStruct((heads // 2, 2, seq_len), f32),
        jax.ShapeDtypeStruct((seq_len, width), f32),
        jax.ShapeDtypeStruct((seq_len, experts), f32),
        jax.ShapeDtypeStruct((slots, width), bf16),
    )
    out_specs = whole_of(outs)
    out_specs[4] = pl.BlockSpec((1, 2, seq_len), lambda p: (p, 0, 0))
    return pl.pallas_call(
        partial(forward_kernel, head_dim),
        grid=(heads // 2,),
        in_specs=whole_of(ins) + [pl.BlockSpec((2, seq_len, seq_len), lambda p: (p, 0, 0))],
        out_specs=out_specs,
        out_shape=outs,
        compiler_params=params(),
        name="attention_forward",
    )(*ins, bias)


def diagonal_fold(values, seq_len):
    rows, wide = seq_len, 2 * seq_len
    folded = None
    tile = 128
    count = seq_len // tile
    for row_tile in range(count):
        piece = values[row_tile * tile : (row_tile + 1) * tile].astype(f32)
        before = (count - 1 - row_tile) * tile
        after = wide - seq_len - before
        parts = []
        if before:
            parts.append(jnp.zeros((tile, before), f32))
        parts.append(piece)
        if after:
            parts.append(jnp.zeros((tile, after), f32))
        padded = jnp.concatenate(parts, axis=1)
        folded = padded if folded is None else folded + padded
    rows = tile
    while rows > 1:
        rows //= 2
        folded = pltpu.roll(folded[:rows], rows, 1) + folded[rows:]
    return folded


def backward_kernel(
    head_dim,
    d_back_ref,
    slot_col_ref,
    d_logits_ref,
    grad_ref,
    middle_ref,
    hidden_ref,
    gain_attn_ref,
    gain_ffn_ref,
    wq_ref,
    wk_ref,
    wv_ref,
    wo_ref,
    wr_ref,
    q_ref,
    k_ref,
    v_ref,
    att_ref,
    bias_ref,
    lse_ref,
    grad_new_ref,
    gwq_ref,
    gwk_ref,
    gwv_ref,
    gwo_ref,
    gwr_ref,
    gga_ref,
    ggf_ref,
    offsets_ref,
    d_att_s,
    d_middle_s,
    dqt_s,
    dk_s,
    dv_s,
    probs_s,
    scores_s,
):
    pair, pairs = pl.program_id(0), pl.num_programs(0)
    seq_len = hidden_ref.shape[0]
    width = 2 * head_dim
    step = min(256, seq_len)
    scale = head_dim**-0.5

    @pl.when(pair == 0)
    def _():
        placing = placing_cols(slot_col_ref[...], d_back_ref.shape[0])
        d_logits = d_logits_ref[...]
        d_ffn = dot(placing, d_back_ref[...]) + dot(d_logits, wr_ref[...], 1, 1)
        middle = middle_ref[...]
        gain_row = gain_ffn_ref[...]
        ffn_in = (middle * rms_factor(middle) * gain_row).astype(bf16)
        gwr_ref[...] = dot(ffn_in, d_logits, 0, 0)
        d_middle, d_gain = rms_pull(middle, gain_row, d_ffn)
        ggf_ref[...] = d_gain
        d_middle = d_middle + grad_ref[...]
        d_middle_s[...] = d_middle
        d_low = d_middle.astype(bf16)
        gwo_ref[...] = dot(att_ref[...], d_low).astype(bf16)
        d_att_s[...] = dot(d_low, wo_ref[...], 1, 1).astype(bf16)

    lanes = pl.ds(pl.multiple_of(pair * width, width), width)
    q2 = q_ref[:, lanes] * jnp.asarray(scale, bf16)
    k2 = k_ref[:, lanes]
    v2 = v_ref[:, lanes]
    da2 = d_att_s[:, lanes]
    k2t = k2.T
    first = half_masks(seq_len, width)
    d_key = jnp.zeros((seq_len, width), f32)
    d_value = jnp.zeros((seq_len, width), f32)
    for half in range(2):
        mask = first if half == 0 else ~first
        q_one = jnp.where(mask, q2, jnp.zeros_like(q2))
        da_one = jnp.where(mask, da2, jnp.zeros_like(da2))
        k_one = k2t[half * head_dim : (half + 1) * head_dim]
        rows = pl.ds(pl.multiple_of(pair * width + half * head_dim, head_dim), head_dim)
        for start in range(0, seq_len, step):
            cols = slice(start, start + step)
            scores = dot(k2, q_one[cols], 1, 1) + bias_ref[half, :, cols].astype(f32)
            probs = jnp.exp(scores - lse_ref[0, half : half + 1, cols])
            d_probs = dot(v2, da_one[cols], 1, 1)
            inner = jnp.sum(probs * d_probs, axis=0, keepdims=True)
            d_scores = (probs * (d_probs - inner)).astype(bf16)
            probs_s[:, cols] = probs.astype(bf16)
            scores_s[:, cols] = d_scores
            dqt_s[rows, cols] = (dot(k_one, d_scores) * scale).astype(bf16)
        d_key = d_key + dot(scores_s[...], q_one)
        d_value = d_value + dot(probs_s[...], da_one)
        offsets_ref[0, half : half + 1, :] = diagonal_fold(scores_s[...], seq_len)
    dk_s[:, lanes] = d_key.astype(bf16)
    dv_s[:, lanes] = d_value.astype(bf16)

    @pl.when(pair == pairs - 1)
    def _():
        hidden = hidden_ref[...].astype(f32)
        gain_row = gain_attn_ref[...]
        normed_t = (hidden * rms_factor(hidden) * gain_row).astype(bf16).T
        d_query = dqt_s[...].T
        d_normed = dot(d_query, wq_ref[...], 1, 1)
        gwq_ref[...] = dot(normed_t, d_query).astype(bf16)
        d_normed = d_normed + dot(dk_s[...], wk_ref[...], 1, 1)
        gwk_ref[...] = dot(normed_t, dk_s[...]).astype(bf16)
        d_normed = d_normed + dot(dv_s[...], wv_ref[...], 1, 1)
        gwv_ref[...] = dot(normed_t, dv_s[...]).astype(bf16)
        d_hidden, d_gain = rms_pull(hidden, gain_row, d_normed)
        gga_ref[...] = d_gain
        grad_new_ref[...] = d_hidden + d_middle_s[...]


def attention_backward(
    d_back, slot_col, d_logits, grad_now, middle, hidden, gains, mats, q_k_v, attended, bias, lse
):
    seq_len, width = hidden.shape
    heads = bias.shape[0]
    head_dim = width // heads
    experts = mats[4].shape[1]
    ins = (
        d_back,
        slot_col,
        d_logits,
        grad_now,
        middle,
        hidden,
        *gains,
        *mats,
        *q_k_v,
        attended,
    )
    square = jax.ShapeDtypeStruct((width, width), bf16)
    row = jax.ShapeDtypeStruct((1, width), f32)
    outs = (
        jax.ShapeDtypeStruct((seq_len, width), f32),
        square,
        square,
        square,
        square,
        jax.ShapeDtypeStruct((width, experts), f32),
        row,
        row,
        jax.ShapeDtypeStruct((heads // 2, 2, 2 * seq_len), f32),
    )
    out_specs = whole_of(outs)
    out_specs[8] = pl.BlockSpec((1, 2, 2 * seq_len), lambda p: (p, 0, 0))
    return pl.pallas_call(
        partial(backward_kernel, head_dim),
        grid=(heads // 2,),
        in_specs=whole_of(ins)
        + [
            pl.BlockSpec((2, seq_len, seq_len), lambda p: (p, 0, 0)),
            pl.BlockSpec((1, 2, seq_len), lambda p: (p, 0, 0)),
        ],
        out_specs=out_specs,
        out_shape=outs,
        scratch_shapes=[
            pltpu.VMEM((seq_len, width), bf16),
            pltpu.VMEM((seq_len, width), f32),
            pltpu.VMEM((width, seq_len), bf16),
            pltpu.VMEM((seq_len, width), bf16),
            pltpu.VMEM((seq_len, width), bf16),
            pltpu.VMEM((seq_len, seq_len), bf16),
            pltpu.VMEM((seq_len, seq_len), bf16),
        ],
        compiler_params=params(),
        name="attention_backward",
    )(*ins, bias, lse)


def combine_kernel(returned_ref, slot_col_ref, chosen_ref, logits_ref, middle_ref, comb_ref, out_ref):
    placing = placing_cols(slot_col_ref[...], returned_ref.shape[0])
    combined = dot(placing, returned_ref[...])
    comb_ref[...] = combined
    gate = jnp.sum(jax.nn.softmax(logits_ref[...], axis=-1) * chosen_ref[...], axis=1, keepdims=True)
    out_ref[...] = middle_ref[...] + gate * combined


def combine(returned, slot_col, chosen_f, logits, middle):
    outs = (jax.ShapeDtypeStruct(middle.shape, f32),) * 2
    ins = (returned, slot_col, chosen_f, logits, middle)
    return pl.pallas_call(
        combine_kernel,
        in_specs=whole_of(ins),
        out_specs=whole_of(outs),
        out_shape=outs,
        grid=(1,),
        compiler_params=params(),
        name="combine",
    )(*ins)


def spread_kernel(grad_ref, comb_ref, slot_row_ref, chosen_ref, logits_ref, d_sent_ref, d_logits_ref):
    grad_now = grad_ref[...].astype(f32)
    d_gate = jnp.sum(grad_now * comb_ref[...], axis=1, keepdims=True)
    shares = jax.nn.softmax(logits_ref[...], axis=-1)
    chosen = chosen_ref[...]
    gate = jnp.sum(shares * chosen, axis=1, keepdims=True)
    d_logits_ref[...] = (d_gate * shares * (chosen - gate)).astype(bf16)
    placing = placing_rows(slot_row_ref[...], d_sent_ref.shape[0])
    d_sent_ref[...] = dot(placing, (gate * grad_now).astype(bf16)).astype(bf16)


def spread(grad_now, combined, slot_row, chosen_f, logits):
    seq_len, width = grad_now.shape
    outs = (
        jax.ShapeDtypeStruct((2 * seq_len, width), bf16),
        jax.ShapeDtypeStruct(logits.shape, bf16),
    )
    ins = (grad_now, combined, slot_row, chosen_f, logits)
    return pl.pallas_call(
        spread_kernel,
        in_specs=whole_of(ins),
        out_specs=whole_of(outs),
        out_shape=outs,
        grid=(1,),
        compiler_params=params(),
        name="spread",
    )(*ins)


def gelu_tanh(pre_vals):
    return jax.nn.gelu(pre_vals, approximate=True)


def body(
    hidden_in,
    route,
    piece_ids,
    buckets,
    rel_table,
    gain_attn,
    gain_ffn,
    w_query,
    w_key,
    w_value,
    w_output,
    w_router,
    w_in,
    w_out,
    cotangent,
):
    count_x = lax.axis_size("gx")
    count_y = lax.axis_size("gy")
    seq_len, width = hidden_in.shape
    layers = w_query.shape[0]
    heads = rel_table.shape[1]
    experts = w_router.shape[2] * count_y
    capacity = 2 * seq_len // experts
    expert_of = route[:, 0]
    chosen = (expert_of[:, None] == jnp.arange(experts, dtype=jnp.int32)[None, :]).astype(jnp.int32)
    ranked = jnp.sum((jnp.cumsum(chosen, axis=0) - 1) * chosen, axis=1)
    slot_of = expert_of * capacity + ranked
    slot_row, slot_col = slot_of[None, :], slot_of[:, None]
    chosen_f = chosen.astype(f32)
    bucket_onehot = (
        buckets[:, None] == jnp.arange(rel_table.shape[0], dtype=jnp.int32)[None, :]
    ).astype(f32)
    bucket_onehot = jnp.pad(bucket_onehot, ((0, 1), (0, 0)))
    offsets = jnp.dot(bucket_onehot, rel_table.astype(f32), precision=highest).T
    bias = bias_of(offsets, piece_ids)
    gain_attn_f = gain_attn.astype(f32)
    gain_ffn_f = gain_ffn.astype(f32)

    tall, wide = w_query.shape[1], w_query.shape[2]

    def gather_mats(layer):
        packed = jnp.concatenate(
            [w_query[layer], w_key[layer], w_value[layer], w_output[layer]], axis=1
        )
        everything = lax.all_gather(packed, ("gx", "gy"), axis=0, tiled=False)
        parted = everything.reshape(count_x, count_y, tall, 4, wide)
        mats = parted.transpose(3, 0, 2, 1, 4).reshape(4, width, width)
        router = lax.all_gather(
            lax.all_gather(w_router[layer], "gy", axis=1, tiled=True), "gx", axis=0, tiled=True
        )
        return (mats[0], mats[1], mats[2], mats[3], router)

    hidden = hidden_in
    kept = []
    for layer in range(layers):
        mats = gather_mats(layer)
        gains = (gain_attn_f[layer][None], gain_ffn_f[layer][None])
        q, k, v, attended, lse, middle, logits, sent = attention_forward(
            hidden, gains[0], gains[1], mats, slot_row, bias
        )
        arrived = lax.all_to_all(
            sent.reshape(experts, capacity, width), "gy", split_axis=0, concat_axis=0, tiled=True
        ).reshape(experts * capacity, width)
        full_in = lax.all_gather(w_in[layer, 0], "gx", axis=1, tiled=True)
        full_out = lax.all_gather(w_out[layer, 0], "gx", axis=1, tiled=True)
        pre_act = dot(arrived, full_in)
        activated = gelu_tanh(pre_act).astype(bf16)
        made = dot(activated, full_out, 1, 1).astype(bf16)
        returned = lax.all_to_all(
            made.reshape(experts, capacity, width), "gy", split_axis=0, concat_axis=0, tiled=True
        ).reshape(experts * capacity, width)
        combined, hidden_next = combine(returned, slot_col, chosen_f, logits, middle)
        kept.append(
            (hidden, gains, mats, (q, k, v), attended, lse, middle, logits, combined)
            + (arrived, full_in, full_out, pre_act, activated)
        )
        hidden = hidden_next

    grad_now = cotangent
    table_sums = None
    parts = []
    for layer in reversed(range(layers)):
        (prior, gains, mats, q_k_v, attended, lse, middle, logits, combined) = kept[layer][:9]
        (arrived, full_in, full_out, pre_act, activated) = kept[layer][9:]
        d_sent, d_logits = spread(grad_now, combined, slot_row, chosen_f, logits)
        d_arrived = lax.all_to_all(
            d_sent.reshape(experts, capacity, width), "gy", split_axis=0, concat_axis=0, tiled=True
        ).reshape(experts * capacity, width)
        d_activated = dot(d_arrived, full_out)
        d_pre = jax.vjp(gelu_tanh, pre_act)[1](d_activated)[0].astype(bf16)
        d_rows = dot(d_pre, full_in, 1, 1).astype(bf16)
        grad_out_part = lax.psum_scatter(
            dot(d_arrived, activated, 0, 0).astype(bf16), "gx", scatter_dimension=1, tiled=True
        )
        grad_in_part = lax.psum_scatter(
            dot(arrived, d_pre, 0, 0).astype(bf16), "gx", scatter_dimension=1, tiled=True
        )
        d_back = lax.all_to_all(
            d_rows.reshape(experts, capacity, width), "gy", split_axis=0, concat_axis=0, tiled=True
        ).reshape(experts * capacity, width)
        grad_now, gwq, gwk, gwv, gwo, gwr, gga, ggf, offset_sums = attention_backward(
            d_back,
            slot_col,
            d_logits,
            grad_now.astype(f32),
            middle,
            prior,
            gains,
            mats,
            q_k_v,
            attended,
            bias,
            lse,
        )
        table_sums = offset_sums if table_sums is None else table_sums + offset_sums
        stacked = jnp.stack([gwq, gwk, gwv, gwo]).reshape(4, count_x, tall, count_y, wide)
        blocked = stacked.transpose(1, 3, 2, 0, 4).reshape(count_x * count_y, tall, 4 * wide)
        summed = lax.psum_scatter(blocked, ("gx", "gy"), scatter_dimension=0, tiled=True)[0]
        summed = summed.astype(f32).reshape(tall, 4, wide)
        parts.append((summed, gwr, gga, ggf, grad_in_part, grad_out_part))
    parts = parts[::-1]
    d_table = jnp.dot(
        table_sums.reshape(heads, 2 * seq_len), bucket_onehot, precision=highest
    ).T
    router_sum, d_table, gga_all, ggf_all = lax.psum(
        (
            jnp.stack([part[1] for part in parts]),
            d_table,
            jnp.concatenate([part[2] for part in parts]),
            jnp.concatenate([part[3] for part in parts]),
        ),
        ("gx", "gy"),
    )
    wide_router = w_router.shape[2]
    router_mine = lax.dynamic_slice(
        router_sum,
        (0, lax.axis_index("gx") * tall, lax.axis_index("gy") * wide_router),
        (layers, tall, wide_router),
    )
    attn_grads = [jnp.stack([part[0][:, index] for part in parts]) for index in range(4)]
    grad_in = jnp.stack([part[4] for part in parts]).astype(f32)[:, None]
    grad_out = jnp.stack([part[5] for part in parts]).astype(f32)[:, None]
    return (
        hidden,
        grad_now,
        d_table,
        gga_all,
        ggf_all,
        *attn_grads,
        router_mine,
        grad_in,
        grad_out,
    )


def solution(mesh):
    rows = P(("gx", "gy"), None)
    square = P(None, "gx", "gy")
    expert = P(None, "gy", None, "gx")
    return jax.shard_map(
        body,
        mesh=mesh,
        in_specs=(rows, rows, P(("gx", "gy")), P(), P(), P(), P())
        + (square,) * 5
        + (expert, expert, rows),
        out_specs=(rows, rows, P(), P(), P()) + (square,) * 5 + (expert, expert),
        check_vma=False,
    )
```

time: 2770 us -> 1160 us (0.42)
  local copies, waits for them, and re-layouts: 1560 us -> 185 us
  waiting for transfers between devices: 493 us -> 339 us
  Pallas kernels: 0 us -> 136 us
  matrix products: 252 us -> 127 us
  blocking collectives: 301 us -> 266 us
    gather x3 -> x0, local copies, waits for them, and re-layouts: 936 us -> none  [the longest x2 933 us: block_terms(): jnp.take(offset_bias, row_pos[:, None] - col_pos[None, :] + (seq_len - 1)...]
    unnamed x295 -> x77, local copies, waits for them, and re-layouts: 205 us -> 7.12 us
    rev x2 -> x0, local copies, waits for them, and re-layouts: 182 us -> none  [diagonal_sums(): flipped = values[:, :, ::-1]]
    reduce_scatter x12 -> x6, waiting for transfers between devices: 356 us -> 209 us  [the longest x2 96.7 us: body(): lax.psum_scatter(dot(d_arrived, activated, 0, 0).astype(bf16), 'gx', scat...]
    pallas_call x0 -> x9, Pallas kernels: none -> 136 us  [the longest x2 61.2 us: attention_backward(): pl.pallas_call(partial(backward_kernel, head_dim), grid=(heads // 2,), in...]
    dot_general x64 -> x14, matrix products: 252 us -> 127 us  [the longest x12 127 us: dot(): lax.dot_general(lhs, rhs, (((lhs_dim,), (rhs_dim,)), ((), ())), preferred...]
    all_gather x2 -> x4, blocking collectives: 183 us -> 87.7 us  [the longest x2 74.3 us: gather_mats(): lax.all_gather(w_router[layer], 'gy', axis=1, tiled=True)]
    reshape x30 -> x7, local copies, waits for them, and re-layouts: 140 us -> 60.4 us  [the longest x4 38.7 us: gather_mats(): parted = everything.reshape(count_x, count_y, tall, 4, wide)]
  transfers between devices with their start and end apart: 30 -> 17, of which waited for: 10 -> 9; matrix products, arithmetic and copies ran while one was open for 63% -> 28% of each run, Pallas kernels for 0% -> 8%
where the time goes in v1:
time: 1160 us; the launch traced here: 1150 us
  waiting for transfers between devices  339 us (29%)
  blocking collectives  266 us (23%)
  local copies, waits for them, and re-layouts  185 us (16%)
  Pallas kernels  136 us (12%)
  matrix products  127 us (11%)
  other arithmetic  57.9 us (5%)
  starting transfers between devices  26.1 us (2%)
  between operations  15.1 us (1%)
    dot_general x12, matrix products, dot(): lax.dot_general(lhs, rhs, (((lhs_dim,), (rhs_dim,)), ((), ())), preferred...  127 us
    reduce_scatter x2, waiting for transfers between devices, body(): lax.psum_scatter(dot(d_arrived, activated, 0, 0).astype(bf16), 'gx', scat...  96.7 us
    reduce_scatter x2, waiting for transfers between devices, body(): lax.psum_scatter(dot(arrived, d_pre, 0, 0).astype(bf16), 'gx', scatter_di...  95.7 us
    all_to_all x2, waiting for transfers between devices, body(): lax.all_to_all(sent.reshape(experts, capacity, width), 'gy', split_axis=0...  76.4 us
    another operation x16, local copies, waits for them, and re-layouts, body(): jnp.stack([gwq, gwk, gwv, gwo]).reshape(4, count_x, tall, count_y, wide)  76 us
    all_gather x2, blocking collectives, gather_mats(): lax.all_gather(w_router[layer], 'gy', axis=1, tiled=True)  74.3 us
    pallas_call x2, Pallas kernels, attention_backward(): pl.pallas_call(partial(backward_kernel, head_dim), grid=(heads // 2,), in...  61.2 us
    all_to_all x1, blocking collectives, body(): lax.all_to_all(d_rows.reshape(experts, capacity, width), 'gy', split_axis...  54.7 us
  transfers between devices with their start and end apart: 17, of which 9 were waited for; matrix products, arithmetic and copies ran while one was open for 28% of the time, Pallas kernels for 8%

profile of v1, /device:TPU:0, one launch (start us, length us, event | category | flops | bytes accessed | tf_op | source)
XLA Modules:
  0.0 1152.2 jit_solution(2224208666153122216)
XLA Ops:
  16.4 22.3 %all-gather.1 = bf16[1,192,8]{1,0,2:T(2,128)(2,1)S(1)} all-gather(bf16[1,192,1]{1,0,2:T(2,128)(2,1)S(1)} %get-tuple-element.159), channel_id=3, replica_groups=mesh['gx'=4,'gy'=8] {'gy'}, dimensions={2}, use_global_device_ids=true | all-gather | bytes 3456 | tf_op jit(solution)/shard_map/all_gather | solution.py:483
  45.0 8.7 bias_table.1.bias_ref
  53.7 6.0 all-gather.2
  60.4 17.8 %all-gather.17.cloned.1.call-done = bf16[6144,384]{1,0:T(8,128)(2,1)} async-done(((bf16[192,384]{1,0:T(8,128)(2,1)}), bf16[6144,384]{1,0:T(8,128)(2,1)}) %all-gather.17.cloned.1.call-update) | async-done | bytes 4718608 | tf_op jit(solution)/shard_map/all_gather | solution.py:479
  78.2 12.5 %reshape.232 = bf16[4,8,192,4,96]{4,3,2,1,0:T(4,128)(2,1)} reshape(bf16[6144,384]{1,0:T(8,128)(2,1)} %all-gather.17.cloned.1.call-done) | data formatting | bytes 9437184 | tf_op jit(solution)/shard_map/reshape | solution.py:480
  90.6 6.8 copy.84
  111.5 23.3 %attention_forward.2 = (bf16[512,768]{1,0:T(8,128)(2,1)}, bf16[512,768]{1,0:T(8,128)(2,1)}, bf16[512,768]{1,0:T(8,128)(2,1)}, bf16[768,512]{1,0:T(8,128)(2,1)}, ...) custom-call(bf16[512,768]{1,0:T(8,128)(2,1)} %hidden_ref.3, ...), custom_call_target="tpu_custom_call" | custom-call | tf_op jit(solution)/shard_map/attention_forward/pallas_call | solution.py:177
  139.7 38.9 %all-to-all-done = bf16[8,128,768]{2,1,0:T(8,128)(2,1)S(1)} async-done(((bf16[8,128,768]{2,1,0:T(8,128)(2,1)}), bf16[8,128,768]{2,1,0:T(8,128)(2,1)S(1)}, u32[]{:S(2)}, u32[]{:S(2)}) %all-to-all-start) | async-done | bytes 1572896 | tf_op jit(solution)/shard_map/all_to_all | solution.py:495
  178.6 10.9 fusion.28
  189.5 12.7 %fusion.37 = bf16[1024,768]{1,0:T(8,128)(2,1)} fusion(bf16[1,1,768,3072]{3,2,1,0:T(8,128)(2,1)} %all-gather.21.cloned.1.call-done, f32[1024,3072]{1,0:T(8,128)} %fusion.28), kind=kOutput, calls=%fused_computation.47 | convolution fusion | flops 4860936192 | bytes 18874368 | tf_op jit(solution)/shard_map/dot_general | solution.py:32
  206.5 52.0 %all-gather.6 = bf16[1,192,8]{1,0,2:T(2,128)(2,1)S(1)} all-gather(bf16[1,192,1]{1,0,2:T(2,128)(2,1)S(1)} %get-tuple-element.158), channel_id=8, replica_groups=mesh['gx'=4,'gy'=8] {'gy'}, dimensions={2}, use_global_device_ids=true | all-gather | bytes 3456 | tf_op jit(solution)/shard_map/all_gather | solution.py:483
  258.7 7.3 all-gather.7
  266.8 12.6 %reshape.238 = bf16[4,8,192,4,96]{4,3,2,1,0:T(4,128)(2,1)} reshape(bf16[6144,384]{1,0:T(8,128)(2,1)} %all-gather.23.cloned.1.call-done) | data formatting | bytes 9437184 | tf_op jit(solution)/shard_map/reshape | solution.py:480
  279.4 6.9 copy.83
  305.2 23.7 %attention_forward.3 = (bf16[512,768]{1,0:T(8,128)(2,1)}, bf16[512,768]{1,0:T(8,128)(2,1)}, bf16[512,768]{1,0:T(8,128)(2,1)}, bf16[768,512]{1,0:T(8,128)(2,1)}, ...) custom-call(f32[512,768]{1,0:T(8,128)} %get-tuple-element.57.hidden_ref, ...), custom_call_target="tpu_custom_call" | custom-call | tf_op jit(solution)/shard_map/attention_forward/pallas_call | solution.py:177
  329.0 8.7 all-to-all-start.2
  337.7 37.5 %all-to-all-done.2 = bf16[8,128,768]{2,1,0:T(8,128)(2,1)S(1)} async-done(((bf16[8,128,768]{2,1,0:T(8,128)(2,1)}), bf16[8,128,768]{2,1,0:T(8,128)(2,1)S(1)}, u32[]{:S(2)}, u32[]{:S(2)}) %all-to-all-start.2) | async-done | bytes 1572896 | tf_op jit(solution)/shard_map/all_to_all | solution.py:495
  375.2 10.9 fusion.20
  386.1 11.8 %fusion.43 = bf16[1024,768]{1,0:T(8,128)(2,1)S(1)} fusion(bf16[1,1,768,3072]{3,2,1,0:T(8,128)(2,1)} %all-gather.27.cloned.1.call-done, f32[1024,3072]{1,0:T(8,128)} %fusion.20), kind=kOutput, calls=%fused_computation.49 | convolution fusion | flops 4860936192 | bytes 18874368 | tf_op jit(solution)/shard_map/dot_general | solution.py:32
  397.9 41.1 %all_to_all.40 = bf16[8,128,768]{2,1,0:T(8,128)(2,1)} all-to-all(bf16[8,128,768]{2,1,0:T(8,128)(2,1)S(1)} %bitcast.164), channel_id=1, replica_groups=mesh['gx'=4,'gy'=8] {'gy'}, dimensions={0} | all-to-all | bytes 3145728 | tf_op jit(solution)/shard_map/all_to_all | solution.py:503
  439.0 4.9 combine.3
  448.2 40.6 %all_to_all.41 = bf16[8,128,768]{2,1,0:T(8,128)(2,1)S(1)} all-to-all(bf16[8,128,768]{2,1,0:T(8,128)(2,1)} %bitcast.162), channel_id=1, replica_groups=mesh['gx'=4,'gy'=8] {'gy'}, dimensions={0} | all-to-all | bytes 3145728 | tf_op jit(solution)/shard_map/all_to_all | solution.py:520
  488.8 13.8 %fusion.13 = bf16[1024,3072]{1,0:T(8,128)(2,1)S(1)} fusion(f32[1024,3072]{1,0:T(8,128)} %fusion.20, bf16[1024,768]{1,0:T(8,128)(2,1)S(1)} %bitcast.156, bf16[1,1,768,3072]{3,2,1,0:T(8,128)(2,1)S(1)} %bitcast.192), kind=kOutput, calls=%fused_computation.17 | convolution fusion | flops 4894752768 | bytes 25165824 | tf_op jit(solution)/shard_map/dot_general | solution.py:32
  502.7 6.2 fusion.40
  514.0 35.2 %all-to-all-done.5 = bf16[8,128,768]{2,1,0:T(8,128)(2,1)S(1)} async-done(((bf16[8,128,768]{2,1,0:T(8,128)(2,1)}), bf16[8,128,768]{2,1,0:T(8,128)(2,1)S(1)}, u32[]{:S(2)}, u32[]{:S(2)}) %all-to-all-start.5) | async-done | bytes 1572896 | tf_op jit(solution)/shard_map/all_to_all | solution.py:532
  550.3 30.5 %attention_backward.2 = (f32[512,768]{1,0:T(8,128)}, bf16[768,768]{1,0:T(8,128)(2,1)}, bf16[768,768]{1,0:T(8,128)(2,1)}, bf16[768,768]{1,0:T(8,128)(2,1)}, bf16[...) custom-call(bf16[1024,768]{1,0:T(8,128)(2,1)} %bitcast.145, ...), custom_call_target="tpu_custom_call" | custom-call | tf_op jit(solution)/shard_map/attention_backward/pallas_call | solution.py:355
  601.3 6.3 copy.69
  611.6 6.3 copy.68
  627.2 20.0 %maximum_bitcast_fusion.1 = bf16[4,8,192,4,96]{4,3,2,1,0:T(4,128)(2,1)} fusion(bf16[1,4,192,8,96]{4,0,2,3,1:T(2,128)(2,1)S(1)} %copy.70, bf16[1,4,192,8,96]{4,0,2,3,1:T(2,128)(2,1)S(1)} %copy-done.2, bf16[1,4,192,8,96]{4,0,2,3,1:T(2,128)(2,1)} %copy.68, bf16[1,4,192,8,96]{4,0,2,3,1:T(2,128)(2,1)S(1)} %copy.67), kind=kLoop, calls=%fused_computation.21 | loop fusion | flops 18874368 | bytes 9437184 | tf_op jit(solution)/shard_map/transpose | solution.py:551
  647.2 10.8 reshape.253
  658.1 15.5 %fusion.6 = bf16[1024,3072]{1,0:T(8,128)(2,1)S(1)} fusion(f32[1024,3072]{1,0:T(8,128)} %fusion.28, bf16[1024,768]{1,0:T(8,128)(2,1)} %bitcast.38, bf16[1,1,768,3072]{3,2,1,0:T(8,128)(2,1)} %all-gather.21.cloned.1.call-done), kind=kOutput, calls=%fused_computation.10 | convolution fusion | flops 4894752768 | bytes 25165824 | tf_op jit(solution)/shard_map/dot_general | solution.py:32
  673.7 5.1 fusion.34
  678.8 54.7 %all_to_all.42 = bf16[8,128,768]{2,1,0:T(8,128)(2,1)} all-to-all(bf16[8,128,768]{2,1,0:T(8,128)(2,1)S(1)} %bitcast.163), channel_id=1, replica_groups=mesh['gx'=4,'gy'=8] {'gy'}, dimensions={0} | all-to-all | bytes 3145728 | tf_op jit(solution)/shard_map/all_to_all | solution.py:532
  733.5 30.6 %attention_backward.3 = (f32[512,768]{1,0:T(8,128)}, bf16[768,768]{1,0:T(8,128)(2,1)}, bf16[768,768]{1,0:T(8,128)(2,1)}, bf16[768,768]{1,0:T(8,128)(2,1)}, bf16[...) custom-call(bf16[1024,768]{1,0:T(8,128)(2,1)} %bitcast.146, ...), custom_call_target="tpu_custom_call" | custom-call | tf_op jit(solution)/shard_map/attention_backward/pallas_call | solution.py:355
  777.3 6.3 copy.65
  787.7 6.4 copy.64
  802.9 20.1 %maximum_bitcast_fusion = bf16[4,8,192,4,96]{4,3,2,1,0:T(4,128)(2,1)} fusion(bf16[1,4,192,8,96]{4,0,2,3,1:T(2,128)(2,1)S(1)} %copy.66, bf16[1,4,192,8,96]{4,0,2,3,1:T(2,128)(2,1)S(1)} %copy-done.3, bf16[1,4,192,8,96]{4,0,2,3,1:T(2,128)(2,1)} %copy.64, bf16[1,4,192,8,96]{4,0,2,3,1:T(2,128)(2,1)S(1)} %copy.63), kind=kLoop, calls=%fused_computation.20 | loop fusion | flops 18874368 | bytes 9437184 | tf_op jit(solution)/shard_map/transpose | solution.py:551
  823.0 10.8 reshape.252
  835.2 9.6 convolution_convert_fusion.2
  846.2 9.7 convolution_convert_fusion.3
  857.4 10.2 convolution_convert_fusion
  867.8 10.6 convolution_convert_fusion.1
  880.1 41.7 %all-reduce.1 = (f32[32,12]{0,1:T(8,128)}, f32[2,768]{1,0:T(2,128)}, f32[2,768]{1,0:T(2,128)}, f32[2,768,8]{1,2,0:T(8,128)S(1)}) all-reduce(f32[32,12]{0,1:T(8,128)S(1)} %fusion.47, f32[2,768]{1,0:T(2,128)S(1)} %pad_maximum_fusion.7, f32[2,768]{1,0:T(2,128)S(1)} %pad_maximum_fusion.8, ...), channel_id=1, replica_groups=mesh['gx'=4,'gy'=8] {'gx','gy'}, use_global_device_ids=true, to_apply=%region_3.4 | all-reduce | flops 15744 | bytes 125952 | tf_op jit(solution)/shard_map/psum | solution.py:559
  923.9 16.4 %reduce-scatter.7.cloned.1.call-done = bf16[1,192,384]{2,1,0:T(8,128)(2,1)} async-done(((bf16[32,192,384]{2,1,0:T(8,128)(2,1)}), bf16[1,192,384]{2,1,0:T(8,128)(2,1)}) %reduce-scatter.7.cloned.1.call-update) | async-done | bytes 147472 | tf_op jit(solution)/shard_map/reduce_scatter | solution.py:552
  944.5 45.3 %reduce-scatter.13.cloned.1.call-done = bf16[768,768]{1,0:T(8,128)(2,1)} async-done(((bf16[768,3072]{1,0:T(8,128)(2,1)}), bf16[768,768]{1,0:T(8,128)(2,1)}) %reduce-scatter.13.cloned.1.call-update) | async-done | bytes 1179664 | tf_op jit(solution)/shard_map/reduce_scatter | solution.py:529
  989.7 50.4 %reduce-scatter.11.cloned.1.call-done = bf16[768,768]{1,0:T(8,128)(2,1)} async-done(((bf16[768,3072]{1,0:T(8,128)(2,1)}), bf16[768,768]{1,0:T(8,128)(2,1)}) %reduce-scatter.11.cloned.1.call-update) | async-done | bytes 1179664 | tf_op jit(solution)/shard_map/reduce_scatter | solution.py:529
  1044.3 46.3 %reduce-scatter.17.cloned.1.call-done = bf16[768,768]{1,0:T(8,128)(2,1)} async-done(((bf16[768,3072]{1,0:T(8,128)(2,1)}), bf16[768,768]{1,0:T(8,128)(2,1)}) %reduce-scatter.17.cloned.1.call-update) | async-done | bytes 1179664 | tf_op jit(solution)/shard_map/reduce_scatter | solution.py:526
  1090.6 50.4 %reduce-scatter.15.cloned.1.call-done = bf16[768,768]{1,0:T(8,128)(2,1)} async-done(((bf16[768,3072]{1,0:T(8,128)(2,1)}), bf16[768,768]{1,0:T(8,128)(2,1)}) %reduce-scatter.15.cloned.1.call-update) | async-done | bytes 1179664 | tf_op jit(solution)/shard_map/reduce_scatter | solution.py:526
  (187 shorter events, 150.0 us)
Async XLA Ops:
  7.2 34.8 %copy-start = (bf16[32,12]{0,1:T(8,128)(2,1)S(1)}, bf16[32,12]{0,1:T(8,128)(2,1)}, u32[]{:S(2)}) copy-start(bf16[32,12]{0,1:T(8,128)(2,1)} %param.19) | copy-start | bytes 2308
  7.2 6.2 copy-start.6
  7.2 71.0 %all-gather.17.cloned.1.call-start = ((), (), s32[]{:S(2)}) async-start(), calls=%async_computation.20 | async-start | bytes 4866048 | tf_op jit(solution)/shard_map/all_gather | solution.py:479
  10.0 129.7 %all-gather.19.cloned.1.call-start = ((), (), s32[]{:S(2)}) async-start(), calls=%async_computation.21 | async-start | bytes 5898240 | tf_op jit(solution)/shard_map/all_gather | solution.py:498
  13.2 3.2 copy-start.25
  13.2 25.6 %copy-start.20 = (s32[512,1]{0,1:T(1,128)S(1)}, s32[512,1]{0,1:T(1,128)}, u32[]{:S(2)}) copy-start(s32[512,1]{0,1:T(1,128)} %param.16) | copy-start | bytes 6148
  13.3 27.8 %copy-start.24 = (s32[1023]{0:T(1024)S(1)}, s32[1023]{0:T(1024)}, u32[]{:S(2)}) copy-start(s32[1023]{0:T(1024)} %param.18) | copy-start | bytes 12280
  13.3 29.5 %copy-start.23 = (s32[512]{0:T(512)S(1)}, s32[512]{0:T(512)}, u32[]{:S(2)}) copy-start(s32[512]{0:T(512)} %param.17) | copy-start | bytes 6148
  13.3 176.2 %all-gather.21.cloned.1.call-start = ((), (), s32[]{:S(2)}) async-start(), calls=%async_computation.22 | async-start | bytes 5898240 | tf_op jit(solution)/shard_map/all_gather | solution.py:499
  14.9 251.9 %all-gather.23.cloned.1.call-start = ((), (), s32[]{:S(2)}) async-start(), calls=%async_computation.23 | async-start | bytes 4866048 | tf_op jit(solution)/shard_map/all_gather | solution.py:479
  15.8 321.9 %all-gather.25.cloned.1.call-start = ((), (), s32[]{:S(2)}) async-start(), calls=%async_computation.24 | async-start | bytes 5898240 | tf_op jit(solution)/shard_map/all_gather | solution.py:498
  38.9 20.9 %copy-start.21 = (bf16[2,768]{1,0:T(2,128)(2,1)S(1)}, bf16[2,768]{1,0:T(2,128)(2,1)}, u32[]{:S(2)}) copy-start(bf16[2,768]{1,0:T(2,128)(2,1)} %param.21) | copy-start | bytes 9220
  38.9 20.9 %copy-start.22 = (bf16[2,768]{1,0:T(2,128)(2,1)S(1)}, bf16[2,768]{1,0:T(2,128)(2,1)}, u32[]{:S(2)}) copy-start(bf16[2,768]{1,0:T(2,128)(2,1)} %param.20) | copy-start | bytes 9220
  134.8 43.8 %all-to-all-start = ((bf16[8,128,768]{2,1,0:T(8,128)(2,1)}), bf16[8,128,768]{2,1,0:T(8,128)(2,1)S(1)}, u32[]{:S(2)}, u32[]{:S(2)}) async-start(bf16[8,128,768]{2,1,0:T(8,128)(2,1)} %bitcast.159), calls=%async_computation | async-start | bytes 3145728 | tf_op jit(solution)/shard_map/all_to_all | solution.py:495
  139.1 247.0 %all-gather.27.cloned.1.call-start = ((), (), s32[]{:S(2)}) async-start(), calls=%async_computation.25 | async-start | bytes 5898240 | tf_op jit(solution)/shard_map/all_gather | solution.py:499
  178.6 10.9 copy-start.7
  202.2 98.2 %all-to-all-start.1 = ((bf16[8,128,768]{2,1,0:T(8,128)(2,1)}), bf16[8,128,768]{2,1,0:T(8,128)(2,1)}, u32[]{:S(2)}, u32[]{:S(2)}) async-start(bf16[8,128,768]{2,1,0:T(8,128)(2,1)} %bitcast.18), calls=%async_computation.1 | async-start | bytes 3145728 | tf_op jit(solution)/shard_map/all_to_all | solution.py:503
  329.0 46.3 %all-to-all-start.2 = ((bf16[8,128,768]{2,1,0:T(8,128)(2,1)}), bf16[8,128,768]{2,1,0:T(8,128)(2,1)S(1)}, u32[]{:S(2)}, u32[]{:S(2)}) async-start(bf16[8,128,768]{2,1,0:T(8,128)(2,1)} %bitcast.160), calls=%async_computation.2 | async-start | bytes 3145728 | tf_op jit(solution)/shard_map/all_to_all | solution.py:495
  375.2 10.9 copy-start.9
  397.9 90.9 %slice-start.4 = ((s8[4718592]{0:T(1024)(128)(4,1)}), s8[4194304]{0:T(1024)(128)(4,1)S(1)}, s32[]{:S(2)}) async-start(s8[4718592]{0:T(1024)(128)(4,1)} %bitcast.191), calls=%async_computation.30 | async-start | bytes 8388608
  439.0 49.8 %slice-start.5 = ((s8[4718592]{0:T(1024)(128)(4,1)}), s8[524288]{0:T(1024)(128)(4,1)S(1)}, s32[]{:S(2)}) async-start(s8[4718592]{0:T(1024)(128)(4,1)} %bitcast.191), calls=%async_computation.31 | async-start | bytes 1048576
  448.2 54.4 %slice-start.2 = ((s8[4718592]{0:T(1024)(128)(4,1)}), s8[4194304]{0:T(1024)(128)(4,1)S(1)}, s32[]{:S(2)}) async-start(s8[4718592]{0:T(1024)(128)(4,1)} %bitcast.189), calls=%async_computation.28 | async-start | bytes 8388608
  488.8 13.8 %copy-start.11 = (bf16[8,128,768]{2,1,0:T(8,128)(2,1)}, bf16[8,128,768]{2,1,0:T(8,128)(2,1)S(1)}, u32[]{:S(2)}) copy-start(bf16[8,128,768]{2,1,0:T(8,128)(2,1)S(1)} %all_to_all.41) | copy-start | bytes 4718596
  488.8 13.8 %slice-start.3 = ((s8[4718592]{0:T(1024)(128)(4,1)}), s8[524288]{0:T(1024)(128)(4,1)S(1)}, s32[]{:S(2)}) async-start(s8[4718592]{0:T(1024)(128)(4,1)} %bitcast.189), calls=%async_computation.29 | async-start | bytes 1048576
  502.7 6.2 copy-start.30
  502.7 10.0 copy-start.5
  508.9 40.3 %all-to-all-start.5 = ((bf16[8,128,768]{2,1,0:T(8,128)(2,1)}), bf16[8,128,768]{2,1,0:T(8,128)(2,1)S(1)}, u32[]{:S(2)}, u32[]{:S(2)}) async-start(bf16[8,128,768]{2,1,0:T(8,128)(2,1)} %bitcast.161), calls=%async_computation.5 | async-start | bytes 3145728 | tf_op jit(solution)/shard_map/all_to_all | solution.py:532
  580.9 8.9 copy-start.15
  585.5 72.6 %all-to-all-start.6 = ((bf16[8,128,768]{2,1,0:T(8,128)(2,1)}), bf16[8,128,768]{2,1,0:T(8,128)(2,1)}, u32[]{:S(2)}, u32[]{:S(2)}) async-start(bf16[8,128,768]{2,1,0:T(8,128)(2,1)} %bitcast.158), calls=%async_computation.6 | async-start | bytes 3145728 | tf_op jit(solution)/shard_map/all_to_all | solution.py:520
  589.8 332.6 %reduce-scatter.9.cloned.1.call-start = ((), (), s32[]{:S(2)}) async-start(), calls=%async_computation.15 | async-start | bytes 4866048 | tf_op jit(solution)/shard_map/reduce_scatter | solution.py:552
  622.4 4.8 copy-start.2
  647.2 26.5 %slice-start = ((s8[4718592]{0:T(1024)(128)(4,1)}), s8[524288]{0:T(1024)(128)(4,1)S(1)}, s32[]{:S(2)}) async-start(s8[4718592]{0:T(1024)(128)(4,1)} %bitcast.187), calls=%async_computation.26 | async-start | bytes 1048576
  658.1 282.2 %reduce-scatter.7.cloned.1.call-start = ((), (), s32[]{:S(2)}) async-start(), calls=%async_computation.14 | async-start | bytes 4866048 | tf_op jit(solution)/shard_map/reduce_scatter | solution.py:552
  658.1 15.6 %slice-start.1 = ((s8[4718592]{0:T(1024)(128)(4,1)}), s8[4194304]{0:T(1024)(128)(4,1)S(1)}, s32[]{:S(2)}) async-start(s8[4718592]{0:T(1024)(128)(4,1)} %bitcast.187), calls=%async_computation.27 | async-start | bytes 8388608
  673.7 5.1 copy-start.31
  798.1 4.8 copy-start.3
  833.8 1.4 copy-start.10
  833.8 155.9 %reduce-scatter.13.cloned.1.call-start = ((), (), s32[]{:S(2)}) async-start(), calls=%async_computation.17 | async-start | bytes 5898240 | tf_op jit(solution)/shard_map/reduce_scatter | solution.py:529
  844.8 1.4 copy-start.8
  844.8 195.4 %reduce-scatter.11.cloned.1.call-start = ((), (), s32[]{:S(2)}) async-start(), calls=%async_computation.16 | async-start | bytes 5898240 | tf_op jit(solution)/shard_map/reduce_scatter | solution.py:529
  855.9 1.4 copy-start.12
  855.9 234.6 %reduce-scatter.17.cloned.1.call-start = ((), (), s32[]{:S(2)}) async-start(), calls=%async_computation.19 | async-start | bytes 5898240 | tf_op jit(solution)/shard_map/reduce_scatter | solution.py:526
  867.5 273.4 %reduce-scatter.15.cloned.1.call-start = ((), (), s32[]{:S(2)}) async-start(), calls=%async_computation.18 | async-start | bytes 5898240 | tf_op jit(solution)/shard_map/reduce_scatter | solution.py:526
  878.4 1.3 copy-start.27
  878.4 1.3 copy-start.26
  878.4 1.3 copy-start.28
  878.4 1.4 copy-start.14
  1040.2 104.9 %copy-start.1 = (bf16[32,12]{0,1:T(8,128)(2,1)S(1)}, bf16[32,12]{0,1:T(8,128)(2,1)}, u32[]{:S(2)}) copy-start(bf16[32,12]{0,1:T(8,128)(2,1)} %param.19) | copy-start | bytes 2308
  (7 other events, 7.6 us)
Sparse Core Ops, SparseCore 0:
  11.6 66.5 all-gather.16
  80.3 36.2 all-gather.18
  118.8 37.4 all-gather.20
  159.7 79.0 all-gather.22
  240.1 43.3 all-gather.24
  284.9 37.4 all-gather.26
  658.2 111.6 reduce-scatter.8
  833.9 106.2 reduce-scatter.6
  942.8 46.9 reduce-scatter.12
  992.3 47.8 reduce-scatter.10
  1042.7 47.8 reduce-scatter.16
  1093.1 47.8 reduce-scatter.14

commit v2 on v1

--- a/solution.py
+++ b/solution.py
@@ -12,6 +12,9 @@
 f32 = jnp.float32
 bf16 = jnp.bfloat16
 masked_out = -1e30
+MESH = pl.DeviceIdType.MESH
+vmem_spec = pl.BlockSpec(memory_space=pltpu.VMEM)
+any_spec = pl.BlockSpec(memory_space=pl.ANY)
 vmem_bytes = 56 * 1024 * 1024
 
 
@@ -45,6 +48,14 @@
     d_hidden = factor * scaled - hidden * (factor * factor * factor * inner)
     d_gain = jnp.sum(d_normed * hidden * factor, axis=0, keepdims=True)
     return d_hidden, d_gain
+
+
+def xor_of(index, other, bits):
+    total = 0
+    for bit in range(bits):
+        power = 1 << bit
+        total = total + ((index // power + other // power) % 2) * power
+    return total
 
 
 def placing_rows(slot_row, slots):
@@ -91,18 +102,36 @@
     return lane < (width // 2)
 
 
+def unblock(grid_shape, blocks_ref, mats_ref, router_ref):
+    count_x, count_y = grid_shape
+    tall = mats_ref.shape[1] // count_x
+    wide = mats_ref.shape[2] // count_y
+    router_rows = []
+    for first in range(count_x):
+        block_rows = [first * count_y + second for second in range(count_y)]
+        rows = slice(first * tall, (first + 1) * tall)
+        for which in range(4):
+            lanes = slice(which * wide, (which + 1) * wide)
+            mats_ref[which, rows, :] = jnp.concatenate(
+                [blocks_ref[block, :tall, lanes] for block in block_rows], axis=1
+            )
+        router_rows.append(
+            jnp.concatenate([blocks_ref[block, tall : tall + 1, :tall] for block in block_rows], axis=0)
+        )
+    router_ref[...] = jnp.concatenate(router_rows, axis=1)
+
+
 def forward_kernel(
     head_dim,
+    grid_shape,
     hidden_ref,
     gain_attn_ref,
     gain_ffn_ref,
-    wq_ref,
-    wk_ref,
-    wv_ref,
-    wo_ref,
-    wr_ref,
     slot_row_ref,
+    blocks_ref,
     bias_ref,
+    mats_ref,
+    router_ref,
     q_ref,
     k_ref,
     v_ref,
@@ -119,11 +148,12 @@
 
     @pl.when(pair == 0)
     def _():
+        unblock(grid_shape, blocks_ref, mats_ref, router_ref)
         hidden = hidden_ref[...].astype(f32)
         normed = (hidden * rms_factor(hidden) * gain_attn_ref[...]).astype(bf16)
-        q_ref[...] = dot(normed, wq_ref[...]).astype(bf16)
-        k_ref[...] = dot(normed, wk_ref[...]).astype(bf16)
-        v_ref[...] = dot(normed, wv_ref[...]).astype(bf16)
+        q_ref[...] = dot(normed, mats_ref[0]).astype(bf16)
+        k_ref[...] = dot(normed, mats_ref[1]).astype(bf16)
+        v_ref[...] = dot(normed, mats_ref[2]).astype(bf16)
 
     lanes = pl.ds(pl.multiple_of(pair * width, width), width)
     q2 = q_ref[:, lanes] * jnp.asarray(head_dim**-0.5, bf16)
@@ -146,23 +176,24 @@
 
     @pl.when(pair == pairs - 1)
     def _():
-        middle = hidden_ref[...].astype(f32) + dot(att_ref[...].T, wo_ref[...])
+        middle = hidden_ref[...].astype(f32) + dot(att_ref[...].T, mats_ref[3])
         middle_ref[...] = middle
         ffn_in = (middle * rms_factor(middle) * gain_ffn_ref[...]).astype(bf16)
-        logits_ref[...] = dot(ffn_in, wr_ref[...])
+        logits_ref[...] = dot(ffn_in, router_ref[...], 1, 1)
         placing = placing_rows(slot_row_ref[...], sent_ref.shape[0])
         sent_ref[...] = dot(placing, ffn_in).astype(bf16)
 
 
-def attention_forward(hidden, gain_attn, gain_ffn, mats, slot_row, bias):
+def attention_forward(hidden, gain_attn, gain_ffn, blocks, slot_row, bias, grid_shape, experts):
     seq_len, width = hidden.shape
     heads = bias.shape[0]
     head_dim = width // heads
-    experts = mats[4].shape[1]
     slots = 2 * seq_len
-    ins = (hidden, gain_attn, gain_ffn, *mats, slot_row)
+    ins = (hidden, gain_attn, gain_ffn, slot_row, blocks)
     tall = jax.ShapeDtypeStruct((seq_len, width), bf16)
     outs = (
+        jax.ShapeDtypeStruct((4, width, width), bf16),
+        jax.ShapeDtypeStruct((experts, width), bf16),
         tall,
         tall,
         tall,
@@ -173,9 +204,9 @@
         jax.ShapeDtypeStruct((slots, width), bf16),
     )
     out_specs = whole_of(outs)
-    out_specs[4] = pl.BlockSpec((1, 2, seq_len), lambda p: (p, 0, 0))
+    out_specs[6] = pl.BlockSpec((1, 2, seq_len), lambda p: (p, 0, 0))
     return pl.pallas_call(
-        partial(forward_kernel, head_dim),
+        partial(forward_kernel, head_dim, grid_shape),
         grid=(heads // 2,),
         in_specs=whole_of(ins) + [pl.BlockSpec((2, seq_len, seq_len), lambda p: (p, 0, 0))],
         out_specs=out_specs,
@@ -209,8 +240,20 @@
     return folded
 
 
+def reblock(grid_shape, blocks_ref, which, values):
+    count_x, count_y = grid_shape
+    tall = values.shape[0] // count_x
+    wide = values.shape[1] // count_y
+    for first in range(count_x):
+        for second in range(count_y):
+            blocks_ref[first * count_y + second, :, which * wide : (which + 1) * wide] = values[
+                first * tall : (first + 1) * tall, second * wide : (second + 1) * wide
+            ]
+
+
 def backward_kernel(
     head_dim,
+    grid_shape,
     d_back_ref,
     slot_col_ref,
     d_logits_ref,
@@ -219,11 +262,8 @@
     hidden_ref,
     gain_attn_ref,
     gain_ffn_ref,
-    wq_ref,
-    wk_ref,
-    wv_ref,
-    wo_ref,
-    wr_ref,
+    mats_ref,
+    router_ref,
     q_ref,
     k_ref,
     v_ref,
@@ -231,10 +271,7 @@
     bias_ref,
     lse_ref,
     grad_new_ref,
-    gwq_ref,
-    gwk_ref,
-    gwv_ref,
-    gwo_ref,
+    blocks_ref,
     gwr_ref,
     gga_ref,
     ggf_ref,
@@ -257,18 +294,18 @@
     def _():
         placing = placing_cols(slot_col_ref[...], d_back_ref.shape[0])
         d_logits = d_logits_ref[...]
-        d_ffn = dot(placing, d_back_ref[...]) + dot(d_logits, wr_ref[...], 1, 1)
+        d_ffn = dot(placing, d_back_ref[...]) + dot(d_logits, router_ref[...])
         middle = middle_ref[...]
         gain_row = gain_ffn_ref[...]
         ffn_in = (middle * rms_factor(middle) * gain_row).astype(bf16)
-        gwr_ref[...] = dot(ffn_in, d_logits, 0, 0)
+        gwr_ref[...] = dot(d_logits, ffn_in, 0, 0)
         d_middle, d_gain = rms_pull(middle, gain_row, d_ffn)
         ggf_ref[...] = d_gain
         d_middle = d_middle + grad_ref[...]
         d_middle_s[...] = d_middle
         d_low = d_middle.astype(bf16)
-        gwo_ref[...] = dot(att_ref[...], d_low).astype(bf16)
-        d_att_s[...] = dot(d_low, wo_ref[...], 1, 1).astype(bf16)
+        reblock(grid_shape, blocks_ref, 3, dot(att_ref[...], d_low).astype(bf16))
+        d_att_s[...] = dot(d_low, mats_ref[3], 1, 1).astype(bf16)
 
     lanes = pl.ds(pl.multiple_of(pair * width, width), width)
     q2 = q_ref[:, lanes] * jnp.asarray(scale, bf16)
@@ -307,24 +344,37 @@
         gain_row = gain_attn_ref[...]
         normed_t = (hidden * rms_factor(hidden) * gain_row).astype(bf16).T
         d_query = dqt_s[...].T
-        d_normed = dot(d_query, wq_ref[...], 1, 1)
-        gwq_ref[...] = dot(normed_t, d_query).astype(bf16)
-        d_normed = d_normed + dot(dk_s[...], wk_ref[...], 1, 1)
-        gwk_ref[...] = dot(normed_t, dk_s[...]).astype(bf16)
-        d_normed = d_normed + dot(dv_s[...], wv_ref[...], 1, 1)
-        gwv_ref[...] = dot(normed_t, dv_s[...]).astype(bf16)
+        d_normed = dot(d_query, mats_ref[0], 1, 1)
+        reblock(grid_shape, blocks_ref, 0, dot(normed_t, d_query).astype(bf16))
+        d_normed = d_normed + dot(dk_s[...], mats_ref[1], 1, 1)
+        reblock(grid_shape, blocks_ref, 1, dot(normed_t, dk_s[...]).astype(bf16))
+        d_normed = d_normed + dot(dv_s[...], mats_ref[2], 1, 1)
+        reblock(grid_shape, blocks_ref, 2, dot(normed_t, dv_s[...]).astype(bf16))
         d_hidden, d_gain = rms_pull(hidden, gain_row, d_normed)
         gga_ref[...] = d_gain
         grad_new_ref[...] = d_hidden + d_middle_s[...]
 
 
 def attention_backward(
-    d_back, slot_col, d_logits, grad_now, middle, hidden, gains, mats, q_k_v, attended, bias, lse
+    d_back,
+    slot_col,
+    d_logits,
+    grad_now,
+    middle,
+    hidden,
+    gains,
+    mats,
+    q_k_v,
+    attended,
+    bias,
+    lse,
+    grid_shape,
 ):
     seq_len, width = hidden.shape
     heads = bias.shape[0]
     head_dim = width // heads
-    experts = mats[4].shape[1]
+    experts = mats[1].shape[0]
+    count_x, count_y = grid_shape
     ins = (
         d_back,
         slot_col,
@@ -337,23 +387,21 @@
         *q_k_v,
         attended,
     )
-    square = jax.ShapeDtypeStruct((width, width), bf16)
     row = jax.ShapeDtypeStruct((1, width), f32)
     outs = (
         jax.ShapeDtypeStruct((seq_len, width), f32),
-        square,
-        square,
-        square,
-        square,
-        jax.ShapeDtypeStruct((width, experts), f32),
+        jax.ShapeDtypeStruct(
+            (count_x * count_y, width // count_x, 4 * (width // count_y)), bf16
+        ),
+        jax.ShapeDtypeStruct((experts, width), f32),
         row,
         row,
         jax.ShapeDtypeStruct((heads // 2, 2, 2 * seq_len), f32),
     )
     out_specs = whole_of(outs)
-    out_specs[8] = pl.BlockSpec((1, 2, 2 * seq_len), lambda p: (p, 0, 0))
+    out_specs[5] = pl.BlockSpec((1, 2, 2 * seq_len), lambda p: (p, 0, 0))
     return pl.pallas_call(
-        partial(backward_kernel, head_dim),
+        partial(backward_kernel, head_dim, grid_shape),
         grid=(heads // 2,),
         in_specs=whole_of(ins)
         + [
@@ -376,28 +424,6 @@
     )(*ins, bias, lse)
 
 
-def combine_kernel(returned_ref, slot_col_ref, chosen_ref, logits_ref, middle_ref, comb_ref, out_ref):
-    placing = placing_cols(slot_col_ref[...], returned_ref.shape[0])
-    combined = dot(placing, returned_ref[...])
-    comb_ref[...] = combined
-    gate = jnp.sum(jax.nn.softmax(logits_ref[...], axis=-1) * chosen_ref[...], axis=1, keepdims=True)
-    out_ref[...] = middle_ref[...] + gate * combined
-
-
-def combine(returned, slot_col, chosen_f, logits, middle):
-    outs = (jax.ShapeDtypeStruct(middle.shape, f32),) * 2
-    ins = (returned, slot_col, chosen_f, logits, middle)
-    return pl.pallas_call(
-        combine_kernel,
-        in_specs=whole_of(ins),
-        out_specs=whole_of(outs),
-        out_shape=outs,
-        grid=(1,),
-        compiler_params=params(),
-        name="combine",
-    )(*ins)
-
-
 def spread_kernel(grad_ref, comb_ref, slot_row_ref, chosen_ref, logits_ref, d_sent_ref, d_logits_ref):
     grad_now = grad_ref[...].astype(f32)
     d_gate = jnp.sum(grad_now * comb_ref[...], axis=1, keepdims=True)
@@ -427,8 +453,321 @@
     )(*ins)
 
 
-def gelu_tanh(pre_vals):
-    return jax.nn.gelu(pre_vals, approximate=True)
+def greet(peers):
+    barrier = pltpu.get_barrier_semaphore()
+    for peer in peers:
+        pl.semaphore_signal(barrier, inc=1, device_id=peer, device_id_type=MESH)
+    pl.semaphore_wait(barrier, len(peers))
+
+
+class Exchange:
+    def __init__(self, members, rows, src, dst, send_sems, recv_sems):
+        self.me = lax.axis_index("gy")
+        self.bits = members.bit_length() - 1
+        self.rows, self.src, self.dst = rows, src, dst
+        self.send_sems, self.recv_sems = send_sems, recv_sems
+
+    def block(self, index):
+        return pl.ds(pl.multiple_of(index * self.rows, self.rows), self.rows)
+
+    def copy(self, apart):
+        peer = xor_of(self.me, apart, self.bits)
+        return pltpu.make_async_remote_copy(
+            src_ref=self.src.at[self.block(peer), :],
+            dst_ref=self.dst.at[self.block(self.me), :],
+            send_sem=self.send_sems.at[apart],
+            recv_sem=self.recv_sems.at[apart],
+            device_id={"gy": peer},
+            device_id_type=MESH,
+        )
+
+    def keep_own(self):
+        self.dst[self.block(self.me), :] = self.src[self.block(self.me), :]
+
+
+def peers_along_gy(members):
+    me = lax.axis_index("gy")
+    bits = members.bit_length() - 1
+    return [{"gy": xor_of(me, apart, bits)} for apart in range(1, members)]
+
+
+def gelu_and_slope(pre):
+    inner_scale = 0.7978845608028654
+    square = pre * pre
+    bent = jnp.tanh(inner_scale * pre * (1.0 + 0.044715 * square))
+    act = 0.5 * pre * (1.0 + bent)
+    slope = 0.5 * (1.0 + bent) + 0.5 * pre * (1.0 - bent * bent) * (
+        inner_scale * (1.0 + 3 * 0.044715 * square)
+    )
+    return act, slope
+
+
+def gelu_only(pre):
+    inner_scale = 0.7978845608028654
+    return 0.5 * pre * (1.0 + jnp.tanh(inner_scale * pre * (1.0 + 0.044715 * pre * pre)))
+
+
+def chunk_of(members, rows):
+    return max(1, min(members, 256 // rows))
+
+
+def expert_forward_kernel(
+    members,
+    sent_ref,
+    slot_col_ref,
+    chosen_ref,
+    logits_ref,
+    middle_ref,
+    win_ref,
+    wout_ref,
+    arrived_ref,
+    comb_ref,
+    out_ref,
+    win_s,
+    wout_s,
+    made_s,
+    returned_s,
+    w_sems,
+    send_sems,
+    recv_sems,
+    back_send_sems,
+    back_recv_sems,
+):
+    slots = sent_ref.shape[0]
+    rows = slots // members
+    group = chunk_of(members, rows)
+    chunks = members // group
+    chunk_bits = chunks.bit_length() - 1
+    hidden_units = win_s.shape[1]
+    tile = min(768, hidden_units)
+    load_in = pltpu.make_async_copy(win_ref, win_s, w_sems.at[0])
+    load_out = pltpu.make_async_copy(wout_ref, wout_s, w_sems.at[1])
+    load_in.start()
+    load_out.start()
+    greet(peers_along_gy(members))
+    there = Exchange(members, rows, sent_ref, arrived_ref, send_sems, recv_sems)
+    back = Exchange(members, rows, made_s, returned_s, back_send_sems, back_recv_sems)
+    for apart in range(members - 1, 0, -1):
+        there.copy(apart).start()
+    there.keep_own()
+    load_in.wait()
+    load_out.wait()
+    my_chunk = there.me // group
+
+    def chunk_rows(index):
+        start = xor_of(my_chunk, index, chunk_bits) * (group * rows)
+        return pl.ds(pl.multiple_of(start, group * rows), group * rows)
+
+    def work(index, first):
+        for member in range(first, group):
+            there.copy(index * group + member).wait_recv()
+        here = chunk_rows(index)
+        taken = arrived_ref[here, :]
+        total = jnp.zeros((group * rows, taken.shape[1]), f32)
+        for start in range(0, hidden_units, tile):
+            units = slice(start, start + tile)
+            act = gelu_only(dot(taken, win_s[:, units])).astype(bf16)
+            total = total + dot(act, wout_s[:, units], 1, 1)
+        made_s[here, :] = total.astype(bf16)
+        for member in range(first, group):
+            back.copy(index * group + member).start()
+
+    work(0, 1)
+    back.keep_own()
+
+    @pl.loop(1, chunks)
+    def _(index):
+        work(index, 0)
+
+    slot_col = slot_col_ref[...]
+    width = arrived_ref.shape[1]
+    comb_ref[...] = jnp.zeros_like(comb_ref)
+
+    def gather_back(index, first):
+        for member in range(first, group):
+            back.copy(index * group + member).wait_recv()
+        start = xor_of(my_chunk, index, chunk_bits) * (group * rows)
+        places = lax.broadcasted_iota(jnp.int32, (slot_col.shape[0], group * rows), 1) + start
+        placing = (places == slot_col).astype(f32).astype(bf16)
+        comb_ref[...] += dot(placing, returned_s[chunk_rows(index), :])
+
+    gather_back(0, 1)
+
+    @pl.loop(1, chunks)
+    def _(index):
+        gather_back(index, 0)
+
+    gate = jnp.sum(jax.nn.softmax(logits_ref[...], axis=-1) * chosen_ref[...], axis=1, keepdims=True)
+    out_ref[...] = middle_ref[...] + gate * comb_ref[...]
+
+    @pl.loop(1, members)
+    def _(apart):
+        there.copy(apart).wait_send()
+        back.copy(apart).wait_send()
+
+
+def expert_params(identifier):
+    return pltpu.CompilerParams(
+        vmem_limit_bytes=vmem_bytes, collective_id=identifier, has_side_effects=True
+    )
+
+
+def expert_forward(sent, slot_col, chosen_f, logits, middle, full_in, full_out, members):
+    slots, width = sent.shape
+    outs = (
+        jax.ShapeDtypeStruct(sent.shape, bf16),
+        jax.ShapeDtypeStruct(middle.shape, f32),
+        jax.ShapeDtypeStruct(middle.shape, f32),
+    )
+    ins = (sent, slot_col, chosen_f, logits, middle)
+    sems = pltpu.SemaphoreType.DMA((members,))
+    return pl.pallas_call(
+        partial(expert_forward_kernel, members),
+        in_specs=[vmem_spec] * len(ins) + [any_spec] * 2,
+        out_specs=[vmem_spec] * 3,
+        out_shape=outs,
+        scratch_shapes=[
+            pltpu.VMEM(full_in.shape, bf16),
+            pltpu.VMEM(full_out.shape, bf16),
+            pltpu.VMEM(sent.shape, bf16),
+            pltpu.VMEM(sent.shape, bf16),
+            pltpu.SemaphoreType.DMA((2,)),
+            sems,
+            sems,
+            sems,
+            sems,
+        ],
+        compiler_params=expert_params(1),
+        name="expert_forward",
+    )(*ins, full_in, full_out)
+
+
+def expert_backward_kernel(
+    members,
+    d_sent_ref,
+    arrived_ref,
+    win_ref,
+    wout_ref,
+    d_back_ref,
+    gin_ref,
+    gout_ref,
+    win_s,
+    wout_s,
+    d_arrived_s,
+    d_rows_s,
+    act_s,
+    slope_s,
+    w_sems,
+    send_sems,
+    recv_sems,
+    back_send_sems,
+    back_recv_sems,
+):
+    slots = d_sent_ref.shape[0]
+    rows = slots // members
+    group = chunk_of(members, rows)
+    chunks = members // group
+    chunk_bits = chunks.bit_length() - 1
+    hidden_units = win_s.shape[1]
+    tile = min(768, hidden_units)
+    load_in = pltpu.make_async_copy(win_ref, win_s, w_sems.at[0])
+    load_out = pltpu.make_async_copy(wout_ref, wout_s, w_sems.at[1])
+    load_in.start()
+    load_out.start()
+    greet(peers_along_gy(members))
+    there = Exchange(members, rows, d_sent_ref, d_arrived_s, send_sems, recv_sems)
+    back = Exchange(members, rows, d_rows_s, d_back_ref, back_send_sems, back_recv_sems)
+    for apart in range(members - 1, 0, -1):
+        there.copy(apart).start()
+    there.keep_own()
+    my_chunk = there.me // group
+    load_in.wait()
+
+    @pl.loop(0, slots // 256)
+    def _(index):
+        here = pl.ds(pl.multiple_of(index * 256, 256), 256)
+        taken = arrived_ref[here, :]
+        for start in range(0, hidden_units, tile):
+            units = slice(start, start + tile)
+            act, slope = gelu_and_slope(dot(taken, win_s[:, units]))
+            act_s[here, units] = act.astype(bf16)
+            slope_s[here, units] = slope.astype(bf16)
+
+    load_out.wait()
+
+    def chunk_rows(index):
+        start = xor_of(my_chunk, index, chunk_bits) * (group * rows)
+        return pl.ds(pl.multiple_of(start, group * rows), group * rows)
+
+    def work(index, first):
+        for member in range(first, group):
+            there.copy(index * group + member).wait_recv()
+        here = chunk_rows(index)
+        taken = d_arrived_s[here, :]
+        total = jnp.zeros((group * rows, taken.shape[1]), f32)
+        for start in range(0, hidden_units, tile):
+            units = slice(start, start + tile)
+            d_pre = (dot(taken, wout_s[:, units]) * slope_s[here, units].astype(f32)).astype(bf16)
+            slope_s[here, units] = d_pre
+            total = total + dot(d_pre, win_s[:, units], 1, 1)
+        d_rows_s[here, :] = total.astype(bf16)
+        for member in range(first, group):
+            back.copy(index * group + member).start()
+
+    work(0, 1)
+    back.keep_own()
+
+    @pl.loop(1, chunks)
+    def _(index):
+        work(index, 0)
+
+    for lhs_ref, rhs_ref, out_ref in (
+        (d_arrived_s, act_s, gout_ref),
+        (arrived_ref, slope_s, gin_ref),
+    ):
+        lhs = lhs_ref[...].T
+
+        @pl.loop(0, hidden_units // tile)
+        def _(index, lhs=lhs, rhs_ref=rhs_ref, out_ref=out_ref):
+            units = pl.ds(pl.multiple_of(index * tile, tile), tile)
+            out_ref[:, units] = dot(lhs, rhs_ref[:, units]).astype(bf16)
+
+    @pl.loop(1, members)
+    def _(apart):
+        back.copy(apart).wait_recv()
+        there.copy(apart).wait_send()
+        back.copy(apart).wait_send()
+
+
+def expert_backward(d_sent, arrived, full_in, full_out, members):
+    outs = (
+        jax.ShapeDtypeStruct(d_sent.shape, bf16),
+        jax.ShapeDtypeStruct(full_in.shape, bf16),
+        jax.ShapeDtypeStruct(full_out.shape, bf16),
+    )
+    slots = d_sent.shape[0]
+    sems = pltpu.SemaphoreType.DMA((members,))
+    return pl.pallas_call(
+        partial(expert_backward_kernel, members),
+        in_specs=[vmem_spec] * 2 + [any_spec] * 2,
+        out_specs=[vmem_spec] * 3,
+        out_shape=outs,
+        scratch_shapes=[
+            pltpu.VMEM(full_in.shape, bf16),
+            pltpu.VMEM(full_out.shape, bf16),
+            pltpu.VMEM(d_sent.shape, bf16),
+            pltpu.VMEM(d_sent.shape, bf16),
+            pltpu.VMEM((slots, full_in.shape[1]), bf16),
+            pltpu.VMEM((slots, full_in.shape[1]), bf16),
+            pltpu.SemaphoreType.DMA((2,)),
+            sems,
+            sems,
+            sems,
+            sems,
+        ],
+        compiler_params=expert_params(2),
+        name="expert_backward",
+    )(d_sent, arrived, full_in, full_out)
 
 
 def body(
@@ -472,41 +811,33 @@
 
     tall, wide = w_query.shape[1], w_query.shape[2]
 
-    def gather_mats(layer):
+    grid_shape = (count_x, count_y)
+    tile_rows = 16
+
+    def gather_blocks(layer):
         packed = jnp.concatenate(
             [w_query[layer], w_key[layer], w_value[layer], w_output[layer]], axis=1
         )
-        everything = lax.all_gather(packed, ("gx", "gy"), axis=0, tiled=False)
-        parted = everything.reshape(count_x, count_y, tall, 4, wide)
-        mats = parted.transpose(3, 0, 2, 1, 4).reshape(4, width, width)
-        router = lax.all_gather(
-            lax.all_gather(w_router[layer], "gy", axis=1, tiled=True), "gx", axis=0, tiled=True
-        )
-        return (mats[0], mats[1], mats[2], mats[3], router)
+        router_row = jnp.pad(w_router[layer].T, ((0, tile_rows - 1), (0, 4 * wide - tall)))
+        packed = jnp.concatenate([packed, router_row], axis=0)
+        return lax.all_gather(packed, ("gx", "gy"), axis=0, tiled=False)
 
     hidden = hidden_in
     kept = []
     for layer in range(layers):
-        mats = gather_mats(layer)
+        blocks = gather_blocks(layer)
         gains = (gain_attn_f[layer][None], gain_ffn_f[layer][None])
-        q, k, v, attended, lse, middle, logits, sent = attention_forward(
-            hidden, gains[0], gains[1], mats, slot_row, bias
+        mats, router, q, k, v, attended, lse, middle, logits, sent = attention_forward(
+            hidden, gains[0], gains[1], blocks, slot_row, bias, grid_shape, experts
         )
-        arrived = lax.all_to_all(
-            sent.reshape(experts, capacity, width), "gy", split_axis=0, concat_axis=0, tiled=True
-        ).reshape(experts * capacity, width)
         full_in = lax.all_gather(w_in[layer, 0], "gx", axis=1, tiled=True)
         full_out = lax.all_gather(w_out[layer, 0], "gx", axis=1, tiled=True)
-        pre_act = dot(arrived, full_in)
-        activated = gelu_tanh(pre_act).astype(bf16)
-        made = dot(activated, full_out, 1, 1).astype(bf16)
-        returned = lax.all_to_all(
-            made.reshape(experts, capacity, width), "gy", split_axis=0, concat_axis=0, tiled=True
-        ).reshape(experts * capacity, width)
-        combined, hidden_next = combine(returned, slot_col, chosen_f, logits, middle)
+        arrived, combined, hidden_next = expert_forward(
+            sent, slot_col, chosen_f, logits, middle, full_in, full_out, count_y
+        )
         kept.append(
-            (hidden, gains, mats, (q, k, v), attended, lse, middle, logits, combined)
-            + (arrived, full_in, full_out, pre_act, activated)
+            (hidden, gains, (mats, router), (q, k, v), attended, lse, middle, logits, combined)
+            + (arrived, full_in, full_out)
         )
         hidden = hidden_next
 
@@ -515,24 +846,14 @@
     parts = []
     for layer in reversed(range(layers)):
         (prior, gains, mats, q_k_v, attended, lse, middle, logits, combined) = kept[layer][:9]
-        (arrived, full_in, full_out, pre_act, activated) = kept[layer][9:]
+        (arrived, full_in, full_out) = kept[layer][9:]
         d_sent, d_logits = spread(grad_now, combined, slot_row, chosen_f, logits)
-        d_arrived = lax.all_to_all(
-            d_sent.reshape(experts, capacity, width), "gy", split_axis=0, concat_axis=0, tiled=True
-        ).reshape(experts * capacity, width)
-        d_activated = dot(d_arrived, full_out)
-        d_pre = jax.vjp(gelu_tanh, pre_act)[1](d_activated)[0].astype(bf16)
-        d_rows = dot(d_pre, full_in, 1, 1).astype(bf16)
-        grad_out_part = lax.psum_scatter(
-            dot(d_arrived, activated, 0, 0).astype(bf16), "gx", scatter_dimension=1, tiled=True
+        d_back, grad_in_full, grad_out_full = expert_backward(
+            d_sent, arrived, full_in, full_out, count_y
         )
-        grad_in_part = lax.psum_scatter(
-            dot(arrived, d_pre, 0, 0).astype(bf16), "gx", scatter_dimension=1, tiled=True
-        )
-        d_back = lax.all_to_all(
-            d_rows.reshape(experts, capacity, width), "gy", split_axis=0, concat_axis=0, tiled=True
-        ).reshape(experts * capacity, width)
-        grad_now, gwq, gwk, gwv, gwo, gwr, gga, ggf, offset_sums = attention_backward(
+        grad_out_part = lax.psum_scatter(grad_out_full, "gx", scatter_dimension=1, tiled=True)
+        grad_in_part = lax.psum_scatter(grad_in_full, "gx", scatter_dimension=1, tiled=True)
+        grad_now, blocked, gwr, gga, ggf, offset_sums = attention_backward(
             d_back,
             slot_col,
             d_logits,
@@ -545,10 +866,9 @@
             attended,
             bias,
             lse,
+            grid_shape,
         )
         table_sums = offset_sums if table_sums is None else table_sums + offset_sums
-        stacked = jnp.stack([gwq, gwk, gwv, gwo]).reshape(4, count_x, tall, count_y, wide)
-        blocked = stacked.transpose(1, 3, 2, 0, 4).reshape(count_x * count_y, tall, 4 * wide)
         summed = lax.psum_scatter(blocked, ("gx", "gy"), scatter_dimension=0, tiled=True)[0]
         summed = summed.astype(f32).reshape(tall, 4, wide)
         parts.append((summed, gwr, gga, ggf, grad_in_part, grad_out_part))
@@ -568,9 +888,9 @@
     wide_router = w_router.shape[2]
     router_mine = lax.dynamic_slice(
         router_sum,
-        (0, lax.axis_index("gx") * tall, lax.axis_index("gy") * wide_router),
-        (layers, tall, wide_router),
-    )
+        (0, lax.axis_index("gy") * wide_router, lax.axis_index("gx") * tall),
+        (layers, wide_router, tall),
+    ).transpose(0, 2, 1)
     attn_grads = [jnp.stack([part[0][:, index] for part in parts]) for index in range(4)]
     grad_in = jnp.stack([part[4] for part in parts]).astype(f32)[:, None]
     grad_out = jnp.stack([part[5] for part in parts]).astype(f32)[:, None]

time: 1160 us -> 987 us (0.85)
  Pallas kernels: 136 us -> 455 us
  blocking collectives: 266 us -> 45.1 us
  local copies, waits for them, and re-layouts: 185 us -> 15.3 us
  matrix products: 127 us -> 0.48 us
  waiting for transfers between devices: 339 us -> 428 us
  other arithmetic: 57.9 us -> 17.9 us
  starting transfers between devices: 26.1 us -> 0.48 us
    pallas_call x6 -> x8, Pallas kernels: 118 us -> 438 us  [the longest x2 169 us: expert_backward(): pl.pallas_call(partial(expert_backward_kernel, members), in_specs=[vmem_s...]
    all_to_all x3 -> x0, blocking collectives: 136 us -> none  [the longest x1 54.7 us: body(): lax.all_to_all(d_rows.reshape(experts, capacity, width), 'gy', split_axis...]
    dot_general x12 -> x0, matrix products: 127 us -> none  [dot(): lax.dot_general(lhs, rhs, (((lhs_dim,), (rhs_dim,)), ((), ())), preferred...]
    all_to_all x5 -> x0, waiting for transfers between devices: 112 us -> none  [the longest x2 76.4 us: body(): lax.all_to_all(sent.reshape(experts, capacity, width), 'gy', split_axis=0...]
    all_gather x4 -> x0, blocking collectives: 87.7 us -> none  [the longest x2 74.3 us: gather_mats(): lax.all_gather(w_router[layer], 'gy', axis=1, tiled=True)]
    all_gather x2, waiting for transfers between devices: 0.01 us -> 78 us  [body(): full_out = lax.all_gather(w_out[layer, 0], 'gx', axis=1, tiled=True)]
    another operation x19 -> x2, local copies, waits for them, and re-layouts: 76.3 us -> 0.77 us  [the longest x1 0.76 us: gather_blocks(): w_router[layer]]
    reshape x6 -> x0, local copies, waits for them, and re-layouts: 60.3 us -> none  [the longest x4 38.7 us: gather_mats(): parted = everything.reshape(count_x, count_y, tall, 4, wide)]
  transfers between devices with their start and end apart: 17 -> 12, of which waited for: 9 -> 11; matrix products, arithmetic and copies ran while one was open for 28% -> 3% of each run, Pallas kernels for 8% -> 27%
where the time goes in v2:
time: 987 us; the launch traced here: 978 us
  Pallas kernels  455 us (46%)
  waiting for transfers between devices  428 us (43%)
  blocking collectives  45.1 us (5%)
  other arithmetic  17.9 us (2%)
  local copies, waits for them, and re-layouts  15.3 us (2%)
  between operations  15.1 us (2%)
    pallas_call x2, Pallas kernels, expert_backward(): pl.pallas_call(partial(expert_backward_kernel, members), in_specs=[vmem_s...  169 us
    pallas_call x2, Pallas kernels, expert_forward(): pl.pallas_call(partial(expert_forward_kernel, members), in_specs=[vmem_sp...  155 us
    reduce_scatter x2, waiting for transfers between devices, body(): lax.psum_scatter(grad_out_full, 'gx', scatter_dimension=1, tiled=True)  96.7 us
    reduce_scatter x2, waiting for transfers between devices, body(): lax.psum_scatter(grad_in_full, 'gx', scatter_dimension=1, tiled=True)  95.4 us
    all_gather x2, waiting for transfers between devices, body(): full_out = lax.all_gather(w_out[layer, 0], 'gx', axis=1, tiled=True)  78 us
    all_gather x2, waiting for transfers between devices, gather_blocks(): return lax.all_gather(packed, ('gx', 'gy'), axis=0, tiled=False)  66.6 us
    pallas_call x2, Pallas kernels, attention_backward(): pl.pallas_call(partial(backward_kernel, head_dim, grid_shape), grid=(head...  63.4 us
    reduce_scatter x2, waiting for transfers between devices, body(): lax.psum_scatter(blocked, ('gx', 'gy'), scatter_dimension=0, tiled=True)[0]  63.3 us
  transfers between devices with their start and end apart: 12, of which 11 were waited for; matrix products, arithmetic and copies ran while one was open for 3% of the time, Pallas kernels for 27%

profile of v2, /device:TPU:0, one launch (start us, length us, event | category | flops | bytes accessed | tf_op | source)
XLA Modules:
  0.0 978.0 jit_solution(180860073587251636)
XLA Ops:
  7.2 0.8 slice_bitcast_fusion.8
  8.0 0.9 slice_bitcast_fusion
  8.9 0.9 slice_bitcast_fusion.2
  9.8 0.8 fusion.6
  10.7 3.3 fusion.12
  14.1 1.5 fusion.11
  15.7 0.8 fusion.7
  18.0 1.1 reduce-window.6
  20.4 0.7 broadcast_in_dim.6.offsets_ref
  21.1 0.9 copy.39.piece_col_ref
  21.9 1.3 convert_element_type.65.grad_ref
  23.2 0.7 multiply_add_fusion
  24.6 8.7 bias_table.1.bias_ref
  33.9 0.8 convert_convert_fusion.chosen_ref
  34.7 44.4 %all-gather.13.cloned.1.call-done = bf16[6656,384]{1,0:T(8,128)(2,1)} async-done(((bf16[208,384]{1,0:T(8,128)(2,1)}), bf16[6656,384]{1,0:T(8,128)(2,1)}) %all-gather.13.cloned.1.call-update) | async-done | bytes 5111824 | tf_op jit(solution)/shard_map/all_gather | solution.py:823
  79.1 25.0 %attention_forward.2 = (bf16[4,768,768]{2,1,0:T(8,128)(2,1)}, bf16[8,768]{1,0:T(8,128)(2,1)}, bf16[512,768]{1,0:T(8,128)(2,1)}, bf16[512,768]{1,0:T(8,128)(2,1)}...) custom-call(bf16[512,768]{1,0:T(8,128)(2,1)} %hidden_ref.3, ...), custom_call_target="tpu_custom_call" | custom-call | tf_op jit(solution)/shard_map/attention_forward/pallas_call | solution.py:208
  104.1 13.5 %all-gather.15.cloned.1.call-done = bf16[1,1,768,3072]{3,2,1,0:T(8,128)(2,1)} async-done(((bf16[1,1,768,768]{3,2,1,0:T(8,128)(2,1)}), bf16[1,1,768,3072]{3,2,1,0:T(8,128)(2,1)}) %all-gather.15.cloned.1.call-update) | async-done | bytes 4718608 | tf_op jit(solution)/shard_map/all_gather | solution.py:833
  117.6 39.1 %all-gather.17.cloned.1.call-done = bf16[1,1,768,3072]{3,2,1,0:T(8,128)(2,1)} async-done(((bf16[1,1,768,768]{3,2,1,0:T(8,128)(2,1)}), bf16[1,1,768,3072]{3,2,1,0:T(8,128)(2,1)}) %all-gather.17.cloned.1.call-update) | async-done | bytes 4718608 | tf_op jit(solution)/shard_map/all_gather | solution.py:834
  156.7 81.9 %expert_forward.2 = (bf16[1024,768]{1,0:T(8,128)(2,1)}, f32[512,768]{1,0:T(8,128)}, f32[512,768]{1,0:T(8,128)}) custom-call(bf16[1024,768]{1,0:T(8,128)(2,1)} %get-tuple-element.60.sent_ref, s32[512,1]{1,0:T(8,128)} %get-tuple-element.124.slot_col_ref, f32[512,8]{1,0:T(8,128)} %convert_convert_fusion.chosen_ref, f32[512,8]{1,0:T(8,128)} %get-tuple-element.61.logits_ref, ...), custom_call_target="tpu_custom_call" | custom-call | tf_op jit(solution)/shard_map/expert_forward/pallas_call | solution.py:624
  238.6 22.2 %all-gather.19.cloned.1.call-done = bf16[6656,384]{1,0:T(8,128)(2,1)} async-done(((bf16[208,384]{1,0:T(8,128)(2,1)}), bf16[6656,384]{1,0:T(8,128)(2,1)}) %all-gather.19.cloned.1.call-update) | async-done | bytes 5111824 | tf_op jit(solution)/shard_map/all_gather | solution.py:823
  260.8 25.5 %attention_forward.3 = (bf16[4,768,768]{2,1,0:T(8,128)(2,1)}, bf16[8,768]{1,0:T(8,128)(2,1)}, bf16[512,768]{1,0:T(8,128)(2,1)}, bf16[512,768]{1,0:T(8,128)(2,1)}...) custom-call(f32[512,768]{1,0:T(8,128)} %get-tuple-element.63.hidden_, ...), custom_call_target="tpu_custom_call" | custom-call | tf_op jit(solution)/shard_map/attention_forward/pallas_call | solution.py:208
  286.3 11.5 %all-gather.21.cloned.1.call-done = bf16[1,1,768,3072]{3,2,1,0:T(8,128)(2,1)} async-done(((bf16[1,1,768,768]{3,2,1,0:T(8,128)(2,1)}), bf16[1,1,768,3072]{3,2,1,0:T(8,128)(2,1)}) %all-gather.21.cloned.1.call-update) | async-done | bytes 4718608 | tf_op jit(solution)/shard_map/all_gather | solution.py:833
  297.8 38.9 %all-gather.23.cloned.1.call-done = bf16[1,1,768,3072]{3,2,1,0:T(8,128)(2,1)} async-done(((bf16[1,1,768,768]{3,2,1,0:T(8,128)(2,1)}), bf16[1,1,768,3072]{3,2,1,0:T(8,128)(2,1)}) %all-gather.23.cloned.1.call-update) | async-done | bytes 4718608 | tf_op jit(solution)/shard_map/all_gather | solution.py:834
  336.7 72.8 %expert_forward.3 = (bf16[1024,768]{1,0:T(8,128)(2,1)}, f32[512,768]{1,0:T(8,128)}, f32[512,768]{1,0:T(8,128)}) custom-call(bf16[1024,768]{1,0:T(8,128)(2,1)} %get-tuple-element.64.sent_ref, s32[512,1]{1,0:T(8,128)} %get-tuple-element.124.slot_col_ref, f32[512,8]{1,0:T(8,128)} %convert_convert_fusion.chosen_ref, f32[512,8]{1,0:T(8,128)} %get-tuple-element.65.logits_ref, ...), custom_call_target="tpu_custom_call" | custom-call | tf_op jit(solution)/shard_map/expert_forward/pallas_call | solution.py:624
  409.5 4.3 spread.2
  413.8 79.7 %expert_backward.2 = (bf16[1024,768]{1,0:T(8,128)(2,1)}, bf16[768,3072]{1,0:T(8,128)(2,1)}, bf16[768,3072]{1,0:T(8,128)(2,1)}) custom-call(bf16[1024,768]{1,0:T(8,128)(2,1)} %get-tuple-element.69.d_sent_ref, bf16[1024,768]{1,0:T(8,128)(2,1)} %get-tuple-element.70.arrived_ref, bf16[768,3072]{1,0:T(8,128)(2,1)} %bitcast.80, bf16[768,3072]{1,0:T(8,128)(2,1)} %bitcast.82), custom_call_target="tpu_custom_call" | custom-call | tf_op jit(solution)/shard_map/expert_backward/pallas_call | solution.py:750
  493.5 31.7 %attention_backward.2 = (f32[512,768]{1,0:T(8,128)}, bf16[32,192,384]{2,1,0:T(8,128)(2,1)}, f32[8,768]{1,0:T(8,128)}, f32[1,768]{1,0:T(1,128)}, f32[1,768]{1,0:T(1,128)}, /*index=5*/f32[6,2,1024]{2,1,0:T(2,128)}) custom-call(bf16[1024,768]{1,0:T(8,128)(2,1)} %get-tuple-element.71.d_back_ref, s32[512,1]{1,0:T(8,128)} %get-tuple-element.124.slot_col_ref, ...), custom_call_target="tpu_custom_call" | custom-call | tf_op jit(solution)/shard_map/attention_backward/pallas_call | solution.py:403
  525.3 4.5 spread.3
  529.8 89.5 %expert_backward.3 = (bf16[1024,768]{1,0:T(8,128)(2,1)}, bf16[768,3072]{1,0:T(8,128)(2,1)}, bf16[768,3072]{1,0:T(8,128)(2,1)}) custom-call(bf16[1024,768]{1,0:T(8,128)(2,1)} %get-tuple-element.82.d_sent_ref, bf16[1024,768]{1,0:T(8,128)(2,1)} %get-tuple-element.83.arrived_ref, bf16[768,3072]{1,0:T(8,128)(2,1)} %bitcast.76, bf16[768,3072]{1,0:T(8,128)(2,1)} %bitcast.78), custom_call_target="tpu_custom_call" | custom-call | tf_op jit(solution)/shard_map/expert_backward/pallas_call | solution.py:750
  619.3 31.6 %attention_backward.3 = (f32[512,768]{1,0:T(8,128)}, bf16[32,192,384]{2,1,0:T(8,128)(2,1)}, f32[8,768]{1,0:T(8,128)}, f32[1,768]{1,0:T(1,128)}, f32[1,768]{1,0:T(1,128)}, /*index=5*/f32[6,2,1024]{2,1,0:T(2,128)}) custom-call(bf16[1024,768]{1,0:T(8,128)(2,1)} %get-tuple-element.84.d_back_ref, s32[512,1]{1,0:T(8,128)} %get-tuple-element.124.slot_col_ref, ...), custom_call_target="tpu_custom_call" | custom-call | tf_op jit(solution)/shard_map/attention_backward/pallas_call | solution.py:403
  651.0 0.7 reduce-scatter.13.cloned.1.call-update
  652.4 0.7 reduce-scatter.17.cloned.1.call-update
  654.4 45.1 %all-reduce.3 = (f32[32,12]{0,1:T(8,128)}, f32[2,768]{1,0:T(2,128)}, f32[2,768]{1,0:T(2,128)}, f32[2,8,768]{2,1,0:T(8,128)S(1)}) all-reduce(f32[32,12]{0,1:T(8,128)S(1)} %fusion.1, f32[2,768]{1,0:T(2,128)S(1)} %pad_maximum_fusion.5, f32[2,768]{1,0:T(2,128)S(1)} %pad_maximum_fusion.6, ...), channel_id=1, replica_groups=mesh['gx'=4,'gy'=8] {'gx','gy'}, use_global_device_ids=true, to_apply=%region_3.4 | all-reduce | flops 15744 | bytes 125952 | tf_op jit(solution)/shard_map/psum | solution.py:879
  699.5 0.7 dynamic-slice_bitcast_fusion
  700.1 1.2 reshape.139
  701.3 63.3 %reduce-scatter.7.cloned.1.call-done = bf16[1,192,384]{2,1,0:T(8,128)(2,1)} async-done(((bf16[32,192,384]{2,1,0:T(8,128)(2,1)}), bf16[1,192,384]{2,1,0:T(8,128)(2,1)}) %reduce-scatter.7.cloned.1.call-update) | async-done | bytes 147472 | tf_op jit(solution)/shard_map/reduce_scatter | solution.py:872
  764.6 1.2 reshape.138
  766.3 0.7 pad_maximum_fusion
  767.0 0.7 pad_maximum_fusion.1
  767.7 0.7 pad_maximum_fusion.2
  768.4 0.7 pad_maximum_fusion.3
  769.1 45.0 %reduce-scatter.13.cloned.1.call-done = bf16[768,768]{1,0:T(8,128)(2,1)} async-done(((bf16[768,3072]{1,0:T(8,128)(2,1)}), bf16[768,768]{1,0:T(8,128)(2,1)}) %reduce-scatter.13.cloned.1.call-update) | async-done | bytes 1179664 | tf_op jit(solution)/shard_map/reduce_scatter | solution.py:855
  814.1 50.4 %reduce-scatter.11.cloned.1.call-done = bf16[768,768]{1,0:T(8,128)(2,1)} async-done(((bf16[768,3072]{1,0:T(8,128)(2,1)}), bf16[768,768]{1,0:T(8,128)(2,1)}) %reduce-scatter.11.cloned.1.call-update) | async-done | bytes 1179664 | tf_op jit(solution)/shard_map/reduce_scatter | solution.py:855
  864.5 4.1 maximum_convert_fusion
  868.6 46.3 %reduce-scatter.17.cloned.1.call-done = bf16[768,768]{1,0:T(8,128)(2,1)} async-done(((bf16[768,3072]{1,0:T(8,128)(2,1)}), bf16[768,768]{1,0:T(8,128)(2,1)}) %reduce-scatter.17.cloned.1.call-update) | async-done | bytes 1179664 | tf_op jit(solution)/shard_map/reduce_scatter | solution.py:854
  914.9 50.4 %reduce-scatter.15.cloned.1.call-done = bf16[768,768]{1,0:T(8,128)(2,1)} async-done(((bf16[768,3072]{1,0:T(8,128)(2,1)}), bf16[768,768]{1,0:T(8,128)(2,1)}) %reduce-scatter.15.cloned.1.call-update) | async-done | bytes 1179664 | tf_op jit(solution)/shard_map/reduce_scatter | solution.py:854
  965.3 4.2 maximum_convert_fusion.1
  969.6 1.1 copy.58
  (80 shorter events, 6.5 us)
Async XLA Ops:
  7.2 13.0 %copy-start = (bf16[32,12]{0,1:T(8,128)(2,1)S(1)}, bf16[32,12]{0,1:T(8,128)(2,1)}, u32[]{:S(2)}) copy-start(bf16[32,12]{0,1:T(8,128)(2,1)} %param.19) | copy-start | bytes 2308
  7.2 71.9 %all-gather.13.cloned.1.call-start = ((), (), s32[]{:S(2)}) async-start(), calls=%async_computation.12 | async-start | bytes 5271552 | tf_op jit(solution)/shard_map/all_gather | solution.py:823
  10.6 107.0 %all-gather.15.cloned.1.call-start = ((), (), s32[]{:S(2)}) async-start(), calls=%async_computation.13 | async-start | bytes 5898240 | tf_op jit(solution)/shard_map/all_gather | solution.py:833
  10.7 3.4 copy-start.3
  14.0 142.7 %all-gather.17.cloned.1.call-start = ((), (), s32[]{:S(2)}) async-start(), calls=%async_computation.14 | async-start | bytes 5898240 | tf_op jit(solution)/shard_map/all_gather | solution.py:834
  15.7 2.1 copy-start.7
  15.7 245.2 %all-gather.19.cloned.1.call-start = ((), (), s32[]{:S(2)}) async-start(), calls=%async_computation.15 | async-start | bytes 5271552 | tf_op jit(solution)/shard_map/all_gather | solution.py:823
  16.5 281.3 %all-gather.21.cloned.1.call-start = ((), (), s32[]{:S(2)}) async-start(), calls=%async_computation.16 | async-start | bytes 5898240 | tf_op jit(solution)/shard_map/all_gather | solution.py:833
  16.6 3.4 copy-start.13
  17.1 3.9 copy-start.12
  17.1 4.8 copy-start.2
  17.2 319.6 %all-gather.23.cloned.1.call-start = ((), (), s32[]{:S(2)}) async-start(), calls=%async_computation.17 | async-start | bytes 5898240 | tf_op jit(solution)/shard_map/all_gather | solution.py:834
  17.7 682.4 %reduce-scatter.9.cloned.1.call-start = ((), (), s32[]{:S(2)}) async-start(), calls=%async_computation.7 | async-start | bytes 4866048 | tf_op jit(solution)/shard_map/reduce_scatter | solution.py:872
  24.6 8.7 copy-start.10
  24.6 8.7 copy-start.11
  525.3 239.3 %reduce-scatter.7.cloned.1.call-start = ((), (), s32[]{:S(2)}) async-start(), calls=%async_computation.6 | async-start | bytes 4866048 | tf_op jit(solution)/shard_map/reduce_scatter | solution.py:872
  651.0 163.1 %reduce-scatter.13.cloned.1.call-start = ((), (), s32[]{:S(2)}) async-start(), calls=%async_computation.9 | async-start | bytes 5898240 | tf_op jit(solution)/shard_map/reduce_scatter | solution.py:855
  651.7 212.8 %reduce-scatter.11.cloned.1.call-start = ((), (), s32[]{:S(2)}) async-start(), calls=%async_computation.8 | async-start | bytes 5898240 | tf_op jit(solution)/shard_map/reduce_scatter | solution.py:855
  652.3 262.6 %reduce-scatter.17.cloned.1.call-start = ((), (), s32[]{:S(2)}) async-start(), calls=%async_computation.11 | async-start | bytes 5898240 | tf_op jit(solution)/shard_map/reduce_scatter | solution.py:854
  653.1 312.3 %reduce-scatter.15.cloned.1.call-start = ((), (), s32[]{:S(2)}) async-start(), calls=%async_computation.10 | async-start | bytes 5898240 | tf_op jit(solution)/shard_map/reduce_scatter | solution.py:854
  653.1 0.8 copy-start.5
  653.1 0.8 copy-start.6
  653.1 0.9 copy-start.15
  653.1 0.9 copy-start.17
  653.1 0.9 copy-start.14
  653.2 0.9 copy-start.16
  653.2 0.9 copy-start.8
  653.2 0.9 copy-start.9
  965.3 4.2 copy-start.4
  969.5 1.1 copy-start.1
Sparse Core Ops, SparseCore 0:
  11.6 67.4 all-gather.12
  81.3 36.3 all-gather.14
  119.2 37.4 all-gather.16
  160.1 100.6 all-gather.18
  262.3 35.5 all-gather.20
  299.3 37.4 all-gather.22
  525.4 126.0 reduce-scatter.8
  658.5 106.0 reduce-scatter.6
  767.1 46.9 reduce-scatter.12
  816.6 47.8 reduce-scatter.10
  867.0 47.8 reduce-scatter.16
  917.4 47.8 reduce-scatter.14

commit v3 on v2

--- a/solution.py
+++ b/solution.py
@@ -12,6 +12,7 @@
 f32 = jnp.float32
 bf16 = jnp.bfloat16
 masked_out = -1e30
+tile_rows = 16
 MESH = pl.DeviceIdType.MESH
 vmem_spec = pl.BlockSpec(memory_space=pltpu.VMEM)
 any_spec = pl.BlockSpec(memory_space=pl.ANY)
@@ -27,8 +28,18 @@
     return [whole(array.shape) for array in arrays]
 
 
-def params():
-    return pltpu.CompilerParams(vmem_limit_bytes=vmem_bytes)
+def params(identifier=None):
+    if identifier is None:
+        return pltpu.CompilerParams(vmem_limit_bytes=vmem_bytes)
+    return pltpu.CompilerParams(
+        vmem_limit_bytes=vmem_bytes, collective_id=identifier, has_side_effects=True
+    )
+
+
+def lasting(microseconds):
+    return pl.CostEstimate(
+        flops=int(microseconds * 1e9), bytes_accessed=1 << 20, transcendentals=0
+    )
 
 
 def dot(lhs, rhs, lhs_dim=1, rhs_dim=0):
@@ -68,38 +79,304 @@
     return (places == slot_col).astype(f32).astype(bf16)
 
 
-def bias_kernel(offsets_ref, piece_col_ref, piece_row_ref, bias_ref):
-    seq_len = piece_col_ref.shape[0]
-    row = jnp.broadcast_to(offsets_ref[0], (seq_len, 2 * seq_len))
-    shifted = pltpu.roll(row, seq_len + 1, 1, stride=1, stride_axis=0)[:, :seq_len]
-    key_pos = lax.broadcasted_iota(jnp.int32, (seq_len, seq_len), 0)
-    query_pos = lax.broadcasted_iota(jnp.int32, (seq_len, seq_len), 1)
-    piece_col = piece_col_ref[...]
-    same = (piece_col == piece_row_ref[...]) & (piece_col > 0)
-    allowed = (key_pos <= query_pos) | same
-    bias_ref[0] = jnp.where(allowed, shifted, masked_out).astype(bf16)
-
-
-def bias_of(offsets, piece_ids):
-    heads, seq_len = offsets.shape[0], piece_ids.shape[0]
+def greet(peers):
+    barrier = pltpu.get_barrier_semaphore()
+    for peer in peers:
+        pl.semaphore_signal(barrier, inc=1, device_id=peer, device_id_type=MESH)
+    pl.semaphore_wait(barrier, len(peers))
+
+
+def bits_of(count):
+    return count.bit_length() - 1
+
+
+class Place:
+    def __init__(self, grid_shape):
+        self.count_y, self.count_z = grid_shape[0] // 2, grid_shape[1] // 2
+        first, second = lax.axis_index("gx"), lax.axis_index("gy")
+        self.c, self.y = first % 2, first // 2
+        self.x, self.z = second % 2, second // 2
+
+    def core_peer(self):
+        return {"gx": self.y * 2 + 1 - self.c}
+
+    def x_peer(self):
+        return {"gy": self.z * 2 + 1 - self.x}
+
+    def y_at(self, apart):
+        return xor_of(self.y, apart, bits_of(self.count_y))
+
+    def y_peer(self, apart):
+        return {"gx": self.y_at(apart) * 2 + self.c}
+
+    def y_peers(self):
+        return [self.y_peer(apart) for apart in range(1, self.count_y)]
+
+    def z_at(self, apart):
+        return xor_of(self.z, apart, bits_of(self.count_z))
+
+    def z_peer(self, apart):
+        return {"gy": self.z_at(apart) * 2 + self.x}
+
+    def z_peers(self):
+        return [self.z_peer(apart) for apart in range(1, self.count_z)]
+
+
+def send(src, dst, sems, index, peer):
+    return pltpu.make_async_remote_copy(
+        src_ref=src,
+        dst_ref=dst,
+        send_sem=sems[0].at[index],
+        recv_sem=sems[1].at[index],
+        device_id=peer,
+        device_id_type=MESH,
+    )
+
+
+def start_all(copies):
+    for copy in copies:
+        copy.start()
+
+
+def wait_all(copies):
+    for copy in copies:
+        copy.wait()
+
+
+def gather_z(place, src, landing, sems):
+    return [
+        send(src, landing, sems, apart - 1, place.z_peer(apart)) for apart in range(1, place.count_z)
+    ]
+
+
+def gather_copies(grid_shape):
+    return grid_shape[1] // 2 - 1, 2 * (grid_shape[0] // 2 - 1) + 3
+
+
+def gather_second(place, column, full, split, sems):
+    y, c, x = place.y, place.c, place.x
+    upper, lower = pl.ds(0, split), pl.ds(split, full.shape[4] - split)
+    copies = [
+        send(column.at[:, upper], full.at[y, c, :, x, upper], sems, 0, place.x_peer())
+    ]
+    for apart in range(1, place.count_y):
+        copies.append(
+            send(column.at[:, lower], full.at[y, c, :, x, lower], sems, apart, place.y_peer(apart))
+        )
+    return copies
+
+
+def gather_third(place, full, split, sems):
+    y, c, x = place.y, place.c, place.x
+    upper, lower = pl.ds(0, split), pl.ds(split, full.shape[4] - split)
+    base = place.count_y
+    ref = full.at[:, c, :, x, lower]
+    copies = [send(ref, ref, sems, base, place.x_peer())]
+    ref = full.at[y, c, :, :, upper]
+    for apart in range(1, place.count_y):
+        copies.append(send(ref, ref, sems, base + apart, place.y_peer(apart)))
+    return copies
+
+
+def gather_core(place, full, sems):
+    ref = full.at[:, place.c]
+    return [send(ref, ref, sems, 2 * place.count_y, place.core_peer())]
+
+
+def whole_blocks(shape, split):
+    count_y, _, count_z, _, tall, lanes = shape
+    low = tall - split
+    return [
+        (count_y, count_z, 2, tall, lanes),
+        (count_y - 1, count_z, 2, split, lanes),
+        (count_y, count_z, low, lanes),
+        (count_z, split, lanes),
+        (count_y - 1, count_z, low, lanes),
+        (count_z - 1, split, lanes),
+        (count_z - 1, low, lanes),
+    ]
+
+
+def scatter_copies(grid_shape):
+    return 1 + 2 * (grid_shape[0] // 2) + 2 * (grid_shape[1] // 2 - 1)
+
+
+def add_low(dst, dst_at, *terms):
+    total = terms[0].astype(f32)
+    for term in terms[1:]:
+        total = total + term.astype(f32)
+    dst[dst_at] = total.astype(bf16)
+
+
+class Scatter:
+    def __init__(self, place, src, landings, sems, split):
+        self.place, self.src, self.sems = place, src, sems
+        self.first, self.up2, self.low2, self.up3, self.low3, self.up4, self.low4 = landings
+        tall = src.shape[4]
+        self.upper, self.lower = pl.ds(0, split), pl.ds(split, tall - split)
+
+    def copies(self, stage):
+        at, sems = self.place, self.sems
+        count_y, count_z = at.count_y, at.count_z
+        if stage == 0:
+            return [send(self.src.at[:, 1 - at.c], self.first, sems, 0, at.core_peer())]
+        if stage == 1:
+            copies = [send(self.first.at[:, :, 1 - at.x, self.lower], self.low2, sems, 1, at.x_peer())]
+            for apart in range(1, count_y):
+                src = self.first.at[at.y_at(apart), :, :, self.upper]
+                dst = self.up2.at[apart - 1]
+                copies.append(send(src, dst, sems, 1 + apart, at.y_peer(apart)))
+            return copies
+        if stage == 2:
+            base = 1 + count_y
+            copies = [send(self.up2.at[0, :, 1 - at.x], self.up3, sems, base, at.x_peer())]
+            for apart in range(1, count_y):
+                src, dst = self.low2.at[at.y_at(apart)], self.low3.at[apart - 1]
+                copies.append(send(src, dst, sems, base + apart, at.y_peer(apart)))
+            return copies
+        base = 2 * count_y
+        copies = []
+        for apart in range(1, count_z):
+            there = at.z_at(apart)
+            for src, dst, more in (
+                (self.up3.at[there], self.up4.at[apart - 1], 0),
+                (self.low3.at[0, there], self.low4.at[apart - 1], 1),
+            ):
+                index = base + 2 * apart - 1 + more
+                copies.append(send(src, dst, sems, index, at.z_peer(apart)))
+        return copies
+
+    def add(self, stage):
+        at = self.place
+        count_y, count_z = at.count_y, at.count_z
+        if stage == 0:
+
+            @pl.loop(0, count_y * count_z)
+            def _(index):
+                y, z = index // count_z, index % count_z
+                add_low(self.first, (y, z), self.first[y, z], self.src[y, at.c, z])
+
+        elif stage == 1:
+
+            @pl.loop(0, count_z)
+            def _(z):
+                for x in range(2):
+                    terms = [self.up2[apart, z, x] for apart in range(count_y - 1)]
+                    add_low(self.up2, (0, z, x), self.first[at.y, z, x, self.upper], *terms)
+
+                @pl.loop(0, count_y)
+                def _(y):
+                    add_low(self.low2, (y, z), self.first[y, z, at.x, self.lower], self.low2[y, z])
+
+        elif stage == 2:
+
+            @pl.loop(0, count_z)
+            def _(z):
+                add_low(self.up3, (z,), self.up3[z], self.up2[0, z, at.x])
+                terms = [self.low3[apart, z] for apart in range(count_y - 1)]
+                add_low(self.low3, (0, z), self.low2[at.y, z], *terms)
+
+    def result(self):
+        at = self.place
+        upper, lower = self.up3[at.z].astype(f32), self.low3[0, at.z].astype(f32)
+        for apart in range(at.count_z - 1):
+            upper = upper + self.up4[apart].astype(f32)
+            lower = lower + self.low4[apart].astype(f32)
+        return upper, lower
+
+
+class SmallSum:
+    def __init__(self, grid_shape, totals, landing, sems):
+        self.totals, self.landing, self.sems = totals, landing, sems
+        self.peers = []
+        for name, count in (("gx", grid_shape[0]), ("gy", grid_shape[1])):
+            me = lax.axis_index(name)
+            for bit in range(bits_of(count)):
+                self.peers.append({name: xor_of(me, 1 << bit, bits_of(count))})
+        self.done = 0
+
+    def copy(self):
+        step = self.done
+        return send(self.totals.at[step], self.landing.at[step], self.sems, step, self.peers[step])
+
+    def begin(self):
+        self.copy().start()
+
+    def advance(self):
+        if self.done == len(self.peers):
+            return
+        self.copy().wait()
+        step = self.done
+        self.totals[step + 1] = self.totals[step] + self.landing[step]
+        self.done += 1
+        if self.done < len(self.peers):
+            self.begin()
+
+
+def small_steps(grid_shape):
+    return bits_of(grid_shape[0]) + bits_of(grid_shape[1])
+
+
+def final_kernel(grid_shape, layers, *refs):
+    refs = list(refs)
+    take = refs.pop
+    blocks = [take(0) for _ in range(layers)]
+    small_ref = take(0)
+    outs = [take(0) for _ in range(4)]
+    small_out_ref = take(0)
+    landings = [[take(0) for _ in range(7)] for _ in range(layers)]
+    totals, landing = take(0), take(0)
+    sems = [(take(0), take(0)) for _ in range(layers)]
+    small_sems = (take(0), take(0))
+    place = Place(grid_shape)
+    tall, wide = outs[0].shape[1:]
+    split = tall // 2
+    sums = [Scatter(place, blocks[l], landings[l], sems[l], split) for l in range(layers)][::-1]
+    small = SmallSum(grid_shape, totals, landing, small_sems)
+    totals[0] = small_ref[...]
+    greet([place.core_peer(), place.x_peer()] + place.y_peers() + place.z_peers())
+    small.begin()
+    for one in sums:
+        start_all(one.copies(0))
+    for stage in range(4):
+        for one in sums:
+            small.advance()
+            wait_all(one.copies(stage))
+            if stage < 3:
+                one.add(stage)
+                start_all(one.copies(stage + 1))
+    while small.done < len(small.peers):
+        small.advance()
+    small_out_ref[...] = totals[len(small.peers)]
+    for layer, one in enumerate(sums[::-1]):
+        for part, rows in zip(one.result(), (slice(0, split), slice(split, tall))):
+            for which in range(4):
+                outs[which][layer, rows, :] = part[:, which * wide : (which + 1) * wide]
+
+
+def final_sums(blocks, small, grid_shape, wide):
+    layers = len(blocks)
+    shape = blocks[0].shape
+    tall = shape[4]
+    landings = [pltpu.VMEM(one, bf16) for one in whole_blocks(shape, tall // 2)]
+    steps = small_steps(grid_shape)
+    sems = pltpu.SemaphoreType.DMA((scatter_copies(grid_shape),))
+    small_sems = pltpu.SemaphoreType.DMA((steps,))
+    outs = [jax.ShapeDtypeStruct((layers, tall, wide), f32)] * 4
+    outs.append(jax.ShapeDtypeStruct(small.shape, f32))
     return pl.pallas_call(
-        bias_kernel,
-        grid=(heads,),
-        in_specs=[
-            pl.BlockSpec((1, 1, 2 * seq_len), lambda h: (h, 0, 0)),
-            whole((seq_len, 1)),
-            whole((1, seq_len)),
-        ],
-        out_specs=pl.BlockSpec((1, seq_len, seq_len), lambda h: (h, 0, 0)),
-        out_shape=jax.ShapeDtypeStruct((heads, seq_len, seq_len), bf16),
-        compiler_params=params(),
-        name="bias_table",
-    )(offsets[:, None, :], piece_ids[:, None], piece_ids[None, :])
-
-
-def half_masks(rows, width):
-    lane = lax.broadcasted_iota(jnp.int32, (rows, width), 1)
-    return lane < (width // 2)
+        partial(final_kernel, grid_shape, layers),
+        in_specs=[vmem_spec] * (layers + 1),
+        out_specs=[vmem_spec] * len(outs),
+        out_shape=outs,
+        scratch_shapes=landings * layers
+        + [pltpu.VMEM((steps + 1, *small.shape), f32), pltpu.VMEM((steps, *small.shape), f32)]
+        + [sems, sems] * layers
+        + [small_sems, small_sems],
+        compiler_params=params(20),
+        cost_estimate=lasting(60),
+        name="final_sums",
+    )(*blocks, small)
 
 
 def unblock(grid_shape, blocks_ref, mats_ref, router_ref):
@@ -108,47 +385,211 @@
     wide = mats_ref.shape[2] // count_y
     router_rows = []
     for first in range(count_x):
-        block_rows = [first * count_y + second for second in range(count_y)]
+        spots = [(first // 2, first % 2, second // 2, second % 2) for second in range(count_y)]
         rows = slice(first * tall, (first + 1) * tall)
         for which in range(4):
             lanes = slice(which * wide, (which + 1) * wide)
             mats_ref[which, rows, :] = jnp.concatenate(
-                [blocks_ref[block, :tall, lanes] for block in block_rows], axis=1
+                [blocks_ref[(*spot, slice(0, tall), lanes)] for spot in spots], axis=1
             )
         router_rows.append(
-            jnp.concatenate([blocks_ref[block, tall : tall + 1, :tall] for block in block_rows], axis=0)
+            jnp.concatenate(
+                [blocks_ref[(*spot, slice(tall, tall + 1), slice(0, tall))] for spot in spots],
+                axis=0,
+            )
         )
     router_ref[...] = jnp.concatenate(router_rows, axis=1)
+
+
+def start_kernel(
+    grid_shape,
+    wq_ref,
+    wk_ref,
+    wv_ref,
+    wo_ref,
+    router_rows_ref,
+    buckets_ref,
+    table_ref,
+    piece_col_ref,
+    piece_row_ref,
+    route_col_ref,
+    route_row_ref,
+    mats_ref,
+    router_ref,
+    later_ref,
+    bias_ref,
+    slot_col_ref,
+    slot_row_ref,
+    chosen_ref,
+    full_s,
+    column_s,
+    z_send,
+    z_recv,
+    send_sems,
+    recv_sems,
+):
+    place = Place(grid_shape)
+    layers, tall, wide = wq_ref.shape
+    split = tall // 2
+    y, c, z, x = place.y, place.c, place.z, place.x
+
+    def packed(layer):
+        return jnp.concatenate([ref[layer] for ref in (wq_ref, wk_ref, wv_ref, wo_ref)], axis=1)
+
+    column_s[z, :tall] = packed(0)
+    column_s[z, tall:] = router_rows_ref[0]
+    greet([place.core_peer(), place.x_peer()] + place.y_peers() + place.z_peers())
+    first = gather_z(place, column_s.at[z], column_s.at[z], (z_send, z_recv))
+    start_all(first)
+    for layer in range(1, layers):
+        later_ref[layer - 1, :tall] = packed(layer)
+        later_ref[layer - 1, tall:] = router_rows_ref[layer]
+
+    seq_len, experts = chosen_ref.shape
+    capacity = 2 * seq_len // experts
+    heads = bias_ref.shape[0]
+    buckets_all = buckets_ref[...]
+    in_bucket = lax.broadcasted_iota(jnp.int32, (2 * seq_len, table_ref.shape[1]), 1) == buckets_all
+    offsets = dot(table_ref[...], in_bucket.astype(f32).astype(bf16), 1, 1)
+    key_pos = lax.broadcasted_iota(jnp.int32, (seq_len, seq_len), 0)
+    query_pos = lax.broadcasted_iota(jnp.int32, (seq_len, seq_len), 1)
+    piece_col = piece_col_ref[...]
+    same = (piece_col == piece_row_ref[...]) & (piece_col > 0)
+    allowed = (key_pos <= query_pos) | same
+
+    def bias_for(head):
+        row = jnp.broadcast_to(offsets[head : head + 1], (seq_len, 2 * seq_len))
+        shifted = pltpu.roll(row, seq_len + 1, 1, stride=1, stride_axis=0)[:, :seq_len]
+        bias_ref[head] = jnp.where(allowed, shifted, masked_out).astype(bf16)
+
+    for head in range(heads // 2):
+        bias_for(head)
+    wait_all(first)
+    sems = (send_sems, recv_sems)
+    second = gather_second(place, column_s, full_s, split, sems)
+    start_all(second)
+    full_s[y, c, :, x] = column_s[...]
+    for head in range(heads // 2, heads):
+        bias_for(head)
+    wait_all(second)
+    third = gather_third(place, full_s, split, sems)
+    start_all(third)
+
+    route_col, route_row = route_col_ref[...], route_row_ref[...]
+    chosen = (lax.broadcasted_iota(jnp.int32, (seq_len, experts), 1) == route_col).astype(f32)
+    chosen_t = (lax.broadcasted_iota(jnp.int32, (experts, seq_len), 0) == route_row).astype(f32)
+    chosen_ref[...] = chosen
+    earlier = (key_pos < query_pos).astype(f32).astype(bf16)
+    before_t = dot(chosen_t.astype(bf16), earlier)
+    rank_row = jnp.sum(before_t * chosen_t, axis=0, keepdims=True)
+    slot_row_ref[...] = route_row * capacity + rank_row.astype(jnp.int32)
+    later = (key_pos > query_pos).astype(f32).astype(bf16)
+    before = dot(later, chosen.astype(bf16))
+    rank_col = jnp.sum(before * chosen, axis=1, keepdims=True)
+    slot_col_ref[...] = route_col * capacity + rank_col.astype(jnp.int32)
+
+    wait_all(third)
+    fourth = gather_core(place, full_s, sems)
+    start_all(fourth)
+    wait_all(fourth)
+    unblock(grid_shape, full_s, mats_ref, router_ref)
+
+
+def start(mats, router_rows, buckets, table_t, piece_ids, route, grid_shape):
+    layers, tall, wide = mats[0].shape
+    seq_len = piece_ids.shape[0]
+    heads = table_t.shape[0]
+    width = tall * grid_shape[0]
+    experts = grid_shape[1]
+    block = (router_rows.shape[1] + tall, 4 * wide)
+    half = (grid_shape[0] // 2, 2, grid_shape[1] // 2, 2)
+    ins = (
+        *mats,
+        router_rows,
+        buckets,
+        table_t,
+        piece_ids[:, None],
+        piece_ids[None, :],
+        route,
+        route.reshape(1, seq_len),
+    )
+    outs = (
+        jax.ShapeDtypeStruct((4, width, width), bf16),
+        jax.ShapeDtypeStruct((experts, width), bf16),
+        jax.ShapeDtypeStruct((layers - 1, *block), bf16),
+        jax.ShapeDtypeStruct((heads, seq_len, seq_len), bf16),
+        jax.ShapeDtypeStruct((seq_len, 1), jnp.int32),
+        jax.ShapeDtypeStruct((1, seq_len), jnp.int32),
+        jax.ShapeDtypeStruct((seq_len, experts), f32),
+    )
+    along_z, others = gather_copies(grid_shape)
+    return pl.pallas_call(
+        partial(start_kernel, grid_shape),
+        in_specs=[vmem_spec] * len(ins),
+        out_specs=[vmem_spec] * len(outs),
+        out_shape=outs,
+        scratch_shapes=[
+            pltpu.VMEM((*half, *block), bf16),
+            pltpu.VMEM((half[2], *block), bf16),
+            pltpu.SemaphoreType.DMA((along_z,)),
+            pltpu.SemaphoreType.DMA((along_z,)),
+            pltpu.SemaphoreType.DMA((others,)),
+            pltpu.SemaphoreType.DMA((others,)),
+        ],
+        compiler_params=params(0),
+        cost_estimate=lasting(45),
+        name="start",
+    )(*ins)
+
+
+def half_masks(rows, width):
+    lane = lax.broadcasted_iota(jnp.int32, (rows, width), 1)
+    return lane < (width // 2)
 
 
 def forward_kernel(
     head_dim,
     grid_shape,
+    blocked,
+    sends,
     hidden_ref,
     gain_attn_ref,
     gain_ffn_ref,
     slot_row_ref,
-    blocks_ref,
-    bias_ref,
-    mats_ref,
-    router_ref,
-    q_ref,
-    k_ref,
-    v_ref,
-    att_ref,
-    lse_ref,
-    middle_ref,
-    logits_ref,
-    sent_ref,
+    *refs,
 ):
+    refs = list(refs)
+    take = refs.pop
+    blocks_ref = take(0) if blocked else None
+    mats_ref, router_ref = (None, None) if blocked else (take(0), take(0))
+    next_ref = take(0) if sends else None
+    bias_ref = take(0)
+    if blocked:
+        mats_ref, router_ref = take(0), take(0)
+    q_ref, k_ref, v_ref, att_ref, lse_ref, middle_ref, logits_ref, sent_ref = (
+        take(0) for _ in range(8)
+    )
     pair, pairs = pl.program_id(0), pl.num_programs(0)
     seq_len = hidden_ref.shape[0]
     width = 2 * head_dim
     step = min(256, seq_len)
 
+    if sends:
+        column_ref, z_send, z_recv, own_sem = refs
+        place = Place(grid_shape)
+        own = pltpu.make_async_copy(next_ref, column_ref.at[place.z], own_sem)
+        copies = gather_z(place, next_ref, column_ref.at[place.z], (z_send, z_recv))
+
+        @pl.when(pair == 0)
+        def _():
+            greet(place.z_peers())
+            own.start()
+            start_all(copies)
+
     @pl.when(pair == 0)
     def _():
-        unblock(grid_shape, blocks_ref, mats_ref, router_ref)
+        if blocked:
+            unblock(grid_shape, blocks_ref, mats_ref, router_ref)
         hidden = hidden_ref[...].astype(f32)
         normed = (hidden * rms_factor(hidden) * gain_attn_ref[...]).astype(bf16)
         q_ref[...] = dot(normed, mats_ref[0]).astype(bf16)
@@ -163,8 +604,8 @@
     for half in range(2):
         q_one = jnp.where(first if half == 0 else ~first, q2, jnp.zeros_like(q2))
         v_one = v2t[half * head_dim : (half + 1) * head_dim]
-        for start in range(0, seq_len, step):
-            cols = slice(start, start + step)
+        for begin in range(0, seq_len, step):
+            cols = slice(begin, begin + step)
             scores = dot(k2, q_one[cols], 1, 1) + bias_ref[half, :, cols].astype(f32)
             top = jnp.max(scores, axis=0, keepdims=True)
             raised = jnp.exp(scores - top)
@@ -183,17 +624,32 @@
         placing = placing_rows(slot_row_ref[...], sent_ref.shape[0])
         sent_ref[...] = dot(placing, ffn_in).astype(bf16)
 
-
-def attention_forward(hidden, gain_attn, gain_ffn, blocks, slot_row, bias, grid_shape, experts):
+    if sends:
+
+        @pl.when(pair == pairs - 1)
+        def _():
+            own.wait()
+            wait_all(copies)
+
+
+def attention_forward(
+    hidden, gain_attn, gain_ffn, slot_row, bias, grid_shape, identifier, blocks=None, mats=None, following=None
+):
     seq_len, width = hidden.shape
     heads = bias.shape[0]
     head_dim = width // heads
     slots = 2 * seq_len
-    ins = (hidden, gain_attn, gain_ffn, slot_row, blocks)
+    experts = grid_shape[1]
+    blocked, sends = blocks is not None, following is not None
+    ins = [hidden, gain_attn, gain_ffn, slot_row] + ([blocks] if blocked else list(mats))
+    in_specs = whole_of(ins)
+    if sends:
+        ins.append(following)
+        in_specs.append(any_spec)
+    ins.append(bias)
+    in_specs.append(pl.BlockSpec((2, seq_len, seq_len), lambda p: (p, 0, 0)))
     tall = jax.ShapeDtypeStruct((seq_len, width), bf16)
-    outs = (
-        jax.ShapeDtypeStruct((4, width, width), bf16),
-        jax.ShapeDtypeStruct((experts, width), bf16),
+    outs = [
         tall,
         tall,
         tall,
@@ -202,18 +658,37 @@
         jax.ShapeDtypeStruct((seq_len, width), f32),
         jax.ShapeDtypeStruct((seq_len, experts), f32),
         jax.ShapeDtypeStruct((slots, width), bf16),
-    )
+    ]
     out_specs = whole_of(outs)
-    out_specs[6] = pl.BlockSpec((1, 2, seq_len), lambda p: (p, 0, 0))
-    return pl.pallas_call(
-        partial(forward_kernel, head_dim, grid_shape),
+    out_specs[4] = pl.BlockSpec((1, 2, seq_len), lambda p: (p, 0, 0))
+    if blocked:
+        more = [
+            jax.ShapeDtypeStruct((4, width, width), bf16),
+            jax.ShapeDtypeStruct((experts, width), bf16),
+        ]
+        outs = more + outs
+        out_specs = whole_of(more) + out_specs
+    scratch = []
+    if sends:
+        along_z = grid_shape[1] // 2
+        outs.append(jax.ShapeDtypeStruct((along_z, *following.shape), bf16))
+        out_specs.append(any_spec)
+        sems = pltpu.SemaphoreType.DMA((along_z - 1,))
+        scratch = [sems, sems, pltpu.SemaphoreType.DMA]
+    got = pl.pallas_call(
+        partial(forward_kernel, head_dim, grid_shape, blocked, sends),
         grid=(heads // 2,),
-        in_specs=whole_of(ins) + [pl.BlockSpec((2, seq_len, seq_len), lambda p: (p, 0, 0))],
+        in_specs=in_specs,
         out_specs=out_specs,
         out_shape=outs,
-        compiler_params=params(),
+        scratch_shapes=scratch,
+        compiler_params=params(identifier if sends else None),
+        cost_estimate=lasting(25),
         name="attention_forward",
-    )(*ins, bias)
+    )(*ins)
+    column = got[-1] if sends else None
+    got = got[:-1] if sends else got
+    return (tuple(mats) + tuple(got) if not blocked else tuple(got)), column
 
 
 def diagonal_fold(values, seq_len):
@@ -246,14 +721,28 @@
     wide = values.shape[1] // count_y
     for first in range(count_x):
         for second in range(count_y):
-            blocks_ref[first * count_y + second, :, which * wide : (which + 1) * wide] = values[
+            spot = (first // 2, first % 2, second // 2, second % 2)
+            lanes = slice(which * wide, (which + 1) * wide)
+            blocks_ref[(*spot, slice(None), lanes)] = values[
                 first * tall : (first + 1) * tall, second * wide : (second + 1) * wide
             ]
+
+
+def spread_into(grad_now, comb_ref, slot_row_ref, chosen_ref, logits_ref, d_sent_ref, d_logits_ref):
+    d_gate = jnp.sum(grad_now * comb_ref[...], axis=1, keepdims=True)
+    shares = jax.nn.softmax(logits_ref[...], axis=-1)
+    chosen = chosen_ref[...]
+    gate = jnp.sum(shares * chosen, axis=1, keepdims=True)
+    d_logits_ref[...] = (d_gate * shares * (chosen - gate)).astype(bf16)
+    placing = placing_rows(slot_row_ref[...], d_sent_ref.shape[0])
+    d_sent_ref[...] = dot(placing, (gate * grad_now).astype(bf16)).astype(bf16)
 
 
 def backward_kernel(
     head_dim,
     grid_shape,
+    spreads,
+    unread,
     d_back_ref,
     slot_col_ref,
     d_logits_ref,
@@ -268,22 +757,16 @@
     k_ref,
     v_ref,
     att_ref,
-    bias_ref,
-    lse_ref,
-    grad_new_ref,
-    blocks_ref,
-    gwr_ref,
-    gga_ref,
-    ggf_ref,
-    offsets_ref,
-    d_att_s,
-    d_middle_s,
-    dqt_s,
-    dk_s,
-    dv_s,
-    probs_s,
-    scores_s,
+    *refs,
 ):
+    refs = list(refs)
+    take = refs.pop
+    spread_in = [take(0) for _ in range(4)] if spreads else []
+    bias_ref, lse_ref = take(0), take(0)
+    del refs[:unread]
+    grad_new_ref, blocks_ref, gwr_ref, gga_ref, ggf_ref, offsets_ref = (take(0) for _ in range(6))
+    spread_out = [take(0) for _ in range(2)] if spreads else []
+    d_att_s, d_middle_s, dqt_s, dk_s, dv_s, probs_s, scores_s = refs
     pair, pairs = pl.program_id(0), pl.num_programs(0)
     seq_len = hidden_ref.shape[0]
     width = 2 * head_dim
@@ -301,7 +784,7 @@
         gwr_ref[...] = dot(d_logits, ffn_in, 0, 0)
         d_middle, d_gain = rms_pull(middle, gain_row, d_ffn)
         ggf_ref[...] = d_gain
-        d_middle = d_middle + grad_ref[...]
+        d_middle = d_middle + grad_ref[...].astype(f32)
         d_middle_s[...] = d_middle
         d_low = d_middle.astype(bf16)
         reblock(grid_shape, blocks_ref, 3, dot(att_ref[...], d_low).astype(bf16))
@@ -352,7 +835,10 @@
         reblock(grid_shape, blocks_ref, 2, dot(normed_t, dv_s[...]).astype(bf16))
         d_hidden, d_gain = rms_pull(hidden, gain_row, d_normed)
         gga_ref[...] = d_gain
-        grad_new_ref[...] = d_hidden + d_middle_s[...]
+        grad_new = d_hidden + d_middle_s[...]
+        grad_new_ref[...] = grad_new
+        if spreads:
+            spread_into(grad_new, *spread_in, *spread_out)
 
 
 def attention_backward(
@@ -369,6 +855,8 @@
     bias,
     lse,
     grid_shape,
+    below=None,
+    after=(),
 ):
     seq_len, width = hidden.shape
     heads = bias.shape[0]
@@ -387,27 +875,36 @@
         *q_k_v,
         attended,
     )
+    spreads = below is not None
+    if spreads:
+        ins = ins + tuple(below)
     row = jax.ShapeDtypeStruct((1, width), f32)
     outs = (
         jax.ShapeDtypeStruct((seq_len, width), f32),
         jax.ShapeDtypeStruct(
-            (count_x * count_y, width // count_x, 4 * (width // count_y)), bf16
+            (count_x // 2, 2, count_y // 2, 2, width // count_x, 4 * (width // count_y)), bf16
         ),
         jax.ShapeDtypeStruct((experts, width), f32),
         row,
         row,
         jax.ShapeDtypeStruct((heads // 2, 2, 2 * seq_len), f32),
     )
+    if spreads:
+        outs = outs + (
+            jax.ShapeDtypeStruct((2 * seq_len, width), bf16),
+            jax.ShapeDtypeStruct(d_logits.shape, bf16),
+        )
     out_specs = whole_of(outs)
     out_specs[5] = pl.BlockSpec((1, 2, 2 * seq_len), lambda p: (p, 0, 0))
     return pl.pallas_call(
-        partial(backward_kernel, head_dim, grid_shape),
+        partial(backward_kernel, head_dim, grid_shape, spreads, len(after)),
         grid=(heads // 2,),
         in_specs=whole_of(ins)
         + [
             pl.BlockSpec((2, seq_len, seq_len), lambda p: (p, 0, 0)),
             pl.BlockSpec((1, 2, seq_len), lambda p: (p, 0, 0)),
-        ],
+        ]
+        + [any_spec] * len(after),
         out_specs=out_specs,
         out_shape=outs,
         scratch_shapes=[
@@ -420,44 +917,9 @@
             pltpu.VMEM((seq_len, seq_len), bf16),
         ],
         compiler_params=params(),
+        cost_estimate=lasting(32),
         name="attention_backward",
-    )(*ins, bias, lse)
-
-
-def spread_kernel(grad_ref, comb_ref, slot_row_ref, chosen_ref, logits_ref, d_sent_ref, d_logits_ref):
-    grad_now = grad_ref[...].astype(f32)
-    d_gate = jnp.sum(grad_now * comb_ref[...], axis=1, keepdims=True)
-    shares = jax.nn.softmax(logits_ref[...], axis=-1)
-    chosen = chosen_ref[...]
-    gate = jnp.sum(shares * chosen, axis=1, keepdims=True)
-    d_logits_ref[...] = (d_gate * shares * (chosen - gate)).astype(bf16)
-    placing = placing_rows(slot_row_ref[...], d_sent_ref.shape[0])
-    d_sent_ref[...] = dot(placing, (gate * grad_now).astype(bf16)).astype(bf16)
-
-
-def spread(grad_now, combined, slot_row, chosen_f, logits):
-    seq_len, width = grad_now.shape
-    outs = (
-        jax.ShapeDtypeStruct((2 * seq_len, width), bf16),
-        jax.ShapeDtypeStruct(logits.shape, bf16),
-    )
-    ins = (grad_now, combined, slot_row, chosen_f, logits)
-    return pl.pallas_call(
-        spread_kernel,
-        in_specs=whole_of(ins),
-        out_specs=whole_of(outs),
-        out_shape=outs,
-        grid=(1,),
-        compiler_params=params(),
-        name="spread",
-    )(*ins)
-
-
-def greet(peers):
-    barrier = pltpu.get_barrier_semaphore()
-    for peer in peers:
-        pl.semaphore_signal(barrier, inc=1, device_id=peer, device_id_type=MESH)
-    pl.semaphore_wait(barrier, len(peers))
+    )(*ins, bias, lse, *after)
 
 
 class Exchange:
@@ -512,7 +974,9 @@
 
 
 def expert_forward_kernel(
-    members,
+    grid_shape,
+    gathers,
+    spreads,
     sent_ref,
     slot_col_ref,
     chosen_ref,
@@ -520,19 +984,18 @@
     middle_ref,
     win_ref,
     wout_ref,
-    arrived_ref,
-    comb_ref,
-    out_ref,
-    win_s,
-    wout_s,
-    made_s,
-    returned_s,
-    w_sems,
-    send_sems,
-    recv_sems,
-    back_send_sems,
-    back_recv_sems,
+    *refs,
 ):
+    refs = list(refs)
+    take = refs.pop
+    column_ref = take(0) if gathers else None
+    cotangent_ref, slot_row_ref = (take(0), take(0)) if spreads else (None, None)
+    arrived_ref, comb_ref, out_ref = (take(0) for _ in range(3))
+    full_ref = take(0) if gathers else None
+    spread_out = [take(0) for _ in range(2)] if spreads else []
+    win_s, wout_s, made_s, returned_s, w_sems = (take(0) for _ in range(5))
+    send_sems, recv_sems, back_send_sems, back_recv_sems = (take(0) for _ in range(4))
+    members = grid_shape[1]
     slots = sent_ref.shape[0]
     rows = slots // members
     group = chunk_of(members, rows)
@@ -544,12 +1007,25 @@
     load_out = pltpu.make_async_copy(wout_ref, wout_s, w_sems.at[1])
     load_in.start()
     load_out.start()
-    greet(peers_along_gy(members))
+    place = Place(grid_shape)
+    more_peers = [place.core_peer()] + place.y_peers() if gathers else []
+    greet(peers_along_gy(members) + more_peers)
     there = Exchange(members, rows, sent_ref, arrived_ref, send_sems, recv_sems)
     back = Exchange(members, rows, made_s, returned_s, back_send_sems, back_recv_sems)
     for apart in range(members - 1, 0, -1):
         there.copy(apart).start()
     there.keep_own()
+    if gathers:
+        own_sem, *sems = refs
+        split = (full_ref.shape[4] - tile_rows) // 2
+        own = pltpu.make_async_copy(
+            column_ref, full_ref.at[place.y, place.c, :, place.x], own_sem
+        )
+        own.start()
+        second = gather_second(place, column_ref, full_ref, split, sems)
+        third = gather_third(place, full_ref, split, sems)
+        fourth = gather_core(place, full_ref, sems)
+        start_all(second)
     load_in.wait()
     load_out.wait()
     my_chunk = there.me // group
@@ -574,20 +1050,32 @@
 
     work(0, 1)
     back.keep_own()
-
-    @pl.loop(1, chunks)
+    half = chunks // 2
+
+    @pl.loop(1, half)
     def _(index):
         work(index, 0)
 
+    if gathers:
+        own.wait()
+        wait_all(second)
+        start_all(third)
+
+    @pl.loop(half, chunks)
+    def _(index):
+        work(index, 0)
+
+    if gathers:
+        wait_all(third)
+        start_all(fourth)
     slot_col = slot_col_ref[...]
-    width = arrived_ref.shape[1]
     comb_ref[...] = jnp.zeros_like(comb_ref)
 
     def gather_back(index, first):
         for member in range(first, group):
             back.copy(index * group + member).wait_recv()
-        start = xor_of(my_chunk, index, chunk_bits) * (group * rows)
-        places = lax.broadcasted_iota(jnp.int32, (slot_col.shape[0], group * rows), 1) + start
+        begin = xor_of(my_chunk, index, chunk_bits) * (group * rows)
+        places = lax.broadcasted_iota(jnp.int32, (slot_col.shape[0], group * rows), 1) + begin
         placing = (places == slot_col).astype(f32).astype(bf16)
         comb_ref[...] += dot(placing, returned_s[chunk_rows(index), :])
 
@@ -599,6 +1087,12 @@
 
     gate = jnp.sum(jax.nn.softmax(logits_ref[...], axis=-1) * chosen_ref[...], axis=1, keepdims=True)
     out_ref[...] = middle_ref[...] + gate * comb_ref[...]
+    if spreads:
+        spread_into(
+            cotangent_ref[...].astype(f32), comb_ref, slot_row_ref, chosen_ref, logits_ref, *spread_out
+        )
+    if gathers:
+        wait_all(fourth)
 
     @pl.loop(1, members)
     def _(apart):
@@ -606,40 +1100,57 @@
         back.copy(apart).wait_send()
 
 
-def expert_params(identifier):
-    return pltpu.CompilerParams(
-        vmem_limit_bytes=vmem_bytes, collective_id=identifier, has_side_effects=True
-    )
-
-
-def expert_forward(sent, slot_col, chosen_f, logits, middle, full_in, full_out, members):
-    slots, width = sent.shape
-    outs = (
+def expert_forward(
+    sent, slot_col, chosen_f, logits, middle, full_in, full_out, grid_shape, identifier, column=None, spread_from=None
+):
+    members = grid_shape[1]
+    gathers, spreads = column is not None, spread_from is not None
+    ins = [sent, slot_col, chosen_f, logits, middle, full_in, full_out]
+    in_specs = [vmem_spec] * 5 + [any_spec] * 2
+    outs = [
         jax.ShapeDtypeStruct(sent.shape, bf16),
         jax.ShapeDtypeStruct(middle.shape, f32),
         jax.ShapeDtypeStruct(middle.shape, f32),
-    )
-    ins = (sent, slot_col, chosen_f, logits, middle)
+    ]
+    out_specs = [vmem_spec] * 3
     sems = pltpu.SemaphoreType.DMA((members,))
+    scratch = [
+        pltpu.VMEM(full_in.shape, bf16),
+        pltpu.VMEM(full_out.shape, bf16),
+        pltpu.VMEM(sent.shape, bf16),
+        pltpu.VMEM(sent.shape, bf16),
+        pltpu.SemaphoreType.DMA((2,)),
+        sems,
+        sems,
+        sems,
+        sems,
+    ]
+    if gathers:
+        ins.append(column)
+        in_specs.append(any_spec)
+        half = (grid_shape[0] // 2, 2, grid_shape[1] // 2, 2)
+        outs.append(jax.ShapeDtypeStruct((*half, *column.shape[1:]), bf16))
+        out_specs.append(any_spec)
+        others = pltpu.SemaphoreType.DMA((gather_copies(grid_shape)[1],))
+        scratch += [pltpu.SemaphoreType.DMA, others, others]
+    if spreads:
+        ins += list(spread_from)
+        in_specs += [vmem_spec] * 2
+        outs += [
+            jax.ShapeDtypeStruct(sent.shape, bf16),
+            jax.ShapeDtypeStruct(logits.shape, bf16),
+        ]
+        out_specs += [vmem_spec] * 2
     return pl.pallas_call(
-        partial(expert_forward_kernel, members),
-        in_specs=[vmem_spec] * len(ins) + [any_spec] * 2,
-        out_specs=[vmem_spec] * 3,
+        partial(expert_forward_kernel, grid_shape, gathers, spreads),
+        in_specs=in_specs,
+        out_specs=out_specs,
         out_shape=outs,
-        scratch_shapes=[
-            pltpu.VMEM(full_in.shape, bf16),
-            pltpu.VMEM(full_out.shape, bf16),
-            pltpu.VMEM(sent.shape, bf16),
-            pltpu.VMEM(sent.shape, bf16),
-            pltpu.SemaphoreType.DMA((2,)),
-            sems,
-            sems,
-            sems,
-            sems,
-        ],
-        compiler_params=expert_params(1),
+        scratch_shapes=scratch,
+        compiler_params=params(identifier),
+        cost_estimate=lasting(75),
         name="expert_forward",
-    )(*ins, full_in, full_out)
+    )(*ins)
 
 
 def expert_backward_kernel(
@@ -739,7 +1250,7 @@
         back.copy(apart).wait_send()
 
 
-def expert_backward(d_sent, arrived, full_in, full_out, members):
+def expert_backward(d_sent, arrived, full_in, full_out, members, identifier):
     outs = (
         jax.ShapeDtypeStruct(d_sent.shape, bf16),
         jax.ShapeDtypeStruct(full_in.shape, bf16),
@@ -765,7 +1276,8 @@
             sems,
             sems,
         ],
-        compiler_params=expert_params(2),
+        compiler_params=params(10 + identifier),
+        cost_estimate=lasting(85),
         name="expert_backward",
     )(d_sent, arrived, full_in, full_out)
 
@@ -794,47 +1306,63 @@
     heads = rel_table.shape[1]
     experts = w_router.shape[2] * count_y
     capacity = 2 * seq_len // experts
-    expert_of = route[:, 0]
-    chosen = (expert_of[:, None] == jnp.arange(experts, dtype=jnp.int32)[None, :]).astype(jnp.int32)
-    ranked = jnp.sum((jnp.cumsum(chosen, axis=0) - 1) * chosen, axis=1)
-    slot_of = expert_of * capacity + ranked
-    slot_row, slot_col = slot_of[None, :], slot_of[:, None]
-    chosen_f = chosen.astype(f32)
-    bucket_onehot = (
-        buckets[:, None] == jnp.arange(rel_table.shape[0], dtype=jnp.int32)[None, :]
-    ).astype(f32)
-    bucket_onehot = jnp.pad(bucket_onehot, ((0, 1), (0, 0)))
-    offsets = jnp.dot(bucket_onehot, rel_table.astype(f32), precision=highest).T
-    bias = bias_of(offsets, piece_ids)
+    wide_router = w_router.shape[2]
+    tall, wide = w_query.shape[1], w_query.shape[2]
+    grid_shape = (count_x, count_y)
+    router_rows = jnp.pad(
+        w_router.transpose(0, 2, 1), ((0, 0), (0, tile_rows - wide_router), (0, 4 * wide - tall))
+    )
+    buckets_col = jnp.pad(buckets, (0, 1), constant_values=-1)[:, None]
+    mats, router, later, bias, slot_col, slot_row, chosen_f = start(
+        (w_query, w_key, w_value, w_output),
+        router_rows,
+        buckets_col,
+        rel_table.T,
+        piece_ids,
+        route,
+        grid_shape,
+    )
     gain_attn_f = gain_attn.astype(f32)
     gain_ffn_f = gain_ffn.astype(f32)
 
-    tall, wide = w_query.shape[1], w_query.shape[2]
-
-    grid_shape = (count_x, count_y)
-    tile_rows = 16
-
-    def gather_blocks(layer):
-        packed = jnp.concatenate(
-            [w_query[layer], w_key[layer], w_value[layer], w_output[layer]], axis=1
-        )
-        router_row = jnp.pad(w_router[layer].T, ((0, tile_rows - 1), (0, 4 * wide - tall)))
-        packed = jnp.concatenate([packed, router_row], axis=0)
-        return lax.all_gather(packed, ("gx", "gy"), axis=0, tiled=False)
-
     hidden = hidden_in
     kept = []
+    blocks = None
     for layer in range(layers):
-        blocks = gather_blocks(layer)
+        last = layer == layers - 1
         gains = (gain_attn_f[layer][None], gain_ffn_f[layer][None])
-        mats, router, q, k, v, attended, lse, middle, logits, sent = attention_forward(
-            hidden, gains[0], gains[1], blocks, slot_row, bias, grid_shape, experts
+        (mats, router, q, k, v, attended, lse, middle, logits, sent), column = attention_forward(
+            hidden,
+            gains[0],
+            gains[1],
+            slot_row,
+            bias,
+            grid_shape,
+            1 + layer,
+            blocks=blocks,
+            mats=(mats, router) if blocks is None else None,
+            following=None if last else later[layer],
         )
         full_in = lax.all_gather(w_in[layer, 0], "gx", axis=1, tiled=True)
         full_out = lax.all_gather(w_out[layer, 0], "gx", axis=1, tiled=True)
-        arrived, combined, hidden_next = expert_forward(
-            sent, slot_col, chosen_f, logits, middle, full_in, full_out, count_y
+        got = expert_forward(
+            sent,
+            slot_col,
+            chosen_f,
+            logits,
+            middle,
+            full_in,
+            full_out,
+            grid_shape,
+            5 + layer,
+            column=column,
+            spread_from=(cotangent, slot_row) if last else None,
         )
+        arrived, combined, hidden_next = got[:3]
+        if last:
+            d_sent, d_logits = got[3:]
+        else:
+            blocks = got[3]
         kept.append(
             (hidden, gains, (mats, router), (q, k, v), attended, lse, middle, logits, combined)
             + (arrived, full_in, full_out)
@@ -847,17 +1375,19 @@
     for layer in reversed(range(layers)):
         (prior, gains, mats, q_k_v, attended, lse, middle, logits, combined) = kept[layer][:9]
         (arrived, full_in, full_out) = kept[layer][9:]
-        d_sent, d_logits = spread(grad_now, combined, slot_row, chosen_f, logits)
         d_back, grad_in_full, grad_out_full = expert_backward(
-            d_sent, arrived, full_in, full_out, count_y
+            d_sent, arrived, full_in, full_out, count_y, layer
         )
         grad_out_part = lax.psum_scatter(grad_out_full, "gx", scatter_dimension=1, tiled=True)
         grad_in_part = lax.psum_scatter(grad_in_full, "gx", scatter_dimension=1, tiled=True)
-        grad_now, blocked, gwr, gga, ggf, offset_sums = attention_backward(
+        below = None
+        if layer > 0:
+            below = (kept[layer - 1][8], slot_row, chosen_f, kept[layer - 1][7])
+        got = attention_backward(
             d_back,
             slot_col,
             d_logits,
-            grad_now.astype(f32),
+            grad_now,
             middle,
             prior,
             gains,
@@ -867,31 +1397,39 @@
             bias,
             lse,
             grid_shape,
+            below=below,
+            after=[array for part in parts for array in part[4:6]],
         )
+        grad_now, blocked, gwr, gga, ggf, offset_sums = got[:6]
+        if layer > 0:
+            d_sent, d_logits = got[6:]
         table_sums = offset_sums if table_sums is None else table_sums + offset_sums
-        summed = lax.psum_scatter(blocked, ("gx", "gy"), scatter_dimension=0, tiled=True)[0]
-        summed = summed.astype(f32).reshape(tall, 4, wide)
-        parts.append((summed, gwr, gga, ggf, grad_in_part, grad_out_part))
+        parts.append((blocked, gwr, gga, ggf, grad_in_part, grad_out_part))
     parts = parts[::-1]
+    bucket_onehot = (
+        buckets_col == jnp.arange(rel_table.shape[0], dtype=jnp.int32)[None, :]
+    ).astype(f32)
     d_table = jnp.dot(
         table_sums.reshape(heads, 2 * seq_len), bucket_onehot, precision=highest
     ).T
-    router_sum, d_table, gga_all, ggf_all = lax.psum(
-        (
-            jnp.stack([part[1] for part in parts]),
-            d_table,
-            jnp.concatenate([part[2] for part in parts]),
-            jnp.concatenate([part[3] for part in parts]),
-        ),
-        ("gx", "gy"),
-    )
-    wide_router = w_router.shape[2]
+    buckets_count = rel_table.shape[0]
+    small = jnp.concatenate(
+        [part[1] for part in parts]
+        + [part[2] for part in parts]
+        + [part[3] for part in parts]
+        + [jnp.pad(d_table.reshape(1, -1), ((0, 0), (0, width - d_table.size)))]
+    )
+    small = jnp.pad(small, ((0, -small.shape[0] % 8), (0, 0)))
+    *attn_grads, small = final_sums([part[0] for part in parts], small, grid_shape, wide)
+    router_sum = small[: layers * experts].reshape(layers, experts, width)
+    base = layers * experts
+    gga_all, ggf_all = small[base : base + layers], small[base + layers : base + 2 * layers]
+    d_table = small[base + 2 * layers, : heads * buckets_count].reshape(buckets_count, heads)
     router_mine = lax.dynamic_slice(
         router_sum,
         (0, lax.axis_index("gy") * wide_router, lax.axis_index("gx") * tall),
         (layers, wide_router, tall),
     ).transpose(0, 2, 1)
-    attn_grads = [jnp.stack([part[0][:, index] for part in parts]) for index in range(4)]
     grad_in = jnp.stack([part[4] for part in parts]).astype(f32)[:, None]
     grad_out = jnp.stack([part[5] for part in parts]).astype(f32)[:, None]
     return (

time: 987 us -> 618 us (0.63)
  waiting for transfers between devices: 428 us -> 2.55 us
  Pallas kernels: 455 us -> 567 us
  blocking collectives: 45.1 us -> 0 us
    pallas_call x9 -> x8, Pallas kernels: 286 us -> 418 us  [the longest x2 152 us: expert_forward(): pl.pallas_call(partial(expert_forward_kernel, grid_shape, gathers, spread...]
    reduce_scatter x2, waiting for transfers between devices: 96.7 us -> 0.02 us  [body(): lax.psum_scatter(grad_out_full, 'gx', scatter_dimension=1, tiled=True)]
    reduce_scatter x2, waiting for transfers between devices: 95.4 us -> 0.02 us  [body(): lax.psum_scatter(grad_in_full, 'gx', scatter_dimension=1, tiled=True)]
    all_gather x2, waiting for transfers between devices: 78 us -> 0.04 us  [body(): full_out = lax.all_gather(w_out[layer, 0], 'gx', axis=1, tiled=True)]
    all_gather x2 -> x0, waiting for transfers between devices: 66.6 us -> none  [gather_blocks(): return lax.all_gather(packed, ('gx', 'gy'), axis=0, tiled=False)]
    reduce_scatter x2 -> x0, waiting for transfers between devices: 63.3 us -> none  [body(): lax.psum_scatter(blocked, ('gx', 'gy'), scatter_dimension=0, tiled=True)[0]]
    psum x1 -> x0, blocking collectives: 45.1 us -> none  [body(): lax.psum((jnp.stack([part[1] for part in parts]), d_table, jnp.concatenat...]
    all_gather x2, waiting for transfers between devices: 25 us -> 0.04 us  [body(): full_in = lax.all_gather(w_in[layer, 0], 'gx', axis=1, tiled=True)]
  transfers between devices with their start and end apart: 12 -> 8, of which waited for: 11 -> 0; matrix products, arithmetic and copies ran while one was open for 3% -> 3% of each run, Pallas kernels for 27% -> 68%
where the time goes in v3:
time: 618 us; the launch traced here: 613 us
  Pallas kernels  567 us (92%)
  local copies, waits for them, and re-layouts  19.5 us (3%)
  between operations  14.9 us (2%)
  other arithmetic  8.57 us (1%)
    pallas_call x2, Pallas kernels, expert_forward(): pl.pallas_call(partial(expert_forward_kernel, grid_shape, gathers, spread...  152 us
    pallas_call x2, Pallas kernels, expert_backward(): pl.pallas_call(partial(expert_backward_kernel, members), in_specs=[vmem_s...  149 us
    pallas_call x1, Pallas kernels, final_sums(): pl.pallas_call(partial(final_kernel, grid_shape, layers), in_specs=[vmem_...  85.6 us
    pallas_call x2, Pallas kernels, attention_backward(): pl.pallas_call(partial(backward_kernel, head_dim, grid_shape, spreads, le...  64.6 us
    pallas_call x1, Pallas kernels, start(): pl.pallas_call(partial(start_kernel, grid_shape), in_specs=[vmem_spec] *...  62.4 us
    pallas_call x2, Pallas kernels, attention_forward(): pl.pallas_call(partial(forward_kernel, head_dim, grid_shape, blocked, sen...  53.4 us
  transfers between devices with their start and end apart: 8, of which 0 were waited for; matrix products, arithmetic and copies ran while one was open for 3% of the time, Pallas kernels for 68%

profile of v3, /device:TPU:0, one launch (start us, length us, event | category | flops | bytes accessed | tf_op | source)
XLA Modules:
  0.0 613.0 jit_solution(9245398271519089185)
XLA Ops:
  7.2 0.0 all-gather.9.cloned.1.call-start
  7.2 3.3 fusion.5
  10.6 0.0 all-gather.11.cloned.1.call-start
  10.6 1.6 fusion.4
  12.2 0.0 all-gather.15.cloned.1.call-start
  12.3 0.6 all-gather.15.cloned.1.call-update
  13.0 0.0 all-gather.13.cloned.1.call-start
  13.0 0.5 all-gather.13.cloned.1.call-update
  13.6 0.0 reduce-scatter.7.cloned.1.call-start
  13.6 1.0 copy.31.buckets_ref
  14.7 0.9 copy.32.piece_col_ref
  15.5 0.9 copy.33.route_col_ref
  16.4 0.6 pad.16.router_rows_ref
  17.0 0.6 fusion.7
  17.6 62.4 %start.1 = (bf16[4,768,768]{2,1,0:T(8,128)(2,1)}, bf16[8,768]{1,0:T(8,128)(2,1)}, bf16[1,208,384]{2,1,0:T(8,128)(2,1)}, bf16[12,512,512]{2,1,0:T(8,128)(2,1)}, s...) custom-call(bf16[2,192,96]{2,1,0:T(8,128)(2,1)} %wq_ref.1, bf16[2,192,96]{2,1,0:T(8,128)(2,1)} %wk_ref.1, ...), custom_call_target="tpu_custom_call" | custom-call | flops 44999999488 | bytes 1048576 | tf_op jit(solution)/shard_map/start/pallas_call | solution.py:526
  80.0 27.9 %attention_forward.2 = (bf16[512,768]{1,0:T(8,128)(2,1)}, bf16[512,768]{1,0:T(8,128)(2,1)}, bf16[512,768]{1,0:T(8,128)(2,1)}, bf16[768,512]{1,0:T(8,128)(2,1)}, ...) custom-call(bf16[512,768]{1,0:T(8,128)(2,1)} %hidden_ref.3, ...), custom_call_target="tpu_custom_call" | custom-call | flops 24999999488 | bytes 1048576 | tf_op jit(solution)/shard_map/attention_forward/pallas_call | solution.py:678
  108.0 73.6 %expert_forward.2 = (bf16[1024,768]{1,0:T(8,128)(2,1)}, f32[512,768]{1,0:T(8,128)}, f32[512,768]{1,0:T(8,128)}, bf16[2,2,4,2,208,384]{5,4,3,2,1,0:T(8,128)(2,1)}) custom-call(bf16[1024,768]{1,0:T(8,128)(2,1)} %get-tuple-element.76.sent_ref, s32[512,1]{1,0:T(8,128)} %get-tuple-element.77.slot_col_ref, f32[512,8]{1,0:T(8,128)} %get-tuple-element.78.chosen_ref.refs_2_, ...), custom_call_target="tpu_custom_call" | custom-call | flops 74999996416 | bytes 1048576 | tf_op jit(solution)/shard_map/expert_forward/pallas_call | solution.py:1144
  181.6 25.5 %attention_forward.3 = (bf16[4,768,768]{2,1,0:T(8,128)(2,1)}, bf16[8,768]{1,0:T(8,128)(2,1)}, bf16[512,768]{1,0:T(8,128)(2,1)}, bf16[512,768]{1,0:T(8,128)(2,1)}...) custom-call(f32[512,768]{1,0:T(8,128)} %get-tuple-element.82.hidden_, ...), custom_call_target="tpu_custom_call" | custom-call | flops 24999999488 | bytes 1048576 | tf_op jit(solution)/shard_map/attention_forward/pallas_call | solution.py:678
  207.1 0.0 all-gather.15.cloned.1.call-done
  207.2 78.2 %expert_forward.3 = (bf16[1024,768]{1,0:T(8,128)(2,1)}, f32[512,768]{1,0:T(8,128)}, f32[512,768]{1,0:T(8,128)}, bf16[1024,768]{1,0:T(8,128)(2,1)}, bf16[512,8]{1,0:T(8,128)(2,1)}) custom-call(bf16[1024,768]{1,0:T(8,128)(2,1)} %get-tuple-element.84.sent_ref, s32[512,1]{1,0:T(8,128)} %get-tuple-element.77.slot_col_ref, ...), custom_call_target="tpu_custom_call" | custom-call | flops 74999996416 | bytes 1048576 | tf_op jit(solution)/shard_map/expert_forward/pallas_call | solution.py:1144
  285.4 74.5 %expert_backward.2 = (bf16[1024,768]{1,0:T(8,128)(2,1)}, bf16[768,3072]{1,0:T(8,128)(2,1)}, bf16[768,3072]{1,0:T(8,128)(2,1)}) custom-call(bf16[1024,768]{1,0:T(8,128)(2,1)} %get-tuple-element.88.d_sent_ref, bf16[1024,768]{1,0:T(8,128)(2,1)} %get-tuple-element.89.arrived_ref, bf16[768,3072]{1,0:T(8,128)(2,1)} %bitcast.36, bf16[768,3072]{1,0:T(8,128)(2,1)} %bitcast.34), custom_call_target="tpu_custom_call" | custom-call | flops 85000003584 | bytes 1048576 | tf_op jit(solution)/shard_map/expert_backward/pallas_call | solution.py:1261
  359.9 0.0 reduce-scatter.5.cloned.1.call-start
  359.9 0.5 reduce-scatter.5.cloned.1.call-update
  360.5 0.0 reduce-scatter.11.cloned.1.call-start
  360.5 33.0 %attention_backward.2 = (f32[512,768]{1,0:T(8,128)}, bf16[2,2,4,2,192,384]{5,4,3,2,1,0:T(8,128)(2,1)}, f32[8,768]{1,0:T(8,128)}, f32[1,768]{1,0:T(1,128)}, f32[1...) custom-call(bf16[1024,768]{1,0:T(8,128)(2,1)} %get-tuple-element.90.d_back_ref, ...), custom_call_target="tpu_custom_call" | custom-call | flops 32000000000 | bytes 1048576 | tf_op jit(solution)/shard_map/attention_backward/pallas_call | solution.py:899
  393.5 74.3 %expert_backward.3 = (bf16[1024,768]{1,0:T(8,128)(2,1)}, bf16[768,3072]{1,0:T(8,128)(2,1)}, bf16[768,3072]{1,0:T(8,128)(2,1)}) custom-call(bf16[1024,768]{1,0:T(8,128)(2,1)} %get-tuple-element.100.d_sent_ref, bf16[1024,768]{1,0:T(8,128)(2,1)} %get-tuple-element.101.arrived_ref, bf16[768,3072]{1,0:T(8,128)(2,1)} %bitcast.30, bf16[768,3072]{1,0:T(8,128)(2,1)} %bitcast.32), custom_call_target="tpu_custom_call" | custom-call | flops 85000003584 | bytes 1048576 | tf_op jit(solution)/shard_map/expert_backward/pallas_call | solution.py:1261
  467.8 0.0 reduce-scatter.9.cloned.1.call-start
  467.9 0.7 reduce-scatter.9.cloned.1.call-update
  468.7 31.6 %attention_backward.3 = (f32[512,768]{1,0:T(8,128)}, bf16[2,2,4,2,192,384]{5,4,3,2,1,0:T(8,128)(2,1)}, f32[8,768]{1,0:T(8,128)}, f32[1,768]{1,0:T(1,128)}, f32[1,768]{1,0:T(1,128)}, /*index=5*/f32[6,2,1024]{2,1,0:T(2,128)}) custom-call(bf16[1024,768]{1,0:T(8,128)(2,1)} %get-tuple-element.102.d_back_ref, s32[512,1]{1,0:T(8,128)} %get-tuple-element.77.slot_col_ref, ...), custom_call_target="tpu_custom_call" | custom-call | flops 32000000000 | bytes 1048576 | tf_op jit(solution)/shard_map/attention_backward/pallas_call | solution.py:899
  500.3 0.8 add.25
  501.2 0.6 fusion.1
  501.8 0.1 reshape.101
  502.0 1.5 concatenate.17
  503.4 0.6 pad.19.refs_2_
  504.1 85.6 %final_sums.1 = (f32[2,192,96]{2,1,0:T(8,128)}, f32[2,192,96]{2,1,0:T(8,128)}, f32[2,192,96]{2,1,0:T(8,128)}, f32[2,192,96]{2,1,0:T(8,128)}, f32[24,768]{1,0:T(8,128)}) custom-call(bf16[2,2,4,2,192,384]{5,4,3,2,1,0:T(8,128)(2,1)} %get-tuple-element.113.refs_0_, bf16[2,2,4,2,192,384]{5,4,3,2,1,0:T(8,128)(2,1)} %get-tuple-element.114.refs_1_, ...), custom_call_target="tpu_custom_call" | custom-call | flops 60000002048 | bytes 1048576 | tf_op jit(solution)/shard_map/final_sums/pallas_call | solution.py:367
  589.7 0.7 slice_reduce_fusion
  590.4 0.1 reshape_squeeze.3
  590.5 0.7 copy.35
  591.2 1.4 fusion.6
  592.6 0.8 slice_bitcast_fusion
  593.4 3.9 maximum_convert_fusion.1
  597.3 3.9 maximum_convert_fusion
  601.2 0.7 dynamic-slice_bitcast_fusion
  601.9 1.1 copy.42
  603.0 0.7 copy.43
  603.7 0.7 copy.44
  604.4 0.7 copy.45
  605.1 0.7 copy.46
  (55 shorter events, 0.3 us)
Async XLA Ops:
  7.2 100.8 %all-gather.9.cloned.1.call-start = ((), (), s32[]{:S(2)}) async-start(), calls=%async_computation.8 | async-start | bytes 5898240 | tf_op jit(solution)/shard_map/all_gather | solution.py:1346
  7.2 3.4 copy-start
  10.6 97.4 %all-gather.11.cloned.1.call-start = ((), (), s32[]{:S(2)}) async-start(), calls=%async_computation.9 | async-start | bytes 5898240 | tf_op jit(solution)/shard_map/all_gather | solution.py:1347
  12.2 1.4 copy-start.14
  12.2 2.4 copy-start.17
  12.2 194.9 %all-gather.15.cloned.1.call-start = ((), (), s32[]{:S(2)}) async-start(), calls=%async_computation.11 | async-start | bytes 5898240 | tf_op jit(solution)/shard_map/all_gather | solution.py:1347
  12.3 3.2 copy-start.18
  12.3 4.1 copy-start.19
  12.3 4.7 copy-start.12
  12.3 4.7 copy-start.13
  13.0 194.2 %all-gather.13.cloned.1.call-start = ((), (), s32[]{:S(2)}) async-start(), calls=%async_computation.10 | async-start | bytes 5898240 | tf_op jit(solution)/shard_map/all_gather | solution.py:1346
  13.6 455.1 %reduce-scatter.7.cloned.1.call-start = ((), (), s32[]{:S(2)}) async-start(), calls=%async_computation.5 | async-start | bytes 5898240 | tf_op jit(solution)/shard_map/reduce_scatter | solution.py:1381
  13.6 66.4 %copy-start.10 = (s32[1024]{0:T(1024)}, s32[1024]{0:T(1024)S(1)}, u32[]{:S(2)}) copy-start(s32[1024]{0:T(1024)S(1)} %pad.17) | copy-start | bytes 12292
  359.9 108.7 %reduce-scatter.5.cloned.1.call-start = ((), (), s32[]{:S(2)}) async-start(), calls=%async_computation.4 | async-start | bytes 5898240 | tf_op jit(solution)/shard_map/reduce_scatter | solution.py:1382
  360.5 233.0 %reduce-scatter.11.cloned.1.call-start = ((), (), s32[]{:S(2)}) async-start(), calls=%async_computation.7 | async-start | bytes 5898240 | tf_op jit(solution)/shard_map/reduce_scatter | solution.py:1381
  467.8 129.5 %reduce-scatter.9.cloned.1.call-start = ((), (), s32[]{:S(2)}) async-start(), calls=%async_computation.6 | async-start | bytes 5898240 | tf_op jit(solution)/shard_map/reduce_scatter | solution.py:1382
  468.7 31.7 %copy-start.8 = (f32[6,2,1024]{2,1,0:T(2,128)S(1)}, f32[6,2,1024]{2,1,0:T(2,128)}, u32[]{:S(2)}) copy-start(f32[6,2,1024]{2,1,0:T(2,128)} %get-tuple-element.121) | copy-start | bytes 147460
  468.7 32.5 %copy-start.11 = (s32[1024]{0:T(1024)S(1)}, s32[1024]{0:T(1024)}, u32[]{:S(2)}) copy-start(s32[1024]{0:T(1024)} %copy-done.10) | copy-start | bytes 12292
  468.7 33.3 %copy-start.9 = (f32[8,768]{1,0:T(8,128)S(1)}, f32[8,768]{1,0:T(8,128)}, u32[]{:S(2)}) copy-start(f32[8,768]{1,0:T(8,128)} %get-tuple-element.116) | copy-start | bytes 73732
  468.7 33.2 %copy-start.15 = (f32[1,768]{1,0:T(1,128)S(1)}, f32[1,768]{1,0:T(1,128)}, u32[]{:S(2)}) copy-start(f32[1,768]{1,0:T(1,128)} %get-tuple-element.118) | copy-start | bytes 9220
  468.7 33.2 %copy-start.16 = (f32[1,768]{1,0:T(1,128)S(1)}, f32[1,768]{1,0:T(1,128)}, u32[]{:S(2)}) copy-start(f32[1,768]{1,0:T(1,128)} %get-tuple-element.120) | copy-start | bytes 9220
  504.1 89.4 %copy-start.2 = (bf16[768,768]{1,0:T(8,128)(2,1)S(1)}, bf16[768,768]{1,0:T(8,128)(2,1)}, u32[]{:S(2)}) copy-start(bf16[768,768]{1,0:T(8,128)(2,1)} %reduce-scatter.7.cloned.1.call-done.refs_3_) | copy-start | bytes 3538948
  593.4 3.9 copy-start.3
  597.3 4.5 copy-start.1
  601.8 1.2 copy-start.7
  601.9 1.8 copy-start.6
  601.9 2.5 copy-start.5
  601.9 3.2 copy-start.4
Sparse Core Ops, SparseCore 0:
  10.7 50.0 all-gather.8
  62.9 38.4 all-gather.10
  103.0 56.2 all-gather.14
  161.3 37.3 all-gather.12
  360.0 49.4 reduce-scatter.6
  412.1 47.8 reduce-scatter.4
  468.0 49.0 reduce-scatter.10
  519.7 65.3 reduce-scatter.8

commit v4 on v3

--- a/solution.py
+++ b/solution.py
@@ -317,66 +317,121 @@
     return bits_of(grid_shape[0]) + bits_of(grid_shape[1])
 
 
-def final_kernel(grid_shape, layers, *refs):
+def final_kernel(grid_shape, layers, buckets_count, *refs):
     refs = list(refs)
     take = refs.pop
-    blocks = [take(0) for _ in range(layers)]
-    small_ref = take(0)
+    blocks_ref = take(0)
+    partial_refs = [(take(0), take(0)) for _ in range(layers - 1)]
+    router_refs, gga_refs, ggf_refs, offset_refs = ([take(0) for _ in range(layers)] for _ in range(4))
+    buckets_ref, slot_col_ref, chosen_ref, logits_ref, middle_ref = (take(0) for _ in range(5))
+    first_ref, second_ref = take(0), take(0)
     outs = [take(0) for _ in range(4)]
-    small_out_ref = take(0)
-    landings = [[take(0) for _ in range(7)] for _ in range(layers)]
-    totals, landing = take(0), take(0)
+    small_out_ref, result_ref = take(0), take(0)
+    landings = [take(0) for _ in range(7)]
+    z_landings = [(take(0), take(0)) for _ in range(layers - 1)]
+    totals, landing, returned_s = take(0), take(0), take(0)
     sems = [(take(0), take(0)) for _ in range(layers)]
-    small_sems = (take(0), take(0))
+    small_sems, collect_sems = (take(0), take(0)), take(0)
     place = Place(grid_shape)
     tall, wide = outs[0].shape[1:]
     split = tall // 2
-    sums = [Scatter(place, blocks[l], landings[l], sems[l], split) for l in range(layers)][::-1]
+    members = grid_shape[1]
+    slots = returned_s.shape[0]
+    upper_layers = []
+    for layer in range(1, layers):
+        upper, lower = partial_refs[layer - 1]
+        places = (None, None, None, upper, lower, *z_landings[layer - 1])
+        upper_layers.append(Scatter(place, blocks_ref, places, sems[layer], split))
+    lowest = Scatter(place, blocks_ref, landings, sems[0], split)
+    collected = collect(
+        lax.axis_index("gy"), members, slots // members, first_ref, second_ref, returned_s, collect_sems
+    )
+    start_all(collected)
+    greet([place.core_peer(), place.x_peer()] + place.y_peers() + place.z_peers())
+    start_all(lowest.copies(0))
+    for one in upper_layers:
+        start_all(one.copies(3))
+
+    experts = router_refs[0].shape[0]
+    totals[0] = jnp.zeros(totals.shape[1:], f32)
+    row = 0
+    for refs_of in (router_refs, gga_refs, ggf_refs):
+        for ref in refs_of:
+            totals[0, row : row + ref.shape[0], :] = ref[...]
+            row += ref.shape[0]
+    heads = offset_refs[0].shape[0]
+    offsets = offset_refs[0][...]
+    for ref in offset_refs[1:]:
+        offsets = offsets + ref[...]
+    in_bucket = (
+        lax.broadcasted_iota(jnp.int32, (buckets_count, offsets.shape[1]), 0) == buckets_ref[...]
+    ).astype(f32)
+    totals[0, row : row + heads, :buckets_count] = lax.dot_general(
+        offsets, in_bucket, (((1,), (1,)), ((), ())), precision=highest, preferred_element_type=f32
+    )
     small = SmallSum(grid_shape, totals, landing, small_sems)
-    totals[0] = small_ref[...]
-    greet([place.core_peer(), place.x_peer()] + place.y_peers() + place.z_peers())
     small.begin()
-    for one in sums:
-        start_all(one.copies(0))
-    for stage in range(4):
-        for one in sums:
-            small.advance()
-            wait_all(one.copies(stage))
-            if stage < 3:
-                one.add(stage)
-                start_all(one.copies(stage + 1))
+    wait_all(lowest.copies(0))
+    lowest.add(0)
+    start_all(lowest.copies(1))
+    small.advance()
+    wait_all(collected)
+    placing = placing_cols(slot_col_ref[...], slots)
+    gate = jnp.sum(jax.nn.softmax(logits_ref[...], axis=-1) * chosen_ref[...], axis=1, keepdims=True)
+    result_ref[...] = middle_ref[...] + gate * dot(placing, returned_s[...])
+    small.advance()
+    wait_all(lowest.copies(1))
+    lowest.add(1)
+    start_all(lowest.copies(2))
+    small.advance()
+
+    def finish(layer, one):
+        for part, rows in zip(one.result(), (slice(0, split), slice(split, tall))):
+            for which in range(4):
+                outs[which][layer, rows, :] = part[:, which * wide : (which + 1) * wide]
+
+    for layer, one in enumerate(upper_layers):
+        wait_all(one.copies(3))
+        finish(layer + 1, one)
+    wait_all(lowest.copies(2))
+    lowest.add(2)
+    start_all(lowest.copies(3))
     while small.done < len(small.peers):
         small.advance()
     small_out_ref[...] = totals[len(small.peers)]
-    for layer, one in enumerate(sums[::-1]):
-        for part, rows in zip(one.result(), (slice(0, split), slice(split, tall))):
-            for which in range(4):
-                outs[which][layer, rows, :] = part[:, which * wide : (which + 1) * wide]
-
-
-def final_sums(blocks, small, grid_shape, wide):
-    layers = len(blocks)
-    shape = blocks[0].shape
+    wait_all(lowest.copies(3))
+    finish(0, lowest)
+
+
+def final_sums(blocks, partials, smalls, finishing, returned, grid_shape, wide, buckets_count):
+    layers = len(partials) + 1
+    shape = blocks.shape
     tall = shape[4]
+    width = finishing[-1].shape[1]
     landings = [pltpu.VMEM(one, bf16) for one in whole_blocks(shape, tall // 2)]
     steps = small_steps(grid_shape)
+    rows = sum(one.shape[0] for one in smalls[: 3 * layers]) + smalls[3 * layers].shape[0]
+    small_shape = (rows + -rows % 8, width)
     sems = pltpu.SemaphoreType.DMA((scatter_copies(grid_shape),))
     small_sems = pltpu.SemaphoreType.DMA((steps,))
     outs = [jax.ShapeDtypeStruct((layers, tall, wide), f32)] * 4
-    outs.append(jax.ShapeDtypeStruct(small.shape, f32))
+    outs += [jax.ShapeDtypeStruct(small_shape, f32), jax.ShapeDtypeStruct(finishing[-1].shape, f32)]
+    ins = [blocks, *[array for pair in partials for array in pair], *smalls, *finishing]
     return pl.pallas_call(
-        partial(final_kernel, grid_shape, layers),
-        in_specs=[vmem_spec] * (layers + 1),
+        partial(final_kernel, grid_shape, layers, buckets_count),
+        in_specs=[vmem_spec] * len(ins) + [any_spec] * 2,
         out_specs=[vmem_spec] * len(outs),
         out_shape=outs,
-        scratch_shapes=landings * layers
-        + [pltpu.VMEM((steps + 1, *small.shape), f32), pltpu.VMEM((steps, *small.shape), f32)]
+        scratch_shapes=landings
+        + landings[5:] * (layers - 1)
+        + [pltpu.VMEM((steps + 1, *small_shape), f32), pltpu.VMEM((steps, *small_shape), f32)]
+        + [pltpu.VMEM(returned[0].shape, bf16)]
         + [sems, sems] * layers
-        + [small_sems, small_sems],
-        compiler_params=params(20),
+        + [small_sems, small_sems, pltpu.SemaphoreType.DMA((grid_shape[1],))],
+        compiler_params=params(24),
         cost_estimate=lasting(60),
         name="final_sums",
-    )(*blocks, small)
+    )(*ins, *returned)
 
 
 def unblock(grid_shape, blocks_ref, mats_ref, router_ref):
@@ -401,6 +456,10 @@
     router_ref[...] = jnp.concatenate(router_rows, axis=1)
 
 
+def turned(row):
+    return jnp.broadcast_to(row, (128, row.shape[1])).T[:, 0:1]
+
+
 def start_kernel(
     grid_shape,
     wq_ref,
@@ -410,10 +469,9 @@
     router_rows_ref,
     buckets_ref,
     table_ref,
-    piece_col_ref,
     piece_row_ref,
-    route_col_ref,
     route_row_ref,
+    cotangent_ref,
     mats_ref,
     router_ref,
     later_ref,
@@ -421,8 +479,11 @@
     slot_col_ref,
     slot_row_ref,
     chosen_ref,
+    spread_ref,
     full_s,
     column_s,
+    later_send,
+    later_recv,
     z_send,
     z_recv,
     send_sems,
@@ -441,41 +502,25 @@
     greet([place.core_peer(), place.x_peer()] + place.y_peers() + place.z_peers())
     first = gather_z(place, column_s.at[z], column_s.at[z], (z_send, z_recv))
     start_all(first)
+    along_z = []
     for layer in range(1, layers):
-        later_ref[layer - 1, :tall] = packed(layer)
-        later_ref[layer - 1, tall:] = router_rows_ref[layer]
+        later_ref[layer - 1, z, :tall] = packed(layer)
+        later_ref[layer - 1, z, tall:] = router_rows_ref[layer]
+        mine = later_ref.at[layer - 1, z]
+        along_z += gather_z(place, mine, mine, (later_send.at[layer - 1], later_recv.at[layer - 1]))
 
     seq_len, experts = chosen_ref.shape
     capacity = 2 * seq_len // experts
     heads = bias_ref.shape[0]
-    buckets_all = buckets_ref[...]
-    in_bucket = lax.broadcasted_iota(jnp.int32, (2 * seq_len, table_ref.shape[1]), 1) == buckets_all
-    offsets = dot(table_ref[...], in_bucket.astype(f32).astype(bf16), 1, 1)
+    buckets_count = table_ref.shape[1]
+    in_bucket = (
+        lax.broadcasted_iota(jnp.int32, (buckets_count, 2 * seq_len), 0) == buckets_ref[...]
+    )
+    offsets = dot(table_ref[...], in_bucket.astype(f32).astype(bf16))
     key_pos = lax.broadcasted_iota(jnp.int32, (seq_len, seq_len), 0)
     query_pos = lax.broadcasted_iota(jnp.int32, (seq_len, seq_len), 1)
-    piece_col = piece_col_ref[...]
-    same = (piece_col == piece_row_ref[...]) & (piece_col > 0)
-    allowed = (key_pos <= query_pos) | same
-
-    def bias_for(head):
-        row = jnp.broadcast_to(offsets[head : head + 1], (seq_len, 2 * seq_len))
-        shifted = pltpu.roll(row, seq_len + 1, 1, stride=1, stride_axis=0)[:, :seq_len]
-        bias_ref[head] = jnp.where(allowed, shifted, masked_out).astype(bf16)
-
-    for head in range(heads // 2):
-        bias_for(head)
-    wait_all(first)
-    sems = (send_sems, recv_sems)
-    second = gather_second(place, column_s, full_s, split, sems)
-    start_all(second)
-    full_s[y, c, :, x] = column_s[...]
-    for head in range(heads // 2, heads):
-        bias_for(head)
-    wait_all(second)
-    third = gather_third(place, full_s, split, sems)
-    start_all(third)
-
-    route_col, route_row = route_col_ref[...], route_row_ref[...]
+    route_row, piece_row = route_row_ref[...], piece_row_ref[...]
+    route_col, piece_col = turned(route_row), turned(piece_row)
     chosen = (lax.broadcasted_iota(jnp.int32, (seq_len, experts), 1) == route_col).astype(f32)
     chosen_t = (lax.broadcasted_iota(jnp.int32, (experts, seq_len), 0) == route_row).astype(f32)
     chosen_ref[...] = chosen
@@ -487,15 +532,40 @@
     before = dot(later, chosen.astype(bf16))
     rank_col = jnp.sum(before * chosen, axis=1, keepdims=True)
     slot_col_ref[...] = route_col * capacity + rank_col.astype(jnp.int32)
+    placing = placing_rows(slot_row_ref[...], spread_ref.shape[0])
+    spread_ref[...] = dot(placing, cotangent_ref[...]).astype(bf16)
+
+    same = (piece_col == piece_row) & (piece_col > 0)
+    allowed = (key_pos <= query_pos) | same
+
+    def bias_for(head):
+        row = jnp.broadcast_to(offsets[head : head + 1], (seq_len, 2 * seq_len))
+        shifted = pltpu.roll(row, seq_len + 1, 1, stride=1, stride_axis=0)[:, :seq_len]
+        bias_ref[head] = jnp.where(allowed, shifted, masked_out).astype(bf16)
+
+    for head in range(heads // 2):
+        bias_for(head)
+    wait_all(first)
+    sems = (send_sems, recv_sems)
+    second = gather_second(place, column_s, full_s, split, sems)
+    start_all(second)
+    start_all(along_z)
+    full_s[y, c, :, x] = column_s[...]
+    for head in range(heads // 2, heads):
+        bias_for(head)
+    wait_all(second)
+    third = gather_third(place, full_s, split, sems)
+    start_all(third)
 
     wait_all(third)
     fourth = gather_core(place, full_s, sems)
     start_all(fourth)
     wait_all(fourth)
     unblock(grid_shape, full_s, mats_ref, router_ref)
-
-
-def start(mats, router_rows, buckets, table_t, piece_ids, route, grid_shape):
+    wait_all(along_z)
+
+
+def start(mats, router_rows, buckets, table_t, piece_ids, route, cotangent, grid_shape):
     layers, tall, wide = mats[0].shape
     seq_len = piece_ids.shape[0]
     heads = table_t.shape[0]
@@ -508,19 +578,19 @@
         router_rows,
         buckets,
         table_t,
-        piece_ids[:, None],
         piece_ids[None, :],
-        route,
         route.reshape(1, seq_len),
+        cotangent,
     )
     outs = (
         jax.ShapeDtypeStruct((4, width, width), bf16),
         jax.ShapeDtypeStruct((experts, width), bf16),
-        jax.ShapeDtypeStruct((layers - 1, *block), bf16),
+        jax.ShapeDtypeStruct((layers - 1, half[2], *block), bf16),
         jax.ShapeDtypeStruct((heads, seq_len, seq_len), bf16),
         jax.ShapeDtypeStruct((seq_len, 1), jnp.int32),
         jax.ShapeDtypeStruct((1, seq_len), jnp.int32),
         jax.ShapeDtypeStruct((seq_len, experts), f32),
+        jax.ShapeDtypeStruct((2 * seq_len, width), bf16),
     )
     along_z, others = gather_copies(grid_shape)
     return pl.pallas_call(
@@ -531,6 +601,8 @@
         scratch_shapes=[
             pltpu.VMEM((*half, *block), bf16),
             pltpu.VMEM((half[2], *block), bf16),
+            pltpu.SemaphoreType.DMA((layers - 1, along_z)),
+            pltpu.SemaphoreType.DMA((layers - 1, along_z)),
             pltpu.SemaphoreType.DMA((along_z,)),
             pltpu.SemaphoreType.DMA((along_z,)),
             pltpu.SemaphoreType.DMA((others,)),
@@ -547,44 +619,64 @@
     return lane < (width // 2)
 
 
+def gates_of(logits, slot_col, chosen, gates_ref):
+    experts = gates_ref.shape[0]
+    seq_len = slot_col.shape[0]
+    capacity = 2 * seq_len // experts
+    gate = jnp.sum(jax.nn.softmax(logits, axis=-1) * chosen, axis=1, keepdims=True)
+    places = lax.broadcasted_iota(jnp.int32, (seq_len, 2 * seq_len), 1)
+    row = jnp.sum(jnp.where(places == slot_col, gate, 0.0), axis=0, keepdims=True)
+    gates_ref[...] = jnp.zeros_like(gates_ref)
+    for expert in range(experts):
+        mine = row[:, expert * capacity : (expert + 1) * capacity]
+        gates_ref[expert, :, :capacity] = jnp.broadcast_to(mine, (gates_ref.shape[1], capacity))
+
+
 def forward_kernel(
     head_dim,
     grid_shape,
     blocked,
-    sends,
+    last,
     hidden_ref,
     gain_attn_ref,
     gain_ffn_ref,
     slot_row_ref,
+    slot_col_ref,
+    chosen_ref,
     *refs,
 ):
     refs = list(refs)
     take = refs.pop
     blocks_ref = take(0) if blocked else None
     mats_ref, router_ref = (None, None) if blocked else (take(0), take(0))
-    next_ref = take(0) if sends else None
+    spread_ref = take(0)
     bias_ref = take(0)
     if blocked:
         mats_ref, router_ref = take(0), take(0)
     q_ref, k_ref, v_ref, att_ref, lse_ref, middle_ref, logits_ref, sent_ref = (
         take(0) for _ in range(8)
     )
+    gates_ref = take(0) if last else None
+    far_ref, send_sems, recv_sems, own_sem = refs
     pair, pairs = pl.program_id(0), pl.num_programs(0)
     seq_len = hidden_ref.shape[0]
     width = 2 * head_dim
     step = min(256, seq_len)
 
-    if sends:
-        column_ref, z_send, z_recv, own_sem = refs
-        place = Place(grid_shape)
-        own = pltpu.make_async_copy(next_ref, column_ref.at[place.z], own_sem)
-        copies = gather_z(place, next_ref, column_ref.at[place.z], (z_send, z_recv))
-
-        @pl.when(pair == 0)
-        def _():
-            greet(place.z_peers())
+    members = grid_shape[1]
+    spread = Exchange(members, spread_ref.shape[0] // members, spread_ref, far_ref, send_sems, recv_sems)
+    mine = spread.block(spread.me)
+    own = None
+    if not last:
+        own = pltpu.make_async_copy(spread_ref.at[mine, :], far_ref.at[mine, :], own_sem)
+    aparts = part_of(members, not last)
+
+    @pl.when(pair == 0)
+    def _():
+        greet([spread.peer(apart) for apart in aparts])
+        start_all([spread.copy(apart) for apart in aparts])
+        if not last:
             own.start()
-            start_all(copies)
 
     @pl.when(pair == 0)
     def _():
@@ -620,32 +712,43 @@
         middle = hidden_ref[...].astype(f32) + dot(att_ref[...].T, mats_ref[3])
         middle_ref[...] = middle
         ffn_in = (middle * rms_factor(middle) * gain_ffn_ref[...]).astype(bf16)
-        logits_ref[...] = dot(ffn_in, router_ref[...], 1, 1)
+        logits = dot(ffn_in, router_ref[...], 1, 1)
+        logits_ref[...] = logits
+        if gates_ref is not None:
+            gates_of(logits, slot_col_ref[...], chosen_ref[...], gates_ref)
         placing = placing_rows(slot_row_ref[...], sent_ref.shape[0])
         sent_ref[...] = dot(placing, ffn_in).astype(bf16)
 
-    if sends:
-
-        @pl.when(pair == pairs - 1)
-        def _():
+    @pl.when(pair == pairs - 1)
+    def _():
+        wait_all([spread.copy(apart) for apart in aparts])
+        if not last:
             own.wait()
-            wait_all(copies)
 
 
 def attention_forward(
-    hidden, gain_attn, gain_ffn, slot_row, bias, grid_shape, identifier, blocks=None, mats=None, following=None
+    hidden,
+    gain_attn,
+    gain_ffn,
+    slots_and_chosen,
+    bias,
+    grid_shape,
+    identifier,
+    spread,
+    last,
+    blocks=None,
+    mats=None,
 ):
     seq_len, width = hidden.shape
     heads = bias.shape[0]
     head_dim = width // heads
     slots = 2 * seq_len
     experts = grid_shape[1]
-    blocked, sends = blocks is not None, following is not None
-    ins = [hidden, gain_attn, gain_ffn, slot_row] + ([blocks] if blocked else list(mats))
+    blocked = blocks is not None
+    ins = [hidden, gain_attn, gain_ffn, *slots_and_chosen] + ([blocks] if blocked else list(mats))
     in_specs = whole_of(ins)
-    if sends:
-        ins.append(following)
-        in_specs.append(any_spec)
+    ins.append(spread)
+    in_specs.append(any_spec)
     ins.append(bias)
     in_specs.append(pl.BlockSpec((2, seq_len, seq_len), lambda p: (p, 0, 0)))
     tall = jax.ShapeDtypeStruct((seq_len, width), bf16)
@@ -659,6 +762,8 @@
         jax.ShapeDtypeStruct((seq_len, experts), f32),
         jax.ShapeDtypeStruct((slots, width), bf16),
     ]
+    if last:
+        outs.append(jax.ShapeDtypeStruct((experts, 8, max(128, slots // experts)), f32))
     out_specs = whole_of(outs)
     out_specs[4] = pl.BlockSpec((1, 2, seq_len), lambda p: (p, 0, 0))
     if blocked:
@@ -668,27 +773,22 @@
         ]
         outs = more + outs
         out_specs = whole_of(more) + out_specs
-    scratch = []
-    if sends:
-        along_z = grid_shape[1] // 2
-        outs.append(jax.ShapeDtypeStruct((along_z, *following.shape), bf16))
-        out_specs.append(any_spec)
-        sems = pltpu.SemaphoreType.DMA((along_z - 1,))
-        scratch = [sems, sems, pltpu.SemaphoreType.DMA]
+    outs.append(jax.ShapeDtypeStruct(spread.shape, bf16))
+    out_specs.append(any_spec)
+    sems = pltpu.SemaphoreType.DMA((experts,))
+    scratch = [sems, sems, pltpu.SemaphoreType.DMA]
     got = pl.pallas_call(
-        partial(forward_kernel, head_dim, grid_shape, blocked, sends),
+        partial(forward_kernel, head_dim, grid_shape, blocked, last),
         grid=(heads // 2,),
         in_specs=in_specs,
         out_specs=out_specs,
         out_shape=outs,
         scratch_shapes=scratch,
-        compiler_params=params(identifier if sends else None),
+        compiler_params=params(identifier),
         cost_estimate=lasting(25),
         name="attention_forward",
     )(*ins)
-    column = got[-1] if sends else None
-    got = got[:-1] if sends else got
-    return (tuple(mats) + tuple(got) if not blocked else tuple(got)), column
+    return tuple(got) if blocked else tuple(mats) + tuple(got)
 
 
 def diagonal_fold(values, seq_len):
@@ -728,12 +828,17 @@
             ]
 
 
+def d_logits_of(d_gate, logits, chosen):
+    shares = jax.nn.softmax(logits, axis=-1)
+    gate = jnp.sum(shares * chosen, axis=1, keepdims=True)
+    return (d_gate * shares * (chosen - gate)).astype(bf16)
+
+
 def spread_into(grad_now, comb_ref, slot_row_ref, chosen_ref, logits_ref, d_sent_ref, d_logits_ref):
     d_gate = jnp.sum(grad_now * comb_ref[...], axis=1, keepdims=True)
-    shares = jax.nn.softmax(logits_ref[...], axis=-1)
-    chosen = chosen_ref[...]
-    gate = jnp.sum(shares * chosen, axis=1, keepdims=True)
-    d_logits_ref[...] = (d_gate * shares * (chosen - gate)).astype(bf16)
+    logits, chosen = logits_ref[...], chosen_ref[...]
+    d_logits_ref[...] = d_logits_of(d_gate, logits, chosen)
+    gate = jnp.sum(jax.nn.softmax(logits, axis=-1) * chosen, axis=1, keepdims=True)
     placing = placing_rows(slot_row_ref[...], d_sent_ref.shape[0])
     d_sent_ref[...] = dot(placing, (gate * grad_now).astype(bf16)).astype(bf16)
 
@@ -742,6 +847,7 @@
     head_dim,
     grid_shape,
     spreads,
+    returns,
     unread,
     d_back_ref,
     slot_col_ref,
@@ -763,10 +869,28 @@
     take = refs.pop
     spread_in = [take(0) for _ in range(4)] if spreads else []
     bias_ref, lse_ref = take(0), take(0)
+    made_ref = take(0)
     del refs[:unread]
     grad_new_ref, blocks_ref, gwr_ref, gga_ref, ggf_ref, offsets_ref = (take(0) for _ in range(6))
     spread_out = [take(0) for _ in range(2)] if spreads else []
-    d_att_s, d_middle_s, dqt_s, dk_s, dv_s, probs_s, scores_s = refs
+    returned_ref = take(0)
+    d_att_s, d_middle_s, dqt_s, dk_s, dv_s, probs_s, scores_s = (take(0) for _ in range(7))
+    own_sem, *sems = refs
+    members = grid_shape[1]
+    back = Exchange(members, made_ref.shape[0] // members, made_ref, returned_ref, *sems)
+    mine = back.block(back.me)
+    own = None
+    if returns:
+        own = pltpu.make_async_copy(made_ref.at[mine, :], returned_ref.at[mine, :], own_sem)
+    aparts = part_of(members, returns)
+
+    @pl.when(pl.program_id(0) == 0)
+    def _():
+        greet([back.peer(apart) for apart in aparts])
+        start_all([back.copy(apart) for apart in aparts])
+        if returns:
+            own.start()
+
     pair, pairs = pl.program_id(0), pl.num_programs(0)
     seq_len = hidden_ref.shape[0]
     width = 2 * head_dim
@@ -840,6 +964,12 @@
         if spreads:
             spread_into(grad_new, *spread_in, *spread_out)
 
+    @pl.when(pair == pairs - 1)
+    def _():
+        wait_all([back.copy(apart) for apart in aparts])
+        if returns:
+            own.wait()
+
 
 def attention_backward(
     d_back,
@@ -857,6 +987,9 @@
     grid_shape,
     below=None,
     after=(),
+    made=None,
+    returns=False,
+    identifier=None,
 ):
     seq_len, width = hidden.shape
     heads = bias.shape[0]
@@ -894,17 +1027,19 @@
             jax.ShapeDtypeStruct((2 * seq_len, width), bf16),
             jax.ShapeDtypeStruct(d_logits.shape, bf16),
         )
+    outs = outs + (jax.ShapeDtypeStruct(made.shape, bf16),)
     out_specs = whole_of(outs)
+    out_specs[-1] = any_spec
     out_specs[5] = pl.BlockSpec((1, 2, 2 * seq_len), lambda p: (p, 0, 0))
     return pl.pallas_call(
-        partial(backward_kernel, head_dim, grid_shape, spreads, len(after)),
+        partial(backward_kernel, head_dim, grid_shape, spreads, returns, len(after)),
         grid=(heads // 2,),
         in_specs=whole_of(ins)
         + [
             pl.BlockSpec((2, seq_len, seq_len), lambda p: (p, 0, 0)),
             pl.BlockSpec((1, 2, seq_len), lambda p: (p, 0, 0)),
         ]
-        + [any_spec] * len(after),
+        + [any_spec] * (len(after) + 1),
         out_specs=out_specs,
         out_shape=outs,
         scratch_shapes=[
@@ -915,11 +1050,13 @@
             pltpu.VMEM((seq_len, width), bf16),
             pltpu.VMEM((seq_len, seq_len), bf16),
             pltpu.VMEM((seq_len, seq_len), bf16),
-        ],
-        compiler_params=params(),
+        ]
+        + [pltpu.SemaphoreType.DMA]
+        + [pltpu.SemaphoreType.DMA((count_y,))] * 2,
+        compiler_params=params(identifier),
         cost_estimate=lasting(32),
         name="attention_backward",
-    )(*ins, bias, lse, *after)
+    )(*ins, bias, lse, made, *after)
 
 
 class Exchange:
@@ -931,6 +1068,9 @@
 
     def block(self, index):
         return pl.ds(pl.multiple_of(index * self.rows, self.rows), self.rows)
+
+    def peer(self, apart):
+        return {"gy": xor_of(self.me, apart, self.bits)}
 
     def copy(self, apart):
         peer = xor_of(self.me, apart, self.bits)
@@ -947,6 +1087,19 @@
         self.dst[self.block(self.me), :] = self.src[self.block(self.me), :]
 
 
+class Leading(Exchange):
+    def __init__(self, members, src, dst, send_sems, recv_sems):
+        super().__init__(members, 1, src, dst, send_sems, recv_sems)
+
+    def copy(self, apart):
+        peer = xor_of(self.me, apart, self.bits)
+        sems = (self.send_sems, self.recv_sems)
+        return send(self.src.at[peer], self.dst.at[self.me], sems, apart, {"gy": peer})
+
+    def keep_own(self):
+        self.dst[self.me] = self.src[self.me]
+
+
 def peers_along_gy(members):
     me = lax.axis_index("gy")
     bits = members.bit_length() - 1
@@ -969,6 +1122,30 @@
     return 0.5 * pre * (1.0 + jnp.tanh(inner_scale * pre * (1.0 + 0.044715 * pre * pre)))
 
 
+def send_order(members):
+    return range(1, members)
+
+
+def early(members):
+    quarter = max(1, members // 4)
+    return [apart for apart in range(members) if (apart // quarter) % 2 == 0]
+
+
+def part_of(members, first):
+    chosen = early(members)
+    return [a for a in range(1, members) if (a in chosen) == first]
+
+
+def collect(me, members, rows, first_ref, second_ref, dst, sems):
+    copies = []
+    for apart in range(members):
+        start = xor_of(me, apart, bits_of(members)) * rows
+        here = pl.ds(pl.multiple_of(start, rows), rows)
+        ref = first_ref if apart in early(members) else second_ref
+        copies.append(pltpu.make_async_copy(ref.at[here, :], dst.at[here, :], sems.at[apart]))
+    return copies
+
+
 def chunk_of(members, rows):
     return max(1, min(members, 256 // rows))
 
@@ -976,7 +1153,6 @@
 def expert_forward_kernel(
     grid_shape,
     gathers,
-    spreads,
     sent_ref,
     slot_col_ref,
     chosen_ref,
@@ -989,10 +1165,8 @@
     refs = list(refs)
     take = refs.pop
     column_ref = take(0) if gathers else None
-    cotangent_ref, slot_row_ref = (take(0), take(0)) if spreads else (None, None)
     arrived_ref, comb_ref, out_ref = (take(0) for _ in range(3))
     full_ref = take(0) if gathers else None
-    spread_out = [take(0) for _ in range(2)] if spreads else []
     win_s, wout_s, made_s, returned_s, w_sems = (take(0) for _ in range(5))
     send_sems, recv_sems, back_send_sems, back_recv_sems = (take(0) for _ in range(4))
     members = grid_shape[1]
@@ -1012,7 +1186,7 @@
     greet(peers_along_gy(members) + more_peers)
     there = Exchange(members, rows, sent_ref, arrived_ref, send_sems, recv_sems)
     back = Exchange(members, rows, made_s, returned_s, back_send_sems, back_recv_sems)
-    for apart in range(members - 1, 0, -1):
+    for apart in send_order(members):
         there.copy(apart).start()
     there.keep_own()
     if gathers:
@@ -1087,10 +1261,6 @@
 
     gate = jnp.sum(jax.nn.softmax(logits_ref[...], axis=-1) * chosen_ref[...], axis=1, keepdims=True)
     out_ref[...] = middle_ref[...] + gate * comb_ref[...]
-    if spreads:
-        spread_into(
-            cotangent_ref[...].astype(f32), comb_ref, slot_row_ref, chosen_ref, logits_ref, *spread_out
-        )
     if gathers:
         wait_all(fourth)
 
@@ -1101,10 +1271,10 @@
 
 
 def expert_forward(
-    sent, slot_col, chosen_f, logits, middle, full_in, full_out, grid_shape, identifier, column=None, spread_from=None
+    sent, slot_col, chosen_f, logits, middle, full_in, full_out, grid_shape, identifier, column=None
 ):
     members = grid_shape[1]
-    gathers, spreads = column is not None, spread_from is not None
+    gathers = column is not None
     ins = [sent, slot_col, chosen_f, logits, middle, full_in, full_out]
     in_specs = [vmem_spec] * 5 + [any_spec] * 2
     outs = [
@@ -1133,16 +1303,8 @@
         out_specs.append(any_spec)
         others = pltpu.SemaphoreType.DMA((gather_copies(grid_shape)[1],))
         scratch += [pltpu.SemaphoreType.DMA, others, others]
-    if spreads:
-        ins += list(spread_from)
-        in_specs += [vmem_spec] * 2
-        outs += [
-            jax.ShapeDtypeStruct(sent.shape, bf16),
-            jax.ShapeDtypeStruct(logits.shape, bf16),
-        ]
-        out_specs += [vmem_spec] * 2
     return pl.pallas_call(
-        partial(expert_forward_kernel, grid_shape, gathers, spreads),
+        partial(expert_forward_kernel, grid_shape, gathers),
         in_specs=in_specs,
         out_specs=out_specs,
         out_shape=outs,
@@ -1153,27 +1315,209 @@
     )(*ins)
 
 
+def expert_both_kernel(
+    grid_shape,
+    sent_ref,
+    gates_ref,
+    slot_col_ref,
+    chosen_ref,
+    logits_ref,
+    first_ref,
+    second_ref,
+    win_ref,
+    wout_ref,
+    made_ref,
+    d_back_ref,
+    gin_ref,
+    gout_ref,
+    d_logits_ref,
+    arrived_s,
+    gates_s,
+    win_s,
+    wout_s,
+    d_made_s,
+    d_rows_s,
+    act_s,
+    d_pre_s,
+    d_gates_s,
+    d_gates_back_s,
+    grads_ref,
+    w_sems,
+    *sems,
+):
+    members = grid_shape[1]
+    slots = sent_ref.shape[0]
+    rows = slots // members
+    group = chunk_of(members, rows)
+    chunks = members // group
+    chunk_bits = bits_of(chunks)
+    hidden_units = win_s.shape[1]
+    tile = min(768, hidden_units)
+    load_in = pltpu.make_async_copy(win_ref, win_s, w_sems.at[0])
+    load_out = pltpu.make_async_copy(wout_ref, wout_s, w_sems.at[1])
+    load_in.start()
+    load_out.start()
+    greet(peers_along_gy(members))
+    there = Exchange(members, rows, sent_ref, arrived_s, *sems[0:2])
+    back = Exchange(members, rows, d_rows_s, d_back_ref, *sems[2:4])
+    gates_there = Leading(members, gates_ref, gates_s, *sems[4:6])
+    gates_back = Leading(members, d_gates_s, d_gates_back_s, *sems[6:8])
+
+    for apart in send_order(members):
+        gates_there.copy(apart).start()
+        there.copy(apart).start()
+
+    collected = collect(there.me, members, rows, first_ref, second_ref, grads_ref, sems[8])
+    start_all(collected)
+    there.keep_own()
+    gates_there.keep_own()
+    load_in.wait()
+    load_out.wait()
+    wait_all(collected)
+    my_chunk = there.me // group
+
+    def work(index, first):
+        for member in range(first, group):
+            gates_there.copy(index * group + member).wait_recv()
+            there.copy(index * group + member).wait_recv()
+        chunk = xor_of(my_chunk, index, chunk_bits)
+        here = pl.ds(pl.multiple_of(chunk * (group * rows), group * rows), group * rows)
+        gate = jnp.concatenate(
+            [gates_s[chunk * group + member].T[:rows, 0:1] for member in range(group)], axis=0
+        )
+        taken = arrived_s[here, :]
+        grads = grads_ref[here, :].astype(f32)
+        d_made = (gate * grads).astype(bf16)
+        d_made_s[here, :] = d_made
+        made = jnp.zeros((group * rows, taken.shape[1]), f32)
+        d_rows = made
+        for start in range(0, hidden_units, tile):
+            units = slice(start, start + tile)
+            act, slope = gelu_and_slope(dot(taken, win_s[:, units]))
+            act = act.astype(bf16)
+            act_s[here, units] = act
+            d_pre = (dot(d_made, wout_s[:, units]) * slope).astype(bf16)
+            d_pre_s[here, units] = d_pre
+            d_rows = d_rows + dot(d_pre, win_s[:, units], 1, 1)
+            made = made + dot(act, wout_s[:, units], 1, 1)
+        d_rows_s[here, :] = d_rows.astype(bf16)
+        made = made.astype(bf16)
+        made_ref[here, :] = made
+        d_gate = jnp.sum(grads * made.astype(f32), axis=1, keepdims=True)
+        for member in range(group):
+            part = jnp.broadcast_to(d_gate[member * rows : (member + 1) * rows], (rows, 128)).T
+            d_gates_s[chunk * group + member, :, :rows] = part[: d_gates_s.shape[1]]
+        for member in range(first, group):
+            gates_back.copy(index * group + member).start()
+            back.copy(index * group + member).start()
+
+    work(0, 1)
+    back.keep_own()
+    gates_back.keep_own()
+
+    @pl.loop(1, chunks)
+    def _(index):
+        work(index, 0)
+
+    for lhs_ref, rhs_ref, out_ref in ((d_made_s, act_s, gout_ref), (arrived_s, d_pre_s, gin_ref)):
+        lhs = lhs_ref[...].T
+
+        @pl.loop(0, hidden_units // tile)
+        def _(index, lhs=lhs, rhs_ref=rhs_ref, out_ref=out_ref):
+            units = pl.ds(pl.multiple_of(index * tile, tile), tile)
+            out_ref[:, units] = dot(lhs, rhs_ref[:, units]).astype(bf16)
+
+    @pl.loop(1, members)
+    def _(apart):
+        gates_back.copy(apart).wait_recv()
+
+    row = jnp.concatenate(
+        [d_gates_back_s[expert, 0:1, :rows] for expert in range(members)], axis=1
+    )
+    slot_col = slot_col_ref[...]
+    places = lax.broadcasted_iota(jnp.int32, (slot_col.shape[0], slots), 1)
+    d_gate = jnp.sum(jnp.where(places == slot_col, row, 0.0), axis=1, keepdims=True)
+    d_logits_ref[...] = d_logits_of(d_gate, logits_ref[...], chosen_ref[...])
+
+    @pl.loop(1, members)
+    def _(apart):
+        back.copy(apart).wait_recv()
+        there.copy(apart).wait_send()
+        back.copy(apart).wait_send()
+        gates_there.copy(apart).wait_send()
+        gates_back.copy(apart).wait_send()
+
+
+def expert_both(sent, gates, far_parts, slot_col, chosen_f, logits, full_in, full_out, grid_shape, identifier):
+    members = grid_shape[1]
+    slots = sent.shape[0]
+    outs = (
+        jax.ShapeDtypeStruct(sent.shape, bf16),
+        jax.ShapeDtypeStruct(sent.shape, bf16),
+        jax.ShapeDtypeStruct(full_in.shape, bf16),
+        jax.ShapeDtypeStruct(full_out.shape, bf16),
+        jax.ShapeDtypeStruct(logits.shape, bf16),
+    )
+    tall = pltpu.VMEM(sent.shape, bf16)
+    wide = pltpu.VMEM((slots, full_in.shape[1]), bf16)
+    small = pltpu.VMEM(gates.shape, f32)
+    weights = pltpu.VMEM(full_in.shape, bf16)
+    return pl.pallas_call(
+        partial(expert_both_kernel, grid_shape),
+        in_specs=[vmem_spec] * 5 + [any_spec] * 4,
+        out_specs=[vmem_spec] * len(outs),
+        out_shape=outs,
+        scratch_shapes=[
+            tall,
+            small,
+            weights,
+            weights,
+            tall,
+            tall,
+            wide,
+            wide,
+            small,
+            small,
+            tall,
+            pltpu.SemaphoreType.DMA((2,)),
+        ]
+        + [pltpu.SemaphoreType.DMA((members,))] * 9,
+        compiler_params=params(identifier),
+        cost_estimate=lasting(85),
+        name="expert_both",
+    )(sent, gates, slot_col, chosen_f, logits, *far_parts, full_in, full_out)
+
+
 def expert_backward_kernel(
-    members,
+    grid_shape,
     d_sent_ref,
     arrived_ref,
+    blocks_ref,
     win_ref,
     wout_ref,
     d_back_ref,
     gin_ref,
     gout_ref,
+    upper_ref,
+    lower_ref,
     win_s,
     wout_s,
     d_arrived_s,
     d_rows_s,
     act_s,
     slope_s,
+    first_s,
+    up2_s,
+    low2_s,
     w_sems,
     send_sems,
     recv_sems,
     back_send_sems,
     back_recv_sems,
+    *sum_sems,
 ):
+    members = grid_shape[1]
+    place = Place(grid_shape)
     slots = d_sent_ref.shape[0]
     rows = slots // members
     group = chunk_of(members, rows)
@@ -1185,13 +1529,16 @@
     load_out = pltpu.make_async_copy(wout_ref, wout_s, w_sems.at[1])
     load_in.start()
     load_out.start()
-    greet(peers_along_gy(members))
+    greet(peers_along_gy(members) + [place.core_peer()] + place.y_peers())
+    landings = (first_s, up2_s, low2_s, upper_ref, lower_ref, None, None)
+    sums = Scatter(place, blocks_ref, landings, sum_sems, upper_ref.shape[1])
     there = Exchange(members, rows, d_sent_ref, d_arrived_s, send_sems, recv_sems)
     back = Exchange(members, rows, d_rows_s, d_back_ref, back_send_sems, back_recv_sems)
-    for apart in range(members - 1, 0, -1):
+    for apart in send_order(members):
         there.copy(apart).start()
     there.keep_own()
     my_chunk = there.me // group
+    start_all(sums.copies(0))
     load_in.wait()
 
     @pl.loop(0, slots // 256)
@@ -1204,6 +1551,9 @@
             act_s[here, units] = act.astype(bf16)
             slope_s[here, units] = slope.astype(bf16)
 
+    wait_all(sums.copies(0))
+    sums.add(0)
+    start_all(sums.copies(1))
     load_out.wait()
 
     def chunk_rows(index):
@@ -1232,6 +1582,9 @@
     def _(index):
         work(index, 0)
 
+    wait_all(sums.copies(1))
+    sums.add(1)
+    start_all(sums.copies(2))
     for lhs_ref, rhs_ref, out_ref in (
         (d_arrived_s, act_s, gout_ref),
         (arrived_ref, slope_s, gin_ref),
@@ -1243,6 +1596,9 @@
             units = pl.ds(pl.multiple_of(index * tile, tile), tile)
             out_ref[:, units] = dot(lhs, rhs_ref[:, units]).astype(bf16)
 
+    wait_all(sums.copies(2))
+    sums.add(2)
+
     @pl.loop(1, members)
     def _(apart):
         back.copy(apart).wait_recv()
@@ -1250,18 +1606,21 @@
         back.copy(apart).wait_send()
 
 
-def expert_backward(d_sent, arrived, full_in, full_out, members, identifier):
+def expert_backward(d_sent, arrived, blocks, full_in, full_out, grid_shape, identifier):
+    members = grid_shape[1]
+    landings = whole_blocks(blocks.shape, blocks.shape[4] // 2)
     outs = (
         jax.ShapeDtypeStruct(d_sent.shape, bf16),
         jax.ShapeDtypeStruct(full_in.shape, bf16),
         jax.ShapeDtypeStruct(full_out.shape, bf16),
+        *[jax.ShapeDtypeStruct(one, bf16) for one in landings[3:5]],
     )
     slots = d_sent.shape[0]
     sems = pltpu.SemaphoreType.DMA((members,))
     return pl.pallas_call(
-        partial(expert_backward_kernel, members),
-        in_specs=[vmem_spec] * 2 + [any_spec] * 2,
-        out_specs=[vmem_spec] * 3,
+        partial(expert_backward_kernel, grid_shape),
+        in_specs=[vmem_spec] * 3 + [any_spec] * 2,
+        out_specs=[vmem_spec] * len(outs),
         out_shape=outs,
         scratch_shapes=[
             pltpu.VMEM(full_in.shape, bf16),
@@ -1270,16 +1629,18 @@
             pltpu.VMEM(d_sent.shape, bf16),
             pltpu.VMEM((slots, full_in.shape[1]), bf16),
             pltpu.VMEM((slots, full_in.shape[1]), bf16),
+            *[pltpu.VMEM(one, bf16) for one in landings[:3]],
             pltpu.SemaphoreType.DMA((2,)),
             sems,
             sems,
             sems,
             sems,
+            *[pltpu.SemaphoreType.DMA((scatter_copies(grid_shape),))] * 2,
         ],
         compiler_params=params(10 + identifier),
         cost_estimate=lasting(85),
         name="expert_backward",
-    )(d_sent, arrived, full_in, full_out)
+    )(d_sent, arrived, blocks, full_in, full_out)
 
 
 def body(
@@ -1312,14 +1673,15 @@
     router_rows = jnp.pad(
         w_router.transpose(0, 2, 1), ((0, 0), (0, tile_rows - wide_router), (0, 4 * wide - tall))
     )
-    buckets_col = jnp.pad(buckets, (0, 1), constant_values=-1)[:, None]
-    mats, router, later, bias, slot_col, slot_row, chosen_f = start(
+    buckets_row = jnp.pad(buckets, (0, 1), constant_values=-1)[None, :]
+    mats, router, later, bias, slot_col, slot_row, chosen_f, spread = start(
         (w_query, w_key, w_value, w_output),
         router_rows,
-        buckets_col,
+        buckets_row,
         rel_table.T,
         piece_ids,
         route,
+        cotangent,
         grid_shape,
     )
     gain_attn_f = gain_attn.astype(f32)
@@ -1328,56 +1690,60 @@
     hidden = hidden_in
     kept = []
     blocks = None
+    far_parts = []
     for layer in range(layers):
         last = layer == layers - 1
         gains = (gain_attn_f[layer][None], gain_ffn_f[layer][None])
-        (mats, router, q, k, v, attended, lse, middle, logits, sent), column = attention_forward(
+        mats, router, q, k, v, attended, lse, middle, logits, sent, *gates, far_part = attention_forward(
             hidden,
             gains[0],
             gains[1],
-            slot_row,
+            (slot_row, slot_col, chosen_f),
             bias,
             grid_shape,
             1 + layer,
+            spread,
+            last,
             blocks=blocks,
             mats=(mats, router) if blocks is None else None,
-            following=None if last else later[layer],
         )
+        far_parts.append(far_part)
         full_in = lax.all_gather(w_in[layer, 0], "gx", axis=1, tiled=True)
         full_out = lax.all_gather(w_out[layer, 0], "gx", axis=1, tiled=True)
-        got = expert_forward(
-            sent,
-            slot_col,
-            chosen_f,
-            logits,
-            middle,
-            full_in,
-            full_out,
-            grid_shape,
-            5 + layer,
-            column=column,
-            spread_from=(cotangent, slot_row) if last else None,
-        )
-        arrived, combined, hidden_next = got[:3]
+        state = (hidden, gains, (mats, router), (q, k, v), attended, lse, middle, logits)
         if last:
-            d_sent, d_logits = got[3:]
+            made, d_back, grad_in_full, grad_out_full, d_logits = expert_both(
+                sent, gates[0], far_parts, slot_col, chosen_f, logits, full_in, full_out, grid_shape, 7
+            )
+            kept.append(state)
         else:
-            blocks = got[3]
-        kept.append(
-            (hidden, gains, (mats, router), (q, k, v), attended, lse, middle, logits, combined)
-            + (arrived, full_in, full_out)
-        )
-        hidden = hidden_next
+            arrived, combined, hidden, blocks = expert_forward(
+                sent,
+                slot_col,
+                chosen_f,
+                logits,
+                middle,
+                full_in,
+                full_out,
+                grid_shape,
+                5 + layer,
+                column=later[layer],
+            )
+            kept.append(state + (combined, arrived, full_in, full_out))
 
     grad_now = cotangent
-    table_sums = None
     parts = []
+    partials = []
+    returned = []
     for layer in reversed(range(layers)):
-        (prior, gains, mats, q_k_v, attended, lse, middle, logits, combined) = kept[layer][:9]
-        (arrived, full_in, full_out) = kept[layer][9:]
-        d_back, grad_in_full, grad_out_full = expert_backward(
-            d_sent, arrived, full_in, full_out, count_y, layer
-        )
+        last = layer == layers - 1
+        (prior, gains, mats, q_k_v, attended, lse, middle, logits) = kept[layer][:8]
+        if not last:
+            arrived, full_in, full_out = kept[layer][9:]
+            d_back, grad_in_full, grad_out_full, upper, lower = expert_backward(
+                d_sent, arrived, parts[-1][0], full_in, full_out, grid_shape, layer
+            )
+            partials.append((upper, lower[:1]))
         grad_out_part = lax.psum_scatter(grad_out_full, "gx", scatter_dimension=1, tiled=True)
         grad_in_part = lax.psum_scatter(grad_in_full, "gx", scatter_dimension=1, tiled=True)
         below = None
@@ -1399,32 +1765,35 @@
             grid_shape,
             below=below,
             after=[array for part in parts for array in part[4:6]],
+            made=made,
+            returns=last,
+            identifier=18 + layer,
         )
         grad_now, blocked, gwr, gga, ggf, offset_sums = got[:6]
         if layer > 0:
-            d_sent, d_logits = got[6:]
-        table_sums = offset_sums if table_sums is None else table_sums + offset_sums
-        parts.append((blocked, gwr, gga, ggf, grad_in_part, grad_out_part))
+            d_sent, d_logits = got[6:8]
+        returned.append(got[-1])
+        offset_sums = offset_sums.reshape(heads, 2 * seq_len)
+        parts.append((blocked, gwr, gga, ggf, grad_in_part, grad_out_part, offset_sums))
     parts = parts[::-1]
-    bucket_onehot = (
-        buckets_col == jnp.arange(rel_table.shape[0], dtype=jnp.int32)[None, :]
-    ).astype(f32)
-    d_table = jnp.dot(
-        table_sums.reshape(heads, 2 * seq_len), bucket_onehot, precision=highest
-    ).T
     buckets_count = rel_table.shape[0]
-    small = jnp.concatenate(
-        [part[1] for part in parts]
-        + [part[2] for part in parts]
-        + [part[3] for part in parts]
-        + [jnp.pad(d_table.reshape(1, -1), ((0, 0), (0, width - d_table.size)))]
-    )
-    small = jnp.pad(small, ((0, -small.shape[0] % 8), (0, 0)))
-    *attn_grads, small = final_sums([part[0] for part in parts], small, grid_shape, wide)
+    smalls = [part[which] for which in (1, 2, 3, 6) for part in parts]
+    top = kept[-1]
+    *attn_grads, small, hidden_out = final_sums(
+        parts[0][0],
+        partials[::-1],
+        smalls + [buckets_row],
+        (slot_col, chosen_f, top[7], top[6]),
+        returned,
+        grid_shape,
+        wide,
+        buckets_count,
+    )
     router_sum = small[: layers * experts].reshape(layers, experts, width)
     base = layers * experts
     gga_all, ggf_all = small[base : base + layers], small[base + layers : base + 2 * layers]
-    d_table = small[base + 2 * layers, : heads * buckets_count].reshape(buckets_count, heads)
+    base = base + 2 * layers
+    d_table = small[base : base + heads, :buckets_count].T
     router_mine = lax.dynamic_slice(
         router_sum,
         (0, lax.axis_index("gy") * wide_router, lax.axis_index("gx") * tall),
@@ -1433,7 +1802,7 @@
     grad_in = jnp.stack([part[4] for part in parts]).astype(f32)[:, None]
     grad_out = jnp.stack([part[5] for part in parts]).astype(f32)[:, None]
     return (
-        hidden,
+        hidden_out,
         grad_now,
         d_table,
         gga_all,

time: 618 us -> 543 us (0.88)
  Pallas kernels: 567 us -> 494 us
    pallas_call x9 -> x8, Pallas kernels: 504 us -> 429 us  [the longest x2 87.6 us: attention_backward(): pl.pallas_call(partial(backward_kernel, head_dim, grid_shape, spreads, re...]
  transfers between devices with their start and end apart: 8 -> 8, of which waited for: 0 -> 0; matrix products, arithmetic and copies ran while one was open for 3% -> 2% of each run, Pallas kernels for 68% -> 78%
where the time goes in v4:
time: 543 us; the launch traced here: 538 us
  Pallas kernels  494 us (91%)
  local copies, waits for them, and re-layouts  19.6 us (4%)
  between operations  14.6 us (3%)
  other arithmetic  7.74 us (1%)
    pallas_call x2, Pallas kernels, attention_backward(): pl.pallas_call(partial(backward_kernel, head_dim, grid_shape, spreads, re...  87.6 us
    pallas_call x1, Pallas kernels, expert_backward(): pl.pallas_call(partial(expert_backward_kernel, grid_shape), in_specs=[vme...  73.2 us
    pallas_call x1, Pallas kernels, expert_forward(): pl.pallas_call(partial(expert_forward_kernel, grid_shape, gathers), in_sp...  72.6 us
    pallas_call x1, Pallas kernels, expert_both(): pl.pallas_call(partial(expert_both_kernel, grid_shape), in_specs=[vmem_sp...  72.5 us
    pallas_call x1, Pallas kernels, start(): pl.pallas_call(partial(start_kernel, grid_shape), in_specs=[vmem_spec] *...  65.3 us
    pallas_call x2, Pallas kernels, attention_forward(): pl.pallas_call(partial(forward_kernel, head_dim, grid_shape, blocked, las...  65.2 us
    pallas_call x1, Pallas kernels, final_sums(): pl.pallas_call(partial(final_kernel, grid_shape, layers, buckets_count),...  57.8 us
  transfers between devices with their start and end apart: 8, of which 0 were waited for; matrix products, arithmetic and copies ran while one was open for 2% of the time, Pallas kernels for 78%

profile of v4, /device:TPU:0, one launch (start us, length us, event | category | flops | bytes accessed | tf_op | source)
XLA Modules:
  0.0 538.4 jit_solution(9141999584286566681)
XLA Ops:
  7.2 0.0 all-gather.9.cloned.1.call-start
  7.2 3.3 fusion.1
  10.6 0.0 all-gather.11.cloned.1.call-start
  10.6 1.6 fusion
  12.2 0.0 all-gather.11.cloned.1.call-update
  12.2 0.0 all-gather.13.cloned.1.call-start
  12.3 0.7 all-gather.13.cloned.1.call-update
  13.0 0.0 all-gather.15.cloned.1.call-start
  13.0 0.5 all-gather.15.cloned.1.call-update
  13.6 0.0 reduce-scatter.7.cloned.1.call-start
  13.6 0.6 pad.9
  14.2 0.6 pad.8.router_rows_ref
  14.8 0.6 fusion.3
  15.4 65.3 %start.1 = (bf16[4,768,768]{2,1,0:T(8,128)(2,1)}, bf16[8,768]{1,0:T(8,128)(2,1)}, bf16[1,4,208,384]{3,2,1,0:T(8,128)(2,1)}, bf16[12,512,512]{2,1,0:T(8,128)(2,1)...) custom-call(bf16[2,192,96]{2,1,0:T(8,128)(2,1)} %wq_ref.1, ...), custom_call_target="tpu_custom_call" | custom-call | flops 44999999488 | bytes 1048576 | tf_op jit(solution)/shard_map/start/pallas_call | solution.py:596
  80.8 28.6 %attention_forward.2 = (bf16[512,768]{1,0:T(8,128)(2,1)}, bf16[512,768]{1,0:T(8,128)(2,1)}, bf16[512,768]{1,0:T(8,128)(2,1)}, bf16[768,512]{1,0:T(8,128)(2,1)}, ...) custom-call(bf16[512,768]{1,0:T(8,128)(2,1)} %hidden_ref.3, ...), custom_call_target="tpu_custom_call" | custom-call | flops 24999999488 | bytes 1048576 | tf_op jit(solution)/shard_map/attention_forward/pallas_call | solution.py:780
  109.4 0.0 all-gather.9.cloned.1.call-done
  109.4 0.0 all-gather.11.cloned.1.call-done
  109.5 72.6 %expert_forward.1 = (bf16[1024,768]{1,0:T(8,128)(2,1)}, f32[512,768]{1,0:T(8,128)}, f32[512,768]{1,0:T(8,128)}, bf16[2,2,4,2,208,384]{5,4,3,2,1,0:T(8,128)(2,1)}) custom-call(bf16[1024,768]{1,0:T(8,128)(2,1)} %get-tuple-element.84.sent_ref, s32[512,1]{1,0:T(8,128)} %get-tuple-element.78.slot_col_ref.refs_12_, ...), custom_call_target="tpu_custom_call" | custom-call | flops 74999996416 | bytes 1048576 | tf_op jit(solution)/shard_map/expert_forward/pallas_call | solution.py:1306
  182.1 36.6 %attention_forward.3 = (bf16[4,768,768]{2,1,0:T(8,128)(2,1)}, bf16[8,768]{1,0:T(8,128)(2,1)}, bf16[512,768]{1,0:T(8,128)(2,1)}, bf16[512,768]{1,0:T(8,128)(2,1)}...) custom-call(f32[512,768]{1,0:T(8,128)} %get-tuple-element.88.hidden_, ...), custom_call_target="tpu_custom_call" | custom-call | flops 24999999488 | bytes 1048576 | tf_op jit(solution)/shard_map/attention_forward/pallas_call | solution.py:780
  218.7 0.0 all-gather.13.cloned.1.call-done
  218.7 0.0 all-gather.15.cloned.1.call-done
  218.7 72.5 %expert_both.1 = (bf16[1024,768]{1,0:T(8,128)(2,1)}, bf16[1024,768]{1,0:T(8,128)(2,1)}, bf16[768,3072]{1,0:T(8,128)(2,1)}, bf16[768,3072]{1,0:T(8,128)(2,1)}, bf16[512,8]{1,0:T(8,128)(2,1)}) custom-call(bf16[1024,768]{1,0:T(8,128)(2,1)} %get-tuple-element.90.sent_ref, f32[8,8,128]{2,1,0:T(8,128)} %get-tuple-element.91.gates_ref, ...), custom_call_target="tpu_custom_call" | custom-call | flops 85000003584 | bytes 1048576 | tf_op jit(solution)/shard_map/expert_both/pallas_call | solution.py:1465
  291.3 0.0 reduce-scatter.5.cloned.1.call-start
  291.3 0.5 reduce-scatter.5.cloned.1.call-update
  291.9 0.0 reduce-scatter.11.cloned.1.call-start
  291.9 46.0 %attention_backward.2 = (f32[512,768]{1,0:T(8,128)}, bf16[2,2,4,2,192,384]{5,4,3,2,1,0:T(8,128)(2,1)}, f32[8,768]{1,0:T(8,128)}, f32[1,768]{1,0:T(1,128)}, f32[1...) custom-call(bf16[1024,768]{1,0:T(8,128)(2,1)} %get-tuple-element.95., ...), custom_call_target="tpu_custom_call" | custom-call | flops 32000000000 | bytes 1048576 | tf_op jit(solution)/shard_map/attention_backward/pallas_call | solution.py:1034
  338.0 73.2 %expert_backward.1 = (bf16[1024,768]{1,0:T(8,128)(2,1)}, bf16[768,3072]{1,0:T(8,128)(2,1)}, bf16[768,3072]{1,0:T(8,128)(2,1)}, bf16[4,96,384]{2,1,0:T(8,128)(2,1)}, bf16[1,4,96,384]{3,2,1,0:T(8,128)(2,1)}) custom-call(bf16[1024,768]{1,0:T(8,128)(2,1)} %get-tuple-element.107.d_sent_ref, bf16[1024,768]{1,0:T(8,128)(2,1)} %get-tuple-element.108.arrived_ref, ...), custom_call_target="tpu_custom_call" | custom-call | flops 85000003584 | bytes 1048576 | tf_op jit(solution)/shard_map/expert_backward/pallas_call | solution.py:1620
  411.2 0.0 reduce-scatter.9.cloned.1.call-start
  411.3 0.7 copy-done.9
  412.0 0.7 reshape.100.refs_10_
  412.7 0.0 reduce-scatter.7.cloned.1.call-done.refs_4_
  412.7 0.0 reduce-scatter.5.cloned.1.call-done.refs_3_
  412.7 41.6 %attention_backward.3 = (f32[512,768]{1,0:T(8,128)}, bf16[2,2,4,2,192,384]{5,4,3,2,1,0:T(8,128)(2,1)}, f32[8,768]{1,0:T(8,128)}, f32[1,768]{1,0:T(1,128)}, f32[1...) custom-call(bf16[1024,768]{1,0:T(8,128)(2,1)} %get-tuple-element.110.d_back_ref, ...), custom_call_target="tpu_custom_call" | custom-call | flops 32000000000 | bytes 1048576 | tf_op jit(solution)/shard_map/attention_backward/pallas_call | solution.py:1034
  454.3 1.5 reshape.99.refs_9_
  455.8 57.8 %final_sums.1 = (f32[2,192,96]{2,1,0:T(8,128)}, f32[2,192,96]{2,1,0:T(8,128)}, f32[2,192,96]{2,1,0:T(8,128)}, f32[2,192,96]{2,1,0:T(8,128)}, f32[32,768]{1,0:T(8,128)}, /*index=5*/f32[512,768]{1,0:T(8,128)}) custom-call(bf16[2,2,4,2,192,384]{5,4,3,2,1,0:T(8,128)(2,1)} %get-tuple-element.120.refs_0_, bf16[4,96,384]{2,1,0:T(8,128)(2,1)} %get-tuple-element.121.refs_1_, ...), custom_call_target="tpu_custom_call" | custom-call | flops 60000002048 | bytes 1048576 | tf_op jit(solution)/shard_map/final_sums/pallas_call | solution.py:420
  513.5 1.3 slice_bitcast_fusion.1
  514.8 1.4 fusion.2
  516.3 0.8 slice_bitcast_fusion
  517.1 3.9 maximum_convert_fusion.1
  520.9 3.9 maximum_convert_fusion
  524.8 0.7 dynamic-slice_bitcast_fusion
  525.5 1.1 copy.34
  526.6 0.8 copy-done.1
  527.5 1.1 copy.35
  528.6 0.7 copy.36
  529.3 0.7 copy.37
  530.0 0.7 copy.38
  530.7 0.7 copy.39
  (33 shorter events, 0.1 us)
Async XLA Ops:
  7.2 102.2 %all-gather.9.cloned.1.call-start = ((), (), s32[]{:S(2)}) async-start(), calls=%async_computation.8 | async-start | bytes 5898240 | tf_op jit(solution)/shard_map/all_gather | solution.py:1711
  7.2 3.4 copy-start
  10.6 98.9 %all-gather.11.cloned.1.call-start = ((), (), s32[]{:S(2)}) async-start(), calls=%async_computation.9 | async-start | bytes 5898240 | tf_op jit(solution)/shard_map/all_gather | solution.py:1712
  12.2 1.4 copy-start.13
  12.2 1.4 copy-start.12
  12.2 2.6 copy-start.10
  12.2 2.6 copy-start.11
  12.2 206.5 %all-gather.13.cloned.1.call-start = ((), (), s32[]{:S(2)}) async-start(), calls=%async_computation.10 | async-start | bytes 5898240 | tf_op jit(solution)/shard_map/all_gather | solution.py:1711
  13.0 205.8 %all-gather.15.cloned.1.call-start = ((), (), s32[]{:S(2)}) async-start(), calls=%async_computation.11 | async-start | bytes 5898240 | tf_op jit(solution)/shard_map/all_gather | solution.py:1712
  13.6 399.1 %reduce-scatter.7.cloned.1.call-start = ((), (), s32[]{:S(2)}) async-start(), calls=%async_computation.5 | async-start | bytes 5898240 | tf_op jit(solution)/shard_map/reduce_scatter | solution.py:1747
  291.3 121.4 %reduce-scatter.5.cloned.1.call-start = ((), (), s32[]{:S(2)}) async-start(), calls=%async_computation.4 | async-start | bytes 5898240 | tf_op jit(solution)/shard_map/reduce_scatter | solution.py:1748
  291.9 225.2 %reduce-scatter.11.cloned.1.call-start = ((), (), s32[]{:S(2)}) async-start(), calls=%async_computation.7 | async-start | bytes 5898240 | tf_op jit(solution)/shard_map/reduce_scatter | solution.py:1747
  411.2 0.8 copy-start.9
  411.2 109.7 %reduce-scatter.9.cloned.1.call-start = ((), (), s32[]{:S(2)}) async-start(), calls=%async_computation.6 | async-start | bytes 5898240 | tf_op jit(solution)/shard_map/reduce_scatter | solution.py:1748
  455.8 61.3 %copy-start.3 = (bf16[768,768]{1,0:T(8,128)(2,1)S(1)}, bf16[768,768]{1,0:T(8,128)(2,1)}, u32[]{:S(2)}) copy-start(bf16[768,768]{1,0:T(8,128)(2,1)} %reduce-scatter.7.cloned.1.call-done.refs_4_) | copy-start | bytes 3538948
  517.1 3.9 copy-start.4
  520.9 4.5 copy-start.2
  525.5 2.0 copy-start.1
  527.5 1.2 copy-start.8
  527.5 1.8 copy-start.7
  527.5 2.5 copy-start.6
  527.5 3.2 copy-start.5
Sparse Core Ops, SparseCore 0:
  10.7 52.3 all-gather.8
  65.2 38.4 all-gather.10
  105.8 55.2 all-gather.12
  163.1 36.9 all-gather.14
  291.4 55.8 reduce-scatter.6
  349.9 54.1 reduce-scatter.4
  411.3 52.3 reduce-scatter.10
  466.4 52.1 reduce-scatter.8

commit v5 on v4

--- a/solution.py
+++ b/solution.py
@@ -16,7 +16,7 @@
 MESH = pl.DeviceIdType.MESH
 vmem_spec = pl.BlockSpec(memory_space=pltpu.VMEM)
 any_spec = pl.BlockSpec(memory_space=pl.ANY)
-vmem_bytes = 56 * 1024 * 1024
+vmem_bytes = 60 * 1024 * 1024
 
 
 def whole(shape):
@@ -324,16 +324,15 @@
     partial_refs = [(take(0), take(0)) for _ in range(layers - 1)]
     router_refs, gga_refs, ggf_refs, offset_refs = ([take(0) for _ in range(layers)] for _ in range(4))
     buckets_ref, slot_col_ref, chosen_ref, logits_ref, middle_ref = (take(0) for _ in range(5))
-    first_ref, second_ref = take(0), take(0)
-    outs = [take(0) for _ in range(4)]
-    small_out_ref, result_ref = take(0), take(0)
+    first_ref, second_ref, push_ref = take(0), take(0), take(0)
+    packed_ref, small_out_ref, result_ref, landing_ref = (take(0) for _ in range(4))
     landings = [take(0) for _ in range(7)]
     z_landings = [(take(0), take(0)) for _ in range(layers - 1)]
     totals, landing, returned_s = take(0), take(0), take(0)
     sems = [(take(0), take(0)) for _ in range(layers)]
-    small_sems, collect_sems = (take(0), take(0)), take(0)
+    small_sems, collect_sems, push_sems = (take(0), take(0)), take(0), (take(0), take(0))
     place = Place(grid_shape)
-    tall, wide = outs[0].shape[1:]
+    tall = packed_ref.shape[1]
     split = tall // 2
     members = grid_shape[1]
     slots = returned_s.shape[0]
@@ -344,7 +343,13 @@
         upper_layers.append(Scatter(place, blocks_ref, places, sems[layer], split))
     lowest = Scatter(place, blocks_ref, landings, sems[0], split)
     collected = collect(
-        lax.axis_index("gy"), members, slots // members, first_ref, second_ref, returned_s, collect_sems
+        lax.axis_index("gy"),
+        members,
+        slots // members,
+        (first_ref, second_ref),
+        lambda apart: int(apart not in early(members)),
+        returned_s,
+        collect_sems,
     )
     start_all(collected)
     greet([place.core_peer(), place.x_peer()] + place.y_peers() + place.z_peers())
@@ -383,12 +388,15 @@
     wait_all(lowest.copies(1))
     lowest.add(1)
     start_all(lowest.copies(2))
+    pushed = push_blocks(
+        place, push_ref, landing_ref, push_sems, push_ref.shape[1] - landing_ref.shape[1]
+    )
+    start_all(pushed)
     small.advance()
 
     def finish(layer, one):
         for part, rows in zip(one.result(), (slice(0, split), slice(split, tall))):
-            for which in range(4):
-                outs[which][layer, rows, :] = part[:, which * wide : (which + 1) * wide]
+            packed_ref[layer, rows, :] = part
 
     for layer, one in enumerate(upper_layers):
         wait_all(one.copies(3))
@@ -401,9 +409,10 @@
     small_out_ref[...] = totals[len(small.peers)]
     wait_all(lowest.copies(3))
     finish(0, lowest)
-
-
-def final_sums(blocks, partials, smalls, finishing, returned, grid_shape, wide, buckets_count):
+    wait_all(pushed)
+
+
+def final_sums(blocks, partials, smalls, finishing, returned, push, grid_shape, buckets_count):
     layers = len(partials) + 1
     shape = blocks.shape
     tall = shape[4]
@@ -411,27 +420,29 @@
     landings = [pltpu.VMEM(one, bf16) for one in whole_blocks(shape, tall // 2)]
     steps = small_steps(grid_shape)
     rows = sum(one.shape[0] for one in smalls[: 3 * layers]) + smalls[3 * layers].shape[0]
-    small_shape = (rows + -rows % 8, width)
+    small_shape = (rows, width)
     sems = pltpu.SemaphoreType.DMA((scatter_copies(grid_shape),))
     small_sems = pltpu.SemaphoreType.DMA((steps,))
-    outs = [jax.ShapeDtypeStruct((layers, tall, wide), f32)] * 4
+    outs = [jax.ShapeDtypeStruct((layers, tall, shape[5]), f32)]
     outs += [jax.ShapeDtypeStruct(small_shape, f32), jax.ShapeDtypeStruct(finishing[-1].shape, f32)]
+    outs.append(landing_of(push, push.shape[1] - cut_of(push)))
     ins = [blocks, *[array for pair in partials for array in pair], *smalls, *finishing]
     return pl.pallas_call(
         partial(final_kernel, grid_shape, layers, buckets_count),
-        in_specs=[vmem_spec] * len(ins) + [any_spec] * 2,
-        out_specs=[vmem_spec] * len(outs),
+        in_specs=[vmem_spec] * len(ins) + [any_spec] * 3,
+        out_specs=[vmem_spec] * (len(outs) - 1) + [any_spec],
         out_shape=outs,
         scratch_shapes=landings
         + landings[5:] * (layers - 1)
         + [pltpu.VMEM((steps + 1, *small_shape), f32), pltpu.VMEM((steps, *small_shape), f32)]
         + [pltpu.VMEM(returned[0].shape, bf16)]
         + [sems, sems] * layers
-        + [small_sems, small_sems, pltpu.SemaphoreType.DMA((grid_shape[1],))],
+        + [small_sems, small_sems, pltpu.SemaphoreType.DMA((grid_shape[1],))]
+        + [pltpu.SemaphoreType.DMA((grid_shape[0] // 2 - 1,))] * 2,
         compiler_params=params(24),
         cost_estimate=lasting(60),
         name="final_sums",
-    )(*ins, *returned)
+    )(*ins, *returned, push)
 
 
 def unblock(grid_shape, blocks_ref, mats_ref, router_ref):
@@ -480,8 +491,11 @@
     slot_row_ref,
     chosen_ref,
     spread_ref,
+    far_ref,
     full_s,
     column_s,
+    spread_send,
+    spread_recv,
     later_send,
     later_recv,
     z_send,
@@ -499,7 +513,17 @@
 
     column_s[z, :tall] = packed(0)
     column_s[z, tall:] = router_rows_ref[0]
-    greet([place.core_peer(), place.x_peer()] + place.y_peers() + place.z_peers())
+    members = grid_shape[1]
+    spread = Exchange(
+        members, spread_ref.shape[0] // members, spread_ref, far_ref, spread_send, spread_recv
+    )
+    spread_copies = [spread.copy(apart) for apart in in_third(members, 0)]
+    greet(
+        [place.core_peer(), place.x_peer()]
+        + place.y_peers()
+        + place.z_peers()
+        + [spread.peer(apart) for apart in in_third(members, 0)]
+    )
     first = gather_z(place, column_s.at[z], column_s.at[z], (z_send, z_recv))
     start_all(first)
     along_z = []
@@ -550,6 +574,8 @@
     second = gather_second(place, column_s, full_s, split, sems)
     start_all(second)
     start_all(along_z)
+    start_all(spread_copies)
+    spread.keep_own()
     full_s[y, c, :, x] = column_s[...]
     for head in range(heads // 2, heads):
         bias_for(head)
@@ -563,6 +589,7 @@
     wait_all(fourth)
     unblock(grid_shape, full_s, mats_ref, router_ref)
     wait_all(along_z)
+    wait_all(spread_copies)
 
 
 def start(mats, router_rows, buckets, table_t, piece_ids, route, cotangent, grid_shape):
@@ -591,6 +618,7 @@
         jax.ShapeDtypeStruct((1, seq_len), jnp.int32),
         jax.ShapeDtypeStruct((seq_len, experts), f32),
         jax.ShapeDtypeStruct((2 * seq_len, width), bf16),
+        jax.ShapeDtypeStruct((2 * seq_len, width), bf16),
     )
     along_z, others = gather_copies(grid_shape)
     return pl.pallas_call(
@@ -601,6 +629,8 @@
         scratch_shapes=[
             pltpu.VMEM((*half, *block), bf16),
             pltpu.VMEM((half[2], *block), bf16),
+            pltpu.SemaphoreType.DMA((experts,)),
+            pltpu.SemaphoreType.DMA((experts,)),
             pltpu.SemaphoreType.DMA((layers - 1, along_z)),
             pltpu.SemaphoreType.DMA((layers - 1, along_z)),
             pltpu.SemaphoreType.DMA((along_z,)),
@@ -657,26 +687,20 @@
         take(0) for _ in range(8)
     )
     gates_ref = take(0) if last else None
-    far_ref, send_sems, recv_sems, own_sem = refs
+    far_ref, send_sems, recv_sems = refs
     pair, pairs = pl.program_id(0), pl.num_programs(0)
     seq_len = hidden_ref.shape[0]
     width = 2 * head_dim
-    step = min(256, seq_len)
+    step = min(512, seq_len)
 
     members = grid_shape[1]
     spread = Exchange(members, spread_ref.shape[0] // members, spread_ref, far_ref, send_sems, recv_sems)
-    mine = spread.block(spread.me)
-    own = None
-    if not last:
-        own = pltpu.make_async_copy(spread_ref.at[mine, :], far_ref.at[mine, :], own_sem)
-    aparts = part_of(members, not last)
+    aparts = in_third(members, 2 if last else 1)
 
     @pl.when(pair == 0)
     def _():
         greet([spread.peer(apart) for apart in aparts])
         start_all([spread.copy(apart) for apart in aparts])
-        if not last:
-            own.start()
 
     @pl.when(pair == 0)
     def _():
@@ -702,9 +726,9 @@
             top = jnp.max(scores, axis=0, keepdims=True)
             raised = jnp.exp(scores - top)
             total = jnp.sum(raised, axis=0, keepdims=True)
-            probs = (raised * (1.0 / total)).astype(bf16)
+            probs = raised.astype(bf16)
             rows = pl.ds(pl.multiple_of(pair * width + half * head_dim, head_dim), head_dim)
-            att_ref[rows, cols] = dot(v_one, probs).astype(bf16)
+            att_ref[rows, cols] = (dot(v_one, probs) * (1.0 / total)).astype(bf16)
             lse_ref[0, half : half + 1, cols] = top + jnp.log(total)
 
     @pl.when(pair == pairs - 1)
@@ -722,8 +746,6 @@
     @pl.when(pair == pairs - 1)
     def _():
         wait_all([spread.copy(apart) for apart in aparts])
-        if not last:
-            own.wait()
 
 
 def attention_forward(
@@ -776,7 +798,7 @@
     outs.append(jax.ShapeDtypeStruct(spread.shape, bf16))
     out_specs.append(any_spec)
     sems = pltpu.SemaphoreType.DMA((experts,))
-    scratch = [sems, sems, pltpu.SemaphoreType.DMA]
+    scratch = [sems, sems]
     got = pl.pallas_call(
         partial(forward_kernel, head_dim, grid_shape, blocked, last),
         grid=(heads // 2,),
@@ -848,6 +870,7 @@
     grid_shape,
     spreads,
     returns,
+    pushes,
     unread,
     d_back_ref,
     slot_col_ref,
@@ -870,13 +893,20 @@
     spread_in = [take(0) for _ in range(4)] if spreads else []
     bias_ref, lse_ref = take(0), take(0)
     made_ref = take(0)
+    push_refs = (take(0), take(0)) if pushes else ()
     del refs[:unread]
     grad_new_ref, blocks_ref, gwr_ref, gga_ref, ggf_ref, offsets_ref = (take(0) for _ in range(6))
     spread_out = [take(0) for _ in range(2)] if spreads else []
     returned_ref = take(0)
+    landing_refs = (take(0), take(0)) if pushes else ()
     d_att_s, d_middle_s, dqt_s, dk_s, dv_s, probs_s, scores_s = (take(0) for _ in range(7))
-    own_sem, *sems = refs
+    own_sem, *sems = refs[:3]
     members = grid_shape[1]
+    place = Place(grid_shape)
+    pushed = []
+    for src, landing, last_rows in zip(push_refs, landing_refs, (True, False)):
+        begin = src.shape[1] - landing.shape[1] if last_rows else 0
+        pushed += push_blocks(place, src, landing, refs[3:], begin, len(pushed))
     back = Exchange(members, made_ref.shape[0] // members, made_ref, returned_ref, *sems)
     mine = back.block(back.me)
     own = None
@@ -886,15 +916,15 @@
 
     @pl.when(pl.program_id(0) == 0)
     def _():
-        greet([back.peer(apart) for apart in aparts])
-        start_all([back.copy(apart) for apart in aparts])
+        greet([back.peer(apart) for apart in aparts] + (place.y_peers() if pushes else []))
+        start_all(pushed + [back.copy(apart) for apart in aparts])
         if returns:
             own.start()
 
     pair, pairs = pl.program_id(0), pl.num_programs(0)
     seq_len = hidden_ref.shape[0]
     width = 2 * head_dim
-    step = min(256, seq_len)
+    step = min(512, seq_len)
     scale = head_dim**-0.5
 
     @pl.when(pair == 0)
@@ -941,7 +971,7 @@
             dqt_s[rows, cols] = (dot(k_one, d_scores) * scale).astype(bf16)
         d_key = d_key + dot(scores_s[...], q_one)
         d_value = d_value + dot(probs_s[...], da_one)
-        offsets_ref[0, half : half + 1, :] = diagonal_fold(scores_s[...], seq_len)
+        offsets_ref[pl.ds(2 * pair + half, 1), :] = diagonal_fold(scores_s[...], seq_len)
     dk_s[:, lanes] = d_key.astype(bf16)
     dv_s[:, lanes] = d_value.astype(bf16)
 
@@ -966,7 +996,7 @@
 
     @pl.when(pair == pairs - 1)
     def _():
-        wait_all([back.copy(apart) for apart in aparts])
+        wait_all(pushed + [back.copy(apart) for apart in aparts])
         if returns:
             own.wait()
 
@@ -989,6 +1019,7 @@
     after=(),
     made=None,
     returns=False,
+    push=None,
     identifier=None,
 ):
     seq_len, width = hidden.shape
@@ -1020,7 +1051,7 @@
         jax.ShapeDtypeStruct((experts, width), f32),
         row,
         row,
-        jax.ShapeDtypeStruct((heads // 2, 2, 2 * seq_len), f32),
+        jax.ShapeDtypeStruct((heads, 2 * seq_len), f32),
     )
     if spreads:
         outs = outs + (
@@ -1028,18 +1059,22 @@
             jax.ShapeDtypeStruct(d_logits.shape, bf16),
         )
     outs = outs + (jax.ShapeDtypeStruct(made.shape, bf16),)
+    pushes = push is not None
     out_specs = whole_of(outs)
     out_specs[-1] = any_spec
-    out_specs[5] = pl.BlockSpec((1, 2, 2 * seq_len), lambda p: (p, 0, 0))
+    if pushes:
+        rows = [push[0].shape[1] - cut_of(push[0]), cut_of(push[1])]
+        outs = outs + tuple(landing_of(one, many) for one, many in zip(push, rows))
+        out_specs += [any_spec] * 2
     return pl.pallas_call(
-        partial(backward_kernel, head_dim, grid_shape, spreads, returns, len(after)),
+        partial(backward_kernel, head_dim, grid_shape, spreads, returns, pushes, len(after)),
         grid=(heads // 2,),
         in_specs=whole_of(ins)
         + [
             pl.BlockSpec((2, seq_len, seq_len), lambda p: (p, 0, 0)),
             pl.BlockSpec((1, 2, seq_len), lambda p: (p, 0, 0)),
         ]
-        + [any_spec] * (len(after) + 1),
+        + [any_spec] * (len(after) + 1 + 2 * pushes),
         out_specs=out_specs,
         out_shape=outs,
         scratch_shapes=[
@@ -1052,11 +1087,12 @@
             pltpu.VMEM((seq_len, seq_len), bf16),
         ]
         + [pltpu.SemaphoreType.DMA]
-        + [pltpu.SemaphoreType.DMA((count_y,))] * 2,
+        + [pltpu.SemaphoreType.DMA((count_y,))] * 2
+        + [pltpu.SemaphoreType.DMA((2 * (count_x // 2 - 1),))] * (2 * pushes),
         compiler_params=params(identifier),
         cost_estimate=lasting(32),
         name="attention_backward",
-    )(*ins, bias, lse, made, *after)
+    )(*ins, bias, lse, made, *(push if pushes else ()), *after)
 
 
 class Exchange:
@@ -1136,14 +1172,98 @@
     return [a for a in range(1, members) if (a in chosen) == first]
 
 
-def collect(me, members, rows, first_ref, second_ref, dst, sems):
+def third_of(members, apart):
+    quarter = max(1, members // 4)
+    if (apart // quarter) % 2 == 0:
+        return 0
+    return 1 + (2 * (apart % quarter)) // quarter
+
+
+def in_third(members, third):
+    return [apart for apart in range(1, members) if third_of(members, apart) == third]
+
+
+def collect(me, members, rows, refs, which_of, dst, sems):
     copies = []
     for apart in range(members):
         start = xor_of(me, apart, bits_of(members)) * rows
         here = pl.ds(pl.multiple_of(start, rows), rows)
-        ref = first_ref if apart in early(members) else second_ref
+        ref = refs[which_of(apart)]
         copies.append(pltpu.make_async_copy(ref.at[here, :], dst.at[here, :], sems.at[apart]))
     return copies
+
+
+class Weights:
+    def __init__(self, place, halves, whole_refs, local_sems, sems):
+        blocks, _, units = halves[0].shape
+        self.local, self.remote = [], []
+        for which, (part, into) in enumerate(zip(halves, whole_refs)):
+            for block in range(blocks):
+                index = which * blocks + block
+                begin = pl.multiple_of((place.c * blocks + block) * units, units)
+                dst = into.at[:, pl.ds(begin, units)]
+                src = part.at[block]
+                self.local.append(pltpu.make_async_copy(src, dst, local_sems.at[index]))
+                self.remote.append(send(src, dst, sems, index, place.core_peer()))
+        self.blocks = blocks
+
+    def start_local(self):
+        start_all(self.local)
+
+    def start_remote(self):
+        start_all(self.remote)
+
+    def wait(self, which):
+        mine = slice(which * self.blocks, (which + 1) * self.blocks)
+        for copy in self.local[mine] + self.remote[mine]:
+            copy.wait()
+
+
+def weight_gradients(place, products, sends, landings, outs, sems, after_first=()):
+    blocks, _, units = outs[0].shape
+
+    def product(lhs, rhs_ref, which, into_ref):
+        @pl.loop(0, blocks)
+        def _(block):
+            begin = pl.multiple_of((which * blocks + block) * units, units)
+            into_ref[block] = dot(lhs, rhs_ref[:, pl.ds(begin, units)]).astype(bf16)
+
+    for index, (lhs_ref, rhs_ref) in enumerate(products):
+        lhs = lhs_ref[...].T
+        product(lhs, rhs_ref, 1 - place.c, sends[index])
+        copy = send(sends[index], landings[index], sems, index, place.core_peer())
+        copy.start()
+        product(lhs, rhs_ref, place.c, outs[index])
+        copy.wait()
+
+        @pl.loop(0, blocks)
+        def _(block, index=index):
+            add_low(outs[index], (block,), outs[index][block], landings[index][block])
+
+        if index == 0:
+            start_all(after_first)
+
+
+def push_blocks(place, src, landing, sems, begin, base=0):
+    rows = pl.ds(begin, landing.shape[1])
+    return [
+        send(
+            src.at[place.y_at(apart), rows],
+            landing.at[apart - 1],
+            sems,
+            base + apart - 1,
+            place.y_peer(apart),
+        )
+        for apart in range(1, place.count_y)
+    ]
+
+
+def cut_of(blocks):
+    return blocks.shape[1] // 3 * 2
+
+
+def landing_of(blocks, rows):
+    return jax.ShapeDtypeStruct((blocks.shape[0] - 1, rows, blocks.shape[2]), bf16)
 
 
 def chunk_of(members, rows):
@@ -1169,6 +1289,7 @@
     full_ref = take(0) if gathers else None
     win_s, wout_s, made_s, returned_s, w_sems = (take(0) for _ in range(5))
     send_sems, recv_sems, back_send_sems, back_recv_sems = (take(0) for _ in range(4))
+    weight_sems = (take(0), take(0))
     members = grid_shape[1]
     slots = sent_ref.shape[0]
     rows = slots // members
@@ -1177,13 +1298,12 @@
     chunk_bits = chunks.bit_length() - 1
     hidden_units = win_s.shape[1]
     tile = min(768, hidden_units)
-    load_in = pltpu.make_async_copy(win_ref, win_s, w_sems.at[0])
-    load_out = pltpu.make_async_copy(wout_ref, wout_s, w_sems.at[1])
-    load_in.start()
-    load_out.start()
     place = Place(grid_shape)
-    more_peers = [place.core_peer()] + place.y_peers() if gathers else []
-    greet(peers_along_gy(members) + more_peers)
+    weights = Weights(place, (win_ref, wout_ref), (win_s, wout_s), w_sems, weight_sems)
+    weights.start_local()
+    more_peers = place.y_peers() if gathers else []
+    greet(peers_along_gy(members) + [place.core_peer()] + more_peers)
+    weights.start_remote()
     there = Exchange(members, rows, sent_ref, arrived_ref, send_sems, recv_sems)
     back = Exchange(members, rows, made_s, returned_s, back_send_sems, back_recv_sems)
     for apart in send_order(members):
@@ -1200,8 +1320,8 @@
         third = gather_third(place, full_ref, split, sems)
         fourth = gather_core(place, full_ref, sems)
         start_all(second)
-    load_in.wait()
-    load_out.wait()
+    weights.wait(0)
+    weights.wait(1)
     my_chunk = there.me // group
 
     def chunk_rows(index):
@@ -1268,6 +1388,10 @@
     def _(apart):
         there.copy(apart).wait_send()
         back.copy(apart).wait_send()
+
+
+def doubled(half):
+    return pltpu.VMEM((half.shape[1], 2 * half.shape[0] * half.shape[2]), bf16)
 
 
 def expert_forward(
@@ -1285,15 +1409,17 @@
     out_specs = [vmem_spec] * 3
     sems = pltpu.SemaphoreType.DMA((members,))
     scratch = [
-        pltpu.VMEM(full_in.shape, bf16),
-        pltpu.VMEM(full_out.shape, bf16),
+        doubled(full_in),
+        doubled(full_out),
         pltpu.VMEM(sent.shape, bf16),
         pltpu.VMEM(sent.shape, bf16),
-        pltpu.SemaphoreType.DMA((2,)),
+        pltpu.SemaphoreType.DMA((2 * full_in.shape[0],)),
         sems,
         sems,
         sems,
         sems,
+        pltpu.SemaphoreType.DMA((2 * full_in.shape[0],)),
+        pltpu.SemaphoreType.DMA((2 * full_in.shape[0],)),
     ]
     if gathers:
         ins.append(column)
@@ -1322,8 +1448,9 @@
     slot_col_ref,
     chosen_ref,
     logits_ref,
-    first_ref,
-    second_ref,
+    far_first_ref,
+    far_second_ref,
+    far_third_ref,
     win_ref,
     wout_ref,
     made_ref,
@@ -1342,10 +1469,16 @@
     d_gates_s,
     d_gates_back_s,
     grads_ref,
+    gin_send,
+    gin_land,
+    gout_send,
+    gout_land,
     w_sems,
     *sems,
 ):
+    far_refs = (far_first_ref, far_second_ref, far_third_ref)
     members = grid_shape[1]
+    weight_sems, sum_sems = sems[9:11], sems[11:13]
     slots = sent_ref.shape[0]
     rows = slots // members
     group = chunk_of(members, rows)
@@ -1353,11 +1486,11 @@
     chunk_bits = bits_of(chunks)
     hidden_units = win_s.shape[1]
     tile = min(768, hidden_units)
-    load_in = pltpu.make_async_copy(win_ref, win_s, w_sems.at[0])
-    load_out = pltpu.make_async_copy(wout_ref, wout_s, w_sems.at[1])
-    load_in.start()
-    load_out.start()
-    greet(peers_along_gy(members))
+    place = Place(grid_shape)
+    weights = Weights(place, (win_ref, wout_ref), (win_s, wout_s), w_sems, weight_sems)
+    weights.start_local()
+    greet(peers_along_gy(members) + [place.core_peer()])
+    weights.start_remote()
     there = Exchange(members, rows, sent_ref, arrived_s, *sems[0:2])
     back = Exchange(members, rows, d_rows_s, d_back_ref, *sems[2:4])
     gates_there = Leading(members, gates_ref, gates_s, *sems[4:6])
@@ -1367,12 +1500,14 @@
         gates_there.copy(apart).start()
         there.copy(apart).start()
 
-    collected = collect(there.me, members, rows, first_ref, second_ref, grads_ref, sems[8])
+    collected = collect(
+        there.me, members, rows, far_refs, partial(third_of, members), grads_ref, sems[8]
+    )
     start_all(collected)
     there.keep_own()
     gates_there.keep_own()
-    load_in.wait()
-    load_out.wait()
+    weights.wait(0)
+    weights.wait(1)
     wait_all(collected)
     my_chunk = there.me // group
 
@@ -1419,13 +1554,14 @@
     def _(index):
         work(index, 0)
 
-    for lhs_ref, rhs_ref, out_ref in ((d_made_s, act_s, gout_ref), (arrived_s, d_pre_s, gin_ref)):
-        lhs = lhs_ref[...].T
-
-        @pl.loop(0, hidden_units // tile)
-        def _(index, lhs=lhs, rhs_ref=rhs_ref, out_ref=out_ref):
-            units = pl.ds(pl.multiple_of(index * tile, tile), tile)
-            out_ref[:, units] = dot(lhs, rhs_ref[:, units]).astype(bf16)
+    weight_gradients(
+        place,
+        ((d_made_s, act_s), (arrived_s, d_pre_s)),
+        (gout_send, gin_send),
+        (gout_land, gin_land),
+        (gout_ref, gin_ref),
+        sum_sems,
+    )
 
     @pl.loop(1, members)
     def _(apart):
@@ -1459,12 +1595,13 @@
         jax.ShapeDtypeStruct(logits.shape, bf16),
     )
     tall = pltpu.VMEM(sent.shape, bf16)
-    wide = pltpu.VMEM((slots, full_in.shape[1]), bf16)
+    wide = pltpu.VMEM((slots, 2 * full_in.shape[0] * full_in.shape[2]), bf16)
+    half = pltpu.VMEM(full_in.shape, bf16)
     small = pltpu.VMEM(gates.shape, f32)
-    weights = pltpu.VMEM(full_in.shape, bf16)
+    weights = doubled(full_in)
     return pl.pallas_call(
         partial(expert_both_kernel, grid_shape),
-        in_specs=[vmem_spec] * 5 + [any_spec] * 4,
+        in_specs=[vmem_spec] * 5 + [any_spec] * 5,
         out_specs=[vmem_spec] * len(outs),
         out_shape=outs,
         scratch_shapes=[
@@ -1479,9 +1616,14 @@
             small,
             small,
             tall,
-            pltpu.SemaphoreType.DMA((2,)),
+            half,
+            half,
+            half,
+            half,
+            pltpu.SemaphoreType.DMA((2 * full_in.shape[0],)),
         ]
-        + [pltpu.SemaphoreType.DMA((members,))] * 9,
+        + [pltpu.SemaphoreType.DMA((members,))] * 9
+        + [pltpu.SemaphoreType.DMA((2 * full_in.shape[0],))] * 4,
         compiler_params=params(identifier),
         cost_estimate=lasting(85),
         name="expert_both",
@@ -1500,6 +1642,7 @@
     gout_ref,
     upper_ref,
     lower_ref,
+    landing_ref,
     win_s,
     wout_s,
     d_arrived_s,
@@ -1509,15 +1652,20 @@
     first_s,
     up2_s,
     low2_s,
+    gin_send,
+    gin_land,
+    gout_send,
+    gout_land,
     w_sems,
     send_sems,
     recv_sems,
     back_send_sems,
     back_recv_sems,
-    *sum_sems,
+    *more_sems,
 ):
     members = grid_shape[1]
-    place = Place(grid_shape)
+    sum_sems, weight_sems, gradient_sems = more_sems[0:2], more_sems[2:4], more_sems[4:6]
+    push_sems = more_sems[6:8]
     slots = d_sent_ref.shape[0]
     rows = slots // members
     group = chunk_of(members, rows)
@@ -1525,11 +1673,11 @@
     chunk_bits = chunks.bit_length() - 1
     hidden_units = win_s.shape[1]
     tile = min(768, hidden_units)
-    load_in = pltpu.make_async_copy(win_ref, win_s, w_sems.at[0])
-    load_out = pltpu.make_async_copy(wout_ref, wout_s, w_sems.at[1])
-    load_in.start()
-    load_out.start()
+    place = Place(grid_shape)
+    weights = Weights(place, (win_ref, wout_ref), (win_s, wout_s), w_sems, weight_sems)
+    weights.start_local()
     greet(peers_along_gy(members) + [place.core_peer()] + place.y_peers())
+    weights.start_remote()
     landings = (first_s, up2_s, low2_s, upper_ref, lower_ref, None, None)
     sums = Scatter(place, blocks_ref, landings, sum_sems, upper_ref.shape[1])
     there = Exchange(members, rows, d_sent_ref, d_arrived_s, send_sems, recv_sems)
@@ -1539,7 +1687,7 @@
     there.keep_own()
     my_chunk = there.me // group
     start_all(sums.copies(0))
-    load_in.wait()
+    weights.wait(0)
 
     @pl.loop(0, slots // 256)
     def _(index):
@@ -1554,7 +1702,7 @@
     wait_all(sums.copies(0))
     sums.add(0)
     start_all(sums.copies(1))
-    load_out.wait()
+    weights.wait(1)
 
     def chunk_rows(index):
         start = xor_of(my_chunk, index, chunk_bits) * (group * rows)
@@ -1585,17 +1733,16 @@
     wait_all(sums.copies(1))
     sums.add(1)
     start_all(sums.copies(2))
-    for lhs_ref, rhs_ref, out_ref in (
-        (d_arrived_s, act_s, gout_ref),
-        (arrived_ref, slope_s, gin_ref),
-    ):
-        lhs = lhs_ref[...].T
-
-        @pl.loop(0, hidden_units // tile)
-        def _(index, lhs=lhs, rhs_ref=rhs_ref, out_ref=out_ref):
-            units = pl.ds(pl.multiple_of(index * tile, tile), tile)
-            out_ref[:, units] = dot(lhs, rhs_ref[:, units]).astype(bf16)
-
+    pushed = push_blocks(place, gout_ref, landing_ref, push_sems, 0)
+    weight_gradients(
+        place,
+        ((d_arrived_s, act_s), (arrived_ref, slope_s)),
+        (gout_send, gin_send),
+        (gout_land, gin_land),
+        (gout_ref, gin_ref),
+        gradient_sems,
+        pushed,
+    )
     wait_all(sums.copies(2))
     sums.add(2)
 
@@ -1604,6 +1751,8 @@
         back.copy(apart).wait_recv()
         there.copy(apart).wait_send()
         back.copy(apart).wait_send()
+
+    wait_all(pushed)
 
 
 def expert_backward(d_sent, arrived, blocks, full_in, full_out, grid_shape, identifier):
@@ -1614,33 +1763,153 @@
         jax.ShapeDtypeStruct(full_in.shape, bf16),
         jax.ShapeDtypeStruct(full_out.shape, bf16),
         *[jax.ShapeDtypeStruct(one, bf16) for one in landings[3:5]],
+        landing_of(full_out, cut_of(full_out)),
     )
     slots = d_sent.shape[0]
     sems = pltpu.SemaphoreType.DMA((members,))
     return pl.pallas_call(
         partial(expert_backward_kernel, grid_shape),
         in_specs=[vmem_spec] * 3 + [any_spec] * 2,
-        out_specs=[vmem_spec] * len(outs),
+        out_specs=[vmem_spec] * (len(outs) - 1) + [any_spec],
         out_shape=outs,
         scratch_shapes=[
-            pltpu.VMEM(full_in.shape, bf16),
-            pltpu.VMEM(full_out.shape, bf16),
+            doubled(full_in),
+            doubled(full_out),
             pltpu.VMEM(d_sent.shape, bf16),
             pltpu.VMEM(d_sent.shape, bf16),
-            pltpu.VMEM((slots, full_in.shape[1]), bf16),
-            pltpu.VMEM((slots, full_in.shape[1]), bf16),
+            pltpu.VMEM((slots, 2 * full_in.shape[0] * full_in.shape[2]), bf16),
+            pltpu.VMEM((slots, 2 * full_in.shape[0] * full_in.shape[2]), bf16),
             *[pltpu.VMEM(one, bf16) for one in landings[:3]],
-            pltpu.SemaphoreType.DMA((2,)),
+            *[pltpu.VMEM(full_in.shape, bf16)] * 4,
+            pltpu.SemaphoreType.DMA((2 * full_in.shape[0],)),
             sems,
             sems,
             sems,
             sems,
             *[pltpu.SemaphoreType.DMA((scatter_copies(grid_shape),))] * 2,
+            *[pltpu.SemaphoreType.DMA((2 * full_in.shape[0],))] * 4,
+            *[pltpu.SemaphoreType.DMA((full_in.shape[0] - 1,))] * 2,
         ],
         compiler_params=params(10 + identifier),
         cost_estimate=lasting(85),
         name="expert_backward",
     )(d_sent, arrived, blocks, full_in, full_out)
+
+
+def emit_kernel(
+    table_shape,
+    at_ref,
+    gin_ref,
+    gin_first_ref,
+    gin_second_ref,
+    gin_up_ref,
+    gout_ref,
+    gout_first_ref,
+    gout_second_ref,
+    gout_up_ref,
+    result_ref,
+    grad_ref,
+    packed_ref,
+    small_ref,
+    gin_out_ref,
+    gout_out_ref,
+    result_out_ref,
+    grad_out_ref,
+    wq_ref,
+    wk_ref,
+    wv_ref,
+    wo_ref,
+    router_out_ref,
+    gga_ref,
+    ggf_ref,
+    table_ref,
+):
+    step = pl.program_id(0)
+
+    def landed(ref):
+        total = ref[0].astype(f32)
+        for index in range(1, ref.shape[0]):
+            total = total + ref[index].astype(f32)
+        return total
+
+    begins = step < pl.num_programs(0) // 3 * 2
+    for own, first, second, up, out in (
+        (gin_ref, gin_first_ref, gin_second_ref, gin_up_ref, gin_out_ref),
+        (gout_ref, gout_first_ref, gout_second_ref, gout_up_ref, gout_out_ref),
+    ):
+        out[0, 0] = own[0].astype(f32) + jnp.where(begins, landed(first), landed(second))
+        out[1, 0] = up[...].astype(f32)
+
+    @pl.when(step == 0)
+    def _():
+        result_out_ref[...] = result_ref[...]
+        grad_out_ref[...] = grad_ref[...]
+        layers, tall, wide = wq_ref.shape
+        for which, ref in enumerate((wq_ref, wk_ref, wv_ref, wo_ref)):
+            ref[...] = packed_ref[:, :, which * wide : (which + 1) * wide]
+        buckets_count, heads = table_shape
+        width = small_ref.shape[1]
+        experts = (small_ref.shape[0] - 2 * layers - heads) // layers
+        base = layers * experts
+        gga_ref[...] = small_ref[base : base + layers, :]
+        ggf_ref[...] = small_ref[base + layers : base + 2 * layers, :]
+        base = base + 2 * layers
+        table_ref[...] = small_ref[base : base + heads, :buckets_count]
+        for layer in range(layers):
+            row = small_ref[pl.ds(layer * experts + at_ref[1], 1), :]
+            row = jnp.broadcast_to(row, (8, width))
+            mine = pltpu.roll(row, lax.rem(width - at_ref[0] * tall, width), 1)
+            router_out_ref[layer] = mine[0:1, :tall]
+
+
+def emit(at, grads_in, grads_out, result, grad_now, packed, small, table_shape):
+    layers, tall, lanes = packed.shape
+    gin, gin_first, gin_second, gin_up = grads_in
+    gout, gout_first, gout_second, gout_up = grads_out
+    _, rows, units = gin.shape
+    steps = 6
+    early_steps = steps // 3 * 2
+    tile = rows // steps
+    wide = lanes // 4
+    whole_in = [result, grad_now, packed, small]
+    own = pl.BlockSpec((1, tile, units), lambda i, at: (at[2], i, 0))
+    up = pl.BlockSpec((tile, units), lambda i, at: (i, 0))
+
+    def land(array, index):
+        return pl.BlockSpec((array.shape[0], tile, units), lambda i, at: (0, index(i), 0))
+
+    out = pl.BlockSpec((layers, 1, tile, units), lambda i, at: (0, 0, i, 0))
+    expert = jax.ShapeDtypeStruct((layers, 1, rows, units), f32)
+    square = jax.ShapeDtypeStruct((layers, tall, wide), f32)
+    gain = jax.ShapeDtypeStruct((layers, small.shape[1]), f32)
+    rest = [jax.ShapeDtypeStruct(result.shape, f32)] * 2 + [square] * 4
+    rest += [jax.ShapeDtypeStruct((layers, 1, tall), f32), gain, gain]
+    rest.append(jax.ShapeDtypeStruct(table_shape[::-1], f32))
+
+    def first_index(i):
+        return jnp.minimum(i, early_steps - 1)
+
+    def second_index(i):
+        return jnp.maximum(i - early_steps, 0)
+
+    def expert_specs(first_land, second_land):
+        return [own, land(first_land, first_index), land(second_land, second_index), up]
+
+    return pl.pallas_call(
+        partial(emit_kernel, table_shape),
+        grid_spec=pltpu.PrefetchScalarGridSpec(
+            num_scalar_prefetch=1,
+            grid=(steps,),
+            in_specs=expert_specs(gin_first, gin_second)
+            + expert_specs(gout_first, gout_second)
+            + whole_of(whole_in),
+            out_specs=[out, out] + whole_of(rest),
+        ),
+        out_shape=[expert, expert] + rest,
+        compiler_params=params(),
+        cost_estimate=lasting(7),
+        name="emit",
+    )(at, *grads_in, *grads_out, *whole_in)
 
 
 def body(
@@ -1670,11 +1939,12 @@
     wide_router = w_router.shape[2]
     tall, wide = w_query.shape[1], w_query.shape[2]
     grid_shape = (count_x, count_y)
+    same_core = [list(range(core, count_x, 2)) for core in range(2)]
     router_rows = jnp.pad(
         w_router.transpose(0, 2, 1), ((0, 0), (0, tile_rows - wide_router), (0, 4 * wide - tall))
     )
     buckets_row = jnp.pad(buckets, (0, 1), constant_values=-1)[None, :]
-    mats, router, later, bias, slot_col, slot_row, chosen_f, spread = start(
+    mats, router, later, bias, slot_col, slot_row, chosen_f, spread, far_part = start(
         (w_query, w_key, w_value, w_output),
         router_rows,
         buckets_row,
@@ -1690,7 +1960,7 @@
     hidden = hidden_in
     kept = []
     blocks = None
-    far_parts = []
+    far_parts = [far_part]
     for layer in range(layers):
         last = layer == layers - 1
         gains = (gain_attn_f[layer][None], gain_ffn_f[layer][None])
@@ -1708,8 +1978,10 @@
             mats=(mats, router) if blocks is None else None,
         )
         far_parts.append(far_part)
-        full_in = lax.all_gather(w_in[layer, 0], "gx", axis=1, tiled=True)
-        full_out = lax.all_gather(w_out[layer, 0], "gx", axis=1, tiled=True)
+        full_in, full_out = (
+            lax.all_gather(one[layer, 0], "gx", axis=0, tiled=False, axis_index_groups=same_core)
+            for one in (w_in, w_out)
+        )
         state = (hidden, gains, (mats, router), (q, k, v), attended, lse, middle, logits)
         if last:
             made, d_back, grad_in_full, grad_out_full, d_logits = expert_both(
@@ -1740,12 +2012,18 @@
         (prior, gains, mats, q_k_v, attended, lse, middle, logits) = kept[layer][:8]
         if not last:
             arrived, full_in, full_out = kept[layer][9:]
-            d_back, grad_in_full, grad_out_full, upper, lower = expert_backward(
+            d_back, grad_in_full, grad_out_full, upper, lower, out_first = expert_backward(
                 d_sent, arrived, parts[-1][0], full_in, full_out, grid_shape, layer
             )
             partials.append((upper, lower[:1]))
-        grad_out_part = lax.psum_scatter(grad_out_full, "gx", scatter_dimension=1, tiled=True)
-        grad_in_part = lax.psum_scatter(grad_in_full, "gx", scatter_dimension=1, tiled=True)
+        experts_parts = []
+        if layer > 0:
+            experts_parts = [
+                lax.psum_scatter(
+                    one, "gx", scatter_dimension=0, tiled=False, axis_index_groups=same_core
+                )
+                for one in (grad_in_full, grad_out_full)
+            ]
         below = None
         if layer > 0:
             below = (kept[layer - 1][8], slot_row, chosen_f, kept[layer - 1][7])
@@ -1764,51 +2042,55 @@
             lse,
             grid_shape,
             below=below,
-            after=[array for part in parts for array in part[4:6]],
+            after=[array for part in parts for array in part[4]],
             made=made,
             returns=last,
+            push=(grad_out_full, grad_in_full) if layer == 0 else None,
             identifier=18 + layer,
         )
         grad_now, blocked, gwr, gga, ggf, offset_sums = got[:6]
         if layer > 0:
             d_sent, d_logits = got[6:8]
+        if layer == 0:
+            *got, out_second, in_first = got
         returned.append(got[-1])
-        offset_sums = offset_sums.reshape(heads, 2 * seq_len)
-        parts.append((blocked, gwr, gga, ggf, grad_in_part, grad_out_part, offset_sums))
+        parts.append((blocked, gwr, gga, ggf, experts_parts, offset_sums))
     parts = parts[::-1]
     buckets_count = rel_table.shape[0]
-    smalls = [part[which] for which in (1, 2, 3, 6) for part in parts]
+    smalls = [part[which] for which in (1, 2, 3, 5) for part in parts]
     top = kept[-1]
-    *attn_grads, small, hidden_out = final_sums(
+    packed, small, hidden_out, in_second = final_sums(
         parts[0][0],
         partials[::-1],
         smalls + [buckets_row],
         (slot_col, chosen_f, top[7], top[6]),
         returned,
+        grad_in_full,
         grid_shape,
-        wide,
         buckets_count,
     )
-    router_sum = small[: layers * experts].reshape(layers, experts, width)
-    base = layers * experts
-    gga_all, ggf_all = small[base : base + layers], small[base + layers : base + 2 * layers]
-    base = base + 2 * layers
-    d_table = small[base : base + heads, :buckets_count].T
-    router_mine = lax.dynamic_slice(
-        router_sum,
-        (0, lax.axis_index("gy") * wide_router, lax.axis_index("gx") * tall),
-        (layers, wide_router, tall),
-    ).transpose(0, 2, 1)
-    grad_in = jnp.stack([part[4] for part in parts]).astype(f32)[:, None]
-    grad_out = jnp.stack([part[5] for part in parts]).astype(f32)[:, None]
+    first, second = lax.axis_index("gx"), lax.axis_index("gy")
+    grad_in, grad_out, hidden_out, grad_now, gwq, gwk, gwv, gwo, gwr, gga_all, ggf_all, d_table = emit(
+        jnp.stack([first, second, first // 2]).astype(jnp.int32),
+        (grad_in_full, in_first, in_second, parts[1][4][0]),
+        (grad_out_full, out_first, out_second, parts[1][4][1]),
+        hidden_out,
+        grad_now,
+        packed,
+        small,
+        rel_table.shape,
+    )
     return (
         hidden_out,
         grad_now,
-        d_table,
+        d_table.T,
         gga_all,
         ggf_all,
-        *attn_grads,
-        router_mine,
+        gwq,
+        gwk,
+        gwv,
+        gwo,
+        gwr.transpose(0, 2, 1),
         grad_in,
         grad_out,
     )

time: 543 us -> 525 us (0.967)
  local copies, waits for them, and re-layouts: 19.6 us -> 6.71 us
  other arithmetic: 7.74 us -> 0.56 us
    pallas_call x2, Pallas kernels: 65.2 us -> 49.4 us  [attention_forward(): pl.pallas_call(partial(forward_kernel, head_dim, grid_shape, blocked, las...]
    pallas_call x0 -> x1, Pallas kernels: none -> 12 us  [emit(): pl.pallas_call(partial(emit_kernel, table_shape), grid_spec=pltpu.Prefetc...]
    pallas_call x1, Pallas kernels: 73.2 us -> 81.4 us  [expert_backward(): pl.pallas_call(partial(expert_backward_kernel, grid_shape), in_specs=[vme...]
    convert_element_type x2 -> x0, other arithmetic: 7.74 us -> none  [the longest x1 3.88 us: body(): grad_in = jnp.stack([part[4] for part in parts]).astype(f32)[:, None]]
    unnamed x34 -> x10, local copies, waits for them, and re-layouts: 6.58 us -> 0.02 us
  transfers between devices with their start and end apart: 8 -> 6, of which waited for: 0 -> 0; matrix products, arithmetic and copies ran while one was open for 2% -> 1% of each run, Pallas kernels for 78% -> 61%
where the time goes in v5:
time: 525 us; the launch traced here: 520 us
  Pallas kernels  497 us (95%)
  between operations  14.5 us (3%)
  local copies, waits for them, and re-layouts  6.71 us (1%)
    pallas_call x2, Pallas kernels, attention_backward(): pl.pallas_call(partial(backward_kernel, head_dim, grid_shape, spreads, re...  86.4 us
    pallas_call x1, Pallas kernels, expert_backward(): pl.pallas_call(partial(expert_backward_kernel, grid_shape), in_specs=[vme...  81.4 us
    pallas_call x1, Pallas kernels, expert_forward(): pl.pallas_call(partial(expert_forward_kernel, grid_shape, gathers), in_sp...  72 us
    pallas_call x1, Pallas kernels, expert_both(): pl.pallas_call(partial(expert_both_kernel, grid_shape), in_specs=[vmem_sp...  71.6 us
    pallas_call x1, Pallas kernels, start(): pl.pallas_call(partial(start_kernel, grid_shape), in_specs=[vmem_spec] *...  67.6 us
    pallas_call x1, Pallas kernels, final_sums(): pl.pallas_call(partial(final_kernel, grid_shape, layers, buckets_count),...  56.5 us
    pallas_call x2, Pallas kernels, attention_forward(): pl.pallas_call(partial(forward_kernel, head_dim, grid_shape, blocked, las...  49.4 us
    pallas_call x1, Pallas kernels, emit(): pl.pallas_call(partial(emit_kernel, table_shape), grid_spec=pltpu.Prefetc...  12 us
  transfers between devices with their start and end apart: 6, of which 0 were waited for; matrix products, arithmetic and copies ran while one was open for 1% of the time, Pallas kernels for 61%

profile of v5, /device:TPU:0, one launch (start us, length us, event | category | flops | bytes accessed | tf_op | source)
XLA Modules:
  0.0 520.3 jit_solution(18085627745761327804)
XLA Ops:
  7.2 0.0 all-gather.9.cloned.1.call-start
  7.2 0.0 copy-start
  7.2 3.3 fusion.1
  10.6 0.0 all-gather.9.cloned.1.call-update
  10.6 0.0 all-gather.11.cloned.1.call-start
  10.6 0.0 copy-done
  10.6 1.6 fusion
  12.2 0.0 copy-start.4
  12.2 0.0 copy-start.3
  12.2 0.0 copy-start.1
  12.2 0.0 copy-start.2
  12.2 0.0 all-gather.11.cloned.1.call-update
  12.2 0.0 all-gather.13.cloned.1.call-start
  12.3 0.7 all-gather.13.cloned.1.call-update
  13.0 0.0 all-gather.15.cloned.1.call-start
  13.0 0.5 all-gather.15.cloned.1.call-update
  13.6 0.0 reduce-scatter.3.cloned.1.call-start
  13.6 0.0 copy-done.4
  13.6 0.0 copy-done.3
  13.6 0.6 pad.9
  14.2 0.6 pad.8.router_rows_ref
  14.8 0.0 copy-done.1
  14.8 0.0 copy-done.2
  14.8 0.6 fusion.2
  15.4 67.6 %start.1 = (bf16[4,768,768]{2,1,0:T(8,128)(2,1)}, bf16[8,768]{1,0:T(8,128)(2,1)}, bf16[1,4,208,384]{3,2,1,0:T(8,128)(2,1)}, bf16[12,512,512]{2,1,0:T(8,128)(2,1)...) custom-call(bf16[2,192,96]{2,1,0:T(8,128)(2,1)} %wq_ref.1, ...), custom_call_target="tpu_custom_call" | custom-call | flops 44999999488 | bytes 1048576 | tf_op jit(solution)/shard_map/start/pallas_call | solution.py:624
  83.1 20.9 %attention_forward.2 = (bf16[512,768]{1,0:T(8,128)(2,1)}, bf16[512,768]{1,0:T(8,128)(2,1)}, bf16[512,768]{1,0:T(8,128)(2,1)}, bf16[768,512]{1,0:T(8,128)(2,1)}, ...) custom-call(bf16[512,768]{1,0:T(8,128)(2,1)} %hidden_ref.3, ...), custom_call_target="tpu_custom_call" | custom-call | flops 24999999488 | bytes 1048576 | tf_op jit(solution)/shard_map/attention_forward/pallas_call | solution.py:802
  104.0 0.0 all-gather.9.cloned.1.call-done
  104.1 0.0 all-gather.11.cloned.1.call-done
  104.1 72.0 %expert_forward.1 = (bf16[1024,768]{1,0:T(8,128)(2,1)}, f32[512,768]{1,0:T(8,128)}, f32[512,768]{1,0:T(8,128)}, bf16[2,2,4,2,208,384]{5,4,3,2,1,0:T(8,128)(2,1)}) custom-call(bf16[1024,768]{1,0:T(8,128)(2,1)} %get-tuple-element.98.sent_ref, s32[512,1]{1,0:T(8,128)} %get-tuple-element.92.slot_col_ref.refs_12_, ...), custom_call_target="tpu_custom_call" | custom-call | flops 74999996416 | bytes 1048576 | tf_op jit(solution)/shard_map/expert_forward/pallas_call | solution.py:1432
  176.1 28.5 %attention_forward.3 = (bf16[4,768,768]{2,1,0:T(8,128)(2,1)}, bf16[8,768]{1,0:T(8,128)(2,1)}, bf16[512,768]{1,0:T(8,128)(2,1)}, bf16[512,768]{1,0:T(8,128)(2,1)}...) custom-call(f32[512,768]{1,0:T(8,128)} %get-tuple-element.102.hidden, ...), custom_call_target="tpu_custom_call" | custom-call | flops 24999999488 | bytes 1048576 | tf_op jit(solution)/shard_map/attention_forward/pallas_call | solution.py:802
  204.5 0.0 all-gather.13.cloned.1.call-done
  204.6 0.0 all-gather.15.cloned.1.call-done
  204.6 71.6 %expert_both.1 = (bf16[1024,768]{1,0:T(8,128)(2,1)}, bf16[1024,768]{1,0:T(8,128)(2,1)}, bf16[2,768,768]{2,1,0:T(8,128)(2,1)}, bf16[2,768,768]{2,1,0:T(8,128)(2,1)}, bf16[512,8]{1,0:T(8,128)(2,1)}) custom-call(bf16[1024,768]{1,0:T(8,128)(2,1)} %get-tuple-element.104.sent_ref, f32[8,8,128]{2,1,0:T(8,128)} %get-tuple-element.105.gates_ref, ...), custom_call_target="tpu_custom_call" | custom-call | flops 85000003584 | bytes 1048576 | tf_op jit(solution)/shard_map/expert_both/pallas_call | solution.py:1602
  276.2 0.0 reduce-scatter.3.cloned.1.call-update
  276.2 0.0 reduce-scatter.5.cloned.1.call-start
  276.3 0.6 pad_add_fusion.at_ref
  276.8 0.0 reduce-scatter.5.cloned.1.call-update
  276.9 47.7 %attention_backward.2 = (f32[512,768]{1,0:T(8,128)}, bf16[2,2,4,2,192,384]{5,4,3,2,1,0:T(8,128)(2,1)}, f32[8,768]{1,0:T(8,128)}, f32[1,768]{1,0:T(1,128)}, f32[1...) custom-call(bf16[1024,768]{1,0:T(8,128)(2,1)} %get-tuple-element.110, ...), custom_call_target="tpu_custom_call" | custom-call | flops 32000000000 | bytes 1048576 | tf_op jit(solution)/shard_map/attention_backward/pallas_call | solution.py:1069
  324.6 81.4 %expert_backward.1 = (bf16[1024,768]{1,0:T(8,128)(2,1)}, bf16[2,768,768]{2,1,0:T(8,128)(2,1)}, bf16[2,768,768]{2,1,0:T(8,128)(2,1)}, bf16[4,96,384]{2,1,0:T(8,12...) custom-call(bf16[1024,768]{1,0:T(8,128)(2,1)} %get-tuple-element.122.d_sent_ref, ...), custom_call_target="tpu_custom_call" | custom-call | flops 85000003584 | bytes 1048576 | tf_op jit(solution)/shard_map/expert_backward/pallas_call | solution.py:1770
  405.9 0.0 reduce-scatter.3.cloned.1.call-done
  406.0 0.0 reduce-scatter.5.cloned.1.call-done
  406.0 38.7 %attention_backward.3 = (f32[512,768]{1,0:T(8,128)}, bf16[2,2,4,2,192,384]{5,4,3,2,1,0:T(8,128)(2,1)}, f32[8,768]{1,0:T(8,128)}, f32[1,768]{1,0:T(1,128)}, f32[1...) custom-call(bf16[1024,768]{1,0:T(8,128)(2,1)} %get-tuple-element.126, ...), custom_call_target="tpu_custom_call" | custom-call | flops 32000000000 | bytes 1048576 | tf_op jit(solution)/shard_map/attention_backward/pallas_call | solution.py:1069
  444.7 56.5 %final_sums.1 = (f32[2,192,384]{2,1,0:T(8,128)}, f32[32,768]{1,0:T(8,128)}, f32[512,768]{1,0:T(8,128)}, bf16[1,256,768]{2,1,0:T(8,128)(2,1)}) custom-call(bf16[2,2,4,2,192,384]{5,4,3,2,1,0:T(8,128)(2,1)} %get-tuple-element.138.refs_0_, bf16[4,96,384]{2,1,0:T(8,128)(2,1)} %get-tuple-element.139.refs_1_, bf16[1,4,96,384]{3,2,1,0:T(8,128)(2,1)} %get-tuple-element.140.refs_2_, ...), custom_call_target="tpu_custom_call" | custom-call | flops 60000002048 | bytes 1048576 | tf_op jit(solution)/shard_map/final_sums/pallas_call | solution.py:430
  501.2 12.0 %emit.1 = (f32[2,1,768,768]{3,2,1,0:T(8,128)}, f32[2,1,768,768]{3,2,1,0:T(8,128)}, f32[512,768]{1,0:T(8,128)}, f32[512,768]{1,0:T(8,128)}, f32[2,192,96]{2,1,0:T...) custom-call(s32[3]{0:T(128)} %pad_add_fusion.at_ref, ...), custom_call_target="tpu_custom_call" | custom-call | flops 7000000000 | bytes 1048576 | tf_op jit(solution)/shard_map/emit/pallas_call | solution.py:1898
  (1 shorter events, 0.0 us)
Async XLA Ops:
  7.2 96.9 %all-gather.9.cloned.1.call-start = ((), (), s32[]{:S(2)}) async-start(), calls=%async_computation.4 | async-start | bytes 3538944 | tf_op jit(solution)/shard_map/all_gather | solution.py:1982
  7.2 3.4 copy-start
  10.6 93.5 %all-gather.11.cloned.1.call-start = ((), (), s32[]{:S(2)}) async-start(), calls=%async_computation.5 | async-start | bytes 3538944 | tf_op jit(solution)/shard_map/all_gather | solution.py:1982
  12.2 1.4 copy-start.4
  12.2 1.4 copy-start.3
  12.2 2.6 copy-start.1
  12.2 2.6 copy-start.2
  12.2 192.3 %all-gather.13.cloned.1.call-start = ((), (), s32[]{:S(2)}) async-start(), calls=%async_computation.6 | async-start | bytes 3538944 | tf_op jit(solution)/shard_map/all_gather | solution.py:1982
  13.0 191.6 %all-gather.15.cloned.1.call-start = ((), (), s32[]{:S(2)}) async-start(), calls=%async_computation.7 | async-start | bytes 3538944 | tf_op jit(solution)/shard_map/all_gather | solution.py:1982
  13.6 392.4 %reduce-scatter.3.cloned.1.call-start = ((), (), s32[]{:S(2)}) async-start(), calls=%async_computation.2 | async-start | bytes 3538944 | tf_op jit(solution)/shard_map/reduce_scatter | solution.py:2022
  276.2 129.8 %reduce-scatter.5.cloned.1.call-start = ((), (), s32[]{:S(2)}) async-start(), calls=%async_computation.3 | async-start | bytes 3538944 | tf_op jit(solution)/shard_map/reduce_scatter | solution.py:2022
Sparse Core Ops, SparseCore 0:
  10.7 50.9 all-gather.8
  63.8 37.0 all-gather.10
  103.0 49.5 all-gather.12
  154.5 36.5 all-gather.14
  276.3 46.3 reduce-scatter.2
  324.9 40.0 reduce-scatter.4

commit v6 on v5

--- a/solution.py
+++ b/solution.py
@@ -141,6 +141,17 @@
 def wait_all(copies):
     for copy in copies:
         copy.wait()
+
+
+def local_copies(pairs, sems, base=0):
+    return [
+        pltpu.make_async_copy(src, dst, sems.at[base + index])
+        for index, (src, dst) in enumerate(pairs)
+    ]
+
+
+def scratch_of(arrays):
+    return [pltpu.VMEM(array.shape, array.dtype) for array in arrays]
 
 
 def gather_z(place, src, landing, sems):
@@ -209,8 +220,9 @@
 
 
 class Scatter:
-    def __init__(self, place, src, landings, sems, split):
+    def __init__(self, place, src, landings, sems, split, source=None):
         self.place, self.src, self.sems = place, src, sems
+        self.source = src if source is None else source
         self.first, self.up2, self.low2, self.up3, self.low3, self.up4, self.low4 = landings
         tall = src.shape[4]
         self.upper, self.lower = pl.ds(0, split), pl.ds(split, tall - split)
@@ -219,7 +231,7 @@
         at, sems = self.place, self.sems
         count_y, count_z = at.count_y, at.count_z
         if stage == 0:
-            return [send(self.src.at[:, 1 - at.c], self.first, sems, 0, at.core_peer())]
+            return [send(self.source.at[:, 1 - at.c], self.first, sems, 0, at.core_peer())]
         if stage == 1:
             copies = [send(self.first.at[:, :, 1 - at.x, self.lower], self.low2, sems, 1, at.x_peer())]
             for apart in range(1, count_y):
@@ -320,12 +332,13 @@
 def final_kernel(grid_shape, layers, buckets_count, *refs):
     refs = list(refs)
     take = refs.pop
-    blocks_ref = take(0)
     partial_refs = [(take(0), take(0)) for _ in range(layers - 1)]
     router_refs, gga_refs, ggf_refs, offset_refs = ([take(0) for _ in range(layers)] for _ in range(4))
-    buckets_ref, slot_col_ref, chosen_ref, logits_ref, middle_ref = (take(0) for _ in range(5))
+    buckets_ref, slot_col_ref, chosen_ref, logits_ref = (take(0) for _ in range(4))
+    blocks_in_ref, middle_in_ref = take(0), take(0)
     first_ref, second_ref, push_ref = take(0), take(0), take(0)
     packed_ref, small_out_ref, result_ref, landing_ref = (take(0) for _ in range(4))
+    blocks_ref, middle_ref, move_sems = (take(0) for _ in range(3))
     landings = [take(0) for _ in range(7)]
     z_landings = [(take(0), take(0)) for _ in range(layers - 1)]
     totals, landing, returned_s = take(0), take(0), take(0)
@@ -341,7 +354,12 @@
         upper, lower = partial_refs[layer - 1]
         places = (None, None, None, upper, lower, *z_landings[layer - 1])
         upper_layers.append(Scatter(place, blocks_ref, places, sems[layer], split))
-    lowest = Scatter(place, blocks_ref, landings, sems[0], split)
+    lowest = Scatter(place, blocks_ref, landings, sems[0], split, blocks_in_ref)
+    c = place.c
+    moves = local_copies(
+        [(blocks_in_ref.at[:, c], blocks_ref.at[:, c]), (middle_in_ref, middle_ref)], move_sems
+    )
+    start_all(moves)
     collected = collect(
         lax.axis_index("gy"),
         members,
@@ -376,7 +394,7 @@
     )
     small = SmallSum(grid_shape, totals, landing, small_sems)
     small.begin()
-    wait_all(lowest.copies(0))
+    wait_all(moves + lowest.copies(0))
     lowest.add(0)
     start_all(lowest.copies(1))
     small.advance()
@@ -425,14 +443,17 @@
     small_sems = pltpu.SemaphoreType.DMA((steps,))
     outs = [jax.ShapeDtypeStruct((layers, tall, shape[5]), f32)]
     outs += [jax.ShapeDtypeStruct(small_shape, f32), jax.ShapeDtypeStruct(finishing[-1].shape, f32)]
-    outs.append(landing_of(push, push.shape[1] - cut_of(push)))
-    ins = [blocks, *[array for pair in partials for array in pair], *smalls, *finishing]
+    outs.append(landing_of(push, push.shape[1] - push.shape[1] // 2))
+    ins = [*[array for pair in partials for array in pair], *smalls, *finishing[:3]]
+    moved = [blocks, finishing[-1]]
     return pl.pallas_call(
         partial(final_kernel, grid_shape, layers, buckets_count),
-        in_specs=[vmem_spec] * len(ins) + [any_spec] * 3,
+        in_specs=[vmem_spec] * len(ins) + [any_spec] * 5,
         out_specs=[vmem_spec] * (len(outs) - 1) + [any_spec],
         out_shape=outs,
-        scratch_shapes=landings
+        scratch_shapes=scratch_of(moved)
+        + [pltpu.SemaphoreType.DMA((2,))]
+        + landings
         + landings[5:] * (layers - 1)
         + [pltpu.VMEM((steps + 1, *small_shape), f32), pltpu.VMEM((steps, *small_shape), f32)]
         + [pltpu.VMEM(returned[0].shape, bf16)]
@@ -442,7 +463,7 @@
         compiler_params=params(24),
         cost_estimate=lasting(60),
         name="final_sums",
-    )(*ins, *returned, push)
+    )(*ins, *moved, *returned, push)
 
 
 def unblock(grid_shape, blocks_ref, mats_ref, router_ref):
@@ -486,12 +507,15 @@
     mats_ref,
     router_ref,
     later_ref,
-    bias_ref,
+    bias_out_ref,
     slot_col_ref,
     slot_row_ref,
     chosen_ref,
+    spread_out_ref,
+    far_ref,
+    bias_ref,
     spread_ref,
-    far_ref,
+    write_sems,
     full_s,
     column_s,
     spread_send,
@@ -518,6 +542,14 @@
         members, spread_ref.shape[0] // members, spread_ref, far_ref, spread_send, spread_recv
     )
     spread_copies = [spread.copy(apart) for apart in in_third(members, 0)]
+    mine_here = spread.block(spread.me)
+    half_heads = bias_ref.shape[0] // 2
+    parts = [pl.ds(0, half_heads), pl.ds(half_heads, half_heads)]
+    write_spread, write_own, *write_bias = local_copies(
+        [(spread_ref, spread_out_ref), (spread_ref.at[mine_here, :], far_ref.at[mine_here, :])]
+        + [(bias_ref.at[part], bias_out_ref.at[part]) for part in parts],
+        write_sems,
+    )
     greet(
         [place.core_peer(), place.x_peer()]
         + place.y_peers()
@@ -558,6 +590,7 @@
     slot_col_ref[...] = route_col * capacity + rank_col.astype(jnp.int32)
     placing = placing_rows(slot_row_ref[...], spread_ref.shape[0])
     spread_ref[...] = dot(placing, cotangent_ref[...]).astype(bf16)
+    start_all([write_spread, write_own])
 
     same = (piece_col == piece_row) & (piece_col > 0)
     allowed = (key_pos <= query_pos) | same
@@ -575,10 +608,11 @@
     start_all(second)
     start_all(along_z)
     start_all(spread_copies)
-    spread.keep_own()
+    write_bias[0].start()
     full_s[y, c, :, x] = column_s[...]
     for head in range(heads // 2, heads):
         bias_for(head)
+    write_bias[1].start()
     wait_all(second)
     third = gather_third(place, full_s, split, sems)
     start_all(third)
@@ -590,6 +624,7 @@
     unblock(grid_shape, full_s, mats_ref, router_ref)
     wait_all(along_z)
     wait_all(spread_copies)
+    wait_all([write_spread, write_own, *write_bias])
 
 
 def start(mats, router_rows, buckets, table_t, piece_ids, route, cotangent, grid_shape):
@@ -624,9 +659,11 @@
     return pl.pallas_call(
         partial(start_kernel, grid_shape),
         in_specs=[vmem_spec] * len(ins),
-        out_specs=[vmem_spec] * len(outs),
+        out_specs=[vmem_spec] * 3 + [any_spec] + [vmem_spec] * 3 + [any_spec] * 2,
         out_shape=outs,
         scratch_shapes=[
+            *scratch_of([outs[3], outs[7]]),
+            pltpu.SemaphoreType.DMA((4,)),
             pltpu.VMEM((*half, *block), bf16),
             pltpu.VMEM((half[2], *block), bf16),
             pltpu.SemaphoreType.DMA((experts,)),
@@ -681,13 +718,18 @@
     mats_ref, router_ref = (None, None) if blocked else (take(0), take(0))
     spread_ref = take(0)
     bias_ref = take(0)
+    outs = []
     if blocked:
-        mats_ref, router_ref = take(0), take(0)
-    q_ref, k_ref, v_ref, att_ref, lse_ref, middle_ref, logits_ref, sent_ref = (
-        take(0) for _ in range(8)
-    )
+        outs.append(take(0))
+        router_ref = take(0)
+    outs += [take(0) for _ in range(3)]
+    att_ref, lse_ref, middle_ref, logits_ref, sent_ref = (take(0) for _ in range(5))
     gates_ref = take(0) if last else None
-    far_ref, send_sems, recv_sems = refs
+    far_ref, send_sems, recv_sems, write_sems, *made_here = refs
+    q_ref, k_ref, v_ref = made_here[-3:]
+    if blocked:
+        mats_ref = made_here[0]
+    writes = local_copies(list(zip(made_here, outs)), write_sems)
     pair, pairs = pl.program_id(0), pl.num_programs(0)
     seq_len = hidden_ref.shape[0]
     width = 2 * head_dim
@@ -711,6 +753,7 @@
         q_ref[...] = dot(normed, mats_ref[0]).astype(bf16)
         k_ref[...] = dot(normed, mats_ref[1]).astype(bf16)
         v_ref[...] = dot(normed, mats_ref[2]).astype(bf16)
+        start_all(writes)
 
     lanes = pl.ds(pl.multiple_of(pair * width, width), width)
     q2 = q_ref[:, lanes] * jnp.asarray(head_dim**-0.5, bf16)
@@ -746,6 +789,7 @@
     @pl.when(pair == pairs - 1)
     def _():
         wait_all([spread.copy(apart) for apart in aparts])
+        wait_all(writes)
 
 
 def attention_forward(
@@ -787,6 +831,8 @@
     if last:
         outs.append(jax.ShapeDtypeStruct((experts, 8, max(128, slots // experts)), f32))
     out_specs = whole_of(outs)
+    out_specs[:3] = [any_spec] * 3
+    written = outs[:3]
     out_specs[4] = pl.BlockSpec((1, 2, seq_len), lambda p: (p, 0, 0))
     if blocked:
         more = [
@@ -794,11 +840,12 @@
             jax.ShapeDtypeStruct((experts, width), bf16),
         ]
         outs = more + outs
-        out_specs = whole_of(more) + out_specs
+        out_specs = [any_spec] + whole_of(more[1:]) + out_specs
+        written = more[:1] + written
     outs.append(jax.ShapeDtypeStruct(spread.shape, bf16))
     out_specs.append(any_spec)
     sems = pltpu.SemaphoreType.DMA((experts,))
-    scratch = [sems, sems]
+    scratch = [sems, sems, pltpu.SemaphoreType.DMA((len(written),)), *scratch_of(written)]
     got = pl.pallas_call(
         partial(forward_kernel, head_dim, grid_shape, blocked, last),
         grid=(heads // 2,),
@@ -877,14 +924,9 @@
     d_logits_ref,
     grad_ref,
     middle_ref,
-    hidden_ref,
     gain_attn_ref,
     gain_ffn_ref,
-    mats_ref,
     router_ref,
-    q_ref,
-    k_ref,
-    v_ref,
     att_ref,
     *refs,
 ):
@@ -894,12 +936,23 @@
     bias_ref, lse_ref = take(0), take(0)
     made_ref = take(0)
     push_refs = (take(0), take(0)) if pushes else ()
+    later = [take(0) for _ in range(5)]
     del refs[:unread]
     grad_new_ref, blocks_ref, gwr_ref, gga_ref, ggf_ref, offsets_ref = (take(0) for _ in range(6))
     spread_out = [take(0) for _ in range(2)] if spreads else []
     returned_ref = take(0)
     landing_refs = (take(0), take(0)) if pushes else ()
     d_att_s, d_middle_s, dqt_s, dk_s, dv_s, probs_s, scores_s = (take(0) for _ in range(7))
+    loaded = [take(0) for _ in range(5)]
+    load_sems = take(0)
+    mats_ref, q_ref, k_ref, v_ref, hidden_ref = loaded
+    mats_later = later[0]
+    load_output = local_copies([(mats_later.at[3], mats_ref.at[3])], load_sems)
+    load_heads = local_copies(list(zip(later[1:4], loaded[1:4])), load_sems, 1)
+    first_three = pl.ds(0, 3)
+    load_rest = local_copies(
+        [(mats_later.at[first_three], mats_ref.at[first_three]), (later[4], hidden_ref)], load_sems, 4
+    )
     own_sem, *sems = refs[:3]
     members = grid_shape[1]
     place = Place(grid_shape)
@@ -916,13 +969,14 @@
 
     @pl.when(pl.program_id(0) == 0)
     def _():
+        start_all(load_output + load_heads + load_rest)
         greet([back.peer(apart) for apart in aparts] + (place.y_peers() if pushes else []))
         start_all(pushed + [back.copy(apart) for apart in aparts])
         if returns:
             own.start()
 
     pair, pairs = pl.program_id(0), pl.num_programs(0)
-    seq_len = hidden_ref.shape[0]
+    seq_len = att_ref.shape[1]
     width = 2 * head_dim
     step = min(512, seq_len)
     scale = head_dim**-0.5
@@ -941,8 +995,10 @@
         d_middle = d_middle + grad_ref[...].astype(f32)
         d_middle_s[...] = d_middle
         d_low = d_middle.astype(bf16)
+        wait_all(load_output)
         reblock(grid_shape, blocks_ref, 3, dot(att_ref[...], d_low).astype(bf16))
         d_att_s[...] = dot(d_low, mats_ref[3], 1, 1).astype(bf16)
+        wait_all(load_heads)
 
     lanes = pl.ds(pl.multiple_of(pair * width, width), width)
     q2 = q_ref[:, lanes] * jnp.asarray(scale, bf16)
@@ -977,6 +1033,7 @@
 
     @pl.when(pair == pairs - 1)
     def _():
+        wait_all(load_rest)
         hidden = hidden_ref[...].astype(f32)
         gain_row = gain_attn_ref[...]
         normed_t = (hidden * rms_factor(hidden) * gain_row).astype(bf16).T
@@ -1033,12 +1090,11 @@
         d_logits,
         grad_now,
         middle,
-        hidden,
         *gains,
-        *mats,
-        *q_k_v,
+        mats[1],
         attended,
     )
+    later = [mats[0], *q_k_v, hidden]
     spreads = below is not None
     if spreads:
         ins = ins + tuple(below)
@@ -1063,7 +1119,7 @@
     out_specs = whole_of(outs)
     out_specs[-1] = any_spec
     if pushes:
-        rows = [push[0].shape[1] - cut_of(push[0]), cut_of(push[1])]
+        rows = [push[0].shape[1] - cut_of(push[0]), push[1].shape[1] // 2]
         outs = outs + tuple(landing_of(one, many) for one, many in zip(push, rows))
         out_specs += [any_spec] * 2
     return pl.pallas_call(
@@ -1074,7 +1130,7 @@
             pl.BlockSpec((2, seq_len, seq_len), lambda p: (p, 0, 0)),
             pl.BlockSpec((1, 2, seq_len), lambda p: (p, 0, 0)),
         ]
-        + [any_spec] * (len(after) + 1 + 2 * pushes),
+        + [any_spec] * (len(after) + 6 + 2 * pushes),
         out_specs=out_specs,
         out_shape=outs,
         scratch_shapes=[
@@ -1086,13 +1142,14 @@
             pltpu.VMEM((seq_len, seq_len), bf16),
             pltpu.VMEM((seq_len, seq_len), bf16),
         ]
-        + [pltpu.SemaphoreType.DMA]
+        + scratch_of(later)
+        + [pltpu.SemaphoreType.DMA((6,)), pltpu.SemaphoreType.DMA]
         + [pltpu.SemaphoreType.DMA((count_y,))] * 2
         + [pltpu.SemaphoreType.DMA((2 * (count_x // 2 - 1),))] * (2 * pushes),
         compiler_params=params(identifier),
         cost_estimate=lasting(32),
         name="attention_backward",
-    )(*ins, bias, lse, made, *(push if pushes else ()), *after)
+    )(*ins, bias, lse, made, *(push if pushes else ()), *later, *after)
 
 
 class Exchange:
@@ -1219,7 +1276,7 @@
             copy.wait()
 
 
-def weight_gradients(place, products, sends, landings, outs, sems, after_first=()):
+def weight_gradients(place, products, sends, landings, outs, sems, after):
     blocks, _, units = outs[0].shape
 
     def product(lhs, rhs_ref, which, into_ref):
@@ -1240,8 +1297,7 @@
         def _(block, index=index):
             add_low(outs[index], (block,), outs[index][block], landings[index][block])
 
-        if index == 0:
-            start_all(after_first)
+        start_all(after[index])
 
 
 def push_blocks(place, src, landing, sems, begin, base=0):
@@ -1277,7 +1333,7 @@
     slot_col_ref,
     chosen_ref,
     logits_ref,
-    middle_ref,
+    middle_in_ref,
     win_ref,
     wout_ref,
     *refs,
@@ -1285,8 +1341,12 @@
     refs = list(refs)
     take = refs.pop
     column_ref = take(0) if gathers else None
-    arrived_ref, comb_ref, out_ref = (take(0) for _ in range(3))
+    arrived_out_ref, comb_ref, out_ref = (take(0) for _ in range(3))
     full_ref = take(0) if gathers else None
+    arrived_ref, middle_ref, move_sems = (take(0) for _ in range(3))
+    load_middle, write_arrived = local_copies(
+        [(middle_in_ref, middle_ref), (arrived_ref, arrived_out_ref)], move_sems
+    )
     win_s, wout_s, made_s, returned_s, w_sems = (take(0) for _ in range(5))
     send_sems, recv_sems, back_send_sems, back_recv_sems = (take(0) for _ in range(4))
     weight_sems = (take(0), take(0))
@@ -1301,6 +1361,7 @@
     place = Place(grid_shape)
     weights = Weights(place, (win_ref, wout_ref), (win_s, wout_s), w_sems, weight_sems)
     weights.start_local()
+    load_middle.start()
     more_peers = place.y_peers() if gathers else []
     greet(peers_along_gy(members) + [place.core_peer()] + more_peers)
     weights.start_remote()
@@ -1362,6 +1423,7 @@
     if gathers:
         wait_all(third)
         start_all(fourth)
+    write_arrived.start()
     slot_col = slot_col_ref[...]
     comb_ref[...] = jnp.zeros_like(comb_ref)
 
@@ -1379,6 +1441,7 @@
     def _(index):
         gather_back(index, 0)
 
+    load_middle.wait()
     gate = jnp.sum(jax.nn.softmax(logits_ref[...], axis=-1) * chosen_ref[...], axis=1, keepdims=True)
     out_ref[...] = middle_ref[...] + gate * comb_ref[...]
     if gathers:
@@ -1388,6 +1451,8 @@
     def _(apart):
         there.copy(apart).wait_send()
         back.copy(apart).wait_send()
+
+    write_arrived.wait()
 
 
 def doubled(half):
@@ -1400,15 +1465,17 @@
     members = grid_shape[1]
     gathers = column is not None
     ins = [sent, slot_col, chosen_f, logits, middle, full_in, full_out]
-    in_specs = [vmem_spec] * 5 + [any_spec] * 2
+    in_specs = [vmem_spec] * 4 + [any_spec] * 3
     outs = [
         jax.ShapeDtypeStruct(sent.shape, bf16),
         jax.ShapeDtypeStruct(middle.shape, f32),
         jax.ShapeDtypeStruct(middle.shape, f32),
     ]
-    out_specs = [vmem_spec] * 3
+    out_specs = [any_spec] + [vmem_spec] * 2
     sems = pltpu.SemaphoreType.DMA((members,))
     scratch = [
+        *scratch_of([sent, middle]),
+        pltpu.SemaphoreType.DMA((2,)),
         doubled(full_in),
         doubled(full_out),
         pltpu.VMEM(sent.shape, bf16),
@@ -1453,10 +1520,10 @@
     far_third_ref,
     win_ref,
     wout_ref,
-    made_ref,
+    made_out_ref,
     d_back_ref,
-    gin_ref,
-    gout_ref,
+    gin_out_ref,
+    gout_out_ref,
     d_logits_ref,
     arrived_s,
     gates_s,
@@ -1473,6 +1540,10 @@
     gin_land,
     gout_send,
     gout_land,
+    made_ref,
+    gin_ref,
+    gout_ref,
+    write_sems,
     w_sems,
     *sems,
 ):
@@ -1554,6 +1625,10 @@
     def _(index):
         work(index, 0)
 
+    write_made, write_out, write_in = local_copies(
+        [(made_ref, made_out_ref), (gout_ref, gout_out_ref), (gin_ref, gin_out_ref)], write_sems
+    )
+    write_made.start()
     weight_gradients(
         place,
         ((d_made_s, act_s), (arrived_s, d_pre_s)),
@@ -1561,6 +1636,7 @@
         (gout_land, gin_land),
         (gout_ref, gin_ref),
         sum_sems,
+        ([write_out], [write_in]),
     )
 
     @pl.loop(1, members)
@@ -1582,6 +1658,8 @@
         back.copy(apart).wait_send()
         gates_there.copy(apart).wait_send()
         gates_back.copy(apart).wait_send()
+
+    wait_all([write_made, write_out, write_in])
 
 
 def expert_both(sent, gates, far_parts, slot_col, chosen_f, logits, full_in, full_out, grid_shape, identifier):
@@ -1602,7 +1680,7 @@
     return pl.pallas_call(
         partial(expert_both_kernel, grid_shape),
         in_specs=[vmem_spec] * 5 + [any_spec] * 5,
-        out_specs=[vmem_spec] * len(outs),
+        out_specs=[any_spec, vmem_spec, any_spec, any_spec, vmem_spec],
         out_shape=outs,
         scratch_shapes=[
             tall,
@@ -1620,6 +1698,10 @@
             half,
             half,
             half,
+            tall,
+            half,
+            half,
+            pltpu.SemaphoreType.DMA((3,)),
             pltpu.SemaphoreType.DMA((2 * full_in.shape[0],)),
         ]
         + [pltpu.SemaphoreType.DMA((members,))] * 9
@@ -1633,13 +1715,13 @@
 def expert_backward_kernel(
     grid_shape,
     d_sent_ref,
-    arrived_ref,
-    blocks_ref,
+    arrived_in_ref,
+    blocks_in_ref,
     win_ref,
     wout_ref,
     d_back_ref,
-    gin_ref,
-    gout_ref,
+    gin_out_ref,
+    gout_out_ref,
     upper_ref,
     lower_ref,
     landing_ref,
@@ -1656,6 +1738,11 @@
     gin_land,
     gout_send,
     gout_land,
+    arrived_ref,
+    blocks_ref,
+    gin_ref,
+    gout_ref,
+    move_sems,
     w_sems,
     send_sems,
     recv_sems,
@@ -1676,10 +1763,20 @@
     place = Place(grid_shape)
     weights = Weights(place, (win_ref, wout_ref), (win_s, wout_s), w_sems, weight_sems)
     weights.start_local()
+    moves = local_copies(
+        [
+            (arrived_in_ref, arrived_ref),
+            (blocks_in_ref.at[:, place.c], blocks_ref.at[:, place.c]),
+            (gout_ref, gout_out_ref),
+            (gin_ref, gin_out_ref),
+        ],
+        move_sems,
+    )
+    start_all(moves[:2])
     greet(peers_along_gy(members) + [place.core_peer()] + place.y_peers())
     weights.start_remote()
     landings = (first_s, up2_s, low2_s, upper_ref, lower_ref, None, None)
-    sums = Scatter(place, blocks_ref, landings, sum_sems, upper_ref.shape[1])
+    sums = Scatter(place, blocks_ref, landings, sum_sems, upper_ref.shape[1], blocks_in_ref)
     there = Exchange(members, rows, d_sent_ref, d_arrived_s, send_sems, recv_sems)
     back = Exchange(members, rows, d_rows_s, d_back_ref, back_send_sems, back_recv_sems)
     for apart in send_order(members):
@@ -1687,6 +1784,7 @@
     there.keep_own()
     my_chunk = there.me // group
     start_all(sums.copies(0))
+    wait_all(moves[:2])
     weights.wait(0)
 
     @pl.loop(0, slots // 256)
@@ -1741,7 +1839,7 @@
         (gout_land, gin_land),
         (gout_ref, gin_ref),
         gradient_sems,
-        pushed,
+        ([*pushed, moves[2]], [moves[3]]),
     )
     wait_all(sums.copies(2))
     sums.add(2)
@@ -1752,7 +1850,7 @@
         there.copy(apart).wait_send()
         back.copy(apart).wait_send()
 
-    wait_all(pushed)
+    wait_all(pushed + moves[2:])
 
 
 def expert_backward(d_sent, arrived, blocks, full_in, full_out, grid_shape, identifier):
@@ -1769,8 +1867,8 @@
     sems = pltpu.SemaphoreType.DMA((members,))
     return pl.pallas_call(
         partial(expert_backward_kernel, grid_shape),
-        in_specs=[vmem_spec] * 3 + [any_spec] * 2,
-        out_specs=[vmem_spec] * (len(outs) - 1) + [any_spec],
+        in_specs=[vmem_spec] + [any_spec] * 4,
+        out_specs=[vmem_spec] + [any_spec] * 2 + [vmem_spec] * 2 + [any_spec],
         out_shape=outs,
         scratch_shapes=[
             doubled(full_in),
@@ -1781,6 +1879,8 @@
             pltpu.VMEM((slots, 2 * full_in.shape[0] * full_in.shape[2]), bf16),
             *[pltpu.VMEM(one, bf16) for one in landings[:3]],
             *[pltpu.VMEM(full_in.shape, bf16)] * 4,
+            *scratch_of([arrived, blocks, full_in, full_out]),
+            pltpu.SemaphoreType.DMA((4,)),
             pltpu.SemaphoreType.DMA((2 * full_in.shape[0],)),
             sems,
             sems,
@@ -1832,18 +1932,21 @@
             total = total + ref[index].astype(f32)
         return total
 
-    begins = step < pl.num_programs(0) // 3 * 2
-    for own, first, second, up, out in (
-        (gin_ref, gin_first_ref, gin_second_ref, gin_up_ref, gin_out_ref),
-        (gout_ref, gout_first_ref, gout_second_ref, gout_up_ref, gout_out_ref),
+    steps = pl.num_programs(0)
+    for own, first, second, up, out, early_steps in (
+        (gin_ref, gin_first_ref, gin_second_ref, gin_up_ref, gin_out_ref, steps // 2),
+        (gout_ref, gout_first_ref, gout_second_ref, gout_up_ref, gout_out_ref, steps // 3 * 2),
     ):
-        out[0, 0] = own[0].astype(f32) + jnp.where(begins, landed(first), landed(second))
+        out[0, 0] = own[0].astype(f32) + jnp.where(step < early_steps, landed(first), landed(second))
         out[1, 0] = up[...].astype(f32)
 
-    @pl.when(step == 0)
+    @pl.when(step < 4)
     def _():
         result_out_ref[...] = result_ref[...]
         grad_out_ref[...] = grad_ref[...]
+
+    @pl.when(step == 0)
+    def _():
         layers, tall, wide = wq_ref.shape
         for which, ref in enumerate((wq_ref, wk_ref, wv_ref, wo_ref)):
             ref[...] = packed_ref[:, :, which * wide : (which + 1) * wide]
@@ -1868,10 +1971,10 @@
     gout, gout_first, gout_second, gout_up = grads_out
     _, rows, units = gin.shape
     steps = 6
-    early_steps = steps // 3 * 2
     tile = rows // steps
     wide = lanes // 4
-    whole_in = [result, grad_now, packed, small]
+    whole_in = [packed, small]
+    passed = pl.BlockSpec((result.shape[0] // 4, result.shape[1]), lambda i, at: (jnp.minimum(i, 3), 0))
     own = pl.BlockSpec((1, tile, units), lambda i, at: (at[2], i, 0))
     up = pl.BlockSpec((tile, units), lambda i, at: (i, 0))
 
@@ -1882,18 +1985,18 @@
     expert = jax.ShapeDtypeStruct((layers, 1, rows, units), f32)
     square = jax.ShapeDtypeStruct((layers, tall, wide), f32)
     gain = jax.ShapeDtypeStruct((layers, small.shape[1]), f32)
-    rest = [jax.ShapeDtypeStruct(result.shape, f32)] * 2 + [square] * 4
+    rest = [square] * 4
     rest += [jax.ShapeDtypeStruct((layers, 1, tall), f32), gain, gain]
     rest.append(jax.ShapeDtypeStruct(table_shape[::-1], f32))
 
-    def first_index(i):
-        return jnp.minimum(i, early_steps - 1)
-
-    def second_index(i):
-        return jnp.maximum(i - early_steps, 0)
-
     def expert_specs(first_land, second_land):
-        return [own, land(first_land, first_index), land(second_land, second_index), up]
+        early_steps = first_land.shape[1] // tile
+        return [
+            own,
+            land(first_land, lambda i: jnp.minimum(i, early_steps - 1)),
+            land(second_land, lambda i: jnp.maximum(i - early_steps, 0)),
+            up,
+        ]
 
     return pl.pallas_call(
         partial(emit_kernel, table_shape),
@@ -1902,14 +2005,15 @@
             grid=(steps,),
             in_specs=expert_specs(gin_first, gin_second)
             + expert_specs(gout_first, gout_second)
+            + [passed, passed]
             + whole_of(whole_in),
-            out_specs=[out, out] + whole_of(rest),
+            out_specs=[out, out, passed, passed] + whole_of(rest),
         ),
-        out_shape=[expert, expert] + rest,
+        out_shape=[expert, expert] + [jax.ShapeDtypeStruct(result.shape, f32)] * 2 + rest,
         compiler_params=params(),
         cost_estimate=lasting(7),
         name="emit",
-    )(at, *grads_in, *grads_out, *whole_in)
+    )(at, *grads_in, *grads_out, result, grad_now, *whole_in)
 
 
 def body(

time: 525 us -> 507 us (0.966)
  Pallas kernels: 497 us -> 478 us
    pallas_call x2, Pallas kernels: 86.4 us -> 76.5 us  [attention_backward(): pl.pallas_call(partial(backward_kernel, head_dim, grid_shape, spreads, re...]
  transfers between devices with their start and end apart: 6 -> 6, of which waited for: 0 -> 1; matrix products, arithmetic and copies ran while one was open for 1% -> 1% of each run, Pallas kernels for 61% -> 61%
where the time goes in v6:
time: 507 us; the launch traced here: 501 us
  Pallas kernels  478 us (94%)
  between operations  14.5 us (3%)
  local copies, waits for them, and re-layouts  6.71 us (1%)
    pallas_call x1, Pallas kernels, expert_backward(): pl.pallas_call(partial(expert_backward_kernel, grid_shape), in_specs=[vme...  78.4 us
    pallas_call x2, Pallas kernels, attention_backward(): pl.pallas_call(partial(backward_kernel, head_dim, grid_shape, spreads, re...  76.5 us
    pallas_call x1, Pallas kernels, expert_forward(): pl.pallas_call(partial(expert_forward_kernel, grid_shape, gathers), in_sp...  71.3 us
    pallas_call x1, Pallas kernels, expert_both(): pl.pallas_call(partial(expert_both_kernel, grid_shape), in_specs=[vmem_sp...  70.2 us
    pallas_call x1, Pallas kernels, start(): pl.pallas_call(partial(start_kernel, grid_shape), in_specs=[vmem_spec] *...  64.8 us
    pallas_call x1, Pallas kernels, final_sums(): pl.pallas_call(partial(final_kernel, grid_shape, layers, buckets_count),...  56.8 us
    pallas_call x2, Pallas kernels, attention_forward(): pl.pallas_call(partial(forward_kernel, head_dim, grid_shape, blocked, las...  47.8 us
    pallas_call x1, Pallas kernels, emit(): pl.pallas_call(partial(emit_kernel, table_shape), grid_spec=pltpu.Prefetc...  11.8 us
  transfers between devices with their start and end apart: 6, of which 1 were waited for; matrix products, arithmetic and copies ran while one was open for 1% of the time, Pallas kernels for 61%

profile of v6, /device:TPU:0, one launch (start us, length us, event | category | flops | bytes accessed | tf_op | source)
XLA Modules:
  0.0 501.4 jit_solution(3324446944625174051)
XLA Ops:
  7.2 0.0 all-gather.9.cloned.1.call-start
  7.2 0.0 copy-start
  7.2 3.3 fusion.1
  10.6 0.0 all-gather.9.cloned.1.call-update
  10.6 0.0 all-gather.11.cloned.1.call-start
  10.6 0.0 copy-done
  10.6 1.6 fusion
  12.2 0.0 copy-start.4
  12.2 0.0 copy-start.3
  12.2 0.0 copy-start.1
  12.2 0.0 copy-start.2
  12.2 0.0 all-gather.11.cloned.1.call-update
  12.2 0.0 all-gather.13.cloned.1.call-start
  12.3 0.7 all-gather.13.cloned.1.call-update
  13.0 0.0 all-gather.15.cloned.1.call-start
  13.0 0.5 all-gather.15.cloned.1.call-update
  13.6 0.0 reduce-scatter.3.cloned.1.call-start
  13.6 0.0 copy-done.4
  13.6 0.0 copy-done.3
  13.6 0.6 pad.9
  14.2 0.6 pad.8.router_rows_ref
  14.8 0.0 copy-done.1
  14.8 0.0 copy-done.2
  14.8 0.6 fusion.2
  15.4 64.8 %start.1 = (bf16[4,768,768]{2,1,0:T(8,128)(2,1)}, bf16[8,768]{1,0:T(8,128)(2,1)}, bf16[1,4,208,384]{3,2,1,0:T(8,128)(2,1)}, bf16[12,512,512]{2,1,0:T(8,128)(2,1)...) custom-call(bf16[2,192,96]{2,1,0:T(8,128)(2,1)} %wq_ref.1, ...), custom_call_target="tpu_custom_call" | custom-call | flops 44999999488 | bytes 1048576 | tf_op jit(solution)/shard_map/start/pallas_call | solution.py:659
  80.2 20.2 %attention_forward.2 = (bf16[512,768]{1,0:T(8,128)(2,1)}, bf16[512,768]{1,0:T(8,128)(2,1)}, bf16[512,768]{1,0:T(8,128)(2,1)}, bf16[768,512]{1,0:T(8,128)(2,1)}, ...) custom-call(bf16[512,768]{1,0:T(8,128)(2,1)} %refs_9_.1, ...), custom_call_target="tpu_custom_call" | custom-call | flops 24999999488 | bytes 1048576 | tf_op jit(solution)/shard_map/attention_forward/pallas_call | solution.py:849
  100.5 0.0 all-gather.9.cloned.1.call-done
  100.5 0.4 all-gather.11.cloned.1.call-done
  100.9 71.3 %expert_forward.1 = (bf16[1024,768]{1,0:T(8,128)(2,1)}, f32[512,768]{1,0:T(8,128)}, f32[512,768]{1,0:T(8,128)}, bf16[2,2,4,2,208,384]{5,4,3,2,1,0:T(8,128)(2,1)}) custom-call(bf16[1024,768]{1,0:T(8,128)(2,1)} %get-tuple-element.98.sent_ref, s32[512,1]{1,0:T(8,128)} %get-tuple-element.92.slot_col_ref.refs_11_, ...), custom_call_target="tpu_custom_call" | custom-call | flops 74999996416 | bytes 1048576 | tf_op jit(solution)/shard_map/expert_forward/pallas_call | solution.py:1499
  172.2 27.6 %attention_forward.3 = (bf16[4,768,768]{2,1,0:T(8,128)(2,1)}, bf16[8,768]{1,0:T(8,128)(2,1)}, bf16[512,768]{1,0:T(8,128)(2,1)}, bf16[512,768]{1,0:T(8,128)(2,1)}...) custom-call(f32[512,768]{1,0:T(8,128)} %get-tuple-element.102.hidden, ...), custom_call_target="tpu_custom_call" | custom-call | flops 24999999488 | bytes 1048576 | tf_op jit(solution)/shard_map/attention_forward/pallas_call | solution.py:849
  199.8 0.0 all-gather.13.cloned.1.call-done
  199.8 0.0 all-gather.15.cloned.1.call-done
  199.8 70.2 %expert_both.1 = (bf16[1024,768]{1,0:T(8,128)(2,1)}, bf16[1024,768]{1,0:T(8,128)(2,1)}, bf16[2,768,768]{2,1,0:T(8,128)(2,1)}, bf16[2,768,768]{2,1,0:T(8,128)(2,1)}, bf16[512,8]{1,0:T(8,128)(2,1)}) custom-call(bf16[1024,768]{1,0:T(8,128)(2,1)} %get-tuple-element.104.sent_ref, f32[8,8,128]{2,1,0:T(8,128)} %get-tuple-element.105.gates_ref, ...), custom_call_target="tpu_custom_call" | custom-call | flops 85000003584 | bytes 1048576 | tf_op jit(solution)/shard_map/expert_both/pallas_call | solution.py:1680
  270.0 0.0 reduce-scatter.3.cloned.1.call-update
  270.0 0.0 reduce-scatter.5.cloned.1.call-start
  270.1 0.6 pad_add_fusion.at_ref
  270.7 0.0 reduce-scatter.5.cloned.1.call-update
  270.7 45.1 %attention_backward.2 = (f32[512,768]{1,0:T(8,128)}, bf16[2,2,4,2,192,384]{5,4,3,2,1,0:T(8,128)(2,1)}, f32[8,768]{1,0:T(8,128)}, f32[1,768]{1,0:T(1,128)}, f32[1...) custom-call(bf16[1024,768]{1,0:T(8,128)(2,1)} %get-tuple-element.110, ...), custom_call_target="tpu_custom_call" | custom-call | flops 32000000000 | bytes 1048576 | tf_op jit(solution)/shard_map/attention_backward/pallas_call | solution.py:1125
  315.8 78.4 %expert_backward.1 = (bf16[1024,768]{1,0:T(8,128)(2,1)}, bf16[2,768,768]{2,1,0:T(8,128)(2,1)}, bf16[2,768,768]{2,1,0:T(8,128)(2,1)}, bf16[4,96,384]{2,1,0:T(8,12...) custom-call(bf16[1024,768]{1,0:T(8,128)(2,1)} %get-tuple-element.122.d_sent_ref, ...), custom_call_target="tpu_custom_call" | custom-call | flops 85000003584 | bytes 1048576 | tf_op jit(solution)/shard_map/expert_backward/pallas_call | solution.py:1868
  394.3 0.0 reduce-scatter.3.cloned.1.call-done
  394.3 0.0 reduce-scatter.5.cloned.1.call-done
  394.3 31.4 %attention_backward.3 = (f32[512,768]{1,0:T(8,128)}, bf16[2,2,4,2,192,384]{5,4,3,2,1,0:T(8,128)(2,1)}, f32[8,768]{1,0:T(8,128)}, f32[1,768]{1,0:T(1,128)}, f32[1...) custom-call(bf16[1024,768]{1,0:T(8,128)(2,1)} %get-tuple-element.126, ...), custom_call_target="tpu_custom_call" | custom-call | flops 32000000000 | bytes 1048576 | tf_op jit(solution)/shard_map/attention_backward/pallas_call | solution.py:1125
  425.7 56.8 %final_sums.1 = (f32[2,192,384]{2,1,0:T(8,128)}, f32[32,768]{1,0:T(8,128)}, f32[512,768]{1,0:T(8,128)}, bf16[1,384,768]{2,1,0:T(8,128)(2,1)}) custom-call(bf16[4,96,384]{2,1,0:T(8,128)(2,1)} %get-tuple-element.138.refs_0_, bf16[1,4,96,384]{3,2,1,0:T(8,128)(2,1)} %get-tuple-element.139.refs_1_, f32[8,768]{1,0:T(8,128)} %get-tuple-element.140.refs_2_, ...), custom_call_target="tpu_custom_call" | custom-call | flops 60000002048 | bytes 1048576 | tf_op jit(solution)/shard_map/final_sums/pallas_call | solution.py:449
  482.6 11.8 %emit.1 = (f32[2,1,768,768]{3,2,1,0:T(8,128)}, f32[2,1,768,768]{3,2,1,0:T(8,128)}, f32[512,768]{1,0:T(8,128)}, f32[512,768]{1,0:T(8,128)}, f32[2,192,96]{2,1,0:T...) custom-call(s32[3]{0:T(128)} %pad_add_fusion.at_ref, ...), custom_call_target="tpu_custom_call" | custom-call | flops 7000000000 | bytes 1048576 | tf_op jit(solution)/shard_map/emit/pallas_call | solution.py:2001
  (1 shorter events, 0.0 us)
Async XLA Ops:
  7.2 93.3 %all-gather.9.cloned.1.call-start = ((), (), s32[]{:S(2)}) async-start(), calls=%async_computation.4 | async-start | bytes 3538944 | tf_op jit(solution)/shard_map/all_gather | solution.py:2086
  7.2 3.4 copy-start
  10.6 90.3 %all-gather.11.cloned.1.call-start = ((), (), s32[]{:S(2)}) async-start(), calls=%async_computation.5 | async-start | bytes 3538944 | tf_op jit(solution)/shard_map/all_gather | solution.py:2086
  12.2 1.4 copy-start.4
  12.2 1.4 copy-start.3
  12.2 2.6 copy-start.1
  12.2 2.6 copy-start.2
  12.2 187.6 %all-gather.13.cloned.1.call-start = ((), (), s32[]{:S(2)}) async-start(), calls=%async_computation.6 | async-start | bytes 3538944 | tf_op jit(solution)/shard_map/all_gather | solution.py:2086
  13.0 186.9 %all-gather.15.cloned.1.call-start = ((), (), s32[]{:S(2)}) async-start(), calls=%async_computation.7 | async-start | bytes 3538944 | tf_op jit(solution)/shard_map/all_gather | solution.py:2086
  13.6 380.7 %reduce-scatter.3.cloned.1.call-start = ((), (), s32[]{:S(2)}) async-start(), calls=%async_computation.2 | async-start | bytes 3538944 | tf_op jit(solution)/shard_map/reduce_scatter | solution.py:2126
  270.0 124.3 %reduce-scatter.5.cloned.1.call-start = ((), (), s32[]{:S(2)}) async-start(), calls=%async_computation.3 | async-start | bytes 3538944 | tf_op jit(solution)/shard_map/reduce_scatter | solution.py:2126
Sparse Core Ops, SparseCore 0:
  10.7 50.9 all-gather.8
  63.8 37.0 all-gather.10
  103.0 48.8 all-gather.12
  153.9 35.0 all-gather.14
  270.2 46.9 reduce-scatter.2
  319.4 47.3 reduce-scatter.4

commit v7 on v6

--- a/solution.py
+++ b/solution.py
@@ -329,6 +329,17 @@
     return bits_of(grid_shape[0]) + bits_of(grid_shape[1])
 
 
+def lane_parts(lanes):
+    return lanes // 128 if lanes % 128 == 0 else 1
+
+
+def lane_part(ref, part, parts):
+    if parts == 1:
+        return ref
+    lanes = ref.shape[-1] // parts
+    return ref.at[..., pl.ds(part * lanes, lanes)]
+
+
 def final_kernel(grid_shape, layers, buckets_count, *refs):
     refs = list(refs)
     take = refs.pop
@@ -354,7 +365,25 @@
         upper, lower = partial_refs[layer - 1]
         places = (None, None, None, upper, lower, *z_landings[layer - 1])
         upper_layers.append(Scatter(place, blocks_ref, places, sems[layer], split))
-    lowest = Scatter(place, blocks_ref, landings, sems[0], split, blocks_in_ref)
+    parts = lane_parts(packed_ref.shape[2])
+    lowest = [
+        Scatter(
+            place,
+            lane_part(blocks_ref, part, parts),
+            [lane_part(landing_part, part, parts) for landing_part in landings],
+            (sems[0][0].at[part], sems[0][1].at[part]),
+            split,
+            lane_part(blocks_in_ref, part, parts),
+        )
+        for part in range(parts)
+    ]
+
+    def step(stage):
+        for one in lowest:
+            wait_all(one.copies(stage))
+            one.add(stage)
+            start_all(one.copies(stage + 1))
+
     c = place.c
     moves = local_copies(
         [(blocks_in_ref.at[:, c], blocks_ref.at[:, c]), (middle_in_ref, middle_ref)], move_sems
@@ -371,7 +400,8 @@
     )
     start_all(collected)
     greet([place.core_peer(), place.x_peer()] + place.y_peers() + place.z_peers())
-    start_all(lowest.copies(0))
+    for one in lowest:
+        start_all(one.copies(0))
     for one in upper_layers:
         start_all(one.copies(3))
 
@@ -394,39 +424,36 @@
     )
     small = SmallSum(grid_shape, totals, landing, small_sems)
     small.begin()
-    wait_all(moves + lowest.copies(0))
-    lowest.add(0)
-    start_all(lowest.copies(1))
+    wait_all(moves)
+    step(0)
     small.advance()
     wait_all(collected)
     placing = placing_cols(slot_col_ref[...], slots)
     gate = jnp.sum(jax.nn.softmax(logits_ref[...], axis=-1) * chosen_ref[...], axis=1, keepdims=True)
     result_ref[...] = middle_ref[...] + gate * dot(placing, returned_s[...])
     small.advance()
-    wait_all(lowest.copies(1))
-    lowest.add(1)
-    start_all(lowest.copies(2))
-    pushed = push_blocks(
-        place, push_ref, landing_ref, push_sems, push_ref.shape[1] - landing_ref.shape[1]
-    )
-    start_all(pushed)
+    step(1)
     small.advance()
 
-    def finish(layer, one):
+    def finish(layer, one, lanes=slice(None)):
         for part, rows in zip(one.result(), (slice(0, split), slice(split, tall))):
-            packed_ref[layer, rows, :] = part
+            packed_ref[layer, rows, lanes] = part
 
     for layer, one in enumerate(upper_layers):
         wait_all(one.copies(3))
         finish(layer + 1, one)
-    wait_all(lowest.copies(2))
-    lowest.add(2)
-    start_all(lowest.copies(3))
+    step(2)
+    pushed = push_blocks(
+        place, push_ref, landing_ref, push_sems, push_ref.shape[1] - landing_ref.shape[1]
+    )
+    start_all(pushed)
     while small.done < len(small.peers):
         small.advance()
     small_out_ref[...] = totals[len(small.peers)]
-    wait_all(lowest.copies(3))
-    finish(0, lowest)
+    each = packed_ref.shape[2] // parts
+    for part, one in enumerate(lowest):
+        wait_all(one.copies(3))
+        finish(0, one, slice(part * each, (part + 1) * each))
     wait_all(pushed)
 
 
@@ -440,6 +467,7 @@
     rows = sum(one.shape[0] for one in smalls[: 3 * layers]) + smalls[3 * layers].shape[0]
     small_shape = (rows, width)
     sems = pltpu.SemaphoreType.DMA((scatter_copies(grid_shape),))
+    first_sems = pltpu.SemaphoreType.DMA((lane_parts(shape[5]), scatter_copies(grid_shape)))
     small_sems = pltpu.SemaphoreType.DMA((steps,))
     outs = [jax.ShapeDtypeStruct((layers, tall, shape[5]), f32)]
     outs += [jax.ShapeDtypeStruct(small_shape, f32), jax.ShapeDtypeStruct(finishing[-1].shape, f32)]
@@ -457,7 +485,8 @@
         + landings[5:] * (layers - 1)
         + [pltpu.VMEM((steps + 1, *small_shape), f32), pltpu.VMEM((steps, *small_shape), f32)]
         + [pltpu.VMEM(returned[0].shape, bf16)]
-        + [sems, sems] * layers
+        + [first_sems, first_sems]
+        + [sems, sems] * (layers - 1)
         + [small_sems, small_sems, pltpu.SemaphoreType.DMA((grid_shape[1],))]
         + [pltpu.SemaphoreType.DMA((grid_shape[0] // 2 - 1,))] * 2,
         compiler_params=params(24),

time: 507 us -> 501 us (0.988)
  Pallas kernels: 478 us -> 472 us
    pallas_call x1, Pallas kernels: 56.8 us -> 51 us  [final_sums(): pl.pallas_call(partial(final_kernel, grid_shape, layers, buckets_count),...]
  transfers between devices with their start and end apart: 6 -> 6, of which waited for: 1 -> 1; matrix products, arithmetic and copies ran while one was open for 1% -> 1% of each run, Pallas kernels for 61% -> 62%
where the time goes in v7:
time: 501 us; the launch traced here: 496 us
  Pallas kernels  472 us (94%)
  between operations  14.5 us (3%)
  local copies, waits for them, and re-layouts  6.71 us (1%)
    pallas_call x1, Pallas kernels, expert_backward(): pl.pallas_call(partial(expert_backward_kernel, grid_shape), in_specs=[vme...  78.4 us
    pallas_call x2, Pallas kernels, attention_backward(): pl.pallas_call(partial(backward_kernel, head_dim, grid_shape, spreads, re...  76.5 us
    pallas_call x1, Pallas kernels, expert_forward(): pl.pallas_call(partial(expert_forward_kernel, grid_shape, gathers), in_sp...  71.3 us
    pallas_call x1, Pallas kernels, expert_both(): pl.pallas_call(partial(expert_both_kernel, grid_shape), in_specs=[vmem_sp...  70.2 us
    pallas_call x1, Pallas kernels, start(): pl.pallas_call(partial(start_kernel, grid_shape), in_specs=[vmem_spec] *...  64.8 us
    pallas_call x1, Pallas kernels, final_sums(): pl.pallas_call(partial(final_kernel, grid_shape, layers, buckets_count),...  51 us
    pallas_call x2, Pallas kernels, attention_forward(): pl.pallas_call(partial(forward_kernel, head_dim, grid_shape, blocked, las...  47.8 us
    pallas_call x1, Pallas kernels, emit(): pl.pallas_call(partial(emit_kernel, table_shape), grid_spec=pltpu.Prefetc...  11.8 us
  transfers between devices with their start and end apart: 6, of which 1 were waited for; matrix products, arithmetic and copies ran while one was open for 1% of the time, Pallas kernels for 62%

profile of v7, /device:TPU:0, one launch (start us, length us, event | category | flops | bytes accessed | tf_op | source)
XLA Modules:
  0.0 495.6 jit_solution(5053236608166051683)
XLA Ops:
  7.2 0.0 all-gather.9.cloned.1.call-start
  7.2 0.0 copy-start
  7.2 3.3 fusion.1
  10.6 0.0 all-gather.9.cloned.1.call-update
  10.6 0.0 all-gather.11.cloned.1.call-start
  10.6 0.0 copy-done
  10.6 1.6 fusion
  12.2 0.0 copy-start.4
  12.2 0.0 copy-start.3
  12.2 0.0 copy-start.1
  12.2 0.0 copy-start.2
  12.2 0.0 all-gather.11.cloned.1.call-update
  12.2 0.0 all-gather.13.cloned.1.call-start
  12.3 0.7 all-gather.13.cloned.1.call-update
  13.0 0.0 all-gather.15.cloned.1.call-start
  13.0 0.5 all-gather.15.cloned.1.call-update
  13.6 0.0 reduce-scatter.3.cloned.1.call-start
  13.6 0.0 copy-done.4
  13.6 0.0 copy-done.3
  13.6 0.6 pad.9
  14.2 0.6 pad.8.router_rows_ref
  14.8 0.0 copy-done.1
  14.8 0.0 copy-done.2
  14.8 0.6 fusion.2
  15.4 64.8 %start.1 = (bf16[4,768,768]{2,1,0:T(8,128)(2,1)}, bf16[8,768]{1,0:T(8,128)(2,1)}, bf16[1,4,208,384]{3,2,1,0:T(8,128)(2,1)}, bf16[12,512,512]{2,1,0:T(8,128)(2,1)...) custom-call(bf16[2,192,96]{2,1,0:T(8,128)(2,1)} %wq_ref.1, ...), custom_call_target="tpu_custom_call" | custom-call | flops 44999999488 | bytes 1048576 | tf_op jit(solution)/shard_map/start/pallas_call | solution.py:688
  80.2 20.2 %attention_forward.2 = (bf16[512,768]{1,0:T(8,128)(2,1)}, bf16[512,768]{1,0:T(8,128)(2,1)}, bf16[512,768]{1,0:T(8,128)(2,1)}, bf16[768,512]{1,0:T(8,128)(2,1)}, ...) custom-call(bf16[512,768]{1,0:T(8,128)(2,1)} %refs_9_.1, ...), custom_call_target="tpu_custom_call" | custom-call | flops 24999999488 | bytes 1048576 | tf_op jit(solution)/shard_map/attention_forward/pallas_call | solution.py:878
  100.5 0.0 all-gather.9.cloned.1.call-done
  100.5 0.4 all-gather.11.cloned.1.call-done
  100.9 71.3 %expert_forward.1 = (bf16[1024,768]{1,0:T(8,128)(2,1)}, f32[512,768]{1,0:T(8,128)}, f32[512,768]{1,0:T(8,128)}, bf16[2,2,4,2,208,384]{5,4,3,2,1,0:T(8,128)(2,1)}) custom-call(bf16[1024,768]{1,0:T(8,128)(2,1)} %get-tuple-element.98.sent_ref, s32[512,1]{1,0:T(8,128)} %get-tuple-element.92.slot_col_ref.refs_11_, ...), custom_call_target="tpu_custom_call" | custom-call | flops 74999996416 | bytes 1048576 | tf_op jit(solution)/shard_map/expert_forward/pallas_call | solution.py:1528
  172.2 27.6 %attention_forward.3 = (bf16[4,768,768]{2,1,0:T(8,128)(2,1)}, bf16[8,768]{1,0:T(8,128)(2,1)}, bf16[512,768]{1,0:T(8,128)(2,1)}, bf16[512,768]{1,0:T(8,128)(2,1)}...) custom-call(f32[512,768]{1,0:T(8,128)} %get-tuple-element.102.hidden, ...), custom_call_target="tpu_custom_call" | custom-call | flops 24999999488 | bytes 1048576 | tf_op jit(solution)/shard_map/attention_forward/pallas_call | solution.py:878
  199.8 0.0 all-gather.13.cloned.1.call-done
  199.8 0.0 all-gather.15.cloned.1.call-done
  199.8 70.2 %expert_both.1 = (bf16[1024,768]{1,0:T(8,128)(2,1)}, bf16[1024,768]{1,0:T(8,128)(2,1)}, bf16[2,768,768]{2,1,0:T(8,128)(2,1)}, bf16[2,768,768]{2,1,0:T(8,128)(2,1)}, bf16[512,8]{1,0:T(8,128)(2,1)}) custom-call(bf16[1024,768]{1,0:T(8,128)(2,1)} %get-tuple-element.104.sent_ref, f32[8,8,128]{2,1,0:T(8,128)} %get-tuple-element.105.gates_ref, ...), custom_call_target="tpu_custom_call" | custom-call | flops 85000003584 | bytes 1048576 | tf_op jit(solution)/shard_map/expert_both/pallas_call | solution.py:1709
  270.0 0.0 reduce-scatter.3.cloned.1.call-update
  270.0 0.0 reduce-scatter.5.cloned.1.call-start
  270.1 0.6 pad_add_fusion.at_ref
  270.7 0.0 reduce-scatter.5.cloned.1.call-update
  270.7 45.1 %attention_backward.2 = (f32[512,768]{1,0:T(8,128)}, bf16[2,2,4,2,192,384]{5,4,3,2,1,0:T(8,128)(2,1)}, f32[8,768]{1,0:T(8,128)}, f32[1,768]{1,0:T(1,128)}, f32[1...) custom-call(bf16[1024,768]{1,0:T(8,128)(2,1)} %get-tuple-element.110, ...), custom_call_target="tpu_custom_call" | custom-call | flops 32000000000 | bytes 1048576 | tf_op jit(solution)/shard_map/attention_backward/pallas_call | solution.py:1154
  315.8 78.4 %expert_backward.1 = (bf16[1024,768]{1,0:T(8,128)(2,1)}, bf16[2,768,768]{2,1,0:T(8,128)(2,1)}, bf16[2,768,768]{2,1,0:T(8,128)(2,1)}, bf16[4,96,384]{2,1,0:T(8,12...) custom-call(bf16[1024,768]{1,0:T(8,128)(2,1)} %get-tuple-element.122.d_sent_ref, ...), custom_call_target="tpu_custom_call" | custom-call | flops 85000003584 | bytes 1048576 | tf_op jit(solution)/shard_map/expert_backward/pallas_call | solution.py:1897
  394.3 0.0 reduce-scatter.3.cloned.1.call-done
  394.3 0.0 reduce-scatter.5.cloned.1.call-done
  394.3 31.4 %attention_backward.3 = (f32[512,768]{1,0:T(8,128)}, bf16[2,2,4,2,192,384]{5,4,3,2,1,0:T(8,128)(2,1)}, f32[8,768]{1,0:T(8,128)}, f32[1,768]{1,0:T(1,128)}, f32[1...) custom-call(bf16[1024,768]{1,0:T(8,128)(2,1)} %get-tuple-element.126, ...), custom_call_target="tpu_custom_call" | custom-call | flops 32000000000 | bytes 1048576 | tf_op jit(solution)/shard_map/attention_backward/pallas_call | solution.py:1154
  425.7 51.0 %final_sums.1 = (f32[2,192,384]{2,1,0:T(8,128)}, f32[32,768]{1,0:T(8,128)}, f32[512,768]{1,0:T(8,128)}, bf16[1,384,768]{2,1,0:T(8,128)(2,1)}) custom-call(bf16[4,96,384]{2,1,0:T(8,128)(2,1)} %get-tuple-element.138.refs_0_, bf16[1,4,96,384]{3,2,1,0:T(8,128)(2,1)} %get-tuple-element.139.refs_1_, f32[8,768]{1,0:T(8,128)} %get-tuple-element.140.refs_2_, ...), custom_call_target="tpu_custom_call" | custom-call | flops 60000002048 | bytes 1048576 | tf_op jit(solution)/shard_map/final_sums/pallas_call | solution.py:477
  476.7 11.8 %emit.1 = (f32[2,1,768,768]{3,2,1,0:T(8,128)}, f32[2,1,768,768]{3,2,1,0:T(8,128)}, f32[512,768]{1,0:T(8,128)}, f32[512,768]{1,0:T(8,128)}, f32[2,192,96]{2,1,0:T...) custom-call(s32[3]{0:T(128)} %pad_add_fusion.at_ref, ...), custom_call_target="tpu_custom_call" | custom-call | flops 7000000000 | bytes 1048576 | tf_op jit(solution)/shard_map/emit/pallas_call | solution.py:2030
  (1 shorter events, 0.0 us)
Async XLA Ops:
  7.2 93.3 %all-gather.9.cloned.1.call-start = ((), (), s32[]{:S(2)}) async-start(), calls=%async_computation.4 | async-start | bytes 3538944 | tf_op jit(solution)/shard_map/all_gather | solution.py:2115
  7.2 3.4 copy-start
  10.6 90.3 %all-gather.11.cloned.1.call-start = ((), (), s32[]{:S(2)}) async-start(), calls=%async_computation.5 | async-start | bytes 3538944 | tf_op jit(solution)/shard_map/all_gather | solution.py:2115
  12.2 1.4 copy-start.4
  12.2 1.4 copy-start.3
  12.2 2.6 copy-start.1
  12.2 2.6 copy-start.2
  12.2 187.6 %all-gather.13.cloned.1.call-start = ((), (), s32[]{:S(2)}) async-start(), calls=%async_computation.6 | async-start | bytes 3538944 | tf_op jit(solution)/shard_map/all_gather | solution.py:2115
  13.0 186.9 %all-gather.15.cloned.1.call-start = ((), (), s32[]{:S(2)}) async-start(), calls=%async_computation.7 | async-start | bytes 3538944 | tf_op jit(solution)/shard_map/all_gather | solution.py:2115
  13.6 380.7 %reduce-scatter.3.cloned.1.call-start = ((), (), s32[]{:S(2)}) async-start(), calls=%async_computation.2 | async-start | bytes 3538944 | tf_op jit(solution)/shard_map/reduce_scatter | solution.py:2155
  270.0 124.3 %reduce-scatter.5.cloned.1.call-start = ((), (), s32[]{:S(2)}) async-start(), calls=%async_computation.3 | async-start | bytes 3538944 | tf_op jit(solution)/shard_map/reduce_scatter | solution.py:2155
Sparse Core Ops, SparseCore 0:
  10.7 50.9 all-gather.8
  63.8 37.0 all-gather.10
  103.0 48.8 all-gather.12
  153.9 35.0 all-gather.14
  270.2 46.9 reduce-scatter.2
  319.4 47.3 reduce-scatter.4

commit v8 on v7

--- a/solution.py
+++ b/solution.py
@@ -1585,7 +1585,7 @@
     chunks = members // group
     chunk_bits = bits_of(chunks)
     hidden_units = win_s.shape[1]
-    tile = min(768, hidden_units)
+    tile = min(384, hidden_units)
     place = Place(grid_shape)
     weights = Weights(place, (win_ref, wout_ref), (win_s, wout_s), w_sems, weight_sems)
     weights.start_local()

time: 501 us -> 493 us (0.984)
  Pallas kernels: 472 us -> 464 us
    pallas_call x2, Pallas kernels: 76.5 us -> 69.4 us  [attention_backward(): pl.pallas_call(partial(backward_kernel, head_dim, grid_shape, spreads, re...]
  transfers between devices with their start and end apart: 6 -> 6, of which waited for: 1 -> 1; matrix products, arithmetic and copies ran while one was open for 1% -> 1% of each run, Pallas kernels for 62% -> 61%
where the time goes in v8:
time: 493 us; the launch traced here: 488 us
  Pallas kernels  464 us (94%)
  between operations  14.5 us (3%)
  local copies, waits for them, and re-layouts  6.71 us (1%)
    pallas_call x1, Pallas kernels, expert_backward(): pl.pallas_call(partial(expert_backward_kernel, grid_shape), in_specs=[vme...  78.3 us
    pallas_call x1, Pallas kernels, expert_forward(): pl.pallas_call(partial(expert_forward_kernel, grid_shape, gathers), in_sp...  71.3 us
    pallas_call x1, Pallas kernels, expert_both(): pl.pallas_call(partial(expert_both_kernel, grid_shape), in_specs=[vmem_sp...  70.1 us
    pallas_call x2, Pallas kernels, attention_backward(): pl.pallas_call(partial(backward_kernel, head_dim, grid_shape, spreads, re...  69.4 us
    pallas_call x1, Pallas kernels, start(): pl.pallas_call(partial(start_kernel, grid_shape), in_specs=[vmem_spec] *...  64.8 us
    pallas_call x1, Pallas kernels, final_sums(): pl.pallas_call(partial(final_kernel, grid_shape, layers, buckets_count),...  50.7 us
    pallas_call x2, Pallas kernels, attention_forward(): pl.pallas_call(partial(forward_kernel, head_dim, grid_shape, blocked, las...  47.5 us
    pallas_call x1, Pallas kernels, emit(): pl.pallas_call(partial(emit_kernel, table_shape), grid_spec=pltpu.Prefetc...  11.8 us
  transfers between devices with their start and end apart: 6, of which 1 were waited for; matrix products, arithmetic and copies ran while one was open for 1% of the time, Pallas kernels for 61%

profile of v8, /device:TPU:0, one launch (start us, length us, event | category | flops | bytes accessed | tf_op | source)
XLA Modules:
  0.0 488.0 jit_solution(692892694551396238)
XLA Ops:
  7.2 0.0 all-gather.9.cloned.1.call-start
  7.2 0.0 copy-start
  7.2 3.3 fusion.1
  10.6 0.0 all-gather.9.cloned.1.call-update
  10.6 0.0 all-gather.11.cloned.1.call-start
  10.6 0.0 copy-done
  10.6 1.6 fusion
  12.2 0.0 copy-start.4
  12.2 0.0 copy-start.3
  12.2 0.0 copy-start.1
  12.2 0.0 copy-start.2
  12.2 0.0 all-gather.11.cloned.1.call-update
  12.2 0.0 all-gather.13.cloned.1.call-start
  12.3 0.7 all-gather.13.cloned.1.call-update
  13.0 0.0 all-gather.15.cloned.1.call-start
  13.0 0.5 all-gather.15.cloned.1.call-update
  13.6 0.0 reduce-scatter.3.cloned.1.call-start
  13.6 0.0 copy-done.4
  13.6 0.0 copy-done.3
  13.6 0.6 pad.9
  14.2 0.6 pad.8.router_rows_ref
  14.8 0.0 copy-done.1
  14.8 0.0 copy-done.2
  14.8 0.6 fusion.2
  15.4 64.8 %start.1 = (bf16[4,768,768]{2,1,0:T(8,128)(2,1)}, bf16[8,768]{1,0:T(8,128)(2,1)}, bf16[1,4,208,384]{3,2,1,0:T(8,128)(2,1)}, bf16[12,512,512]{2,1,0:T(8,128)(2,1)...) custom-call(bf16[2,192,96]{2,1,0:T(8,128)(2,1)} %wq_ref.1, ...), custom_call_target="tpu_custom_call" | custom-call | flops 44999999488 | bytes 1048576 | tf_op jit(solution)/shard_map/start/pallas_call | solution.py:688
  80.2 19.9 %attention_forward.2 = (bf16[512,768]{1,0:T(8,128)(2,1)}, bf16[512,768]{1,0:T(8,128)(2,1)}, bf16[512,768]{1,0:T(8,128)(2,1)}, bf16[768,512]{1,0:T(8,128)(2,1)}, ...) custom-call(bf16[512,768]{1,0:T(8,128)(2,1)} %refs_9_.1, ...), custom_call_target="tpu_custom_call" | custom-call | flops 24999999488 | bytes 1048576 | tf_op jit(solution)/shard_map/attention_forward/pallas_call | solution.py:878
  100.2 0.0 all-gather.9.cloned.1.call-done
  100.2 0.7 all-gather.11.cloned.1.call-done
  100.9 71.3 %expert_forward.1 = (bf16[1024,768]{1,0:T(8,128)(2,1)}, f32[512,768]{1,0:T(8,128)}, f32[512,768]{1,0:T(8,128)}, bf16[2,2,4,2,208,384]{5,4,3,2,1,0:T(8,128)(2,1)}) custom-call(bf16[1024,768]{1,0:T(8,128)(2,1)} %get-tuple-element.98.sent_ref, s32[512,1]{1,0:T(8,128)} %get-tuple-element.92.slot_col_ref.refs_11_, ...), custom_call_target="tpu_custom_call" | custom-call | flops 74999996416 | bytes 1048576 | tf_op jit(solution)/shard_map/expert_forward/pallas_call | solution.py:1528
  172.2 27.6 %attention_forward.3 = (bf16[4,768,768]{2,1,0:T(8,128)(2,1)}, bf16[8,768]{1,0:T(8,128)(2,1)}, bf16[512,768]{1,0:T(8,128)(2,1)}, bf16[512,768]{1,0:T(8,128)(2,1)}...) custom-call(f32[512,768]{1,0:T(8,128)} %get-tuple-element.102.hidden, ...), custom_call_target="tpu_custom_call" | custom-call | flops 24999999488 | bytes 1048576 | tf_op jit(solution)/shard_map/attention_forward/pallas_call | solution.py:878
  199.8 0.0 all-gather.13.cloned.1.call-done
  199.8 0.0 all-gather.15.cloned.1.call-done
  199.8 70.1 %expert_both.1 = (bf16[1024,768]{1,0:T(8,128)(2,1)}, bf16[1024,768]{1,0:T(8,128)(2,1)}, bf16[2,768,768]{2,1,0:T(8,128)(2,1)}, bf16[2,768,768]{2,1,0:T(8,128)(2,1)}, bf16[512,8]{1,0:T(8,128)(2,1)}) custom-call(bf16[1024,768]{1,0:T(8,128)(2,1)} %get-tuple-element.104.sent_ref, f32[8,8,128]{2,1,0:T(8,128)} %get-tuple-element.105.gates_ref, ...), custom_call_target="tpu_custom_call" | custom-call | flops 85000003584 | bytes 1048576 | tf_op jit(solution)/shard_map/expert_both/pallas_call | solution.py:1709
  270.0 0.0 reduce-scatter.3.cloned.1.call-update
  270.0 0.0 reduce-scatter.5.cloned.1.call-start
  270.1 0.6 pad_add_fusion.at_ref
  270.6 0.0 reduce-scatter.5.cloned.1.call-update
  270.7 38.0 %attention_backward.2 = (f32[512,768]{1,0:T(8,128)}, bf16[2,2,4,2,192,384]{5,4,3,2,1,0:T(8,128)(2,1)}, f32[8,768]{1,0:T(8,128)}, f32[1,768]{1,0:T(1,128)}, f32[1...) custom-call(bf16[1024,768]{1,0:T(8,128)(2,1)} %get-tuple-element.110, ...), custom_call_target="tpu_custom_call" | custom-call | flops 32000000000 | bytes 1048576 | tf_op jit(solution)/shard_map/attention_backward/pallas_call | solution.py:1154
  308.7 78.3 %expert_backward.1 = (bf16[1024,768]{1,0:T(8,128)(2,1)}, bf16[2,768,768]{2,1,0:T(8,128)(2,1)}, bf16[2,768,768]{2,1,0:T(8,128)(2,1)}, bf16[4,96,384]{2,1,0:T(8,12...) custom-call(bf16[1024,768]{1,0:T(8,128)(2,1)} %get-tuple-element.122.d_sent_ref, ...), custom_call_target="tpu_custom_call" | custom-call | flops 85000003584 | bytes 1048576 | tf_op jit(solution)/shard_map/expert_backward/pallas_call | solution.py:1897
  387.0 0.0 reduce-scatter.3.cloned.1.call-done
  387.0 0.0 reduce-scatter.5.cloned.1.call-done
  387.1 31.4 %attention_backward.3 = (f32[512,768]{1,0:T(8,128)}, bf16[2,2,4,2,192,384]{5,4,3,2,1,0:T(8,128)(2,1)}, f32[8,768]{1,0:T(8,128)}, f32[1,768]{1,0:T(1,128)}, f32[1...) custom-call(bf16[1024,768]{1,0:T(8,128)(2,1)} %get-tuple-element.126, ...), custom_call_target="tpu_custom_call" | custom-call | flops 32000000000 | bytes 1048576 | tf_op jit(solution)/shard_map/attention_backward/pallas_call | solution.py:1154
  418.4 50.7 %final_sums.1 = (f32[2,192,384]{2,1,0:T(8,128)}, f32[32,768]{1,0:T(8,128)}, f32[512,768]{1,0:T(8,128)}, bf16[1,384,768]{2,1,0:T(8,128)(2,1)}) custom-call(bf16[4,96,384]{2,1,0:T(8,128)(2,1)} %get-tuple-element.138.refs_0_, bf16[1,4,96,384]{3,2,1,0:T(8,128)(2,1)} %get-tuple-element.139.refs_1_, f32[8,768]{1,0:T(8,128)} %get-tuple-element.140.refs_2_, ...), custom_call_target="tpu_custom_call" | custom-call | flops 60000002048 | bytes 1048576 | tf_op jit(solution)/shard_map/final_sums/pallas_call | solution.py:477
  469.1 11.8 %emit.1 = (f32[2,1,768,768]{3,2,1,0:T(8,128)}, f32[2,1,768,768]{3,2,1,0:T(8,128)}, f32[512,768]{1,0:T(8,128)}, f32[512,768]{1,0:T(8,128)}, f32[2,192,96]{2,1,0:T...) custom-call(s32[3]{0:T(128)} %pad_add_fusion.at_ref, ...), custom_call_target="tpu_custom_call" | custom-call | flops 7000000000 | bytes 1048576 | tf_op jit(solution)/shard_map/emit/pallas_call | solution.py:2030
  (1 shorter events, 0.0 us)
Async XLA Ops:
  7.2 93.0 %all-gather.9.cloned.1.call-start = ((), (), s32[]{:S(2)}) async-start(), calls=%async_computation.4 | async-start | bytes 3538944 | tf_op jit(solution)/shard_map/all_gather | solution.py:2115
  7.2 3.4 copy-start
  10.6 90.3 %all-gather.11.cloned.1.call-start = ((), (), s32[]{:S(2)}) async-start(), calls=%async_computation.5 | async-start | bytes 3538944 | tf_op jit(solution)/shard_map/all_gather | solution.py:2115
  12.2 1.4 copy-start.4
  12.2 1.4 copy-start.3
  12.2 2.6 copy-start.1
  12.2 2.6 copy-start.2
  12.2 187.6 %all-gather.13.cloned.1.call-start = ((), (), s32[]{:S(2)}) async-start(), calls=%async_computation.6 | async-start | bytes 3538944 | tf_op jit(solution)/shard_map/all_gather | solution.py:2115
  13.0 186.9 %all-gather.15.cloned.1.call-start = ((), (), s32[]{:S(2)}) async-start(), calls=%async_computation.7 | async-start | bytes 3538944 | tf_op jit(solution)/shard_map/all_gather | solution.py:2115
  13.6 373.5 %reduce-scatter.3.cloned.1.call-start = ((), (), s32[]{:S(2)}) async-start(), calls=%async_computation.2 | async-start | bytes 3538944 | tf_op jit(solution)/shard_map/reduce_scatter | solution.py:2155
  270.0 117.0 %reduce-scatter.5.cloned.1.call-start = ((), (), s32[]{:S(2)}) async-start(), calls=%async_computation.3 | async-start | bytes 3538944 | tf_op jit(solution)/shard_map/reduce_scatter | solution.py:2155
Sparse Core Ops, SparseCore 0:
  10.7 50.9 all-gather.8
  63.8 37.0 all-gather.10
  103.0 48.8 all-gather.12
  153.9 35.0 all-gather.14
  270.1 39.8 reduce-scatter.2
  312.3 47.3 reduce-scatter.4

commit v9 on v8

--- a/solution.py
+++ b/solution.py
@@ -1585,7 +1585,7 @@
     chunks = members // group
     chunk_bits = bits_of(chunks)
     hidden_units = win_s.shape[1]
-    tile = min(384, hidden_units)
+    tile = min(256, hidden_units)
     place = Place(grid_shape)
     weights = Weights(place, (win_ref, wout_ref), (win_s, wout_s), w_sems, weight_sems)
     weights.start_local()

time: 493 us -> 511 us (1.037)
  Pallas kernels: 464 us -> 482 us
    pallas_call x2, Pallas kernels: 69.4 us -> 80.9 us  [attention_backward(): pl.pallas_call(partial(backward_kernel, head_dim, grid_shape, spreads, re...]
    pallas_call x1, Pallas kernels: 78.3 us -> 86.5 us  [expert_backward(): pl.pallas_call(partial(expert_backward_kernel, grid_shape), in_specs=[vme...]
where the time goes in v9:
time: 511 us; the launch traced here: 506 us
  Pallas kernels  482 us (94%)
  between operations  14.5 us (3%)
  local copies, waits for them, and re-layouts  6.71 us (1%)
    pallas_call x1, Pallas kernels, expert_backward(): pl.pallas_call(partial(expert_backward_kernel, grid_shape), in_specs=[vme...  86.5 us
    pallas_call x2, Pallas kernels, attention_backward(): pl.pallas_call(partial(backward_kernel, head_dim, grid_shape, spreads, re...  80.9 us
    pallas_call x1, Pallas kernels, expert_forward(): pl.pallas_call(partial(expert_forward_kernel, grid_shape, gathers), in_sp...  71.3 us
    pallas_call x1, Pallas kernels, expert_both(): pl.pallas_call(partial(expert_both_kernel, grid_shape), in_specs=[vmem_sp...  69.9 us
    pallas_call x1, Pallas kernels, start(): pl.pallas_call(partial(start_kernel, grid_shape), in_specs=[vmem_spec] *...  64.8 us
    pallas_call x1, Pallas kernels, final_sums(): pl.pallas_call(partial(final_kernel, grid_shape, layers, buckets_count),...  49.2 us
    pallas_call x2, Pallas kernels, attention_forward(): pl.pallas_call(partial(forward_kernel, head_dim, grid_shape, blocked, las...  47.1 us
    pallas_call x1, Pallas kernels, emit(): pl.pallas_call(partial(emit_kernel, table_shape), grid_spec=pltpu.Prefetc...  11.8 us
  transfers between devices with their start and end apart: 6, of which 1 were waited for; matrix products, arithmetic and copies ran while one was open for 1% of the time, Pallas kernels for 61%

profile of v9, /device:TPU:0, one launch (start us, length us, event | category | flops | bytes accessed | tf_op | source)
XLA Modules:
  0.0 505.7 jit_solution(10659621113629299106)
XLA Ops:
  7.2 0.0 all-gather.9.cloned.1.call-start
  7.2 0.0 copy-start
  7.2 3.3 fusion.1
  10.6 0.0 all-gather.9.cloned.1.call-update
  10.6 0.0 all-gather.11.cloned.1.call-start
  10.6 0.0 copy-done
  10.6 1.6 fusion
  12.2 0.0 copy-start.4
  12.2 0.0 copy-start.3
  12.2 0.0 copy-start.1
  12.2 0.0 copy-start.2
  12.2 0.0 all-gather.11.cloned.1.call-update
  12.2 0.0 all-gather.13.cloned.1.call-start
  12.3 0.7 all-gather.13.cloned.1.call-update
  13.0 0.0 all-gather.15.cloned.1.call-start
  13.0 0.5 all-gather.15.cloned.1.call-update
  13.6 0.0 reduce-scatter.3.cloned.1.call-start
  13.6 0.0 copy-done.4
  13.6 0.0 copy-done.3
  13.6 0.6 pad.9
  14.2 0.6 pad.8.router_rows_ref
  14.8 0.0 copy-done.1
  14.8 0.0 copy-done.2
  14.8 0.6 fusion.2
  15.4 64.8 %start.1 = (bf16[4,768,768]{2,1,0:T(8,128)(2,1)}, bf16[8,768]{1,0:T(8,128)(2,1)}, bf16[1,4,208,384]{3,2,1,0:T(8,128)(2,1)}, bf16[12,512,512]{2,1,0:T(8,128)(2,1)...) custom-call(bf16[2,192,96]{2,1,0:T(8,128)(2,1)} %wq_ref.1, ...), custom_call_target="tpu_custom_call" | custom-call | flops 44999999488 | bytes 1048576 | tf_op jit(solution)/shard_map/start/pallas_call | solution.py:688
  80.2 19.9 %attention_forward.2 = (bf16[512,768]{1,0:T(8,128)(2,1)}, bf16[512,768]{1,0:T(8,128)(2,1)}, bf16[512,768]{1,0:T(8,128)(2,1)}, bf16[768,512]{1,0:T(8,128)(2,1)}, ...) custom-call(bf16[512,768]{1,0:T(8,128)(2,1)} %refs_9_.1, ...), custom_call_target="tpu_custom_call" | custom-call | flops 24999999488 | bytes 1048576 | tf_op jit(solution)/shard_map/attention_forward/pallas_call | solution.py:878
  100.2 0.0 all-gather.9.cloned.1.call-done
  100.2 0.7 all-gather.11.cloned.1.call-done
  100.9 71.3 %expert_forward.1 = (bf16[1024,768]{1,0:T(8,128)(2,1)}, f32[512,768]{1,0:T(8,128)}, f32[512,768]{1,0:T(8,128)}, bf16[2,2,4,2,208,384]{5,4,3,2,1,0:T(8,128)(2,1)}) custom-call(bf16[1024,768]{1,0:T(8,128)(2,1)} %get-tuple-element.98.sent_ref, s32[512,1]{1,0:T(8,128)} %get-tuple-element.92.slot_col_ref.refs_11_, ...), custom_call_target="tpu_custom_call" | custom-call | flops 74999996416 | bytes 1048576 | tf_op jit(solution)/shard_map/expert_forward/pallas_call | solution.py:1528
  172.2 27.2 %attention_forward.3 = (bf16[4,768,768]{2,1,0:T(8,128)(2,1)}, bf16[8,768]{1,0:T(8,128)(2,1)}, bf16[512,768]{1,0:T(8,128)(2,1)}, bf16[512,768]{1,0:T(8,128)(2,1)}...) custom-call(f32[512,768]{1,0:T(8,128)} %get-tuple-element.102.hidden, ...), custom_call_target="tpu_custom_call" | custom-call | flops 24999999488 | bytes 1048576 | tf_op jit(solution)/shard_map/attention_forward/pallas_call | solution.py:878
  199.4 0.0 all-gather.13.cloned.1.call-done
  199.4 0.0 all-gather.15.cloned.1.call-done
  199.5 69.9 %expert_both.1 = (bf16[1024,768]{1,0:T(8,128)(2,1)}, bf16[1024,768]{1,0:T(8,128)(2,1)}, bf16[2,768,768]{2,1,0:T(8,128)(2,1)}, bf16[2,768,768]{2,1,0:T(8,128)(2,1)}, bf16[512,8]{1,0:T(8,128)(2,1)}) custom-call(bf16[1024,768]{1,0:T(8,128)(2,1)} %get-tuple-element.104.sent_ref, f32[8,8,128]{2,1,0:T(8,128)} %get-tuple-element.105.gates_ref, ...), custom_call_target="tpu_custom_call" | custom-call | flops 85000003584 | bytes 1048576 | tf_op jit(solution)/shard_map/expert_both/pallas_call | solution.py:1709
  269.4 0.0 reduce-scatter.3.cloned.1.call-update
  269.4 0.0 reduce-scatter.5.cloned.1.call-start
  269.5 0.6 pad_add_fusion.at_ref
  270.1 0.0 reduce-scatter.5.cloned.1.call-update
  270.1 37.5 %attention_backward.2 = (f32[512,768]{1,0:T(8,128)}, bf16[2,2,4,2,192,384]{5,4,3,2,1,0:T(8,128)(2,1)}, f32[8,768]{1,0:T(8,128)}, f32[1,768]{1,0:T(1,128)}, f32[1...) custom-call(bf16[1024,768]{1,0:T(8,128)(2,1)} %get-tuple-element.110, ...), custom_call_target="tpu_custom_call" | custom-call | flops 32000000000 | bytes 1048576 | tf_op jit(solution)/shard_map/attention_backward/pallas_call | solution.py:1154
  307.6 86.5 %expert_backward.1 = (bf16[1024,768]{1,0:T(8,128)(2,1)}, bf16[2,768,768]{2,1,0:T(8,128)(2,1)}, bf16[2,768,768]{2,1,0:T(8,128)(2,1)}, bf16[4,96,384]{2,1,0:T(8,12...) custom-call(bf16[1024,768]{1,0:T(8,128)(2,1)} %get-tuple-element.122.d_sent_ref, ...), custom_call_target="tpu_custom_call" | custom-call | flops 85000003584 | bytes 1048576 | tf_op jit(solution)/shard_map/expert_backward/pallas_call | solution.py:1897
  394.1 0.0 reduce-scatter.3.cloned.1.call-done
  394.1 0.0 reduce-scatter.5.cloned.1.call-done
  394.1 43.4 %attention_backward.3 = (f32[512,768]{1,0:T(8,128)}, bf16[2,2,4,2,192,384]{5,4,3,2,1,0:T(8,128)(2,1)}, f32[8,768]{1,0:T(8,128)}, f32[1,768]{1,0:T(1,128)}, f32[1...) custom-call(bf16[1024,768]{1,0:T(8,128)(2,1)} %get-tuple-element.126, ...), custom_call_target="tpu_custom_call" | custom-call | flops 32000000000 | bytes 1048576 | tf_op jit(solution)/shard_map/attention_backward/pallas_call | solution.py:1154
  437.5 49.2 %final_sums.1 = (f32[2,192,384]{2,1,0:T(8,128)}, f32[32,768]{1,0:T(8,128)}, f32[512,768]{1,0:T(8,128)}, bf16[1,384,768]{2,1,0:T(8,128)(2,1)}) custom-call(bf16[4,96,384]{2,1,0:T(8,128)(2,1)} %get-tuple-element.138.refs_0_, bf16[1,4,96,384]{3,2,1,0:T(8,128)(2,1)} %get-tuple-element.139.refs_1_, f32[8,768]{1,0:T(8,128)} %get-tuple-element.140.refs_2_, ...), custom_call_target="tpu_custom_call" | custom-call | flops 60000002048 | bytes 1048576 | tf_op jit(solution)/shard_map/final_sums/pallas_call | solution.py:477
  486.8 11.8 %emit.1 = (f32[2,1,768,768]{3,2,1,0:T(8,128)}, f32[2,1,768,768]{3,2,1,0:T(8,128)}, f32[512,768]{1,0:T(8,128)}, f32[512,768]{1,0:T(8,128)}, f32[2,192,96]{2,1,0:T...) custom-call(s32[3]{0:T(128)} %pad_add_fusion.at_ref, ...), custom_call_target="tpu_custom_call" | custom-call | flops 7000000000 | bytes 1048576 | tf_op jit(solution)/shard_map/emit/pallas_call | solution.py:2030
  (1 shorter events, 0.0 us)
Async XLA Ops:
  7.2 93.0 %all-gather.9.cloned.1.call-start = ((), (), s32[]{:S(2)}) async-start(), calls=%async_computation.4 | async-start | bytes 3538944 | tf_op jit(solution)/shard_map/all_gather | solution.py:2115
  7.2 3.4 copy-start
  10.6 90.3 %all-gather.11.cloned.1.call-start = ((), (), s32[]{:S(2)}) async-start(), calls=%async_computation.5 | async-start | bytes 3538944 | tf_op jit(solution)/shard_map/all_gather | solution.py:2115
  12.2 1.4 copy-start.4
  12.2 1.4 copy-start.3
  12.2 2.6 copy-start.1
  12.2 2.6 copy-start.2
  12.2 187.2 %all-gather.13.cloned.1.call-start = ((), (), s32[]{:S(2)}) async-start(), calls=%async_computation.6 | async-start | bytes 3538944 | tf_op jit(solution)/shard_map/all_gather | solution.py:2115
  13.0 186.5 %all-gather.15.cloned.1.call-start = ((), (), s32[]{:S(2)}) async-start(), calls=%async_computation.7 | async-start | bytes 3538944 | tf_op jit(solution)/shard_map/all_gather | solution.py:2115
  13.6 380.5 %reduce-scatter.3.cloned.1.call-start = ((), (), s32[]{:S(2)}) async-start(), calls=%async_computation.2 | async-start | bytes 3538944 | tf_op jit(solution)/shard_map/reduce_scatter | solution.py:2155
  269.4 124.7 %reduce-scatter.5.cloned.1.call-start = ((), (), s32[]{:S(2)}) async-start(), calls=%async_computation.3 | async-start | bytes 3538944 | tf_op jit(solution)/shard_map/reduce_scatter | solution.py:2155
Sparse Core Ops, SparseCore 0:
  10.7 50.9 all-gather.8
  63.8 37.0 all-gather.10
  103.0 48.8 all-gather.12
  153.9 35.0 all-gather.14
  269.6 47.3 reduce-scatter.2
  319.2 47.3 reduce-scatter.4
